TPU v7x, 32 devices: a whole 2x2x4 slice. The times are simulated.
32 devices in a mesh: rep: 2 (over y), fsdp: 16 (over z, x, core).
Axes of the slice: x: 2, y: 2, z: 4, core: 2. Of those that a mesh axis runs over, the one named last changes fastest.
Arguments:
- tokens: bfloat16 [8192, 1536], P(('rep', 'fsdp')), may hold values from -6 to 6
- doc_ids: int32 [8192], P(('rep', 'fsdp')), may hold values from 0 to 127, never falling along the last dimension, each value on 1 to 256 neighbouring positions
- norm_gain: bfloat16 [1536], P('fsdp'), may hold values from 0.5 to 1.5
- qkv_weight: bfloat16 [1536, 4608], P(None, 'fsdp'), may hold values from -0.15625 to 0.15625
- group_gain: bfloat16 [1536], P('fsdp'), may hold values from 0.5 to 1.5
- out_weight: bfloat16 [1536, 1536], P(None, 'fsdp'), may hold values from -0.15625 to 0.15625
- ffn_gain: bfloat16 [1536], P('fsdp'), may hold values from 0.5 to 1.5
- gate_weight: bfloat16 [1536, 4096], P(None, 'fsdp'), may hold values from -0.15625 to 0.15625
- up_weight: bfloat16 [1536, 4096], P(None, 'fsdp'), may hold values from -0.15625 to 0.15625
- down_weight: bfloat16 [4096, 1536], P('fsdp'), may hold values from -0.09375 to 0.09375
- conv_kernel: float32 [16, 66], replicated, may hold values from -1.5 to 1.5
- head_mix: float32 [8, 2, 2], replicated, may hold values from 0.25 to 1
- out_grad: float32 [8192, 1536], P(('rep', 'fsdp')), may hold values from -6 to 6
Outputs:
- layer_out: bfloat16 [8192, 1536], P(('rep', 'fsdp'))
- input_grad: float32 [8192, 1536], P(('rep', 'fsdp'))
- norm_gain_grad: float32 [1536], P('fsdp')
- qkv_weight_grad: float32 [1536, 4608], P(None, 'fsdp')
- group_gain_grad: float32 [1536], P('fsdp')
- out_weight_grad: float32 [1536, 1536], P(None, 'fsdp')
- ffn_gain_grad: float32 [1536], P('fsdp')
- gate_weight_grad: float32 [1536, 4096], P(None, 'fsdp')
- up_weight_grad: float32 [1536, 4096], P(None, 'fsdp')
- down_weight_grad: float32 [4096, 1536], P('fsdp')
- conv_kernel_grad: float32 [16, 66], replicated
- head_mix_grad: float32 [8, 2, 2], replicated
Inputs may be any that keep to these rules, and one draw needn't show every extreme that they name: `doc_ids`: document numbers never fall along the tokens; each document has 1 to 256 tokens.
All inputs are finite; a program needn't handle non-finite values.
Results may differ from a plain program's by a relative error of at most 0.018.
The roundings to bfloat16 on the way count: a program that leaves them out, or rounds other values in their place, can miss the bound.
Values may be sent and summed in bfloat16 or wider, within the bound.
No kernel may reach another device: no remote copies, remote signals or barrier semaphores. Data moves between devices by JAX's collectives and lax.ppermute only.
A program may use at most 320 MiB of HBM per device.

v0:
```python
import jax
import jax.numpy as jnp
from jax import lax
from jax.sharding import PartitionSpec as P

D = 1536
H = 16
HD = 96
CQ = 6
CK = 11


def rms_norm(values, gain):
    return values * lax.rsqrt(jnp.mean(values * values, axis=-1, keepdims=True) + 1e-05) * gain


def group_norm(values, gain):
    centre = values - jnp.mean(values, axis=-1, keepdims=True)
    spread = jnp.mean(centre * centre, axis=-1, keepdims=True)
    return centre * lax.rsqrt(spread + 1e-05) * gain


def swiglu(gate, upper):
    return jax.nn.silu(gate) * upper


def mixed_probs(logits, row_doc, row_pos, key_doc, kernel, mixing):
    head_count, ext_count, key_count = logits.shape
    row_lag = CQ - 1
    row_count = ext_count - row_lag
    key_left = CK // 2
    key_place = jnp.arange(key_count, dtype=jnp.int32)
    allowed = (key_place[None, :] <= row_pos[:, None]) & (key_doc[None, :] == row_doc[:, None])
    masked = jnp.where(allowed[None], logits, 0.0)
    padded = jnp.pad(masked, ((0, 0), (0, 0), (key_left, CK - 1 - key_left)))
    out_doc = row_doc[row_lag:]
    summed = jnp.zeros((head_count, row_count, key_count), jnp.float32)
    for shift in range(CQ):
        same_doc = (row_doc[row_lag - shift : row_lag - shift + row_count] == out_doc).astype(
            jnp.float32
        )
        partial_sum = jnp.zeros((head_count, row_count, key_count), jnp.float32)
        for column in range(CK):
            offset = 2 * key_left - column
            partial_sum = (
                partial_sum
                + kernel[:, shift * CK + column][:, None, None]
                * padded[
                    :, row_lag - shift : row_lag - shift + row_count, offset : offset + key_count
                ]
            )
        summed = summed + same_doc[None, :, None] * partial_sum
    scores = jnp.where(allowed[None, row_lag:], summed, -1e30)
    row_max = jnp.max(scores, axis=-1, keepdims=True)
    weights = jnp.exp(scores - row_max)
    attend = weights / jnp.sum(weights, axis=-1, keepdims=True)
    grouped = attend.reshape(head_count // 2, 2, row_count, key_count)
    mixed = jnp.einsum("gcd,gdrk->gcrk", mixing, grouped, precision=lax.Precision.HIGHEST)
    return mixed.reshape(head_count, row_count, key_count)


def padded_rows(queries, docs):
    row_lag = CQ - 1
    seq_len = queries.shape[0]
    q_pad = jnp.pad(queries, ((row_lag, row_lag), (0, 0), (0, 0)))
    doc_pad = jnp.concatenate(
        [jnp.full((row_lag,), -1, jnp.int32), docs, jnp.full((row_lag,), -2, jnp.int32)]
    )
    pos_pad = jnp.arange(-row_lag, seq_len + row_lag, dtype=jnp.int32)
    return (q_pad, doc_pad, pos_pad)


def attention_forward(queries, key_vecs, values, docs, kernel, mixing):
    seq_len = queries.shape[0]
    block_len = min(512, seq_len)
    row_lag = CQ - 1
    scale = HD ** (-0.5)
    q_pad, doc_pad, pos_pad = padded_rows(queries, docs)
    logits = (
        jnp.einsum(
            "qhd,khd->hqk",
            q_pad[0 : block_len + row_lag],
            key_vecs,
            preferred_element_type=jnp.float32,
        )
        * scale
    )
    mixed = mixed_probs(
        logits,
        doc_pad[0 : block_len + row_lag],
        pos_pad[0 : block_len + row_lag],
        docs,
        kernel,
        mixing,
    )
    outputs = jnp.einsum(
        "hqk,khd->qhd", mixed.astype(jnp.bfloat16), values, preferred_element_type=jnp.float32
    )
    return outputs


def attention_backward(queries, key_vecs, values, docs, kernel, mixing, grad_att):
    seq_len = queries.shape[0]
    key_count = key_vecs.shape[0]
    block_len = min(512, seq_len)
    row_lag = CQ - 1
    scale = HD ** (-0.5)
    q_pad, doc_pad, pos_pad = padded_rows(queries, docs)
    grad_pad = jnp.pad(grad_att, ((0, row_lag), (0, 0), (0, 0)))
    kern_pairs = kernel.reshape(H // 2, 2, CQ * CK)
    mix_pairs = mixing.reshape(H // 2, 1, 2, 2)
    ext_len = block_len + 2 * row_lag
    logits = jnp.einsum("qhd,khd->hqk", q_pad, key_vecs, preferred_element_type=jnp.float32) * scale
    main_doc = doc_pad[0 : block_len + row_lag]
    main_pos = pos_pad[0 : block_len + row_lag]
    tail_doc = doc_pad[block_len:ext_len]
    tail_pos = pos_pad[block_len:ext_len]

    def both_parts(block_logits, kern_main, mix_main, kern_tail, mix_tail):
        main_part = mixed_probs(
            block_logits[:, : block_len + row_lag], main_doc, main_pos, docs, kern_main, mix_main
        )
        tail_part = mixed_probs(
            block_logits[:, block_len:], tail_doc, tail_pos, docs, kern_tail, mix_tail
        )
        return (main_part, tail_part)

    grad_main = jnp.einsum("qhd,khd->hqk", grad_att, values, preferred_element_type=jnp.float32)
    grad_tail = jnp.einsum(
        "qhd,khd->hqk",
        grad_pad[block_len : block_len + row_lag],
        values,
        preferred_element_type=jnp.float32,
    )

    def pair_back(item):
        pair_logits, pair_kern, pair_mix, pair_main, pair_tail = item
        (main_mixed, tail_mixed), pullback = jax.vjp(
            both_parts, pair_logits, pair_kern, pair_mix, pair_kern, pair_mix
        )
        grad_logits, kern_part, mix_part, kern_unused, mix_unused = pullback((pair_main, pair_tail))
        return (main_mixed, grad_logits, kern_part, mix_part)

    pair_out = lax.map(
        pair_back,
        (
            logits.reshape(H // 2, 2, ext_len, key_count),
            kern_pairs,
            mix_pairs,
            grad_main.reshape(H // 2, 2, block_len, key_count),
            grad_tail.reshape(H // 2, 2, row_lag, key_count),
        ),
    )
    main_mixed = pair_out[0].reshape(H, block_len, key_count)
    grad_logits = pair_out[1].reshape(H, ext_len, key_count)
    grad_values = jnp.einsum(
        "hqk,qhd->khd",
        main_mixed.astype(jnp.bfloat16),
        grad_att,
        preferred_element_type=jnp.float32,
    )
    logit_low = grad_logits[:, row_lag : row_lag + block_len].astype(jnp.bfloat16)
    grad_queries = (
        jnp.einsum("hqk,khd->qhd", logit_low, key_vecs, preferred_element_type=jnp.float32) * scale
    )
    grad_keys = (
        jnp.einsum("hqk,qhd->khd", logit_low, queries, preferred_element_type=jnp.float32) * scale
    )
    grad_kernel = pair_out[2].reshape(H, CQ * CK)
    grad_mixing = pair_out[3].reshape(H // 2, 2, 2)
    return (grad_queries, grad_keys, grad_values, grad_kernel, grad_mixing)


def on_device(
    tokens,
    doc_ids,
    norm_gain,
    qkv_weight,
    group_gain,
    out_weight,
    ffn_gain,
    gate_weight,
    up_weight,
    down_weight,
    conv_kernel,
    head_mix,
    out_grad,
):
    seq_len = tokens.shape[0]
    attn_set = (
        lax.all_gather(norm_gain, "fsdp", axis=0, tiled=True),
        lax.all_gather(qkv_weight, "fsdp", axis=1, tiled=True),
        lax.all_gather(group_gain, "fsdp", axis=0, tiled=True),
        lax.all_gather(out_weight, "fsdp", axis=1, tiled=True),
    )
    inputs = tokens.astype(jnp.float32)
    normed, norm_pull = jax.vjp(rms_norm, inputs, attn_set[0].astype(jnp.float32))
    normed_low = normed.astype(jnp.bfloat16)
    packed = jnp.dot(normed_low, attn_set[1], preferred_element_type=jnp.float32).astype(
        jnp.bfloat16
    )
    queries = packed[:, :D].reshape(seq_len, H, HD)
    key_vecs = packed[:, D : 2 * D].reshape(seq_len, H, HD)
    values = packed[:, 2 * D :].reshape(seq_len, H, HD)
    attended = attention_forward(queries, key_vecs, values, doc_ids, conv_kernel, head_mix)
    grouped, group_pull = jax.vjp(
        group_norm, attended, attn_set[2].astype(jnp.float32).reshape(H, HD)
    )
    grouped_low = grouped.reshape(seq_len, D).astype(jnp.bfloat16)
    middle = inputs + jnp.dot(grouped_low, attn_set[3], preferred_element_type=jnp.float32)
    ffn_set = (
        lax.all_gather(ffn_gain, "fsdp", axis=0, tiled=True),
        lax.all_gather(gate_weight, "fsdp", axis=1, tiled=True),
        lax.all_gather(up_weight, "fsdp", axis=1, tiled=True),
        lax.all_gather(down_weight, "fsdp", axis=0, tiled=True),
    )
    second, second_pull = jax.vjp(rms_norm, middle, ffn_set[0].astype(jnp.float32))
    second_low = second.astype(jnp.bfloat16)
    gate = jnp.dot(second_low, ffn_set[1], preferred_element_type=jnp.float32)
    upper = jnp.dot(second_low, ffn_set[2], preferred_element_type=jnp.float32)
    hidden, swiglu_pull = jax.vjp(swiglu, gate, upper)
    hidden_low = hidden.astype(jnp.bfloat16)
    layer_out = (
        middle + jnp.dot(hidden_low, ffn_set[3], preferred_element_type=jnp.float32)
    ).astype(jnp.bfloat16)
    ffn_back = (
        lax.all_gather(ffn_gain, "fsdp", axis=0, tiled=True),
        lax.all_gather(gate_weight, "fsdp", axis=1, tiled=True),
        lax.all_gather(up_weight, "fsdp", axis=1, tiled=True),
        lax.all_gather(down_weight, "fsdp", axis=0, tiled=True),
    )
    grad_ffn_low = out_grad.astype(jnp.bfloat16)
    grad_hidden = jnp.einsum(
        "sd,fd->sf", grad_ffn_low, ffn_back[3], preferred_element_type=jnp.float32
    )
    grad_down = jnp.einsum(
        "sf,sd->fd", hidden_low, grad_ffn_low, preferred_element_type=jnp.float32
    )
    grad_gate, grad_upper = swiglu_pull(grad_hidden)
    gate_low = grad_gate.astype(jnp.bfloat16)
    upper_low = grad_upper.astype(jnp.bfloat16)
    grad_second = jnp.einsum(
        "sf,df->sd", gate_low, ffn_back[1], preferred_element_type=jnp.float32
    ) + jnp.einsum("sf,df->sd", upper_low, ffn_back[2], preferred_element_type=jnp.float32)
    grad_wgate = jnp.einsum("sd,sf->df", second_low, gate_low, preferred_element_type=jnp.float32)
    grad_wup = jnp.einsum("sd,sf->df", second_low, upper_low, preferred_element_type=jnp.float32)
    grad_mid_norm, grad_gain_two = second_pull(grad_second)
    ffn_sums = (
        lax.psum_scatter(grad_gain_two, "fsdp", scatter_dimension=0, tiled=True),
        lax.psum_scatter(grad_wgate, "fsdp", scatter_dimension=1, tiled=True),
        lax.psum_scatter(grad_wup, "fsdp", scatter_dimension=1, tiled=True),
        lax.psum_scatter(grad_down, "fsdp", scatter_dimension=0, tiled=True),
    )
    grad_middle = out_grad + grad_mid_norm
    attn_back = (
        lax.all_gather(norm_gain, "fsdp", axis=0, tiled=True),
        lax.all_gather(qkv_weight, "fsdp", axis=1, tiled=True),
        lax.all_gather(group_gain, "fsdp", axis=0, tiled=True),
        lax.all_gather(out_weight, "fsdp", axis=1, tiled=True),
    )
    branch_low = grad_middle.astype(jnp.bfloat16)
    grad_grouped = jnp.einsum(
        "se,de->sd", branch_low, attn_back[3], preferred_element_type=jnp.float32
    )
    grad_wout = jnp.einsum("sd,se->de", grouped_low, branch_low, preferred_element_type=jnp.float32)
    grad_attended, grad_gain_group = group_pull(grad_grouped.reshape(seq_len, H, HD))
    grad_queries, grad_keys, grad_values, grad_kernel, grad_mixing = attention_backward(
        queries,
        key_vecs,
        values,
        doc_ids,
        conv_kernel,
        head_mix,
        grad_attended.astype(jnp.bfloat16),
    )
    grad_packed = jnp.concatenate(
        [
            grad_queries.reshape(seq_len, D),
            grad_keys.reshape(seq_len, D),
            grad_values.reshape(seq_len, D),
        ],
        axis=1,
    ).astype(jnp.bfloat16)
    grad_normed = jnp.einsum(
        "se,de->sd", grad_packed, attn_back[1], preferred_element_type=jnp.float32
    )
    grad_wqkv = jnp.einsum("sd,se->de", normed_low, grad_packed, preferred_element_type=jnp.float32)
    grad_in_norm, grad_gain_one = norm_pull(grad_normed)
    input_grad = grad_middle + grad_in_norm
    attn_sums = (
        lax.psum_scatter(grad_gain_one, "fsdp", scatter_dimension=0, tiled=True),
        lax.psum_scatter(grad_wqkv, "fsdp", scatter_dimension=1, tiled=True),
        lax.psum_scatter(grad_gain_group.reshape(D), "fsdp", scatter_dimension=0, tiled=True),
        lax.psum_scatter(grad_wout, "fsdp", scatter_dimension=1, tiled=True),
    )
    totals = (
        lax.psum(attn_sums[0].astype(jnp.bfloat16), "rep").astype(jnp.float32),
        lax.psum(attn_sums[1].astype(jnp.bfloat16), "rep").astype(jnp.float32),
        lax.psum(attn_sums[2].astype(jnp.bfloat16), "rep").astype(jnp.float32),
        lax.psum(attn_sums[3].astype(jnp.bfloat16), "rep").astype(jnp.float32),
        lax.psum(ffn_sums[0].astype(jnp.bfloat16), "rep").astype(jnp.float32),
        lax.psum(ffn_sums[1].astype(jnp.bfloat16), "rep").astype(jnp.float32),
        lax.psum(ffn_sums[2].astype(jnp.bfloat16), "rep").astype(jnp.float32),
        lax.psum(ffn_sums[3].astype(jnp.bfloat16), "rep").astype(jnp.float32),
    )
    mixer = lax.psum((grad_kernel, grad_mixing), ("rep", "fsdp"))
    return (
        layer_out,
        input_grad,
        totals[0],
        totals[1],
        totals[2],
        totals[3],
        totals[4],
        totals[5],
        totals[6],
        totals[7],
        mixer[0],
        mixer[1],
    )


def solution(mesh):
    placed = (
        P(("rep", "fsdp"), None),
        P(("rep", "fsdp")),
        P("fsdp"),
        P(None, "fsdp"),
        P("fsdp"),
        P(None, "fsdp"),
        P("fsdp"),
        P(None, "fsdp"),
        P(None, "fsdp"),
        P("fsdp", None),
        P(),
        P(),
        P(("rep", "fsdp"), None),
    )
    return jax.shard_map(
        on_device,
        mesh=mesh,
        in_specs=placed,
        out_specs=(
            P(("rep", "fsdp"), None),
            P(("rep", "fsdp"), None),
            P("fsdp"),
            P(None, "fsdp"),
            P("fsdp"),
            P(None, "fsdp"),
            P("fsdp"),
            P(None, "fsdp"),
            P(None, "fsdp"),
            P("fsdp", None),
            P(),
            P(),
        ),
        check_vma=False,
    )
```

profile of v0, /device:TPU:0, one launch (start us, length us, event | category | flops | bytes accessed | tf_op | source)
XLA Modules:
  0.0 1865.3 jit_solution(4741139551104197545)
XLA Ops:
  15.2 65.4 %all-reduce.214 = (bf16[1536]{0:T(1024)(128)(2,1)S(1)}, bf16[1536]{0:T(1024)(128)(2,1)S(1)}, bf16[1536]{0:T(1024)(128)(2,1)S(1)}) all-reduce(bf16[1536]{0:T(1024)(128)(2,1)S(1)} %dynamic-update-slice, bf16[1536]{0:T(1024)(128)(2,1)S(1)} %dynamic-update-slice.1, ...), channel_id=1, replica_groups=mesh['rep'=2,'fsdp'=16] {'fsdp'}, use_global_device_ids=true, to_apply=%add.206 | all-reduce | flops 4608 | bytes 18432
  88.9 35.2 %all-gather.6.cloned.1.call-done = bf16[1536,4608]{0,1:T(8,128)(2,1)} async-done(((bf16[1536,288]{0,1:T(8,128)(2,1)}), bf16[1536,4608]{0,1:T(8,128)(2,1)}) %all-gather.6.cloned.1.call-update) | async-done | bytes 14155792 | tf_op jit(solution)/shard_map/all_gather | solution.py:192
  124.2 15.5 convolution_convert_fusion
  147.9 260.6 %fusion.373 = (f32[16,256]{1,0:T(8,128)S(1)}, f32[16,256,256]{2,1,0:T(8,128)}) fusion(f32[16,261,256]{2,1,0:T(8,128)} %multiply_select_fusion, f32[16]{0:T(128)S(1)} %get-tuple-element.493, f32[16]{0:T(128)S(1)} %get-tuple-element.429, f32[16]{0:T(128)S(1)} %get-tuple-element.430, f32[16]{0:T(128)S(1)} %get-tuple-element.431, ...), kind=kOutput, calls=%fused_computation.990 | output fusion | flops 145752320 | bytes 33776768 | tf_op jit(solution)/shard_map/sub | solution.py:55
  411.1 18.0 fusion.301
  456.1 32.0 %all-gather.14.cloned.1.call-done = bf16[4096,1536]{1,0:T(8,128)(2,1)} async-done(((bf16[256,1536]{1,0:T(8,128)(2,1)}), bf16[4096,1536]{1,0:T(8,128)(2,1)}) %all-gather.14.cloned.1.call-update) | async-done | bytes 12582928 | tf_op jit(solution)/shard_map/all_gather | solution.py:215
  488.1 10.8 multiply_convert_fusion
  521.1 16.7 fusion.378
  537.9 14.8 fusion.379
  570.0 10.5 fusion.330
  581.2 851.3 %while.18 = (s32[]{:T(128)}, bf16[8,2,256,256]{3,2,1,0:T(8,128)(2,1)}, bf16[8,2,266,256]{3,2,1,0:T(8,128)(2,1)}, f32[8,2,66]{2,1,0:T(2,128)}, f32[8,1,2,2]{3,2,1...) while((s32[]{:T(128)}, ...), condition=%wide.region_86.87_spmd, body=%wide.region_9.86_spmd.sunk | while | flops 68294704 | bytes 108565712 | solution.py:144
  611.3 11.0 fusion.439
  661.5 20.3 %pad_add_fusion.16 = f32[2,261,266]{2,1,0:T(8,128)S(1)} fusion(f32[2,256,256]{2,1,0:T(8,128)} %get-tuple-element.1326, f32[2,256,256]{2,1,0:T(8,128)} %get-tuple-element.1327, f32[2,256,256]{2,1,0:T(8,128)} %get-tuple-element.1328, f32[2,256,256]{2,1,0:T(8,128)} %get-tuple-element.1329, f32[2,256,256]{2,1,0:T(8,128)} %get-tuple-element.1330, ...), kind=kLoop, calls=%fused_computation.63.clone.1 | loop fusion | flops 8192268 | bytes 32012688 | tf_op jit(solution)/shard_map/while/body/eval_jaxpr/transpose(jvp())/add_any | solution.py:48
  717.7 11.0 fusion.439
  765.6 18.0 pad_add_fusion.16
  819.7 11.0 fusion.439
  867.7 18.0 pad_add_fusion.16
  922.0 11.0 fusion.439
  970.0 18.2 pad_add_fusion.16
  1024.1 11.0 fusion.439
  1072.0 17.9 pad_add_fusion.16
  1125.7 11.0 fusion.439
  1176.0 17.9 pad_add_fusion.16
  1230.0 11.0 fusion.439
  1277.9 18.1 pad_add_fusion.16
  1332.0 11.0 fusion.439
  1380.0 17.9 pad_add_fusion.16
  1438.3 14.0 fusion.324
  1462.0 258.6 %reduce-scatter.6.cloned.1.call-done = f32[1536,288]{0,1:T(8,128)} async-done(((f32[1536,4608]{0,1:T(8,128)}), f32[1536,288]{0,1:T(8,128)}) %reduce-scatter.6.cloned.1.call-update) | async-done | bytes 1769488 | tf_op jit(solution)/shard_map/reduce_scatter | solution.py:292
  1723.9 11.7 fusion.312
  1735.6 58.5 %all-reduce.213 = (bf16[1536]{0:T(1024)(128)(2,1)S(1)}, bf16[1536]{0:T(1024)(128)(2,1)S(1)}, bf16[1536]{0:T(1024)(128)(2,1)S(1)}) all-reduce(f32[1536]{0:T(1024)S(1)} %get-tuple-element.426, f32[1536]{0:T(1024)S(1)} %reshape.809, f32[1536]{0:T(1024)S(1)} %copy-done.161), channel_id=2, replica_groups=mesh['rep'=2,'fsdp'=16] {'fsdp'}, use_global_device_ids=true, to_apply=%region_89.90.clone | all-reduce | flops 4608 | bytes 27648
  1801.0 37.4 %all-reduce.212 = (f32[16,66]{1,0:T(8,128)}, f32[8,2,2]{0,2,1:T(2,128)}) all-reduce(f32[16,66]{1,0:T(8,128)S(1)} %bitcast.617, f32[8,2,2]{0,2,1:T(2,128)S(1)} %bitcast.616), channel_id=1, replica_groups=mesh['rep'=2,'fsdp'=16] {'rep','fsdp'}, use_global_device_ids=true, to_apply=%region_107.108 | all-reduce | flops 1088 | bytes 8704 | tf_op jit(solution)/shard_map/psum | solution.py:306
  (2605 shorter events, 711.9 us)
Async XLA Ops:
  7.2 81.1 %copy-start.109 = (s32[256]{0:T(256)S(1)}, s32[256]{0:T(256)}, u32[]{:S(2)}) copy-start(s32[256]{0:T(256)} %param.16) | copy-start | bytes 3076
  7.2 79.2 %copy-start.2 = (f32[16,66]{1,0:T(8,128)S(1)}, f32[16,66]{1,0:T(8,128)}, u32[]{:S(2)}) copy-start(f32[16,66]{1,0:T(8,128)} %param.25) | copy-start | bytes 12676
  7.2 80.8 %copy-start.16 = (bf16[256,1536]{1,0:T(8,128)(2,1)S(1)}, bf16[256,1536]{1,0:T(8,128)(2,1)}, u32[]{:S(2)}) copy-start(bf16[256,1536]{1,0:T(8,128)(2,1)} %param.15) | copy-start | bytes 2359300
  7.2 117.0 %all-gather.6.cloned.1.call-start = ((), (), s32[]{:S(2)}) async-start(), calls=%async_computation.5 | async-start | bytes 15040512 | tf_op jit(solution)/shard_map/all_gather | solution.py:192
  7.9 422.9 %all-gather.8.cloned.1.call-start = ((), (), s32[]{:S(2)}) async-start(), calls=%async_computation.6 | async-start | bytes 5013504 | tf_op jit(solution)/shard_map/all_gather | solution.py:194
  8.7 427.7 %all-gather.10.cloned.1.call-start = ((), (), s32[]{:S(2)}) async-start(), calls=%async_computation.7 | async-start | bytes 13369344 | tf_op jit(solution)/shard_map/all_gather | solution.py:213
  9.4 436.8 %all-gather.12.cloned.1.call-start = ((), (), s32[]{:S(2)}) async-start(), calls=%async_computation.8 | async-start | bytes 13369344 | tf_op jit(solution)/shard_map/all_gather | solution.py:214
  10.0 478.1 %all-gather.14.cloned.1.call-start = ((), (), s32[]{:S(2)}) async-start(), calls=%async_computation.9 | async-start | bytes 13369344 | tf_op jit(solution)/shard_map/all_gather | solution.py:215
  10.6 1441.8 %reduce-scatter.8.cloned.1.call-start = ((), (), s32[]{:S(2)}) async-start(), calls=%async_computation.11 | async-start | bytes 10027008 | tf_op jit(solution)/shard_map/reduce_scatter | solution.py:294
  141.8 287.7 %copy-start.8 = (bf16[256,1536]{0,1:T(8,128)(2,1)}, bf16[256,1536]{0,1:T(8,128)(2,1)S(1)}, u32[]{:S(2)}) copy-start(bf16[256,1536]{0,1:T(8,128)(2,1)S(1)} %copy.89) | copy-start | bytes 2359300
  144.9 263.6 %copy-start.11 = (bf16[256,16,96]{2,0,1:T(8,128)(2,1)}, bf16[256,16,96]{2,0,1:T(8,128)(2,1)S(1)}, u32[]{:S(2)}) copy-start(bf16[256,16,96]{2,0,1:T(8,128)(2,1)S(1)} %copy.91) | copy-start | bytes 2359300
  520.8 933.4 %reduce-scatter.10.cloned.1.call-start = ((), (), s32[]{:S(2)}) async-start(), calls=%async_computation.12 | async-start | bytes 26738688 | tf_op jit(solution)/shard_map/reduce_scatter | solution.py:250
  537.9 918.7 %reduce-scatter.12.cloned.1.call-start = ((), (), s32[]{:S(2)}) async-start(), calls=%async_computation.13 | async-start | bytes 26738688 | tf_op jit(solution)/shard_map/reduce_scatter | solution.py:251
  552.7 906.7 %reduce-scatter.14.cloned.1.call-start = ((), (), s32[]{:S(2)}) async-start(), calls=%async_computation.14 | async-start | bytes 26738688 | tf_op jit(solution)/shard_map/reduce_scatter | solution.py:252
  580.5 1140.1 %reduce-scatter.6.cloned.1.call-start = ((), (), s32[]{:S(2)}) async-start(), calls=%async_computation.10 | async-start | bytes 30081024 | tf_op jit(solution)/shard_map/reduce_scatter | solution.py:292
  607.2 46.1 %copy-start.55 = (f32[2]{0:T(128)}, f32[2]{0:T(128)S(1)}, u32[]{:S(2)}) copy-start(f32[2]{0:T(128)S(1)} %get-tuple-element.1281) | copy-start | bytes 28 | tf_op jit(solution)/shard_map/while
  607.2 46.1 %copy-start.57 = (f32[2]{0:T(128)}, f32[2]{0:T(128)S(1)}, u32[]{:S(2)}) copy-start(f32[2]{0:T(128)S(1)} %get-tuple-element.1282) | copy-start | bytes 28 | tf_op jit(solution)/shard_map/while
  609.2 44.1 %copy-start.59 = (f32[2]{0:T(128)}, f32[2]{0:T(128)S(1)}, u32[]{:S(2)}) copy-start(f32[2]{0:T(128)S(1)} %get-tuple-element.1283) | copy-start | bytes 28 | tf_op jit(solution)/shard_map/while
  609.2 44.1 %copy-start.61 = (f32[2]{0:T(128)}, f32[2]{0:T(128)S(1)}, u32[]{:S(2)}) copy-start(f32[2]{0:T(128)S(1)} %get-tuple-element.1284) | copy-start | bytes 28 | tf_op jit(solution)/shard_map/while
  609.3 44.1 %copy-start.63 = (f32[2]{0:T(128)}, f32[2]{0:T(128)S(1)}, u32[]{:S(2)}) copy-start(f32[2]{0:T(128)S(1)} %get-tuple-element.1285) | copy-start | bytes 28 | tf_op jit(solution)/shard_map/while
  1121.7 46.4 %copy-start.55 = (f32[2]{0:T(128)}, f32[2]{0:T(128)S(1)}, u32[]{:S(2)}) copy-start(f32[2]{0:T(128)S(1)} %get-tuple-element.1281) | copy-start | bytes 28 | tf_op jit(solution)/shard_map/while
  1121.7 46.4 %copy-start.57 = (f32[2]{0:T(128)}, f32[2]{0:T(128)S(1)}, u32[]{:S(2)}) copy-start(f32[2]{0:T(128)S(1)} %get-tuple-element.1282) | copy-start | bytes 28 | tf_op jit(solution)/shard_map/while
  1123.7 44.4 %copy-start.59 = (f32[2]{0:T(128)}, f32[2]{0:T(128)S(1)}, u32[]{:S(2)}) copy-start(f32[2]{0:T(128)S(1)} %get-tuple-element.1283) | copy-start | bytes 28 | tf_op jit(solution)/shard_map/while
  1123.7 44.4 %copy-start.61 = (f32[2]{0:T(128)}, f32[2]{0:T(128)S(1)}, u32[]{:S(2)}) copy-start(f32[2]{0:T(128)S(1)} %get-tuple-element.1284) | copy-start | bytes 28 | tf_op jit(solution)/shard_map/while
  1123.7 44.4 %copy-start.63 = (f32[2]{0:T(128)}, f32[2]{0:T(128)S(1)}, u32[]{:S(2)}) copy-start(f32[2]{0:T(128)S(1)} %get-tuple-element.1285) | copy-start | bytes 28 | tf_op jit(solution)/shard_map/while
  1123.7 44.4 %copy-start.65 = (f32[2]{0:T(128)}, f32[2]{0:T(128)S(1)}, u32[]{:S(2)}) copy-start(f32[2]{0:T(128)S(1)} %get-tuple-element.1286) | copy-start | bytes 28 | tf_op jit(solution)/shard_map/while
  1452.3 396.7 %all-reduce.219.cloned.1.call-start = ((), (), s32[]{:S(2)}) async-start(), calls=%async_computation.15 | async-start | bytes 7077888 | tf_op jit(solution)/shard_map/psum | solution.py:298
  1459.4 264.4 %copy-start.156 = (f32[16,96]{1,0:T(8,128)S(1)}, f32[16,96]{1,0:T(8,128)}, u32[]{:S(2)}) copy-start(f32[16,96]{1,0:T(8,128)} %get-tuple-element.422) | copy-start | bytes 18436
  1723.9 77.0 %copy-start.164 = (f32[8,1,2,2]{3,2,1,0:T(2,128)S(1)}, f32[8,1,2,2]{3,2,1,0:T(2,128)}, u32[]{:S(2)}) copy-start(f32[8,1,2,2]{3,2,1,0:T(2,128)} %get-tuple-element.1718) | copy-start | bytes 388
  1723.9 77.1 %copy-start.163 = (f32[8,2,66]{2,1,0:T(2,128)S(1)}, f32[8,2,66]{2,1,0:T(2,128)}, u32[]{:S(2)}) copy-start(f32[8,2,66]{2,1,0:T(2,128)} %get-tuple-element.1717) | copy-start | bytes 12676
  1723.9 114.5 %copy-start.160 = (f32[256]{0:T(256)S(1)}, f32[256]{0:T(256)}, u32[]{:S(2)}) copy-start(f32[256]{0:T(256)} %copy-done.159) | copy-start | bytes 3076
  1723.9 114.5 %copy-start.4 = (f32[256,1536]{1,0:T(8,128)S(1)}, f32[256,1536]{1,0:T(8,128)}, u32[]{:S(2)}) copy-start(f32[256,1536]{1,0:T(8,128)} %copy-done.3) | copy-start | bytes 4718596
  (967 other events, 16429.8 us)
Sparse Core Ops, SparseCore 0:
  10.3 113.7 all-gather.5
  126.5 51.6 all-gather.7
  180.3 102.4 all-gather.9
  284.8 102.1 all-gather.11
  389.1 98.9 all-gather.13
  520.9 109.5 reduce-scatter.7
  635.2 243.5 reduce-scatter.9
  883.4 242.8 reduce-scatter.11
  1131.0 242.9 reduce-scatter.13
  1452.4 268.1 reduce-scatter.5
  1724.0 94.9 all-reduce.218
where the time goes:
time: 1880 us; the launch traced here: 1870 us
  other arithmetic  950 us (51%)
  waiting for transfers between devices  329 us (18%)
  matrix products  277 us (15%)
  blocking collectives  166 us (9%)
  local copies, waits for them, and re-layouts  81.8 us (4%)
  loops' own time  43.5 us (2%)
    sub x1, other arithmetic, mixed_probs(): weights = jnp.exp(scores - row_max)  261 us
    reduce_scatter x1, waiting for transfers between devices, on_device(): lax.psum_scatter(grad_wqkv, 'fsdp', scatter_dimension=1, tiled=True)  259 us
    mul x80, other arithmetic, mixed_probs(): kernel[:, shift * CK + column][:, None, None]  153 us
    add_any x16, other arithmetic, mixed_probs(): padded[:, row_lag - shift:row_lag - shift + row_count, offset:offset + ke...  152 us
    reduce_sum x40, other arithmetic, mixed_probs(): kernel[:, shift * CK + column][:, None, None]  136 us
    unnamed x2, blocking collectives  124 us
    dot_general x33, matrix products, mixed_probs(): jnp.einsum('gcd,gdrk->gcrk', mixing, grouped, precision=lax.Precision.HIG...  112 us
    reduce_max x16, other arithmetic, mixed_probs(): row_max = jnp.max(scores, axis=-1, keepdims=True)  99.6 us
  transfers between devices with their start and end apart: 11, of which 3 were waited for; matrix products, arithmetic and copies ran while one was open for 67% of the time, Pallas kernels for 0%

commit v1 on v0

v1 whole, which is shorter than its diff:
```python
import functools
import jax
import jax.numpy as jnp
from jax import lax
from jax.experimental import pallas as pl
from jax.experimental.pallas import tpu as pltpu
from jax.sharding import PartitionSpec as P

D = 1536
H = 16
HD = 96
CQ = 6
CK = 11
NEG = -1e30
PAIRS = H // 2
PW = 2 * HD
BF = jnp.bfloat16
F32 = jnp.float32


def dot(a, b, ca, cb):
    return lax.dot_general(a, b, (((ca,), (cb,)), ((), ())), preferred_element_type=F32)


def split(v):
    hi = v.astype(BF)
    return hi, (v - hi.astype(F32)).astype(BF)


def taps_kernel(fwd_ref, bwd_ref, th_ref, tl_ref, tt_ref):
    n = th_ref.shape[-1]
    row = lax.broadcasted_iota(jnp.int32, (n, n), 0)
    col = lax.broadcasted_iota(jnp.int32, (n, n), 1)
    near = jnp.abs(row - col) <= CK // 2
    for a in range(CQ):
        wide = jnp.broadcast_to(fwd_ref[0, a : a + 1, :], (n, n))
        band = jnp.where(near, pltpu.roll(wide, 0, 1, stride=1, stride_axis=0), 0.0)
        hi, lo = split(band)
        th_ref[0, a * n : (a + 1) * n, :] = hi
        tl_ref[0, a * n : (a + 1) * n, :] = lo
        wide = jnp.broadcast_to(bwd_ref[0, a : a + 1, :], (n, n))
        band = jnp.where(near, pltpu.roll(wide, 0, 1, stride=1, stride_axis=0), 0.0)
        tt_ref[0, a * n : (a + 1) * n, :] = band.astype(BF)


def band_taps(kernel, n):
    taps = kernel.reshape(H, CQ, CK)
    half = CK // 2
    fwd = jnp.zeros((H, 8, n), F32)
    fwd = fwd.at[:, :CQ, : half + 1].set(taps[:, :, half:]).at[:, :CQ, n - half :].set(taps[:, :, :half])
    flip = taps[:, :, ::-1]
    bwd = jnp.zeros((H, 8, n), F32)
    bwd = bwd.at[:, :CQ, : half + 1].set(flip[:, :, half:]).at[:, :CQ, n - half :].set(flip[:, :, :half])
    row = pl.BlockSpec((1, 8, n), lambda h: (h, 0, 0))
    out = pl.BlockSpec((1, CQ * n, n), lambda h: (h, 0, 0))
    shape = jax.ShapeDtypeStruct((H, CQ * n, n), BF)
    return pl.pallas_call(
        taps_kernel,
        grid=(H,),
        in_specs=[row, row],
        out_specs=[out, out, out],
        out_shape=[shape, shape, shape],
        cost_estimate=pl.CostEstimate(flops=H * 12 * n * n, bytes_accessed=6 * H * CQ * n * n, transcendentals=0),
    )(fwd, bwd)


def doc_masks(drow_ref, dcol_ref, allow_ref, same_ref):
    n = allow_ref.shape[0]
    row = lax.broadcasted_iota(jnp.int32, (n, n), 0)
    col = lax.broadcasted_iota(jnp.int32, (n, n), 1)
    same = dcol_ref[...] == drow_ref[...]
    same_ref[...] = jnp.where(same, 1.0, 0.0)
    allow_ref[...] = jnp.where(same & (col <= row), 1.0, 0.0)


def attend_kernel(
    mix_ref, q_ref, k_ref, v_ref, th_ref, tl_ref, drow_ref, dcol_ref, gain_ref,
    prob_ref, att_ref, grp_ref, allow_ref, same_ref, pad_ref, xh_ref, xl_ref,
):
    g = pl.program_id(0)
    n = q_ref.shape[1]

    @pl.when(g == 0)
    def _():
        doc_masks(drow_ref, dcol_ref, allow_ref, same_ref)
        pad_ref[0:8, :] = jnp.zeros((8, n), F32)

    for e in range(2):
        q = q_ref[e * HD : (e + 1) * HD, :]
        k = k_ref[e * HD : (e + 1) * HD, :]
        logits = dot(q, k, 0, 0) * (HD ** (-0.5))
        pad_ref[8 : 8 + n, :] = jnp.where(allow_ref[...] > 0, logits, 0.0)
        for a in range(CQ):
            part = jnp.where(same_ref[...] > 0, pad_ref[8 - a : 8 - a + n, :], 0.0)
            hi, lo = split(part)
            xh_ref[:, a * n : (a + 1) * n] = hi
            xl_ref[:, a * n : (a + 1) * n] = lo
        conv = (
            dot(xh_ref[...], th_ref[e], 1, 0)
            + dot(xh_ref[...], tl_ref[e], 1, 0)
            + dot(xl_ref[...], th_ref[e], 1, 0)
        )
        scores = jnp.where(allow_ref[...] > 0, conv, NEG)
        weights = jnp.exp(scores - jnp.max(scores, axis=1, keepdims=True))
        prob_ref[e] = weights * (1.0 / jnp.sum(weights, axis=1, keepdims=True))
    for c in range(2):
        mixed = (mix_ref[g, 2 * c] * prob_ref[0] + mix_ref[g, 2 * c + 1] * prob_ref[1]).astype(BF)
        att = dot(v_ref[c * HD : (c + 1) * HD, :], mixed, 1, 1)
        att_ref[c * HD : (c + 1) * HD, :] = att
        centre = att - jnp.mean(att, axis=0, keepdims=True)
        spread = jnp.mean(centre * centre, axis=0, keepdims=True)
        grp_ref[c * HD : (c + 1) * HD, :] = (
            centre * lax.rsqrt(spread + 1e-05) * gain_ref[c * HD : (c + 1) * HD, :]
        ).astype(BF)


def attend(packed_t, docs, th, tl, mix, gain):
    n = packed_t.shape[1]
    blk = lambda off: pl.BlockSpec((PW, n), lambda g: (g + off, 0))
    tap = pl.BlockSpec((2, CQ * n, n), lambda g: (g, 0, 0))
    whole = lambda s: pl.BlockSpec(s, lambda g: (0, 0))
    return pl.pallas_call(
        attend_kernel,
        grid=(PAIRS,),
        in_specs=[
            pl.BlockSpec(memory_space=pltpu.SMEM),
            blk(0), blk(PAIRS), blk(2 * PAIRS), tap, tap,
            whole((1, n)), whole((n, 1)),
            pl.BlockSpec((PW, 1), lambda g: (g, 0)),
        ],
        out_specs=[pl.BlockSpec((2, n, n), lambda g: (g, 0, 0)), blk(0), blk(0)],
        out_shape=[
            jax.ShapeDtypeStruct((H, n, n), F32),
            jax.ShapeDtypeStruct((D, n), F32),
            jax.ShapeDtypeStruct((D, n), BF),
        ],
        scratch_shapes=[
            pltpu.VMEM((n, n), F32), pltpu.VMEM((n, n), F32), pltpu.VMEM((n + 8, n), F32),
            pltpu.VMEM((n, CQ * n), BF), pltpu.VMEM((n, CQ * n), BF),
        ],
        compiler_params=pltpu.CompilerParams(vmem_limit_bytes=40 * 2**20),
        cost_estimate=pl.CostEstimate(flops=42 * H * n * n * n, bytes_accessed=34 * 2**20, transcendentals=H * n * n),
    )(mix.reshape(PAIRS, 4), packed_t, packed_t, packed_t, th, tl, docs.reshape(1, n), docs.reshape(n, 1), gain)


def attend_back_kernel(
    mix_ref, q_ref, k_ref, v_ref, tt_ref, drow_ref, dcol_ref, gain_ref, prob_ref, att_ref, dgrp_ref,
    dq_ref, dk_ref, dv_ref, dgain_ref, dtap_ref, dmix_ref,
    allow_ref, same_ref, pad_ref, y_ref, dm_ref,
):
    g = pl.program_id(0)
    n = q_ref.shape[1]
    scale = HD ** (-0.5)

    @pl.when(g == 0)
    def _():
        doc_masks(drow_ref, dcol_ref, allow_ref, same_ref)
        pad_ref[n : n + 8, :] = jnp.zeros((8, n), F32)

    for c in range(2):
        rows = slice(c * HD, (c + 1) * HD)
        att = att_ref[rows, :]
        centre = att - jnp.mean(att, axis=0, keepdims=True)
        rstd = lax.rsqrt(jnp.mean(centre * centre, axis=0, keepdims=True) + 1e-05)
        hat = centre * rstd
        dgrp = dgrp_ref[rows, :]
        dgain_ref[rows, :] = jnp.sum(dgrp * hat, axis=1, keepdims=True)
        dhat = dgrp * gain_ref[rows, :]
        datt = rstd * (
            dhat
            - jnp.mean(dhat, axis=0, keepdims=True)
            - hat * jnp.mean(dhat * hat, axis=0, keepdims=True)
        )
        datt = datt.astype(BF)
        mixed = (mix_ref[g, 2 * c] * prob_ref[0] + mix_ref[g, 2 * c + 1] * prob_ref[1]).astype(BF)
        dv_ref[rows, :] = dot(datt, mixed, 1, 0).astype(BF)
        dmixed = dot(datt, v_ref[rows, :], 0, 0)
        dm_ref[c] = dmixed
        for e in range(2):
            dmix_ref[0, 2 * c + e : 2 * c + e + 1, :] = jnp.sum(dmixed * prob_ref[e], axis=0, keepdims=True)
    dmix_ref[0, 4:8, :] = jnp.zeros((4, n), F32)
    row = lax.broadcasted_iota(jnp.int32, (128, 128), 0)
    col = lax.broadcasted_iota(jnp.int32, (128, 128), 1)
    off = col - row
    half = CK // 2
    for e in range(2):
        rows = slice(e * HD, (e + 1) * HD)
        q = q_ref[rows, :]
        k = k_ref[rows, :]
        allowed = allow_ref[...] > 0
        masked_t = dot(k, q, 0, 0) * scale
        prob = prob_ref[e]
        dprob = mix_ref[g, e] * dm_ref[0] + mix_ref[g, 2 + e] * dm_ref[1]
        pad_ref[0:n, :] = prob * (dprob - jnp.sum(prob * dprob, axis=1, keepdims=True))
        for a in range(CQ):
            y_ref[:, a * n : (a + 1) * n] = jnp.where(same_ref[...] > 0, pad_ref[a : a + n, :], 0.0).astype(BF)
        dlog = jnp.where(allowed, dot(y_ref[...], tt_ref[e], 1, 0), 0.0).astype(BF)
        dq_ref[rows, :] = (dot(k, dlog, 1, 1) * scale).astype(BF)
        dk_ref[rows, :] = (dot(q, dlog, 1, 0) * scale).astype(BF)
        krow = lax.broadcasted_iota(jnp.int32, (n, n), 0)
        qcol = lax.broadcasted_iota(jnp.int32, (n, n), 1)
        masked_t = jnp.where((same_ref[...] > 0) & (krow <= qcol), masked_t, 0.0).astype(BF)
        for a in range(CQ):
            full = dot(masked_t, y_ref[:, a * n : (a + 1) * n], 1, 0)
            fold = jnp.zeros((128, 128), F32)
            blocks = n // 128
            for r in range(blocks):
                fold = fold + full[r * 128 : (r + 1) * 128, r * 128 : (r + 1) * 128]
            fold = jnp.where(jnp.abs(off) <= half, fold, 0.0)
            for r in range(blocks - 1):
                up = full[r * 128 : (r + 1) * 128, (r + 1) * 128 : (r + 2) * 128]
                down = full[(r + 1) * 128 : (r + 2) * 128, r * 128 : (r + 1) * 128]
                fold = fold + jnp.where(off <= half - 128, up, 0.0) + jnp.where(off >= 128 - half, down, 0.0)
            lined = fold[0:8, :]
            for t in range(1, 16):
                lined = lined + pltpu.roll(fold[8 * t : 8 * t + 8, :], 128 - 8 * t, 1)
            dtap_ref[e, 8 * a : 8 * a + 8, :] = lined


def attend_back(packed_t, docs, tt, mix, gain, prob, att, dgrp):
    n = packed_t.shape[1]
    blk = lambda off: pl.BlockSpec((PW, n), lambda g: (g + off, 0))
    whole = lambda s: pl.BlockSpec(s, lambda g: (0, 0))
    thin = pl.BlockSpec((PW, 1), lambda g: (g, 0))
    dq, dk, dv, dgain, dtap, dmix = pl.pallas_call(
        attend_back_kernel,
        grid=(PAIRS,),
        in_specs=[
            pl.BlockSpec(memory_space=pltpu.SMEM),
            blk(0), blk(PAIRS), blk(2 * PAIRS),
            pl.BlockSpec((2, CQ * n, n), lambda g: (g, 0, 0)),
            whole((1, n)), whole((n, 1)), thin,
            pl.BlockSpec((2, n, n), lambda g: (g, 0, 0)),
            blk(0), blk(0),
        ],
        out_specs=[
            blk(0), blk(0), blk(0), thin,
            pl.BlockSpec((2, 8 * CQ, 128), lambda g: (g, 0, 0)),
            pl.BlockSpec((1, 8, n), lambda g: (g, 0, 0)),
        ],
        out_shape=[
            jax.ShapeDtypeStruct((D, n), BF),
            jax.ShapeDtypeStruct((D, n), BF),
            jax.ShapeDtypeStruct((D, n), BF),
            jax.ShapeDtypeStruct((D, 1), F32),
            jax.ShapeDtypeStruct((H, 8 * CQ, 128), F32),
            jax.ShapeDtypeStruct((PAIRS, 8, n), F32),
        ],
        scratch_shapes=[
            pltpu.VMEM((n, n), F32), pltpu.VMEM((n, n), F32), pltpu.VMEM((n + 8, n), F32),
            pltpu.VMEM((n, CQ * n), BF), pltpu.VMEM((2, n, n), F32),
        ],
        compiler_params=pltpu.CompilerParams(vmem_limit_bytes=40 * 2**20),
        cost_estimate=pl.CostEstimate(flops=40 * H * n * n * n, bytes_accessed=24 * 2**20, transcendentals=0),
    )(mix.reshape(PAIRS, 4), packed_t, packed_t, packed_t, tt, docs.reshape(1, n), docs.reshape(n, 1), gain, prob, att, dgrp)
    lane = jnp.arange(128)[None, None, :] - jnp.arange(8)[None, :, None]
    tap = jnp.arange(CK)[:, None, None] - CK // 2
    pick = (jnp.remainder(lane - tap, 128) == 0).astype(F32)
    dtap = jnp.sum(dtap.reshape(H, CQ, 1, 8, 128) * pick, axis=(3, 4))
    dmix = jnp.sum(dmix[:, :4, :], axis=2)
    return dq, dk, dv, dgain[:, 0], dtap.reshape(H, CQ * CK), dmix.reshape(PAIRS, 2, 2)


def rms_norm(values, gain):
    return values * lax.rsqrt(jnp.mean(values * values, axis=-1, keepdims=True) + 1e-05) * gain


def rms_back(values, gain, grad):
    rstd = lax.rsqrt(jnp.mean(values * values, axis=-1, keepdims=True) + 1e-05)
    hat = values * rstd
    dhat = grad * gain
    dvalues = rstd * (dhat - hat * jnp.mean(dhat * hat, axis=-1, keepdims=True))
    return dvalues, jnp.sum(grad * hat, axis=0)


class Slice:
    def __init__(self, reps, shards):
        self.axes = ("rep", "fsdp")
        self.shards = shards
        self.lines = [[4 * o + i for o in range(shards // 4)] for i in range(4)]
        places = [(y, f) for y in range(reps) for f in range(shards)]

        def perm(move):
            out = []
            for y, f in places:
                to = move(y, f)
                out.append((y * shards + f, to[0] * shards + to[1]))
            return out

        self.hops = {
            (dy, di): perm(lambda y, f, dy=dy, di=di: (y ^ dy, f ^ di))
            for dy in range(2)
            for di in range(4)
        }
        self.corner = perm(lambda y, f: (y, f ^ 2) if f & 1 else (1 - y, f))
        self.doubling = []
        bit = 1
        while bit < shards:
            self.doubling.append((bit, perm(lambda y, f, bit=bit: (y, f ^ bit))))
            bit *= 2
        self.rep = lax.axis_index("rep")
        self.fsdp = lax.axis_index("fsdp")
        self.odd = (self.fsdp & 1) == 1

    def hop(self, value, dy, di):
        return lax.ppermute(value, self.axes, self.hops[dy, di])

    def gather_line(self, value):
        return lax.all_gather(value, "fsdp", axis=0, tiled=True, axis_index_groups=self.lines)

    def scatter_line(self, value):
        return lax.psum_scatter(
            value.astype(BF), "fsdp", scatter_dimension=0, tiled=True, axis_index_groups=self.lines
        )

    def gather_small(self, value):
        for bit, perm in self.doubling:
            other = lax.ppermute(value, self.axes, perm)
            high = (self.fsdp & bit) != 0
            value = jnp.concatenate(
                [jnp.where(high, other, value), jnp.where(high, value, other)], axis=0
            )
        return value

    def gather_plane(self, value):
        along_x = self.hop(value, 0, 2)
        along_y = self.hop(value, 1, 0)
        corner = lax.ppermute(jnp.where(self.odd, along_y, along_x), self.axes, self.corner)
        near = jnp.concatenate([value, along_x, along_y, corner], axis=0)
        return near, self.hop(near, 0, 1)

    def scatter_plane(self, near, far):
        rows = near.shape[0] // 4
        total = near + self.hop(far.astype(BF), 0, 1)
        blocks = [total[b * rows : (b + 1) * rows] for b in range(4)]
        corner = lax.ppermute(blocks[3].astype(BF), self.axes, self.corner).astype(F32)
        along_x = blocks[1] + jnp.where(self.odd, 0.0, corner)
        along_y = blocks[2] + jnp.where(self.odd, corner, 0.0)
        return (
            blocks[0]
            + self.hop(along_x.astype(BF), 0, 2).astype(F32)
            + self.hop(along_y.astype(BF), 1, 0).astype(F32)
        )

    def both_halves(self, half):
        other = self.hop(half, 1, 0)
        first = self.rep == 0
        return jnp.concatenate(
            [jnp.where(first, half, other), jnp.where(first, other, half)], axis=0
        ).astype(F32)

    def own_half(self, shard):
        rows = shard.shape[0] // 2
        return lax.dynamic_slice_in_dim(shard, self.rep * rows, rows, axis=0)


def on_device(
    reps,
    shards,
    tokens,
    doc_ids,
    norm_gain,
    qkv_weight,
    group_gain,
    out_weight,
    ffn_gain,
    gate_weight,
    up_weight,
    down_weight,
    conv_kernel,
    head_mix,
    out_grad,
):
    net = Slice(reps, shards)
    lines = shards // 4
    n = tokens.shape[0]
    cols = 3 * D // shards // 2
    wide = gate_weight.shape[1] // 2

    w_qkv = net.gather_line(net.own_half(qkv_weight.T))
    x_near, x_far = net.gather_plane(tokens)
    gains = net.gather_small(jnp.stack([norm_gain, group_gain, ffn_gain])[None])
    gains = gains.transpose(1, 0, 2).reshape(3, D).astype(F32)
    w_down = net.gather_line(net.own_half(down_weight))
    w_gu = net.gather_line(
        jnp.concatenate([net.own_half(gate_weight.T), net.own_half(up_weight.T)], axis=0)
    )
    w_out = lax.all_gather(out_weight.T, "fsdp", axis=0, tiled=True)
    taps_hi, taps_lo, taps_back = band_taps(conv_kernel, n)
    inputs = tokens.astype(F32)

    normed = [rms_norm(b.astype(F32), gains[0]).astype(BF) for b in (x_near, x_far)]
    parts = [dot(w_qkv, b, 1, 1).astype(BF) for b in normed]
    place = net.rep * 4 + (net.fsdp & 3)
    packed_t = jnp.zeros((lines, 4, 2, cols, n), BF)
    for dy in range(2):
        for di in range(4):
            block = 2 * dy + di // 2
            piece = parts[di % 2][:, block * n : (block + 1) * n]
            if dy or di:
                piece = net.hop(piece, dy, di)
            source = place ^ (4 * dy + di)
            packed_t = lax.dynamic_update_slice(
                packed_t, piece.reshape(lines, 1, 1, cols, n), (0, source & 3, source >> 2, 0, 0)
            )
    packed_t = packed_t.reshape(3 * D, n)
    group_col = gains[1].reshape(D, 1)
    probs, attended, grouped = attend(packed_t, doc_ids, taps_hi, taps_lo, head_mix, group_col)

    middle = inputs + dot(grouped, w_out, 0, 1)
    second_low = rms_norm(middle, gains[2]).astype(BF)
    second = net.gather_plane(second_low)
    d_ffn = net.gather_plane(out_grad.astype(BF))

    hidden, d_gu, d_hid = [], [], [dot(b, w_down, 1, 1) for b in d_ffn]
    for s in range(2):
        gu = dot(second[s], w_gu, 1, 1).reshape(-1, lines, 2, wide)
        gate, upper = gu[:, :, 0], gu[:, :, 1]
        dh = d_hid[s].reshape(-1, lines, wide)
        sig = jax.nn.sigmoid(gate)
        act = gate * sig
        hidden.append((act * upper).astype(BF).reshape(-1, lines * wide))
        d_gate = (dh * upper * (sig * (1.0 + gate * (1.0 - sig)))).astype(BF)
        d_up = (dh * act).astype(BF)
        d_gu.append(jnp.stack([d_gate, d_up], axis=2).reshape(-1, lines * 2 * wide))
    d_second = net.scatter_plane(*[dot(b, w_gu, 1, 0) for b in d_gu])
    ffn_out = net.scatter_plane(*[dot(b, w_down, 1, 0) for b in hidden])
    layer_out = (middle + ffn_out).astype(BF)
    g_down = dot(hidden[0], d_ffn[0], 0, 0) + dot(hidden[1], d_ffn[1], 0, 0)
    g_gu = dot(d_gu[0], second[0], 0, 0) + dot(d_gu[1], second[1], 0, 0)
    g_down = net.both_halves(net.scatter_line(g_down))
    g_gu = net.scatter_line(g_gu)
    g_gate = net.both_halves(g_gu[:wide]).T
    g_up = net.both_halves(g_gu[wide:]).T

    d_norm, g_ffn_gain = rms_back(middle, gains[2], d_second)
    d_middle = out_grad + d_norm
    branch = d_middle.astype(BF)
    d_grouped = dot(w_out, branch, 0, 1)
    g_out = dot(branch, grouped, 0, 1).astype(BF)
    g_out = lax.psum_scatter(g_out, "fsdp", scatter_dimension=0, tiled=True)
    g_out = (g_out.astype(F32) + net.hop(g_out, 1, 0).astype(F32)).T
    d_q, d_k, d_v, g_group, g_taps, g_mix = attend_back(
        packed_t, doc_ids, taps_back, head_mix, group_col, probs, attended, d_grouped
    )

    d_packed = jnp.concatenate([d_q, d_k, d_v], axis=0).reshape(lines, 4, 2, cols, n)
    pieces = [[], []]
    for dy in range(2):
        for di in range(4):
            target = place ^ (4 * dy + di)
            piece = lax.dynamic_slice(
                d_packed, (0, target & 3, target >> 2, 0, 0), (lines, 1, 1, cols, n)
            ).reshape(lines * cols, n)
            if dy or di:
                piece = net.hop(piece, dy, di)
            pieces[di % 2].append(piece)
    d_packed = [jnp.concatenate(p, axis=1) for p in pieces]
    d_normed = net.scatter_plane(*[dot(b, w_qkv, 0, 0) for b in d_packed])
    g_qkv = dot(d_packed[0], normed[0], 1, 0) + dot(d_packed[1], normed[1], 1, 0)
    g_qkv = net.both_halves(net.scatter_line(g_qkv)).T
    d_in, g_norm = rms_back(inputs, gains[0], d_normed)
    input_grad = d_middle + d_in

    small = lax.psum(
        jnp.concatenate([g_norm, g_group, g_ffn_gain, g_taps.reshape(-1), g_mix.reshape(-1)]),
        ("rep", "fsdp"),
    )
    part = D // shards
    gain_grads = [
        lax.dynamic_slice_in_dim(small, b * D + net.fsdp * part, part) for b in range(3)
    ]
    g_taps = small[3 * D : 3 * D + H * CQ * CK].reshape(H, CQ * CK)
    g_mix = small[3 * D + H * CQ * CK :].reshape(PAIRS, 2, 2)
    return (
        layer_out,
        input_grad,
        gain_grads[0],
        g_qkv,
        gain_grads[1],
        g_out,
        gain_grads[2],
        g_gate,
        g_up,
        g_down,
        g_taps,
        g_mix,
    )


def solution(mesh):
    placed = (
        P(("rep", "fsdp"), None),
        P(("rep", "fsdp")),
        P("fsdp"),
        P(None, "fsdp"),
        P("fsdp"),
        P(None, "fsdp"),
        P("fsdp"),
        P(None, "fsdp"),
        P(None, "fsdp"),
        P("fsdp", None),
        P(),
        P(),
        P(("rep", "fsdp"), None),
    )
    return jax.shard_map(
        functools.partial(on_device, mesh.shape["rep"], mesh.shape["fsdp"]),
        mesh=mesh,
        in_specs=placed,
        out_specs=(
            P(("rep", "fsdp"), None),
            P(("rep", "fsdp"), None),
            P("fsdp"),
            P(None, "fsdp"),
            P("fsdp"),
            P(None, "fsdp"),
            P("fsdp"),
            P(None, "fsdp"),
            P(None, "fsdp"),
            P("fsdp", None),
            P(),
            P(),
        ),
        check_vma=False,
    )
```

time: 1880 us -> 609 us (0.32)
  other arithmetic: 950 us -> 64.8 us
  matrix products: 277 us -> 105 us
  blocking collectives: 166 us -> 38.8 us
  waiting for transfers between devices: 329 us -> 218 us
  Pallas kernels: 0 us -> 57.6 us
  starting transfers between devices: 1.13 us -> 48.3 us
  loops' own time: 43.5 us -> 0 us
  local copies, waits for them, and re-layouts: 81.8 us -> 56 us
    sub x1 -> x2, other arithmetic: 261 us -> 0.01 us  [the longest x1 0.01 us: attend_back(): lane = jnp.arange(128)[None, None, :] - jnp.arange(8)[None, :, None]]
    reduce_scatter x5 -> x4, waiting for transfers between devices: 259 us -> 26.1 us  [the longest x1 26.1 us: on_device(): g_out = lax.psum_scatter(g_out, 'fsdp', scatter_dimension=0, tiled=True)]
    ppermute x0 -> x47, waiting for transfers between devices: none -> 174 us  [the longest x37 141 us: hop(): return lax.ppermute(value, self.axes, self.hops[dy, di])]
    dot_general x56 -> x21, matrix products: 277 us -> 105 us  [dot(): lax.dot_general(a, b, (((ca,), (cb,)), ((), ())), preferred_element_type=...]
    mul x80 -> x0, other arithmetic: 153 us -> none  [mixed_probs(): kernel[:, shift * CK + column][:, None, None]]
    add_any x16 -> x0, other arithmetic: 152 us -> none  [mixed_probs(): padded[:, row_lag - shift:row_lag - shift + row_count, offset:offset + ke...]
    reduce_sum x91 -> x5, other arithmetic: 150 us -> 7.01 us  [the longest x2 4.94 us: rms_back(): return (dvalues, jnp.sum(grad * hat, axis=0))]
    unnamed x2 -> x0, blocking collectives: 124 us -> none
  transfers between devices with their start and end apart: 11 -> 55, of which waited for: 3 -> 25; matrix products, arithmetic and copies ran while one was open for 67% -> 33% of each run, Pallas kernels for 0% -> 10%
where the time goes in v1:
time: 609 us; the launch traced here: 604 us
  waiting for transfers between devices  218 us (36%)
  matrix products  105 us (17%)
  other arithmetic  64.8 us (11%)
  Pallas kernels  57.6 us (9%)
  local copies, waits for them, and re-layouts  56 us (9%)
  starting transfers between devices  48.3 us (8%)
  blocking collectives  38.8 us (6%)
  between operations  15.6 us (3%)
    ppermute x37, waiting for transfers between devices, hop(): return lax.ppermute(value, self.axes, self.hops[dy, di])  141 us
    dot_general x21, matrix products, dot(): lax.dot_general(a, b, (((ca,), (cb,)), ((), ())), preferred_element_type=...  105 us
    psum x1, blocking collectives, on_device(): lax.psum(jnp.concatenate([g_norm, g_group, g_ffn_gain, g_taps.reshape(-1)...  38.8 us
    ppermute x37, starting transfers between devices, hop(): return lax.ppermute(value, self.axes, self.hops[dy, di])  37.2 us
    reduce_scatter x1, waiting for transfers between devices, on_device(): g_out = lax.psum_scatter(g_out, 'fsdp', scatter_dimension=0, tiled=True)  26.1 us
    ppermute x3, waiting for transfers between devices, gather_plane(): lax.ppermute(jnp.where(self.odd, along_y, along_x), self.axes, self.corner)  25.4 us
    unnamed x146, local copies, waits for them, and re-layouts  24.4 us
    pallas_call x1, Pallas kernels, attend(): pl.pallas_call(attend_kernel, grid=(PAIRS,), in_specs=[pl.BlockSpec(memor...  21.8 us
  transfers between devices with their start and end apart: 55, of which 25 were waited for; matrix products, arithmetic and copies ran while one was open for 33% of the time, Pallas kernels for 10%

profile of v1, /device:TPU:0, one launch (start us, length us, event | category | flops | bytes accessed | tf_op | source)
XLA Modules:
  0.0 604.5 jit_solution(1992360297632361199)
XLA Ops:
  19.0 12.7 %collective-permute-done.1 = bf16[256,1536]{1,0:T(8,128)(2,1)} collective-permute-done((bf16[256,1536]{1,0:T(8,128)(2,1)}, bf16[256,1536]{1,0:T(8,128)(2,1)}, u32[]{:S(2)}, u32[]{:S(2)}) %collective-permute-start.1) | collective-permute-done | bytes 786464 | tf_op jit(solution)/shard_map/ppermute | solution.py:306
  41.3 14.8 %collective-permute-done.2 = bf16[256,1536]{1,0:T(8,128)(2,1)S(1)} collective-permute-done((bf16[256,1536]{1,0:T(8,128)(2,1)}, bf16[256,1536]{1,0:T(8,128)(2,1)S(1)}, u32[]{:S(2)}, u32[]{:S(2)}) %collective-permute-start.2) | collective-permute-done | bytes 786464 | tf_op jit(solution)/shard_map/ppermute | solution.py:328
  68.8 6.4 %scatter.19.bwd_ref = f32[16,8,256]{2,1,0:T(8,128)S(1)} dynamic-update-slice(f32[16,8,256]{2,1,0:T(8,128)S(1)} %scatter.16, f32[16,6,5]{2,1,0:T(8,128)S(1)} %dynamic-slice_select_fusion, s32[]{:T(128)} %constant.146.clone.1, s32[]{:T(128)} %bitcast.24, s32[]{:T(128)} %bitcast.25) | dynamic-update-slice | bytes 3844 | tf_op jit(solution)/shard_map/scatter | solution.py:53
  75.2 6.3 %scatter.15.fwd_ref = f32[16,8,256]{2,1,0:T(8,128)S(1)} dynamic-update-slice(f32[16,8,256]{2,1,0:T(8,128)S(1)} %scatter.14, f32[16,6,5]{2,1,0:T(8,128)S(1)} %get-tuple-element.171, s32[]{:T(128)} %constant.146.clone.1, s32[]{:T(128)} %bitcast.24, s32[]{:T(128)} %bitcast.25) | dynamic-update-slice | bytes 3844 | tf_op jit(solution)/shard_map/scatter | solution.py:50
  82.1 15.9 %shard_map.220 = (bf16[16,1536,256]{2,1,0:T(8,128)(2,1)}, bf16[16,1536,256]{2,1,0:T(8,128)(2,1)}, bf16[16,1536,256]{2,1,0:T(8,128)(2,1)}) custom-call(f32[16,8,256]{2,1,0:T(8,128)} %copy-done.39, f32[16,8,256]{2,1,0:T(8,128)} %copy-done.40), custom_call_target="tpu_custom_call" | custom-call | flops 12582912 | bytes 37748736 | tf_op jit(solution)/shard_map/pallas_call | solution.py:57
  121.2 15.7 %collective-permute-done.10 = bf16[576,256]{1,0:T(8,128)(2,1)S(1)} collective-permute-done((bf16[576,256]{1,0:T(8,128)(2,1)S(1)}, bf16[576,256]{1,0:T(8,128)(2,1)S(1)}, u32[]{:S(2)}, u32[]{:S(2)}) %collective-permute-start.10) | collective-permute-done | bytes 294944 | tf_op jit(solution)/shard_map/ppermute | solution.py:306
  137.0 12.7 %collective-permute-done.11 = bf16[576,256]{1,0:T(8,128)(2,1)S(1)} collective-permute-done((bf16[576,256]{1,0:T(8,128)(2,1)S(1)}, bf16[576,256]{1,0:T(8,128)(2,1)S(1)}, u32[]{:S(2)}, u32[]{:S(2)}) %collective-permute-start.11) | collective-permute-done | bytes 294944 | tf_op jit(solution)/shard_map/ppermute | solution.py:306
  151.1 21.8 %shard_map.221 = (f32[16,256,256]{2,1,0:T(8,128)S(1)}, f32[1536,256]{1,0:T(8,128)S(1)}, bf16[1536,256]{1,0:T(8,128)(2,1)S(1)}) custom-call(f32[8,4]{1,0:T(8,128)S(1)} %copy.73.mix_ref, bf16[4608,256]{1,0:T(8,128)(2,1)S(1)} %bitcast.144, bf16[4608,256]{1,0:T(8,128)(2,1)S(1)} %bitcast.145, bf16[4608,256]{1,0:T(8,128)(2,1)S(1)} %bitcast.146, ...), custom_call_target="tpu_custom_call" | custom-call | flops 11274289152 | bytes 35651584 | tf_op jit(solution)/shard_map/pallas_call | solution.py:122
  190.5 13.1 %collective-permute-done.15 = bf16[256,1536]{1,0:T(8,128)(2,1)} collective-permute-done((bf16[256,1536]{1,0:T(8,128)(2,1)}, bf16[256,1536]{1,0:T(8,128)(2,1)}, u32[]{:S(2)}, u32[]{:S(2)}) %collective-permute-start.15) | collective-permute-done | bytes 786464 | tf_op jit(solution)/shard_map/ppermute | solution.py:306
  207.6 10.6 %collective-permute-done.17 = bf16[256,1536]{1,0:T(8,128)(2,1)S(1)} collective-permute-done((bf16[256,1536]{1,0:T(8,128)(2,1)S(1)}, bf16[256,1536]{1,0:T(8,128)(2,1)S(1)}, u32[]{:S(2)}, u32[]{:S(2)}) %collective-permute-start.17) | collective-permute-done | bytes 786464 | tf_op jit(solution)/shard_map/ppermute | solution.py:328
  221.9 5.6 fusion.61
  227.5 5.1 fusion.62
  232.5 16.7 %all-gather.9.cloned.1.call-done = bf16[1024,1536]{0,1:T(8,128)(2,1)} async-done(((bf16[256,1536]{0,1:T(8,128)(2,1)}), bf16[1024,1536]{0,1:T(8,128)(2,1)}) %all-gather.9.cloned.1.call-update) | async-done | bytes 3145744 | tf_op jit(solution)/shard_map/all_gather | solution.py:309
  249.2 6.6 %fusion.53 = f32[1024,1024]{0,1:T(8,128)S(1)} fusion(bf16[1024,1536]{0,1:T(8,128)(2,1)} %all-gather.9.cloned.1.call-done, bf16[256,1536]{1,0:T(8,128)(2,1)} %copy-done.37, bf16[256,1536]{1,0:T(8,128)(2,1)} %collective-permute-done.16, bf16[256,1536]{1,0:T(8,128)(2,1)} %collective-permute-done.15, bf16[256,1536]{1,0:T(8,128)(2,1)} %multiply_convert_fusion.4), kind=kOutput, calls=%fused_computation.184 | convolution fusion | flops 3233808384 | bytes 10485760 | tf_op jit(solution)/shard_map/dot_general | solution.py:22
  255.8 5.6 fusion.60
  287.1 6.1 %fusion.63 = f32[1024,1536]{1,0:T(8,128)S(1)} fusion(bf16[1024,1024]{0,1:T(8,128)(2,1)} %bitcast.160, bf16[1024,1536]{1,0:T(8,128)(2,1)} %collective-permute-done.18), kind=kOutput, calls=%fused_computation.194 | convolution fusion | flops 3221225472 | bytes 11534336 | tf_op jit(solution)/shard_map/dot_general | solution.py:22
  302.2 7.1 %convert_add_fusion.1 = f32[1024,1536]{1,0:T(8,128)} fusion(bf16[1024,1536]{1,0:T(8,128)(2,1)} %collective-permute-done.27, bf16[1024,1024]{0,1:T(8,128)(2,1)S(1)} %bitcast.157, bf16[1024,1536]{0,1:T(8,128)(2,1)S(1)} %copy-done.58), kind=kOutput, calls=%fused_computation.13 | convolution fusion | flops 3224371200 | bytes 14680064 | tf_op jit(solution)/shard_map/dot_general | solution.py:22
  312.3 6.7 %add_convert_fusion = bf16[1024,1536]{1,0:T(8,128)(2,1)} fusion(f32[1024,1536]{1,0:T(8,128)S(1)} %fusion.63, bf16[1024,1024]{0,1:T(8,128)(2,1)S(1)} %bitcast.158, bf16[256,1536]{1,0:T(8,128)(2,1)S(1)} %copy-done.38, bf16[256,1536]{1,0:T(8,128)(2,1)} %collective-permute-done.16, bf16[256,1536]{1,0:T(8,128)(2,1)} %collective-permute-done.15, ...), kind=kOutput, calls=%fused_computation.11 | convolution fusion | flops 3236954112 | bytes 14680064 | tf_op jit(solution)/shard_map/dot_general | solution.py:22
  319.1 5.0 collective-permute-done.28
  333.6 13.5 %collective-permute-done.29 = bf16[256,1536]{1,0:T(8,128)(2,1)S(1)} collective-permute-done((bf16[256,1536]{1,0:T(8,128)(2,1)S(1)}, bf16[256,1536]{1,0:T(8,128)(2,1)S(1)}, u32[]{:S(2)}, u32[]{:S(2)}) %collective-permute-start.29) | collective-permute-done | bytes 786464 | tf_op jit(solution)/shard_map/ppermute | solution.py:306
  350.8 11.1 %collective-permute-done.21 = bf16[256,1536]{1,0:T(8,128)(2,1)S(1)} collective-permute-done((bf16[256,1536]{1,0:T(8,128)(2,1)S(1)}, bf16[256,1536]{1,0:T(8,128)(2,1)S(1)}, u32[]{:S(2)}, u32[]{:S(2)}) %collective-permute-start.21) | collective-permute-done | bytes 786464 | tf_op jit(solution)/shard_map/ppermute | solution.py:306
  369.3 19.9 %shard_map.222 = (bf16[1536,256]{1,0:T(8,128)(2,1)S(1)}, bf16[1536,256]{1,0:T(8,128)(2,1)S(1)}, bf16[1536,256]{1,0:T(8,128)(2,1)S(1)}, f32[1536,1]{1,0:T(8,128)S...) custom-call(f32[8,4]{1,0:T(8,128)S(1)} %copy.73.mix_ref, bf16[4608,256]{1,0:T(8,128)(2,1)S(1)} %bitcast.147, ...), custom_call_target="tpu_custom_call" | custom-call | flops 10737418240 | bytes 25165824 | tf_op jit(solution)/shard_map/pallas_call | solution.py:225
  401.7 5.5 collective-permute-done.36
  413.1 7.3 %collective-permute-done.32 = bf16[576,256]{1,0:T(8,128)(2,1)S(1)} collective-permute-done((bf16[576,256]{1,0:T(8,128)(2,1)S(1)}, bf16[576,256]{1,0:T(8,128)(2,1)S(1)}, u32[]{:S(2)}, u32[]{:S(2)}) %collective-permute-start.32) | collective-permute-done | bytes 294944 | tf_op jit(solution)/shard_map/ppermute | solution.py:306
  421.3 5.3 add_convert_fusion.1
  431.4 6.2 %convolution_convert_fusion.1 = bf16[1024,1536]{1,0:T(8,128)(2,1)} fusion(bf16[576,1024]{1,0:T(8,128)(2,1)} %copy-done.44, bf16[576,1536]{1,0:T(8,128)(2,1)} %all-gather.5.cloned.1.call-done), kind=kOutput, calls=%fused_computation.16 | convolution fusion | flops 1813512192 | bytes 6094848 | tf_op jit(solution)/shard_map/dot_general | solution.py:22
  440.1 9.5 %collective-permute-done.46 = bf16[128,1536]{1,0:T(8,128)(2,1)S(1)} collective-permute-done((bf16[128,1536]{1,0:T(8,128)(2,1)}, bf16[128,1536]{1,0:T(8,128)(2,1)S(1)}, u32[]{:S(2)}, u32[]{:S(2)}) %collective-permute-start.46) | collective-permute-done | bytes 393248 | tf_op jit(solution)/shard_map/ppermute | solution.py:306
  467.3 6.3 %convert_add_fusion = f32[1024,1536]{1,0:T(8,128)} fusion(bf16[1024,1536]{1,0:T(8,128)(2,1)} %collective-permute-done.38, bf16[576,1536]{1,0:T(8,128)(2,1)S(1)} %copy-done.60, bf16[576,256]{1,0:T(8,128)(2,1)} %copy-done.66, bf16[576,256]{1,0:T(8,128)(2,1)} %copy-done.65, bf16[576,256]{1,0:T(8,128)(2,1)} %copy-done.64, bf16[576,256]{1,0:T(8,128)(2,1)S(1)} %bitcast.165), kind=kOutput, calls=%fused_computation.12 | convolution fusion | flops 1819803648 | bytes 12386304 | tf_op jit(solution)/shard_map/dot_general | solution.py:22
  493.0 6.2 %collective-permute-done.42 = bf16[144,1536]{1,0:T(8,128)(2,1)S(1)} collective-permute-done((bf16[144,1536]{1,0:T(8,128)(2,1)}, bf16[144,1536]{1,0:T(8,128)(2,1)S(1)}, u32[]{:S(2)}, u32[]{:S(2)}) %collective-permute-start.42) | collective-permute-done | bytes 442400 | tf_op jit(solution)/shard_map/ppermute | solution.py:306
  500.7 20.3 %collective-permute-done.40 = bf16[256,1536]{1,0:T(8,128)(2,1)S(1)} collective-permute-done((bf16[256,1536]{1,0:T(8,128)(2,1)S(1)}, bf16[256,1536]{1,0:T(8,128)(2,1)S(1)}, u32[]{:S(2)}, u32[]{:S(2)}) %collective-permute-start.40) | collective-permute-done | bytes 786464 | tf_op jit(solution)/shard_map/ppermute | solution.py:306
  524.0 26.1 %reduce-scatter.7.cloned.1.call-done = bf16[96,1536]{1,0:T(8,128)(2,1)} async-done(((bf16[1536,1536]{1,0:T(8,128)(2,1)}), bf16[96,1536]{1,0:T(8,128)(2,1)}) %reduce-scatter.7.cloned.1.call-update) | async-done | bytes 294928 | tf_op jit(solution)/shard_map/reduce_scatter | solution.py:441
  555.6 38.8 %psum.7 = f32[5696]{0:T(1024)S(1)} all-reduce(f32[5696]{0:T(1024)S(1)} %concatenate.71), channel_id=1, replica_groups=mesh['rep'=2,'fsdp'=16] {'rep','fsdp'}, use_global_device_ids=true, to_apply=%region_11.12 | all-reduce | flops 5696 | bytes 45568 | tf_op jit(solution)/shard_map/psum | solution.py:465
  (361 shorter events, 218.3 us)
Async XLA Ops:
  7.2 94.4 %all-gather.5.cloned.1.call-start = ((), (), s32[]{:S(2)}) async-start(), calls=%async_computation.4 | async-start | bytes 2211840 | tf_op jit(solution)/shard_map/all_gather | solution.py:309
  9.2 167.9 %all-gather.7.cloned.1.call-start = ((), (), s32[]{:S(2)}) async-start(), calls=%async_computation.5 | async-start | bytes 5013504 | tf_op jit(solution)/shard_map/all_gather | solution.py:388
  9.9 211.9 %all-gather.11.cloned.1.call-start = ((), (), s32[]{:S(2)}) async-start(), calls=%async_computation.7 | async-start | bytes 1966080 | tf_op jit(solution)/shard_map/all_gather | solution.py:309
  10.0 21.7 %collective-permute-start.1 = (bf16[256,1536]{1,0:T(8,128)(2,1)}, bf16[256,1536]{1,0:T(8,128)(2,1)}, u32[]{:S(2)}, u32[]{:S(2)}) collective-permute-start(bf16[256,1536]{1,0:T(8,128)(2,1)} %param.21), channel_id=1, source_target_pairs={{0,16},{1,17},{2,18},{3,19},{4,20},{5,21},{6,22},{7,23},{8,24},{9,... | collective-permute-start | bytes 2359304 | tf_op jit(solution)/shard_map/ppermute | solution.py:306
  13.0 20.8 %collective-permute-start = (bf16[256,1536]{1,0:T(8,128)(2,1)}, bf16[256,1536]{1,0:T(8,128)(2,1)}, u32[]{:S(2)}, u32[]{:S(2)}) collective-permute-start(bf16[256,1536]{1,0:T(8,128)(2,1)} %param.21), channel_id=1, source_target_pairs={{0,2},{1,3},{2,0},{3,1},{4,6},{5,7},{6,4},{7,5},{8,10},{9,11},{10,... | collective-permute-start | bytes 2359304 | tf_op jit(solution)/shard_map/ppermute | solution.py:306
  14.6 100.0 %collective-permute-start.23 = (bf16[256,1536]{1,0:T(8,128)(2,1)S(1)}, bf16[256,1536]{1,0:T(8,128)(2,1)S(1)}, u32[]{:S(2)}, u32[]{:S(2)}) collective-permute-start(bf16[256,1536]{1,0:T(8,128)(2,1)S(1)} %convert_element_type.181), channel_id=1, source_target_pairs={{0,2},{1,3},{2,0},{3,1},{4,6},{5,7},{6,4},{7,5},{8,10},{9,11},{10,... | collective-permute-start | bytes 2359304 | tf_op jit(solution)/shard_map/ppermute | solution.py:306
  15.2 99.5 %collective-permute-start.24 = (bf16[256,1536]{1,0:T(8,128)(2,1)S(1)}, bf16[256,1536]{1,0:T(8,128)(2,1)S(1)}, u32[]{:S(2)}, u32[]{:S(2)}) collective-permute-start(bf16[256,1536]{1,0:T(8,128)(2,1)S(1)} %convert_element_type.181), channel_id=1, source_target_pairs={{0,16},{1,17},{2,18},{3,19},{4,20},{5,21},{6,22},{7,23},{8,24},{9,... | collective-permute-start | bytes 2359304 | tf_op jit(solution)/shard_map/ppermute | solution.py:306
  15.3 42.9 %collective-permute-start.3 = (bf16[1,3,96]{2,1,0:T(4,128)(2,1)S(1)}, bf16[1,3,96]{2,1,0:T(4,128)(2,1)S(1)}, u32[]{:S(2)}, u32[]{:S(2)}) collective-permute-start(bf16[1,3,96]{2,1,0:T(4,128)(2,1)S(1)} %maximum_bitcast_fusion), channel_id=1, source_target_pairs={{0,1},{1,0},{2,3},{3,2},{4,5},{5,4},{6,7},{7,6},{8,9},{9,8},{10,11... | collective-permute-start | bytes 1736 | tf_op jit(solution)/shard_map/ppermute | solution.py:318
  17.2 232.0 %all-gather.9.cloned.1.call-start = ((), (), s32[]{:S(2)}) async-start(), calls=%async_computation.6 | async-start | bytes 3932160 | tf_op jit(solution)/shard_map/all_gather | solution.py:309
  57.0 50.8 %collective-permute-start.7 = (bf16[1024,1536]{1,0:T(8,128)(2,1)}, bf16[1024,1536]{1,0:T(8,128)(2,1)}, u32[]{:S(2)}, u32[]{:S(2)}) collective-permute-start(bf16[1024,1536]{1,0:T(8,128)(2,1)} %constant_dynamic-update-slice_fusion), channel_id=1, source_target_pairs={{0,1},{1,0},{2,3},{3,2},{4,5},{5,4},{6,7},{7,6},{8,9},{9,8},{10,11... | collective-permute-start | bytes 9437192 | tf_op jit(solution)/shard_map/ppermute | solution.py:306
  65.8 32.2 %collective-permute-start.6 = (bf16[8,3,96]{2,1,0:T(4,128)(2,1)S(1)}, bf16[8,3,96]{2,1,0:T(4,128)(2,1)S(1)}, u32[]{:S(2)}, u32[]{:S(2)}) collective-permute-start(bf16[8,3,96]{2,1,0:T(4,128)(2,1)S(1)} %pad_maximum_fusion.9), channel_id=1, source_target_pairs={{0,8},{1,9},{2,10},{3,11},{4,12},{5,13},{6,14},{7,15},{8,0},{9,1},... | collective-permute-start | bytes 13832 | tf_op jit(solution)/shard_map/ppermute | solution.py:318
  115.8 71.2 %collective-permute-start.25 = (bf16[256,1536]{1,0:T(8,128)(2,1)}, bf16[256,1536]{1,0:T(8,128)(2,1)}, u32[]{:S(2)}, u32[]{:S(2)}) collective-permute-start(bf16[256,1536]{1,0:T(8,128)(2,1)} %broadcast_select_fusion), channel_id=1, source_target_pairs={{0,16},{1,3},{2,18},{3,1},{4,20},{5,7},{6,22},{7,5},{8,24},{9,11},... | collective-permute-start | bytes 2359304 | tf_op jit(solution)/shard_map/ppermute | solution.py:328
  116.3 33.4 %collective-permute-start.11 = (bf16[576,256]{1,0:T(8,128)(2,1)S(1)}, bf16[576,256]{1,0:T(8,128)(2,1)S(1)}, u32[]{:S(2)}, u32[]{:S(2)}) collective-permute-start(bf16[576,256]{1,0:T(8,128)(2,1)S(1)} %get-tuple-element.160), channel_id=1, source_target_pairs={{0,16},{1,17},{2,18},{3,19},{4,20},{5,21},{6,22},{7,23},{8,24},{9,... | collective-permute-start | bytes 884744 | tf_op jit(solution)/shard_map/ppermute | solution.py:306
  118.2 32.9 %collective-permute-start.13 = (bf16[576,256]{1,0:T(8,128)(2,1)S(1)}, bf16[576,256]{1,0:T(8,128)(2,1)S(1)}, u32[]{:S(2)}, u32[]{:S(2)}) collective-permute-start(bf16[576,256]{1,0:T(8,128)(2,1)S(1)} %get-tuple-element.159), channel_id=1, source_target_pairs={{0,18},{1,19},{2,16},{3,17},{4,22},{5,23},{6,20},{7,21},{8,26},{9,... | collective-permute-start | bytes 884744 | tf_op jit(solution)/shard_map/ppermute | solution.py:306
  119.8 31.2 %collective-permute-start.12 = (bf16[576,256]{1,0:T(8,128)(2,1)S(1)}, bf16[576,256]{1,0:T(8,128)(2,1)S(1)}, u32[]{:S(2)}, u32[]{:S(2)}) collective-permute-start(bf16[576,256]{1,0:T(8,128)(2,1)S(1)} %get-tuple-element.156), channel_id=1, source_target_pairs={{0,17},{1,16},{2,19},{3,18},{4,21},{5,20},{6,23},{7,22},{8,25},{9,... | collective-permute-start | bytes 884744 | tf_op jit(solution)/shard_map/ppermute | solution.py:306
  187.0 250.9 %reduce-scatter.11.cloned.1.call-start = ((), (), s32[]{:S(2)}) async-start(), calls=%async_computation.11 | async-start | bytes 1966080 | tf_op jit(solution)/shard_map/reduce_scatter | solution.py:312
  190.2 37.2 %collective-permute-start.26 = (bf16[1024,1536]{1,0:T(8,128)(2,1)}, bf16[1024,1536]{1,0:T(8,128)(2,1)}, u32[]{:S(2)}, u32[]{:S(2)}) collective-permute-start(bf16[1024,1536]{1,0:T(8,128)(2,1)} %pad_maximum_fusion.1), channel_id=1, source_target_pairs={{0,1},{1,0},{2,3},{3,2},{4,5},{5,4},{6,7},{7,6},{8,9},{9,8},{10,11... | collective-permute-start | bytes 9437192 | tf_op jit(solution)/shard_map/ppermute | solution.py:306
  221.7 34.1 %collective-permute-start.18 = (bf16[1024,1536]{1,0:T(8,128)(2,1)}, bf16[1024,1536]{1,0:T(8,128)(2,1)}, u32[]{:S(2)}, u32[]{:S(2)}) collective-permute-start(bf16[1024,1536]{1,0:T(8,128)(2,1)} %pad_maximum_fusion), channel_id=1, source_target_pairs={{0,1},{1,0},{2,3},{3,2},{4,5},{5,4},{6,7},{7,6},{8,9},{9,8},{10,11... | collective-permute-start | bytes 9437192 | tf_op jit(solution)/shard_map/ppermute | solution.py:306
  268.6 24.6 %collective-permute-start.19 = (bf16[1024,1536]{1,0:T(8,128)(2,1)}, bf16[1024,1536]{1,0:T(8,128)(2,1)}, u32[]{:S(2)}, u32[]{:S(2)}) collective-permute-start(bf16[1024,1536]{1,0:T(8,128)(2,1)} %convolution_convert_fusion.2), channel_id=1, source_target_pairs={{0,1},{1,0},{2,3},{3,2},{4,5},{5,4},{6,7},{7,6},{8,9},{9,8},{10,11... | collective-permute-start | bytes 9437192 | tf_op jit(solution)/shard_map/ppermute | solution.py:306
  273.7 28.5 %collective-permute-start.27 = (bf16[1024,1536]{1,0:T(8,128)(2,1)}, bf16[1024,1536]{1,0:T(8,128)(2,1)}, u32[]{:S(2)}, u32[]{:S(2)}) collective-permute-start(bf16[1024,1536]{1,0:T(8,128)(2,1)} %convolution_convert_fusion.3), channel_id=1, source_target_pairs={{0,1},{1,0},{2,3},{3,2},{4,5},{5,4},{6,7},{7,6},{8,9},{9,8},{10,11... | collective-permute-start | bytes 9437192 | tf_op jit(solution)/shard_map/ppermute | solution.py:306
  287.0 164.4 %reduce-scatter.9.cloned.1.call-start = ((), (), s32[]{:S(2)}) async-start(), calls=%async_computation.10 | async-start | bytes 3932160 | tf_op jit(solution)/shard_map/reduce_scatter | solution.py:312
  300.7 28.0 %collective-permute-start.20 = (bf16[256,1536]{1,0:T(8,128)(2,1)}, bf16[256,1536]{1,0:T(8,128)(2,1)}, u32[]{:S(2)}, u32[]{:S(2)}) collective-permute-start(bf16[256,1536]{1,0:T(8,128)(2,1)} %slice.363), channel_id=1, source_target_pairs={{0,16},{1,3},{2,18},{3,1},{4,20},{5,7},{6,22},{7,5},{8,24},{9,11},... | collective-permute-start | bytes 2359304 | tf_op jit(solution)/shard_map/ppermute | solution.py:336
  319.0 166.8 %reduce-scatter.5.cloned.1.call-start = ((), (), s32[]{:S(2)}) async-start(), calls=%async_computation.8 | async-start | bytes 2211840 | tf_op jit(solution)/shard_map/reduce_scatter | solution.py:312
  331.2 30.6 %collective-permute-start.21 = (bf16[256,1536]{1,0:T(8,128)(2,1)S(1)}, bf16[256,1536]{1,0:T(8,128)(2,1)S(1)}, u32[]{:S(2)}, u32[]{:S(2)}) collective-permute-start(bf16[256,1536]{1,0:T(8,128)(2,1)S(1)} %get-tuple-element.131), channel_id=1, source_target_pairs={{0,2},{1,3},{2,0},{3,1},{4,6},{5,7},{6,4},{7,5},{8,10},{9,11},{10,... | collective-permute-start | bytes 2359304 | tf_op jit(solution)/shard_map/ppermute | solution.py:306
  332.3 29.8 %collective-permute-start.22 = (bf16[256,1536]{1,0:T(8,128)(2,1)S(1)}, bf16[256,1536]{1,0:T(8,128)(2,1)S(1)}, u32[]{:S(2)}, u32[]{:S(2)}) collective-permute-start(bf16[256,1536]{1,0:T(8,128)(2,1)S(1)} %get-tuple-element.132), channel_id=1, source_target_pairs={{0,16},{1,17},{2,18},{3,19},{4,20},{5,21},{6,22},{7,23},{8,24},{9,... | collective-permute-start | bytes 2359304 | tf_op jit(solution)/shard_map/ppermute | solution.py:306
  395.3 25.1 %collective-permute-start.32 = (bf16[576,256]{1,0:T(8,128)(2,1)S(1)}, bf16[576,256]{1,0:T(8,128)(2,1)S(1)}, u32[]{:S(2)}, u32[]{:S(2)}) collective-permute-start(bf16[576,256]{1,0:T(8,128)(2,1)S(1)} %bitcast.167), channel_id=1, source_target_pairs={{0,16},{1,17},{2,18},{3,19},{4,20},{5,21},{6,22},{7,23},{8,24},{9,... | collective-permute-start | bytes 884744 | tf_op jit(solution)/shard_map/ppermute | solution.py:306
  399.4 20.9 %collective-permute-start.33 = (bf16[576,256]{1,0:T(8,128)(2,1)S(1)}, bf16[576,256]{1,0:T(8,128)(2,1)S(1)}, u32[]{:S(2)}, u32[]{:S(2)}) collective-permute-start(bf16[576,256]{1,0:T(8,128)(2,1)S(1)} %bitcast.166), channel_id=1, source_target_pairs={{0,18},{1,19},{2,16},{3,17},{4,22},{5,23},{6,20},{7,21},{8,26},{9,... | collective-permute-start | bytes 884744 | tf_op jit(solution)/shard_map/ppermute | solution.py:306
  426.6 123.4 %reduce-scatter.7.cloned.1.call-start = ((), (), s32[]{:S(2)}) async-start(), calls=%async_computation.9 | async-start | bytes 5013504 | tf_op jit(solution)/shard_map/reduce_scatter | solution.py:441
  437.6 29.8 %collective-permute-start.38 = (bf16[1024,1536]{1,0:T(8,128)(2,1)}, bf16[1024,1536]{1,0:T(8,128)(2,1)}, u32[]{:S(2)}, u32[]{:S(2)}) collective-permute-start(bf16[1024,1536]{1,0:T(8,128)(2,1)} %convolution_convert_fusion.1), channel_id=1, source_target_pairs={{0,1},{1,0},{2,3},{3,2},{4,5},{5,4},{6,7},{7,6},{8,9},{9,8},{10,11... | collective-permute-start | bytes 9437192 | tf_op jit(solution)/shard_map/ppermute | solution.py:306
  492.4 28.7 %collective-permute-start.40 = (bf16[256,1536]{1,0:T(8,128)(2,1)S(1)}, bf16[256,1536]{1,0:T(8,128)(2,1)S(1)}, u32[]{:S(2)}, u32[]{:S(2)}) collective-permute-start(bf16[256,1536]{1,0:T(8,128)(2,1)S(1)} %get-tuple-element.127), channel_id=1, source_target_pairs={{0,2},{1,3},{2,0},{3,1},{4,6},{5,7},{6,4},{7,5},{8,10},{9,11},{10,... | collective-permute-start | bytes 2359304 | tf_op jit(solution)/shard_map/ppermute | solution.py:306
  492.5 28.6 %collective-permute-start.41 = (bf16[256,1536]{1,0:T(8,128)(2,1)S(1)}, bf16[256,1536]{1,0:T(8,128)(2,1)S(1)}, u32[]{:S(2)}, u32[]{:S(2)}) collective-permute-start(bf16[256,1536]{1,0:T(8,128)(2,1)S(1)} %get-tuple-element.128), channel_id=1, source_target_pairs={{0,16},{1,17},{2,18},{3,19},{4,20},{5,21},{6,22},{7,23},{8,24},{9,... | collective-permute-start | bytes 2359304 | tf_op jit(solution)/shard_map/ppermute | solution.py:306
  550.1 46.4 %collective-permute-start.43 = (bf16[96,1536]{1,0:T(8,128)(2,1)}, bf16[96,1536]{1,0:T(8,128)(2,1)S(1)}, u32[]{:S(2)}, u32[]{:S(2)}) collective-permute-start(bf16[96,1536]{1,0:T(8,128)(2,1)} %reduce-scatter.7.cloned.1.call-done), channel_id=1, source_target_pairs={{0,16},{1,17},{2,18},{3,19},{4,20},{5,21},{6,22},{7,23},{8,24},{9,... | collective-permute-start | bytes 884744 | tf_op jit(solution)/shard_map/ppermute | solution.py:306
  (92 other events, 1075.8 us)
Sparse Core Ops, SparseCore 0:
  10.2 43.0 all-gather.4
  55.5 52.4 all-gather.6
  109.6 35.6 all-gather.10
  187.1 62.0 all-gather.8
  287.1 33.4 reduce-scatter.10
  322.8 59.2 reduce-scatter.8
  426.8 35.7 reduce-scatter.4
  466.9 83.0 reduce-scatter.6

commit v2 on v1

v2 whole, which is shorter than its diff:
```python
import functools
import jax
import jax.numpy as jnp
from jax import lax
from jax.experimental import pallas as pl
from jax.experimental.pallas import tpu as pltpu
from jax.sharding import PartitionSpec as P

D = 1536
H = 16
HD = 96
CQ = 6
CK = 11
NEG = -1e30
PAIRS = H // 2
PW = 2 * HD
BF = jnp.bfloat16
F32 = jnp.float32


def cost(time):
    return pl.CostEstimate(flops=int(time * 5e8), bytes_accessed=0, transcendentals=0)


def dot(a, b, ca, cb):
    return lax.dot_general(a, b, (((ca,), (cb,)), ((), ())), preferred_element_type=F32)


def split(v):
    hi = v.astype(BF)
    return hi, (v - hi.astype(F32)).astype(BF)


def taps_kernel(fwd_ref, bwd_ref, th_ref, tl_ref, tt_ref):
    n = th_ref.shape[-1]
    row = lax.broadcasted_iota(jnp.int32, (n, n), 0)
    col = lax.broadcasted_iota(jnp.int32, (n, n), 1)
    near = jnp.abs(row - col) <= CK // 2
    for a in range(CQ):
        wide = jnp.broadcast_to(fwd_ref[0, a : a + 1, :], (n, n))
        band = jnp.where(near, pltpu.roll(wide, 0, 1, stride=1, stride_axis=0), 0.0)
        hi, lo = split(band)
        th_ref[0, a * n : (a + 1) * n, :] = hi
        tl_ref[0, a * n : (a + 1) * n, :] = lo
        wide = jnp.broadcast_to(bwd_ref[0, a : a + 1, :], (n, n))
        band = jnp.where(near, pltpu.roll(wide, 0, 1, stride=1, stride_axis=0), 0.0)
        tt_ref[0, a * n : (a + 1) * n, :] = band.astype(BF)


def band_taps(kernel, n):
    half = CK // 2

    def around(taps):
        gap = jnp.zeros((H, CQ, n - CK), F32)
        rows = jnp.concatenate([taps[:, :, half:], gap, taps[:, :, :half]], axis=2)
        return jnp.pad(rows, ((0, 0), (0, 8 - CQ), (0, 0)))

    taps = kernel.reshape(H, CQ, CK)
    fwd, bwd = around(taps), around(taps[:, :, ::-1])
    row = pl.BlockSpec((1, 8, n), lambda h: (h, 0, 0))
    out = pl.BlockSpec((1, CQ * n, n), lambda h: (h, 0, 0))
    shape = jax.ShapeDtypeStruct((H, CQ * n, n), BF)
    return pl.pallas_call(
        taps_kernel,
        cost_estimate=cost(16),
        grid=(H,),
        in_specs=[row, row],
        out_specs=[out, out, out],
        out_shape=[shape, shape, shape],
    )(fwd, bwd)


def fence_kernel(*refs):
    del refs


def fence(*values, time=0.1):
    return pl.pallas_call(
        fence_kernel,
        cost_estimate=cost(time),
        in_specs=[pl.BlockSpec(memory_space=pl.ANY)] * len(values),
        out_specs=[pl.BlockSpec(memory_space=pl.ANY)] * len(values),
        out_shape=[jax.ShapeDtypeStruct(v.shape, v.dtype) for v in values],
        input_output_aliases={i: i for i in range(len(values))},
    )(*values)


def project_kernel(x_ref, gain_ref, w_ref, normed_ref, *part_refs):
    cols = part_refs[0].shape[0] // w_ref.shape[0]
    x = x_ref[...].astype(F32)
    normed = rms_norm(x, gain_ref[...]).astype(BF)
    normed_ref[...] = normed
    w = w_ref[:, :cols, :].reshape(-1, D)
    part = dot(w, normed, 1, 1).astype(BF)
    for b, ref in enumerate(part_refs):

        @pl.when(pl.program_id(0) == b)
        def _():
            ref[...] = part


def project(blocks, gain, w_attn, cols, n):
    lines, count = w_attn.shape[0], blocks.shape[0] // n
    rows = lines * cols
    if cols % 16:
        normed = rms_norm(blocks.astype(F32), gain).astype(BF)
        part = dot(w_attn[:, :cols].reshape(rows, D), normed, 1, 1).astype(BF)
        return normed, [part[:, b * n : (b + 1) * n] for b in range(count)]
    out = pl.pallas_call(
        project_kernel,
        cost_estimate=cost(1.2 * count),
        grid=(count,),
        in_specs=[
            pl.BlockSpec((n, D), lambda b: (b, 0)),
            pl.BlockSpec((1, D), lambda b: (0, 0)),
            pl.BlockSpec(w_attn.shape, lambda b: (0, 0, 0)),
        ],
        out_specs=[pl.BlockSpec((n, D), lambda b: (b, 0))]
        + [pl.BlockSpec((rows, n), lambda b: (0, 0))] * count,
        out_shape=[jax.ShapeDtypeStruct(blocks.shape, BF)]
        + [jax.ShapeDtypeStruct((rows, n), BF)] * count,
        compiler_params=pltpu.CompilerParams(vmem_limit_bytes=60 * 2**20),
    )(blocks, gain.reshape(1, D), w_attn)
    return out[0], out[1:]


def move_kernel(joins, count, cols, place_ref, *refs):
    *arrays, sems = refs
    if joins:
        *blocks, held = arrays
    else:
        whole, *blocks, held, sem = arrays
        first = pltpu.make_async_copy(whole, held, sem)
        first.start()
        first.wait()
    lines = held.shape[0]
    rows = lines * cols
    copies = []
    for b in range(8):
        other = place_ref[0] ^ order(b)
        for z in range(lines):
            part = blocks[b // count].at[pl.ds(b % count * rows + z * cols, cols)]
            spot = held.at[z, other & 3, other >> 2]
            pair = (part, spot) if joins else (spot, part)
            copies.append(pltpu.make_async_copy(*pair, sems.at[len(copies)]))
            copies[-1].start()
    for copy in copies:
        copy.wait()


def move(joins, values, place, lines, cols, n, count):
    anywhere = pl.BlockSpec(memory_space=pl.ANY)
    whole = (lines, 4, 2, cols, n)
    held = [pltpu.VMEM(whole, BF), pltpu.SemaphoreType.DMA(())]
    if joins:
        out_specs = pl.BlockSpec(memory_space=pltpu.VMEM)
        shape = jax.ShapeDtypeStruct(whole, BF)
    else:
        out_specs = [anywhere] * (8 // count)
        shape = [jax.ShapeDtypeStruct((lines * cols * count, n), BF)] * (8 // count)
    return pl.pallas_call(
        functools.partial(move_kernel, joins, count, cols),
        cost_estimate=cost(2),
        in_specs=[pl.BlockSpec(memory_space=pltpu.SMEM)] + [anywhere] * len(values),
        out_specs=out_specs,
        out_shape=shape,
        scratch_shapes=([] if joins else held) + [pltpu.SemaphoreType.DMA((8 * lines,))],
        compiler_params=pltpu.CompilerParams(vmem_limit_bytes=60 * 2**20),
    )(place.reshape(1), *values)


def out_grad_kernel(place_ref, branch_ref, grouped_ref, *refs):
    outs, held = refs[:-1], refs[-1]
    lines = outs[0].shape[0] // (held.shape[0] // 8)
    wide, half = held.shape[0], held.shape[0] // 8
    for z in range(lines):
        held[...] = dot(branch_ref[:, z * wide : (z + 1) * wide], grouped_ref[...], 0, 1)
        for b, ref in enumerate(outs):
            other = place_ref[0] ^ order(b)
            start = pl.multiple_of((other & 3) * 2 * half + (other >> 2) * half, half)
            ref[z * half : (z + 1) * half, :] = held[pl.ds(start, half), :].astype(ref.dtype)


def out_weight_grad(branch, grouped, place, lines, half):
    n = branch.shape[0]
    if half % 16:
        full = dot(branch, grouped, 0, 1).reshape(lines, 4, 2, half, D)
        blocks = []
        for b in range(8):
            other = place ^ order(b)
            block = lax.dynamic_slice(full, (0, other & 3, other >> 2, 0, 0), (lines, 1, 1, half, D))
            blocks.append(block.reshape(lines * half, D).astype(F32 if b < 4 else BF))
        return blocks
    vmem = pl.BlockSpec(memory_space=pltpu.VMEM)
    return pl.pallas_call(
        out_grad_kernel,
        cost_estimate=cost(0),
        grid=(1,),
        in_specs=[
            pl.BlockSpec(memory_space=pltpu.SMEM),
            pl.BlockSpec((n, D), lambda t: (0, 0)),
            pl.BlockSpec((D, n), lambda t: (0, 0)),
        ],
        out_specs=[pl.BlockSpec((lines * half, D), lambda t: (0, 0))] * 8,
        out_shape=[
            jax.ShapeDtypeStruct((lines * half, D), F32 if b < 4 else BF) for b in range(8)
        ],
        scratch_shapes=[pltpu.VMEM((8 * half, D), F32)],
        compiler_params=pltpu.CompilerParams(vmem_limit_bytes=60 * 2**20),
    )(place.reshape(1), branch, grouped)


def join(values, place, lines, cols):
    count, n = 8 // len(values), values[0].shape[1]
    if cols % 16 == 0:
        return move(True, values, place, lines, cols, n, count).reshape(-1, n)
    out = jnp.zeros((lines, 4, 2, cols, n), BF)
    for b in range(8):
        source = place ^ order(b)
        block = values[b // count].reshape(count, lines, 1, 1, cols, n)[b % count]
        out = lax.dynamic_update_slice(out, block, (0, source & 3, source >> 2, 0, 0))
    return out.reshape(-1, n)


def cut(value, place, lines, cols):
    n = value.shape[1]
    value = value.reshape(lines, 4, 2, cols, n)
    if cols % 16 == 0:
        return move(False, [value], place, lines, cols, n, 1)
    pieces = []
    for b in range(8):
        target = place ^ order(b)
        piece = lax.dynamic_slice(value, (0, target & 3, target >> 2, 0, 0), (lines, 1, 1, cols, n))
        pieces.append(piece.reshape(lines * cols, n))
    return pieces


def order(b):
    return (b // 2 % 2) * 4 + (b % 2) * 2 + b // 4


def gated(gate, upper, d_hidden):
    sig = 1.0 / (1.0 + jnp.exp(-gate))
    act = gate * sig
    hidden = (act * upper).astype(BF)
    d_gate = (d_hidden * upper * (sig * (1.0 + gate * (1.0 - sig)))).astype(BF)
    return hidden, d_gate, (d_hidden * act).astype(BF)


def ffn_kernel(s_ref, o_ref, w_ref, hid_ref, dgu_ref, ds_ref, yo_ref):
    lines, wide = w_ref.shape[0], w_ref.shape[1] // 3
    w_gu = w_ref[:, : 2 * wide, :].reshape(-1, D)
    w_down = w_ref[:, 2 * wide :, :].reshape(-1, D)
    gu = dot(s_ref[...], w_gu, 1, 1)
    dh = dot(o_ref[...], w_down, 1, 1)
    for z in range(lines):
        lo, mid, hi = 2 * z * wide, (2 * z + 1) * wide, (2 * z + 2) * wide
        cut_h = slice(z * wide, (z + 1) * wide)
        hidden, d_gate, d_up = gated(gu[:, lo:mid], gu[:, mid:hi], dh[:, cut_h])
        hid_ref[:, cut_h] = hidden
        dgu_ref[:, lo:mid] = d_gate
        dgu_ref[:, mid:hi] = d_up
    ds_ref[...] = dot(dgu_ref[...], w_gu, 1, 0).astype(ds_ref.dtype)
    yo_ref[...] = dot(hid_ref[...], w_down, 1, 0).astype(yo_ref.dtype)


def ffn(second, d_ffn, w_ffn, n, dtype, start, count):
    rows, lines, wide = count * n, w_ffn.shape[0], w_ffn.shape[1] // 3
    if wide % 128:
        second, d_ffn = (v[start * n : start * n + rows] for v in (second, d_ffn))
        w_gu = w_ffn[:, : 2 * wide].reshape(-1, D)
        w_down = w_ffn[:, 2 * wide :].reshape(-1, D)
        gu = dot(second, w_gu, 1, 1).reshape(rows, lines, 2, wide)
        dh = dot(d_ffn, w_down, 1, 1).reshape(rows, lines, wide)
        hidden, d_gate, d_up = gated(gu[:, :, 0], gu[:, :, 1], dh)
        hidden = hidden.reshape(rows, lines * wide)
        d_gu = jnp.stack([d_gate, d_up], axis=2).reshape(rows, 2 * lines * wide)
        return hidden, d_gu, dot(d_gu, w_gu, 1, 0).astype(dtype), dot(hidden, w_down, 1, 0).astype(dtype)
    out = lambda width: pl.BlockSpec((n, width), lambda b: (b, 0))
    block = pl.BlockSpec((n, D), lambda b: (b + start, 0))
    return pl.pallas_call(
        ffn_kernel,
        cost_estimate=cost(3.8 * count),
        grid=(count,),
        in_specs=[block, block, pl.BlockSpec(w_ffn.shape, lambda b: (0, 0, 0))],
        out_specs=[out(lines * wide), out(2 * lines * wide), out(D), out(D)],
        out_shape=[
            jax.ShapeDtypeStruct((rows, lines * wide), BF),
            jax.ShapeDtypeStruct((rows, 2 * lines * wide), BF),
            jax.ShapeDtypeStruct((rows, D), dtype),
            jax.ShapeDtypeStruct((rows, D), dtype),
        ],
        compiler_params=pltpu.CompilerParams(vmem_limit_bytes=60 * 2**20),
    )(second, d_ffn, w_ffn)


def ffn_grad_kernel(counts, *refs):
    runs = len(counts)
    hid, dgu, sec, dff = (refs[i * runs : (i + 1) * runs] for i in range(4))
    out_ref, gu_ref, down_ref = refs[4 * runs :]
    t = pl.program_id(0)
    start = 0
    for r in range(runs):

        @pl.when((t >= start) & (t < start + counts[r]))
        def _():
            gu = dot(dgu[r][...], sec[r][...], 0, 0)
            down = dot(hid[r][...], dff[r][...], 0, 0)
            if r == 0:
                gu_ref[...] = jnp.where(t == 0, gu, gu_ref[...] + gu)
                down_ref[...] = jnp.where(t == 0, down, down_ref[...] + down)
            else:
                gu_ref[...] += gu
                down_ref[...] += down

        start += counts[r]

    @pl.when(t == start - 1)
    def _():
        lines, wide = out_ref.shape[0], out_ref.shape[1] // 3
        for z in range(lines):
            out_ref[z, : 2 * wide, :] = gu_ref[2 * z * wide : 2 * (z + 1) * wide, :].astype(BF)
            out_ref[z, 2 * wide :, :] = down_ref[z * wide : (z + 1) * wide, :].astype(BF)


def ffn_grad(hidden, d_gu, second, d_ffn, lines, wide, n):
    counts = [h.shape[0] // n for h in hidden]
    if wide % 128:
        rows = lambda group: [v[f * n : (f + c) * n] for (v, f), c in zip(group, counts)]
        gu = sum(dot(a, b, 0, 0) for a, b in zip(d_gu, rows(second))).reshape(lines, 2 * wide, D)
        down = sum(dot(a, b, 0, 0) for a, b in zip(hidden, rows(d_ffn))).reshape(lines, wide, D)
        return jnp.concatenate([gu, down], axis=1).astype(BF)
    hidden, d_gu = ([(v, 0) for v in group] for group in (hidden, d_gu))
    specs, starts = [], [sum(counts[:r]) for r in range(len(counts))]
    for group in (hidden, d_gu, second, d_ffn):
        for (value, first), start, count in zip(group, starts, counts):
            specs.append(
                pl.BlockSpec(
                    (n, value.shape[1]),
                    lambda t, s=start, c=count, f=first: (jnp.clip(t - s, 0, c - 1) + f, 0),
                )
            )
    out = (lines, 3 * wide, D)
    return pl.pallas_call(
        functools.partial(ffn_grad_kernel, counts),
        cost_estimate=cost(18),
        grid=(sum(counts),),
        in_specs=specs,
        out_specs=pl.BlockSpec(out, lambda t: (0, 0, 0)),
        out_shape=jax.ShapeDtypeStruct(out, BF),
        scratch_shapes=[pltpu.VMEM((2 * lines * wide, D), F32), pltpu.VMEM((lines * wide, D), F32)],
        compiler_params=pltpu.CompilerParams(vmem_limit_bytes=60 * 2**20),
    )(*(v for group in (hidden, d_gu, second, d_ffn) for v, _ in group))


def back_project_kernel(count, *refs):
    parts, (x_ref, normed_ref, w_ref) = refs[:count], refs[count : count + 3]
    before, (dn_ref, out_ref, gain_ref, g_ref) = refs[count + 3 : -4], refs[-4:]
    rows = g_ref.shape[0]
    w = w_ref[:, : rows // w_ref.shape[0], :].reshape(rows, D)
    t = pl.program_id(0)

    @pl.when(t == 0)
    def _():
        if before:
            g_ref[...] = before[0][...]
            gain_ref[...] = before[1][...]
        else:
            g_ref[...] = jnp.zeros_like(g_ref)
            gain_ref[...] = jnp.zeros_like(gain_ref)

    for b in range(count):

        @pl.when(t == b)
        def _():
            grad = parts[b][...]
            g_ref[...] += dot(grad, normed_ref[...], 1, 0)
            dn = dot(grad, w, 0, 0)
            dn_ref[...] = dn.astype(dn_ref.dtype)
            x = x_ref[...].astype(F32)
            hat = x * lax.rsqrt(jnp.mean(x * x, axis=1, keepdims=True) + 1e-05)
            gain_ref[...] += jnp.sum(dn * hat, axis=0, keepdims=True)

    @pl.when(t == count - 1)
    def _():
        out_ref[...] = g_ref[...].astype(out_ref.dtype)


def back_project(parts, x, normed, w_attn, cols, n, dtype, before=()):
    lines, count = w_attn.shape[0], len(parts)
    rows = lines * cols
    if cols % 16:
        grad = jnp.concatenate(parts, axis=1)
        dn = dot(grad, w_attn[:, :cols].reshape(rows, D), 0, 0)
        values = x.astype(F32)
        hat = values * lax.rsqrt(jnp.mean(values * values, axis=1, keepdims=True) + 1e-05)
        sums = (dot(grad, normed, 1, 0), jnp.sum(dn * hat, axis=0, keepdims=True))
        if before:
            sums = (sums[0] + before[0], sums[1] + before[1])
        return (dn.astype(dtype),) + sums
    block = pl.BlockSpec((n, D), lambda b: (b, 0))
    whole = lambda shape: pl.BlockSpec(shape, lambda b: (0,) * len(shape))
    return pl.pallas_call(
        functools.partial(back_project_kernel, count),
        cost_estimate=cost(2.5 * count),
        grid=(count,),
        in_specs=[whole((rows, n))] * count
        + [block, block, whole(w_attn.shape)]
        + [whole(v.shape) for v in before],
        out_specs=[block, whole((rows, D)), whole((1, D))],
        out_shape=[
            jax.ShapeDtypeStruct((count * n, D), dtype),
            jax.ShapeDtypeStruct((rows, D), BF if before else F32),
            jax.ShapeDtypeStruct((1, D), F32),
        ],
        scratch_shapes=[pltpu.VMEM((rows, D), F32)],
        compiler_params=pltpu.CompilerParams(vmem_limit_bytes=60 * 2**20),
    )(*parts, x, normed, w_attn, *before)


def doc_masks(drow_ref, dcol_ref, allow_ref, same_ref):
    n = allow_ref.shape[0]
    row = lax.broadcasted_iota(jnp.int32, (n, n), 0)
    col = lax.broadcasted_iota(jnp.int32, (n, n), 1)
    same = dcol_ref[...] == drow_ref[...]
    same_ref[...] = jnp.where(same, 1.0, 0.0)
    allow_ref[...] = jnp.where(same & (col <= row), 1.0, 0.0)


def attend_kernel(
    mix_ref, q_ref, k_ref, v_ref, th_ref, tl_ref, drow_ref, dcol_ref, gain_ref, *refs
):
    prob_ref, att_ref, grp_ref, allow_ref, same_ref, pad_ref, xh_ref, xl_ref = refs[-8:]
    g = pl.program_id(0)
    n = q_ref.shape[1]

    @pl.when(g == 0)
    def _():
        doc_masks(drow_ref, dcol_ref, allow_ref, same_ref)
        pad_ref[0:8, :] = jnp.zeros((8, n), F32)

    for e in range(2):
        q = q_ref[e * HD : (e + 1) * HD, :]
        k = k_ref[e * HD : (e + 1) * HD, :]
        logits = dot(q, k, 0, 0) * (HD ** (-0.5))
        pad_ref[8 : 8 + n, :] = jnp.where(allow_ref[...] > 0, logits, 0.0)
        for a in range(CQ):
            part = jnp.where(same_ref[...] > 0, pad_ref[8 - a : 8 - a + n, :], 0.0)
            hi, lo = split(part)
            xh_ref[:, a * n : (a + 1) * n] = hi
            xl_ref[:, a * n : (a + 1) * n] = lo
        conv = (
            dot(xh_ref[...], th_ref[e], 1, 0)
            + dot(xh_ref[...], tl_ref[e], 1, 0)
            + dot(xl_ref[...], th_ref[e], 1, 0)
        )
        scores = jnp.where(allow_ref[...] > 0, conv, NEG)
        weights = jnp.exp(scores - jnp.max(scores, axis=1, keepdims=True))
        prob_ref[e] = weights * (1.0 / jnp.sum(weights, axis=1, keepdims=True))
    for c in range(2):
        mixed = (mix_ref[g, 2 * c] * prob_ref[0] + mix_ref[g, 2 * c + 1] * prob_ref[1]).astype(BF)
        att = dot(v_ref[c * HD : (c + 1) * HD, :], mixed, 1, 1)
        att_ref[c * HD : (c + 1) * HD, :] = att
        centre = att - jnp.mean(att, axis=0, keepdims=True)
        spread = jnp.mean(centre * centre, axis=0, keepdims=True)
        grp_ref[c * HD : (c + 1) * HD, :] = (
            centre * lax.rsqrt(spread + 1e-05) * gain_ref[c * HD : (c + 1) * HD, :]
        ).astype(BF)


def attend(packed_t, docs, th, tl, mix, gain, start, count, before=()):
    n = packed_t.shape[1]
    blk = lambda off: pl.BlockSpec((PW, n), lambda g: (g + off, 0))
    tap = pl.BlockSpec((2, CQ * n, n), lambda g: (g + start, 0, 0))
    whole = lambda s: pl.BlockSpec(s, lambda g: (0, 0))
    return pl.pallas_call(
        attend_kernel,
        cost_estimate=cost(2.7 * count),
        grid=(count,),
        in_specs=[
            pl.BlockSpec(memory_space=pltpu.SMEM),
            blk(start), blk(PAIRS + start), blk(2 * PAIRS + start), tap, tap,
            whole((1, n)), whole((n, 1)),
            pl.BlockSpec((PW, 1), lambda g: (g + start, 0)),
        ]
        + [pl.BlockSpec(memory_space=pl.ANY)] * len(before),
        out_specs=[pl.BlockSpec((2, n, n), lambda g: (g, 0, 0)), blk(0), blk(start)],
        out_shape=[
            jax.ShapeDtypeStruct((2 * count, n, n), F32),
            jax.ShapeDtypeStruct((count * PW, n), F32),
            jax.ShapeDtypeStruct((D, n), BF),
        ],
        input_output_aliases={9: 2} if before else {},
        scratch_shapes=[
            pltpu.VMEM((n, n), F32), pltpu.VMEM((n, n), F32), pltpu.VMEM((n + 8, n), F32),
            pltpu.VMEM((n, CQ * n), BF), pltpu.VMEM((n, CQ * n), BF),
        ],
        compiler_params=pltpu.CompilerParams(vmem_limit_bytes=60 * 2**20),
    )(
        mix[start : start + count].reshape(count, 4), packed_t, packed_t, packed_t, th, tl,
        docs.reshape(1, n), docs.reshape(n, 1), gain, *before,
    )


def attend_back_kernel(
    mix_ref, q_ref, k_ref, v_ref, tt_ref, drow_ref, dcol_ref, gain_ref, prob_ref, att_ref, dgrp_ref, *refs
):
    d_ref, dgain_ref, dtap_ref, dmix_ref, allow_ref, same_ref, pad_ref, y_ref, dm_ref = refs[-9:]
    g = pl.program_id(0)
    n = q_ref.shape[1]
    scale = HD ** (-0.5)

    @pl.when(g == 0)
    def _():
        doc_masks(drow_ref, dcol_ref, allow_ref, same_ref)
        pad_ref[n : n + 8, :] = jnp.zeros((8, n), F32)

    for c in range(2):
        rows = slice(c * HD, (c + 1) * HD)
        att = att_ref[rows, :]
        centre = att - jnp.mean(att, axis=0, keepdims=True)
        rstd = lax.rsqrt(jnp.mean(centre * centre, axis=0, keepdims=True) + 1e-05)
        hat = centre * rstd
        dgrp = dgrp_ref[rows, :]
        dgain_ref[rows, :] = jnp.sum(dgrp * hat, axis=1, keepdims=True)
        dhat = dgrp * gain_ref[rows, :]
        datt = rstd * (
            dhat
            - jnp.mean(dhat, axis=0, keepdims=True)
            - hat * jnp.mean(dhat * hat, axis=0, keepdims=True)
        )
        datt = datt.astype(BF)
        mixed = (mix_ref[g, 2 * c] * prob_ref[0] + mix_ref[g, 2 * c + 1] * prob_ref[1]).astype(BF)
        d_ref[2, rows, :] = dot(datt, mixed, 1, 0).astype(BF)
        dmixed = dot(datt, v_ref[rows, :], 0, 0)
        dm_ref[c] = dmixed
        for e in range(2):
            dmix_ref[0, 2 * c + e : 2 * c + e + 1, :] = jnp.sum(dmixed * prob_ref[e], axis=0, keepdims=True)
    dmix_ref[0, 4:8, :] = jnp.zeros((4, n), F32)
    row = lax.broadcasted_iota(jnp.int32, (128, 128), 0)
    col = lax.broadcasted_iota(jnp.int32, (128, 128), 1)
    off = col - row
    half = CK // 2
    for e in range(2):
        rows = slice(e * HD, (e + 1) * HD)
        q = q_ref[rows, :]
        k = k_ref[rows, :]
        allowed = allow_ref[...] > 0
        masked_t = dot(k, q, 0, 0) * scale
        prob = prob_ref[e]
        dprob = mix_ref[g, e] * dm_ref[0] + mix_ref[g, 2 + e] * dm_ref[1]
        pad_ref[0:n, :] = prob * (dprob - jnp.sum(prob * dprob, axis=1, keepdims=True))
        for a in range(CQ):
            y_ref[:, a * n : (a + 1) * n] = jnp.where(same_ref[...] > 0, pad_ref[a : a + n, :], 0.0).astype(BF)
        dlog = jnp.where(allowed, dot(y_ref[...], tt_ref[e], 1, 0), 0.0).astype(BF)
        d_ref[0, rows, :] = (dot(k, dlog, 1, 1) * scale).astype(BF)
        d_ref[1, rows, :] = (dot(q, dlog, 1, 0) * scale).astype(BF)
        krow = lax.broadcasted_iota(jnp.int32, (n, n), 0)
        qcol = lax.broadcasted_iota(jnp.int32, (n, n), 1)
        masked_t = jnp.where((same_ref[...] > 0) & (krow <= qcol), masked_t, 0.0).astype(BF)
        for a in range(CQ):
            full = dot(masked_t, y_ref[:, a * n : (a + 1) * n], 1, 0)
            fold = jnp.zeros((128, 128), F32)
            blocks = n // 128
            for r in range(blocks):
                fold = fold + full[r * 128 : (r + 1) * 128, r * 128 : (r + 1) * 128]
            fold = jnp.where(jnp.abs(off) <= half, fold, 0.0)
            for r in range(blocks - 1):
                up = full[r * 128 : (r + 1) * 128, (r + 1) * 128 : (r + 2) * 128]
                down = full[(r + 1) * 128 : (r + 2) * 128, r * 128 : (r + 1) * 128]
                fold = fold + jnp.where(off <= half - 128, up, 0.0) + jnp.where(off >= 128 - half, down, 0.0)
            lined = fold[0:8, :]
            for t in range(1, 16):
                lined = lined + pltpu.roll(fold[8 * t : 8 * t + 8, :], 128 - 8 * t, 1)
            dtap_ref[e, 8 * a : 8 * a + 8, :] = lined


def attend_back(packed_t, docs, tt, mix, gain, prob, att, dgrp, start, count, before=()):
    n = packed_t.shape[1]
    blk = lambda off: pl.BlockSpec((PW, n), lambda g: (g + off, 0))
    whole = lambda s: pl.BlockSpec(s, lambda g: (0, 0))
    thin = lambda off: pl.BlockSpec((PW, 1), lambda g: (g + off, 0))
    rows = count * PW
    d_packed, dgain, dtap, dmix = pl.pallas_call(
        attend_back_kernel,
        cost_estimate=cost(2.7 * count),
        grid=(count,),
        in_specs=[
            pl.BlockSpec(memory_space=pltpu.SMEM),
            blk(start), blk(PAIRS + start), blk(2 * PAIRS + start),
            pl.BlockSpec((2, CQ * n, n), lambda g: (g + start, 0, 0)),
            whole((1, n)), whole((n, 1)), thin(start),
            pl.BlockSpec((2, n, n), lambda g: (g, 0, 0)),
            blk(0), blk(start),
        ]
        + [pl.BlockSpec(memory_space=pl.ANY)] * len(before),
        out_specs=[
            pl.BlockSpec((3, PW, n), lambda g: (0, g + start, 0)), thin(0),
            pl.BlockSpec((2, 8 * CQ, 128), lambda g: (g, 0, 0)),
            pl.BlockSpec((1, 8, n), lambda g: (g, 0, 0)),
        ],
        out_shape=[
            jax.ShapeDtypeStruct((3, D, n), BF),
            jax.ShapeDtypeStruct((rows, 1), F32),
            jax.ShapeDtypeStruct((2 * count, 8 * CQ, 128), F32),
            jax.ShapeDtypeStruct((count, 8, n), F32),
        ],
        scratch_shapes=[
            pltpu.VMEM((n, n), F32), pltpu.VMEM((n, n), F32), pltpu.VMEM((n + 8, n), F32),
            pltpu.VMEM((n, CQ * n), BF), pltpu.VMEM((2, n, n), F32),
        ],
        input_output_aliases={11: 0} if before else {},
        compiler_params=pltpu.CompilerParams(vmem_limit_bytes=60 * 2**20),
    )(
        mix[start : start + count].reshape(count, 4), packed_t, packed_t, packed_t, tt,
        docs.reshape(1, n), docs.reshape(n, 1), gain, prob, att, dgrp, *before,
    )
    lane = jnp.arange(128)[None, None, :] - jnp.arange(8)[None, :, None]
    tap = jnp.arange(CK)[:, None, None] - CK // 2
    pick = (jnp.remainder(lane - tap, 128) == 0).astype(F32)
    dtap = jnp.sum(dtap.reshape(2 * count, CQ, 1, 8, 128) * pick, axis=(3, 4))
    dmix = jnp.sum(dmix[:, :4, :], axis=2)
    return d_packed, dgain, dtap.reshape(2 * count, CQ * CK), dmix.reshape(count, 2, 2)


def rms_norm(values, gain):
    return values * lax.rsqrt(jnp.mean(values * values, axis=-1, keepdims=True) + 1e-05) * gain


def rms_back(values, gain, grad):
    rstd = lax.rsqrt(jnp.mean(values * values, axis=-1, keepdims=True) + 1e-05)
    hat = values * rstd
    dhat = grad * gain
    dvalues = rstd * (dhat - hat * jnp.mean(dhat * hat, axis=-1, keepdims=True))
    return dvalues, jnp.sum(grad * hat, axis=0)


class Slice:
    def __init__(self, reps, shards):
        self.axes = ("rep", "fsdp")
        self.shards = shards
        self.lines = [[4 * o + i for o in range(shards // 4)] for i in range(4)]
        places = [(y, f) for y in range(reps) for f in range(shards)]

        def perm(move):
            out = []
            for y, f in places:
                to = move(y, f)
                out.append((y * shards + f, to[0] * shards + to[1]))
            return out

        self.hops = {
            (dy, di): perm(lambda y, f, dy=dy, di=di: (y ^ dy, f ^ di))
            for dy in range(2)
            for di in (range(16) if shards == 16 else range(4))
        }
        self.corner = perm(lambda y, f: (y, f ^ 2) if f & 1 else (1 - y, f))
        self.doubling = []
        bit = 1
        while bit < shards:
            self.doubling.append((bit, perm(lambda y, f, bit=bit: (y, f ^ bit))))
            bit *= 2
        self.rep = lax.axis_index("rep")
        self.fsdp = lax.axis_index("fsdp")
        self.odd = (self.fsdp & 1) == 1
        self.place = self.rep * 4 + (self.fsdp & 3)

    def hop(self, value, dy, di):
        return lax.ppermute(value, self.axes, self.hops[dy, di])

    def hop_block(self, value, b):
        return self.hop(value, order(b) >> 2, order(b) & 3) if b else value

    def gather_line(self, value):
        return lax.all_gather(value, "fsdp", axis=0, tiled=True, axis_index_groups=self.lines)

    def scatter_line(self, value):
        return lax.psum_scatter(
            value.astype(BF), "fsdp", scatter_dimension=0, tiled=True, axis_index_groups=self.lines
        )

    def gather_small(self, value):
        for bit, perm in self.doubling:
            other = lax.ppermute(value, self.axes, perm)
            high = (self.fsdp & bit) != 0
            value = jnp.concatenate(
                [jnp.where(high, other, value), jnp.where(high, value, other)], axis=0
            )
        return value

    def sides(self, value):
        return self.hop(value, 0, 2), self.hop(value, 1, 0)

    def far_corner(self, along_x, along_y):
        return lax.ppermute(jnp.where(self.odd, along_y, along_x), self.axes, self.corner)

    def near_blocks(self, value, along_x, along_y, corner):
        near = jnp.concatenate([value, along_x, along_y, jnp.zeros_like(value)], axis=0)
        return lax.dynamic_update_slice(near, corner, (3 * value.shape[0], 0))

    def scatter_corner(self, near, far):
        own, to_x, to_y, last = (a + b.astype(F32) for a, b in zip(near, far))
        corner = lax.ppermute(last.astype(BF), self.axes, self.corner).astype(F32)
        to_x = (to_x + jnp.where(self.odd, 0.0, corner)).astype(BF)
        to_y = (to_y + jnp.where(self.odd, corner, 0.0)).astype(BF)
        return own, to_x, to_y

    def scatter_last(self, own, to_x, to_y):
        return own + self.hop(to_x, 0, 2).astype(F32) + self.hop(to_y, 1, 0).astype(F32)

    def scatter_line_small(self, value):
        lines = self.shards // 4
        if lines != 4:
            return self.scatter_line(value).astype(F32)
        rows = value.shape[0] // lines
        value = value.astype(BF)
        line = self.fsdp // 4
        part = lambda d: lax.dynamic_slice_in_dim(value, (line ^ d) * rows, rows, axis=0)
        return sum([self.hop(part(d), 0, 4 * d).astype(F32) for d in range(1, 4)], part(0).astype(F32))

    def sum_small(self, value):
        value = value + self.hop(value, 1, 0)
        for _, perm in self.doubling:
            value = value + lax.ppermute(value, self.axes, perm)
        return value

    def both_halves(self, half, axis=0, other=None):
        if other is None:
            other = self.hop(half, 1, 0)
        first = self.rep == 0
        return jnp.concatenate(
            [jnp.where(first, half, other), jnp.where(first, other, half)], axis=axis
        ).astype(F32)

    def own_half(self, shard):
        rows = shard.shape[0] // 2
        return lax.dynamic_slice_in_dim(shard, self.rep * rows, rows, axis=0)


def on_device(
    reps,
    shards,
    tokens,
    doc_ids,
    norm_gain,
    qkv_weight,
    group_gain,
    out_weight,
    ffn_gain,
    gate_weight,
    up_weight,
    down_weight,
    conv_kernel,
    head_mix,
    out_grad,
):
    net = Slice(reps, shards)
    lines = shards // 4
    n = tokens.shape[0]
    cols = 3 * D // shards // 2
    wide = gate_weight.shape[1] // 2

    half_out = D // shards // 2
    rows_of = lambda v: [v[b * n : (b + 1) * n] for b in range(v.shape[0] // n)]

    attn_half = jnp.concatenate([net.own_half(qkv_weight.T), net.own_half(out_weight.T)], axis=0)
    attn_half, tokens = fence(attn_half, tokens)
    w_attn = net.gather_line(attn_half).reshape(lines, -1, D)
    x_side = net.sides(tokens)
    ffn_half = jnp.concatenate(
        [net.own_half(gate_weight.T), net.own_half(up_weight.T), net.own_half(down_weight)], axis=0
    )
    taps = band_taps(conv_kernel, n)
    gains = net.gather_small(jnp.stack([norm_gain, group_gain, ffn_gain])[None])
    *x_side, ffn_half, gains, d_low, taps_hi, taps_lo, taps_back = fence(
        *x_side, ffn_half, gains, out_grad.astype(BF), *taps
    )
    w_ffn = net.gather_line(ffn_half).reshape(lines, -1, D)
    gains = gains.transpose(1, 0, 2).reshape(3, D).astype(F32)
    corner = net.far_corner(*x_side)
    d_side = net.sides(d_low)
    w_attn = fence(w_attn, time=100)[0]
    corner, *d_side, w_attn = fence(corner, *d_side, w_attn)
    x_near = net.near_blocks(tokens, *x_side, corner)
    x_far = net.hop(x_near, 0, 1)
    d_near = net.near_blocks(d_low, *d_side, net.far_corner(*d_side))
    inputs = tokens.astype(F32)

    norm_near, parts = project(x_near, gains[0], w_attn, cols, n)
    norm_far, more = project(x_far, gains[0], w_attn, cols, n)
    pieces = [net.hop_block(p, b) for b, p in enumerate((*parts, *more))]
    *pieces, w_cls, d_near = fence(*pieces, w_attn[:, cols:].reshape(-1, D), d_near)
    d_far = net.hop(d_near, 0, 1)
    w_side = (*net.sides(w_cls), net.hop(w_cls, 1, 2))
    packed_t = join(pieces, net.place, lines, cols)
    group_col = gains[1].reshape(D, 1)
    heads = PAIRS // 2
    front = functools.partial(attend, packed_t, doc_ids, taps_hi, taps_lo, head_mix, group_col)
    *w_side, prob_a, att_a, grouped = fence(*w_side, *front(0, heads))
    w_near = (w_cls, *w_side)
    w_far = [net.hop(w, 0, 1) for w in w_near]
    *w_far, prob_b, att_b, grouped = fence(*w_far, *front(heads, PAIRS - heads, (grouped,)))
    w_out = join([*w_near, *w_far], net.place, lines, half_out)

    middle = inputs + dot(grouped, w_out, 0, 1)
    second = rms_norm(middle, gains[2]).astype(BF)
    s_side = net.sides(second)
    s_near = net.near_blocks(second, *s_side, net.far_corner(*s_side))
    s_far = net.hop(s_near, 0, 1)

    w_ffn = fence(w_ffn, time=100)[0]
    run_a = ffn(s_near, d_near, w_ffn, n, F32, 0, 2)
    *run_a, s_far = fence(*run_a, s_far)
    run_f = ffn(s_far, d_far, w_ffn, n, BF, 0, 4)
    run_b = ffn(s_near, d_near, w_ffn, n, F32, 2, 2)
    ds_far, yo_far = net.hop(run_f[2], 0, 1), net.hop(run_f[3], 0, 1)
    own, to_x, to_y = net.scatter_corner(rows_of(run_a[2]) + rows_of(run_b[2]), rows_of(ds_far))
    acts = [r[i] for i in range(2) for r in (run_a, run_f, run_b)]
    to_x, to_y, *acts = fence(to_x, to_y, *acts)
    d_second = net.scatter_last(own, to_x, to_y)
    g_ffn = ffn_grad(
        acts[:3], acts[3:], [(s_near, 0), (s_far, 0), (s_near, 2)], [(d_near, 0), (d_far, 0), (d_near, 2)],
        lines, wide, n,
    )
    d_second, yo_far, g_ffn = fence(d_second, yo_far, g_ffn)
    g_ffn = fence(net.scatter_line(g_ffn.reshape(-1, D)), time=60)[0]

    d_norm, g_ffn_gain = rms_back(middle, gains[2], d_second)
    d_middle = out_grad + d_norm
    branch = d_middle.astype(BF)
    d_grouped = dot(w_out, branch, 0, 1)
    back = functools.partial(attend_back, packed_t, doc_ids, taps_back, head_mix, group_col)
    own, to_x, to_y = net.scatter_corner(rows_of(run_a[3]) + rows_of(run_b[3]), rows_of(yo_far))
    first = back(prob_a, att_a, d_grouped, 0, heads)
    to_x, to_y, *first = fence(to_x, to_y, *first)
    layer_out = (middle + net.scatter_last(own, to_x, to_y)).astype(BF)
    d_packed, *last = back(prob_b, att_b, d_grouped, heads, PAIRS - heads, first[:1])
    g_group, g_taps, g_mix = (jnp.concatenate([a, b], axis=0) for a, b in zip(first[1:], last))
    pieces = cut(d_packed.reshape(3 * D, n), net.place, lines, cols)
    pieces = [net.hop_block(p, b) for b, p in enumerate(pieces)]
    g_blocks = out_weight_grad(branch, grouped, net.place, lines, half_out)
    g_far = [net.hop(g, 0, 1) for g in g_blocks[4:]]
    *pieces, g_ffn = fence(*pieces, g_ffn)
    own, to_x, to_y = net.scatter_corner(g_blocks[:4], g_far)
    g_other = net.hop(g_ffn, 1, 0)
    far = back_project(pieces[4:], x_far, norm_far, w_attn, cols, n, BF)
    to_x, to_y, *far = fence(to_x, to_y, *far)
    g_out = net.scatter_last(own, to_x, to_y)
    dn_far = net.hop(far[0], 0, 1)
    near = back_project(pieces[:4], x_near, norm_near, w_attn, cols, n, F32, far[1:])
    g_other, *near = fence(g_other, *near)
    g_qkv = fence(net.scatter_line(near[1]), time=30)[0]
    g_qkv = net.both_halves(g_qkv).T
    g_out = net.both_halves(net.scatter_line_small(g_out).astype(BF)).T
    shape = (3, wide, D)
    g_ffn = net.both_halves(g_ffn.reshape(shape), 1, g_other.reshape(shape))
    g_gate, g_up, g_down = g_ffn[0].T, g_ffn[1].T, g_ffn[2]
    own, to_x, to_y = net.scatter_corner(rows_of(near[0]), rows_of(dn_far))
    d_normed = net.scatter_last(own, to_x, to_y)
    d_in = rms_back(inputs, gains[0], d_normed)[0]
    input_grad = d_middle + d_in

    small = net.sum_small(
        jnp.concatenate([near[2][0], g_group[:, 0], g_ffn_gain, g_taps.reshape(-1), g_mix.reshape(-1)])
    )
    part = D // shards
    gain_grads = [
        lax.dynamic_slice_in_dim(small, b * D + net.fsdp * part, part) for b in range(3)
    ]
    g_taps = small[3 * D : 3 * D + H * CQ * CK].reshape(H, CQ * CK)
    g_mix = small[3 * D + H * CQ * CK :].reshape(PAIRS, 2, 2)
    return (
        layer_out,
        input_grad,
        gain_grads[0],
        g_qkv,
        gain_grads[1],
        g_out,
        gain_grads[2],
        g_gate,
        g_up,
        g_down,
        g_taps,
        g_mix,
    )


def solution(mesh):
    placed = (
        P(("rep", "fsdp"), None),
        P(("rep", "fsdp")),
        P("fsdp"),
        P(None, "fsdp"),
        P("fsdp"),
        P(None, "fsdp"),
        P("fsdp"),
        P(None, "fsdp"),
        P(None, "fsdp"),
        P("fsdp", None),
        P(),
        P(),
        P(("rep", "fsdp"), None),
    )
    return jax.shard_map(
        functools.partial(on_device, mesh.shape["rep"], mesh.shape["fsdp"]),
        mesh=mesh,
        in_specs=placed,
        out_specs=(
            P(("rep", "fsdp"), None),
            P(("rep", "fsdp"), None),
            P("fsdp"),
            P(None, "fsdp"),
            P("fsdp"),
            P(None, "fsdp"),
            P("fsdp"),
            P(None, "fsdp"),
            P(None, "fsdp"),
            P("fsdp", None),
            P(),
            P(),
        ),
        check_vma=False,
    )
```

time: 609 us -> 527 us (0.87)
  Pallas kernels: 57.6 us -> 178 us
  matrix products: 105 us -> 8.8 us
  waiting for transfers between devices: 218 us -> 140 us
  blocking collectives: 38.8 us -> 0 us
  starting transfers between devices: 48.3 us -> 66.8 us
  local copies, waits for them, and re-layouts: 56 us -> 41.4 us
  other arithmetic: 64.8 us -> 72.5 us
    pallas_call x3 -> x34, Pallas kernels: 57.6 us -> 178 us  [the longest x3 34.4 us: ffn(): pl.pallas_call(ffn_kernel, cost_estimate=cost(3.8 * count), grid=(count,)...]
    dot_general x21 -> x2, matrix products: 105 us -> 8.8 us  [dot(): lax.dot_general(a, b, (((ca,), (cb,)), ((), ())), preferred_element_type=...]
    ppermute x37 -> x52, waiting for transfers between devices: 141 us -> 84.8 us  [hop(): return lax.ppermute(value, self.axes, self.hops[dy, di])]
    psum x1 -> x0, blocking collectives: 38.8 us -> none  [on_device(): lax.psum(jnp.concatenate([g_norm, g_group, g_ffn_gain, g_taps.reshape(-1)...]
    reduce_scatter x1 -> x0, waiting for transfers between devices: 26.1 us -> none  [on_device(): g_out = lax.psum_scatter(g_out, 'fsdp', scatter_dimension=0, tiled=True)]
    convert_element_type x9 -> x14, other arithmetic: 13.5 us -> 34.5 us  [the longest x3 11.2 us: scatter_corner(): to_y = (to_y + jnp.where(self.odd, corner, 0.0)).astype(BF)]
    scatter x4 -> x0, local copies, waits for them, and re-layouts: 12.7 us -> none  [the longest x2 6.41 us: band_taps(): bwd.at[:, :CQ, :half + 1].set(flip[:, :, half:]).at[:, :CQ, n - half:]]
    reduce_scatter x3 -> x2, waiting for transfers between devices: 0.02 us -> 11.7 us  [scatter_line(): lax.psum_scatter(value.astype(BF), 'fsdp', scatter_dimension=0, tiled=Tru...]
  transfers between devices with their start and end apart: 55 -> 71, of which waited for: 25 -> 30; matrix products, arithmetic and copies ran while one was open for 33% -> 20% of each run, Pallas kernels for 10% -> 31%
where the time goes in v2:
time: 527 us; the launch traced here: 522 us
  Pallas kernels  178 us (34%)
  waiting for transfers between devices  140 us (27%)
  other arithmetic  72.5 us (14%)
  starting transfers between devices  66.8 us (13%)
  local copies, waits for them, and re-layouts  41.4 us (8%)
  between operations  14.9 us (3%)
  matrix products  8.8 us (2%)
    ppermute x52, waiting for transfers between devices, hop(): return lax.ppermute(value, self.axes, self.hops[dy, di])  84.8 us
    ppermute x52, starting transfers between devices, hop(): return lax.ppermute(value, self.axes, self.hops[dy, di])  48.7 us
    pallas_call x3, Pallas kernels, ffn(): pl.pallas_call(ffn_kernel, cost_estimate=cost(3.8 * count), grid=(count,)...  34.4 us
    pallas_call x2, Pallas kernels, attend(): pl.pallas_call(attend_kernel, cost_estimate=cost(2.7 * count), grid=(coun...  26.7 us
    pallas_call x2, Pallas kernels, attend_back(): pl.pallas_call(attend_back_kernel, cost_estimate=cost(2.7 * count), grid=...  25.9 us
    pallas_call x2, Pallas kernels, back_project(): pl.pallas_call(functools.partial(back_project_kernel, count), cost_estima...  22.7 us
    pallas_call x1, Pallas kernels, ffn_grad(): pl.pallas_call(functools.partial(ffn_grad_kernel, counts), cost_estimate=...  18.5 us
    unnamed x124, local copies, waits for them, and re-layouts  16.4 us
  transfers between devices with their start and end apart: 71, of which 30 were waited for; matrix products, arithmetic and copies ran while one was open for 20% of the time, Pallas kernels for 31%

profile of v2, /device:TPU:0, one launch (start us, length us, event | category | flops | bytes accessed | tf_op | source)
XLA Modules:
  0.0 522.2 jit_solution(7847920687875822557)
XLA Ops:
  17.0 16.1 %shard_map.221 = (bf16[16,1536,256]{2,1,0:T(8,128)(2,1)}, bf16[16,1536,256]{2,1,0:T(8,128)(2,1)}, bf16[16,1536,256]{2,1,0:T(8,128)(2,1)}) custom-call(f32[16,8,256]{2,1,0:T(8,128)} %pad.7.fwd_ref, f32[16,8,256]{2,1,0:T(8,128)} %pad.8.bwd_ref), custom_call_target="tpu_custom_call" | custom-call | flops 8000000000 | tf_op jit(solution)/shard_map/pallas_call | solution.py:63
  53.2 12.3 %all-gather.3.cloned.1.call-done = bf16[768,1536]{1,0:T(8,128)(2,1)} async-done(((bf16[192,1536]{1,0:T(8,128)(2,1)}), bf16[768,1536]{1,0:T(8,128)(2,1)}) %all-gather.3.cloned.1.call-update) | async-done | bytes 2359312 | tf_op jit(solution)/shard_map/all_gather | solution.py:675
  65.5 10.2 %collective-permute-done.6.refs_0_ = bf16[256,1536]{1,0:T(8,128)(2,1)} collective-permute-done((bf16[256,1536]{1,0:T(8,128)(2,1)}, bf16[256,1536]{1,0:T(8,128)(2,1)}, u32[]{:S(2)}, u32[]{:S(2)}) %collective-permute-start.6) | collective-permute-done | bytes 786464 | tf_op jit(solution)/shard_map/ppermute | solution.py:695
  77.5 4.6 maximum_maximum_fusion.1
  86.5 7.5 %shard_map.225 = (bf16[1024,1536]{1,0:T(8,128)(2,1)}, bf16[576,256]{1,0:T(8,128)(2,1)}, bf16[576,256]{1,0:T(8,128)(2,1)}, bf16[576,256]{1,0:T(8,128)(2,1)}, bf16[576,256]{1,0:T(8,128)(2,1)}) custom-call(bf16[1024,1536]{1,0:T(8,128)(2,1)} %constant_dynamic-update-slice_fusion.2.x_ref.refs_4_, f32[1,1536]{1,0:T(1,128)} %slice.156.gain_ref, ...), custom_call_target="tpu_custom_call" | custom-call | flops 2400000000 | tf_op jit(solution)/shard_map/pallas_call | solution.py:109
  97.5 7.4 %shard_map.226 = (bf16[1024,1536]{1,0:T(8,128)(2,1)}, bf16[576,256]{1,0:T(8,128)(2,1)}, bf16[576,256]{1,0:T(8,128)(2,1)}, bf16[576,256]{1,0:T(8,128)(2,1)}, bf16[576,256]{1,0:T(8,128)(2,1)}) custom-call(bf16[1024,1536]{1,0:T(8,128)(2,1)} %collective-permute-done.12.x_ref.refs_4_, f32[1,1536]{1,0:T(1,128)} %slice.156.gain_ref, ...), custom_call_target="tpu_custom_call" | custom-call | flops 2400000000 | tf_op jit(solution)/shard_map/pallas_call | solution.py:109
  134.0 13.4 %shard_map.229 = (f32[8,256,256]{2,1,0:T(8,128)}, f32[768,256]{1,0:T(8,128)}, bf16[1536,256]{1,0:T(8,128)(2,1)}) custom-call(f32[4,4]{1,0:T(4,128)} %copy.164.mix_ref, bf16[4608,256]{1,0:T(8,128)(2,1)} %bitcast.52, bf16[4608,256]{1,0:T(8,128)(2,1)} %bitcast.53, bf16[4608,256]{1,0:T(8,128)(2,1)} %bitcast.54, ...), custom_call_target="tpu_custom_call" | custom-call | flops 5400000000 | tf_op jit(solution)/shard_map/pallas_call | solution.py:476
  147.4 9.6 %collective-permute-done.20.refs_1_ = bf16[192,1536]{1,0:T(8,128)(2,1)S(1)} collective-permute-done((bf16[192,1536]{1,0:T(8,128)(2,1)}, bf16[192,1536]{1,0:T(8,128)(2,1)S(1)}, u32[]{:S(2)}, u32[]{:S(2)}) %collective-permute-start.20) | collective-permute-done | bytes 589856 | tf_op jit(solution)/shard_map/ppermute | solution.py:669
  159.3 13.4 %shard_map.231 = (f32[8,256,256]{2,1,0:T(8,128)}, f32[768,256]{1,0:T(8,128)}, bf16[1536,256]{1,0:T(8,128)(2,1)}) custom-call(f32[4,4]{1,0:T(4,128)} %copy.167.mix_ref, bf16[4608,256]{1,0:T(8,128)(2,1)} %bitcast.55, bf16[4608,256]{1,0:T(8,128)(2,1)} %bitcast.56, bf16[4608,256]{1,0:T(8,128)(2,1)} %bitcast.57, ...), custom_call_target="tpu_custom_call", output_to_operand_aliasing={{2}: (9, {})} | custom-call | flops 5400000000 | tf_op jit(solution)/shard_map/pallas_call | solution.py:476
  173.9 4.9 shard_map.233
  184.6 18.4 %collective-permute-done.26 = bf16[256,1536]{1,0:T(8,128)(2,1)S(1)} collective-permute-done((bf16[256,1536]{1,0:T(8,128)(2,1)S(1)}, bf16[256,1536]{1,0:T(8,128)(2,1)S(1)}, u32[]{:S(2)}, u32[]{:S(2)}) %collective-permute-start.26) | collective-permute-done | bytes 786464 | tf_op jit(solution)/shard_map/ppermute | solution.py:669
  204.9 5.4 %maximum_maximum_fusion.2 = bf16[1024,1536]{1,0:T(8,128)(2,1)} fusion(bf16[256,1536]{1,0:T(8,128)(2,1)S(1)} %collective-permute-done.26, bf16[256,1536]{1,0:T(8,128)(2,1)S(1)} %collective-permute-done.25, bf16[256,1536]{1,0:T(8,128)(2,1)S(1)} %multiply_convert_fusion, bf16[1024]{0:T(1024)(128)(2,1)S(1)} %pad.32.clone), kind=kLoop, calls=%fused_computation.2 | loop fusion | flops 12582912 | bytes 5507072 | tf_op jit(solution)/shard_map/concatenate | solution.py:698
  210.3 4.9 collective-permute-done.27
  216.2 9.7 %shard_map.235 = (bf16[512,512]{1,0:T(8,128)(2,1)}, bf16[512,1024]{1,0:T(8,128)(2,1)}, f32[512,1536]{1,0:T(8,128)}, f32[512,1536]{1,0:T(8,128)}) custom-call(bf16[1024,1536]{1,0:T(8,128)(2,1)} %constant_dynamic-update-slice_fusion.s_ref.refs_6_.refs_8_, bf16[1024,1536]{1,0:T(8,128)(2,1)} %get-tuple-element.197.o_ref.refs_9_.refs_11_, ...), custom_call_target="tpu_custom_call" | custom-call | flops 3800000000 | tf_op jit(solution)/shard_map/pallas_call | solution.py:281
  225.9 15.0 %shard_map.237 = (bf16[1024,512]{1,0:T(8,128)(2,1)}, bf16[1024,1024]{1,0:T(8,128)(2,1)}, bf16[1024,1536]{1,0:T(8,128)(2,1)}, bf16[1024,1536]{1,0:T(8,128)(2,1)}) custom-call(bf16[1024,1536]{1,0:T(8,128)(2,1)} %get-tuple-element.205.s_ref.refs_7_, bf16[1024,1536]{1,0:T(8,128)(2,1)} %collective-permute-done.29.o_ref.refs_10_, ...), custom_call_target="tpu_custom_call" | custom-call | flops 7600000000 | tf_op jit(solution)/shard_map/pallas_call | solution.py:281
  241.4 9.7 %shard_map.238 = (bf16[512,512]{1,0:T(8,128)(2,1)}, bf16[512,1024]{1,0:T(8,128)(2,1)}, f32[512,1536]{1,0:T(8,128)}, f32[512,1536]{1,0:T(8,128)}) custom-call(bf16[1024,1536]{1,0:T(8,128)(2,1)} %constant_dynamic-update-slice_fusion.s_ref.refs_6_.refs_8_, bf16[1024,1536]{1,0:T(8,128)(2,1)} %get-tuple-element.197.o_ref.refs_9_.refs_11_, ...), custom_call_target="tpu_custom_call" | custom-call | flops 3800000000 | tf_op jit(solution)/shard_map/pallas_call | solution.py:281
  254.8 10.3 %collective-permute-done.31 = bf16[256,1536]{1,0:T(8,128)(2,1)S(1)} collective-permute-done((bf16[256,1536]{1,0:T(8,128)(2,1)S(1)}, bf16[256,1536]{1,0:T(8,128)(2,1)S(1)}, u32[]{:S(2)}, u32[]{:S(2)}) %collective-permute-start.31) | collective-permute-done | bytes 786464 | tf_op jit(solution)/shard_map/ppermute | solution.py:703
  270.8 18.5 %shard_map.240.refs_2_ = bf16[4,384,1536]{2,1,0:T(8,128)(2,1)} custom-call(bf16[512,512]{1,0:T(8,128)(2,1)} %get-tuple-element.217.refs_0_, bf16[1024,512]{1,0:T(8,128)(2,1)} %get-tuple-element.218.refs_1_, bf16[512,512]{1,0:T(8,128)(2,1)} %get-tuple-element.219.refs_2_, bf16[512,1024]{1,0:T(8,128)(2,1)} %get-tuple-element.220.refs_3_, ...), custom_call_target="tpu_custom_call" | custom-call | flops 8999999488 | tf_op jit(solution)/shard_map/pallas_call | solution.py:344
  301.7 6.4 %shard_map.248 = (f32[192,1536]{1,0:T(8,128)}, f32[192,1536]{1,0:T(8,128)}, f32[192,1536]{1,0:T(8,128)}, f32[192,1536]{1,0:T(8,128)}, bf16[192,1536]{1,0:T(8,128...) custom-call(s32[1]{0:T(128)} %bitcast.12.place_ref, ...), custom_call_target="tpu_custom_call" | custom-call | tf_op jit(solution)/shard_map/pallas_call | solution.py:195
  308.1 4.9 fusion.31.dgrp_ref
  313.0 13.1 %shard_map.242 = (bf16[3,1536,256]{2,1,0:T(8,128)(2,1)}, f32[768,1]{1,0:T(8,128)}, f32[8,48,128]{2,1,0:T(8,128)}, f32[4,8,256]{2,1,0:T(8,128)}) custom-call(f32[4,4]{1,0:T(4,128)} %copy.164.mix_ref, bf16[4608,256]{1,0:T(8,128)(2,1)} %bitcast.58, bf16[4608,256]{1,0:T(8,128)(2,1)} %bitcast.59, bf16[4608,256]{1,0:T(8,128)(2,1)} %bitcast.60, ...), custom_call_target="tpu_custom_call" | custom-call | flops 5400000000 | tf_op jit(solution)/shard_map/pallas_call | solution.py:584
  335.3 4.5 fusion.13
  339.8 12.8 %shard_map.244 = (bf16[3,1536,256]{2,1,0:T(8,128)(2,1)}, f32[768,1]{1,0:T(8,128)}, f32[8,48,128]{2,1,0:T(8,128)}, f32[4,8,256]{2,1,0:T(8,128)}) custom-call(f32[4,4]{1,0:T(4,128)} %copy.167.mix_ref, bf16[4608,256]{1,0:T(8,128)(2,1)} %bitcast.61, bf16[4608,256]{1,0:T(8,128)(2,1)} %bitcast.62, ...), custom_call_target="tpu_custom_call", output_to_operand_aliasing={{0}: (11, {})} | custom-call | flops 5400000000 | tf_op jit(solution)/shard_map/pallas_call | solution.py:584
  373.2 4.2 reduce-scatter.3.cloned.1.call-done.refs_0_
  377.8 5.9 %collective-permute-done.43.refs_6_ = bf16[576,256]{1,0:T(8,128)(2,1)S(1)} collective-permute-done((bf16[576,256]{1,0:T(8,128)(2,1)}, bf16[576,256]{1,0:T(8,128)(2,1)S(1)}, u32[]{:S(2)}, u32[]{:S(2)}) %collective-permute-start.43) | collective-permute-done | bytes 294944 | tf_op jit(solution)/shard_map/ppermute | solution.py:669
  385.4 10.8 %shard_map.249 = (bf16[1024,1536]{1,0:T(8,128)(2,1)}, f32[576,1536]{1,0:T(8,128)}, f32[1,1536]{1,0:T(1,128)}) custom-call(bf16[576,256]{1,0:T(8,128)(2,1)} %get-tuple-element.260.refs_0_, bf16[576,256]{1,0:T(8,128)(2,1)} %get-tuple-element.261.refs_1_, bf16[576,256]{1,0:T(8,128)(2,1)} %get-tuple-element.262.refs_2_, ...), custom_call_target="tpu_custom_call" | custom-call | flops 5000000000 | tf_op jit(solution)/shard_map/pallas_call | solution.py:403
  408.0 4.9 collective-permute-done.62
  418.5 11.2 %collective-permute-done.37 = bf16[256,1536]{1,0:T(8,128)(2,1)} collective-permute-done((bf16[256,1536]{1,0:T(8,128)(2,1)}, bf16[256,1536]{1,0:T(8,128)(2,1)}, u32[]{:S(2)}, u32[]{:S(2)}) %collective-permute-start.37) | collective-permute-done | bytes 786464 | tf_op jit(solution)/shard_map/ppermute | solution.py:669
  439.2 12.0 %shard_map.251 = (f32[1024,1536]{1,0:T(8,128)}, bf16[576,1536]{1,0:T(8,128)(2,1)}, f32[1,1536]{1,0:T(1,128)}) custom-call(bf16[576,256]{1,0:T(8,128)(2,1)} %get-tuple-element.249.refs_0_, bf16[576,256]{1,0:T(8,128)(2,1)} %get-tuple-element.250.refs_1_, bf16[576,256]{1,0:T(8,128)(2,1)} %get-tuple-element.251.refs_2_, ...), custom_call_target="tpu_custom_call" | custom-call | flops 5000000000 | tf_op jit(solution)/shard_map/pallas_call | solution.py:403
  482.1 4.1 fusion.15
  488.9 7.5 %reduce-scatter.5.cloned.1.call-done.refs_0_ = bf16[144,1536]{1,0:T(8,128)(2,1)} async-done(((bf16[576,1536]{1,0:T(8,128)(2,1)}), bf16[144,1536]{1,0:T(8,128)(2,1)}) %reduce-scatter.5.cloned.1.call-update) | async-done | bytes 442384 | tf_op jit(solution)/shard_map/reduce_scatter | solution.py:678
  497.8 9.1 %collective-permute-done.53 = bf16[256,1536]{1,0:T(8,128)(2,1)S(1)} collective-permute-done((bf16[256,1536]{1,0:T(8,128)(2,1)}, bf16[256,1536]{1,0:T(8,128)(2,1)S(1)}, u32[]{:S(2)}, u32[]{:S(2)}) %collective-permute-start.53) | collective-permute-done | bytes 786464 | tf_op jit(solution)/shard_map/ppermute | solution.py:669
  (384 shorter events, 204.6 us)
Async XLA Ops:
  7.2 58.3 %all-gather.3.cloned.1.call-start = ((), (), s32[]{:S(2)}) async-start(), calls=%async_computation.2 | async-start | bytes 2949120 | tf_op jit(solution)/shard_map/all_gather | solution.py:675
  10.4 37.0 %collective-permute-start = (bf16[256,1536]{1,0:T(8,128)(2,1)}, bf16[256,1536]{1,0:T(8,128)(2,1)S(1)}, u32[]{:S(2)}, u32[]{:S(2)}) collective-permute-start(bf16[256,1536]{1,0:T(8,128)(2,1)} %get-tuple-element.150), channel_id=1, source_target_pairs={{0,2},{1,3},{2,0},{3,1},{4,6},{5,7},{6,4},{7,5},{8,10},{9,11},{10,... | collective-permute-start | bytes 2359304 | tf_op jit(solution)/shard_map/ppermute | solution.py:669
  13.3 34.0 %collective-permute-start.1 = (bf16[256,1536]{1,0:T(8,128)(2,1)}, bf16[256,1536]{1,0:T(8,128)(2,1)S(1)}, u32[]{:S(2)}, u32[]{:S(2)}) collective-permute-start(bf16[256,1536]{1,0:T(8,128)(2,1)} %get-tuple-element.150), channel_id=1, source_target_pairs={{0,16},{1,17},{2,18},{3,19},{4,20},{5,21},{6,22},{7,23},{8,24},{9,... | collective-permute-start | bytes 2359304 | tf_op jit(solution)/shard_map/ppermute | solution.py:669
  15.0 201.2 %all-gather.5.cloned.1.call-start = ((), (), s32[]{:S(2)}) async-start(), calls=%async_computation.3 | async-start | bytes 5898240 | tf_op jit(solution)/shard_map/all_gather | solution.py:675
  48.5 27.2 %collective-permute-start.7 = (bf16[256,1536]{1,0:T(8,128)(2,1)}, bf16[256,1536]{1,0:T(8,128)(2,1)S(1)}, u32[]{:S(2)}, u32[]{:S(2)}) collective-permute-start(bf16[256,1536]{1,0:T(8,128)(2,1)} %get-tuple-element.156), channel_id=1, source_target_pairs={{0,2},{1,3},{2,0},{3,1},{4,6},{5,7},{6,4},{7,5},{8,10},{9,11},{10,... | collective-permute-start | bytes 2359304 | tf_op jit(solution)/shard_map/ppermute | solution.py:669
  49.1 26.6 %collective-permute-start.8 = (bf16[256,1536]{1,0:T(8,128)(2,1)}, bf16[256,1536]{1,0:T(8,128)(2,1)S(1)}, u32[]{:S(2)}, u32[]{:S(2)}) collective-permute-start(bf16[256,1536]{1,0:T(8,128)(2,1)} %get-tuple-element.156), channel_id=1, source_target_pairs={{0,16},{1,17},{2,18},{3,19},{4,20},{5,21},{6,22},{7,23},{8,24},{9,... | collective-permute-start | bytes 2359304 | tf_op jit(solution)/shard_map/ppermute | solution.py:669
  51.6 24.0 %collective-permute-start.6 = (bf16[256,1536]{1,0:T(8,128)(2,1)}, bf16[256,1536]{1,0:T(8,128)(2,1)}, u32[]{:S(2)}, u32[]{:S(2)}) collective-permute-start(bf16[256,1536]{1,0:T(8,128)(2,1)} %broadcast_select_fusion.4), channel_id=1, source_target_pairs={{0,16},{1,3},{2,18},{3,1},{4,20},{5,7},{6,22},{7,5},{8,24},{9,11},... | collective-permute-start | bytes 2359304 | tf_op jit(solution)/shard_map/ppermute | solution.py:695
  84.3 293.0 %reduce-scatter.3.cloned.1.call-start = ((), (), s32[]{:S(2)}) async-start(), calls=%async_computation.4 | async-start | bytes 5898240 | tf_op jit(solution)/shard_map/reduce_scatter | solution.py:678
  84.7 25.8 %collective-permute-start.17 = (bf16[256,1536]{1,0:T(8,128)(2,1)S(1)}, bf16[256,1536]{1,0:T(8,128)(2,1)}, u32[]{:S(2)}, u32[]{:S(2)}) collective-permute-start(bf16[256,1536]{1,0:T(8,128)(2,1)S(1)} %broadcast_select_fusion.3), channel_id=1, source_target_pairs={{0,16},{1,3},{2,18},{3,1},{4,20},{5,7},{6,22},{7,5},{8,24},{9,11},... | collective-permute-start | bytes 2359304 | tf_op jit(solution)/shard_map/ppermute | solution.py:695
  96.9 23.7 %collective-permute-start.11 = (bf16[576,256]{1,0:T(8,128)(2,1)}, bf16[576,256]{1,0:T(8,128)(2,1)S(1)}, u32[]{:S(2)}, u32[]{:S(2)}) collective-permute-start(bf16[576,256]{1,0:T(8,128)(2,1)} %get-tuple-element.164), channel_id=1, source_target_pairs={{0,18},{1,19},{2,16},{3,17},{4,22},{5,23},{6,20},{7,21},{8,26},{9,... | collective-permute-start | bytes 884744 | tf_op jit(solution)/shard_map/ppermute | solution.py:669
  125.2 47.5 %collective-permute-start.18 = (bf16[192,1536]{1,0:T(8,128)(2,1)}, bf16[192,1536]{1,0:T(8,128)(2,1)S(1)}, u32[]{:S(2)}, u32[]{:S(2)}) collective-permute-start(bf16[192,1536]{1,0:T(8,128)(2,1)} %get-tuple-element.171.refs_0_), channel_id=1, source_target_pairs={{0,1},{1,0},{2,3},{3,2},{4,5},{5,4},{6,7},{7,6},{8,9},{9,8},{10,11... | collective-permute-start | bytes 1769480 | tf_op jit(solution)/shard_map/ppermute | solution.py:669
  125.2 22.2 %collective-permute-start.19 = (bf16[192,1536]{1,0:T(8,128)(2,1)}, bf16[192,1536]{1,0:T(8,128)(2,1)S(1)}, u32[]{:S(2)}, u32[]{:S(2)}) collective-permute-start(bf16[192,1536]{1,0:T(8,128)(2,1)} %get-tuple-element.171.refs_0_), channel_id=1, source_target_pairs={{0,2},{1,3},{2,0},{3,1},{4,6},{5,7},{6,4},{7,5},{8,10},{9,11},{10,... | collective-permute-start | bytes 1769480 | tf_op jit(solution)/shard_map/ppermute | solution.py:669
  129.2 27.9 %collective-permute-start.20 = (bf16[192,1536]{1,0:T(8,128)(2,1)}, bf16[192,1536]{1,0:T(8,128)(2,1)S(1)}, u32[]{:S(2)}, u32[]{:S(2)}) collective-permute-start(bf16[192,1536]{1,0:T(8,128)(2,1)} %get-tuple-element.171.refs_0_), channel_id=1, source_target_pairs={{0,16},{1,17},{2,18},{3,19},{4,20},{5,21},{6,22},{7,23},{8,24},{9,... | collective-permute-start | bytes 1769480 | tf_op jit(solution)/shard_map/ppermute | solution.py:669
  129.4 27.7 %collective-permute-start.21 = (bf16[192,1536]{1,0:T(8,128)(2,1)}, bf16[192,1536]{1,0:T(8,128)(2,1)S(1)}, u32[]{:S(2)}, u32[]{:S(2)}) collective-permute-start(bf16[192,1536]{1,0:T(8,128)(2,1)} %get-tuple-element.171.refs_0_), channel_id=1, source_target_pairs={{0,18},{1,19},{2,16},{3,17},{4,22},{5,23},{6,20},{7,21},{8,26},{9,... | collective-permute-start | bytes 1769480 | tf_op jit(solution)/shard_map/ppermute | solution.py:669
  183.0 20.0 %collective-permute-start.26 = (bf16[256,1536]{1,0:T(8,128)(2,1)S(1)}, bf16[256,1536]{1,0:T(8,128)(2,1)S(1)}, u32[]{:S(2)}, u32[]{:S(2)}) collective-permute-start(bf16[256,1536]{1,0:T(8,128)(2,1)S(1)} %multiply_convert_fusion), channel_id=1, source_target_pairs={{0,16},{1,17},{2,18},{3,19},{4,20},{5,21},{6,22},{7,23},{8,24},{9,... | collective-permute-start | bytes 2359304 | tf_op jit(solution)/shard_map/ppermute | solution.py:669
  183.3 19.7 %collective-permute-start.25 = (bf16[256,1536]{1,0:T(8,128)(2,1)S(1)}, bf16[256,1536]{1,0:T(8,128)(2,1)S(1)}, u32[]{:S(2)}, u32[]{:S(2)}) collective-permute-start(bf16[256,1536]{1,0:T(8,128)(2,1)S(1)} %multiply_convert_fusion), channel_id=1, source_target_pairs={{0,2},{1,3},{2,0},{3,1},{4,6},{5,7},{6,4},{7,5},{8,10},{9,11},{10,... | collective-permute-start | bytes 2359304 | tf_op jit(solution)/shard_map/ppermute | solution.py:669
  204.9 21.0 %collective-permute-start.29 = (bf16[1024,1536]{1,0:T(8,128)(2,1)}, bf16[1024,1536]{1,0:T(8,128)(2,1)}, u32[]{:S(2)}, u32[]{:S(2)}) collective-permute-start(bf16[1024,1536]{1,0:T(8,128)(2,1)} %get-tuple-element.197.o_ref.refs_9_.refs_11_), channel_id=1, source_target_pairs={{0,1},{1,0},{2,3},{3,2},{4,5},{5,4},{6,7},{7,6},{8,9},{9,8},{10,11... | collective-permute-start | bytes 9437192 | tf_op jit(solution)/shard_map/ppermute | solution.py:669
  251.1 41.5 %collective-permute-start.34 = (bf16[1024,1536]{1,0:T(8,128)(2,1)}, bf16[1024,1536]{1,0:T(8,128)(2,1)}, u32[]{:S(2)}, u32[]{:S(2)}) collective-permute-start(bf16[1024,1536]{1,0:T(8,128)(2,1)} %get-tuple-element.216), channel_id=1, source_target_pairs={{0,1},{1,0},{2,3},{3,2},{4,5},{5,4},{6,7},{7,6},{8,9},{9,8},{10,11... | collective-permute-start | bytes 9437192 | tf_op jit(solution)/shard_map/ppermute | solution.py:669
  268.8 20.4 %collective-permute-start.33 = (bf16[256,1536]{1,0:T(8,128)(2,1)}, bf16[256,1536]{1,0:T(8,128)(2,1)S(1)}, u32[]{:S(2)}, u32[]{:S(2)}) collective-permute-start(bf16[256,1536]{1,0:T(8,128)(2,1)} %get-tuple-element.215), channel_id=1, source_target_pairs={{0,16},{1,17},{2,18},{3,19},{4,20},{5,21},{6,22},{7,23},{8,24},{9,... | collective-permute-start | bytes 2359304 | tf_op jit(solution)/shard_map/ppermute | solution.py:669
  292.6 203.8 %reduce-scatter.5.cloned.1.call-start = ((), (), s32[]{:S(2)}) async-start(), calls=%async_computation.5 | async-start | bytes 2211840 | tf_op jit(solution)/shard_map/reduce_scatter | solution.py:678
  297.0 38.3 %collective-permute-start.35 = (bf16[256,1536]{1,0:T(8,128)(2,1)}, bf16[256,1536]{1,0:T(8,128)(2,1)}, u32[]{:S(2)}, u32[]{:S(2)}) collective-permute-start(bf16[256,1536]{1,0:T(8,128)(2,1)} %add_convert_fusion.2), channel_id=1, source_target_pairs={{0,16},{1,3},{2,18},{3,1},{4,20},{5,7},{6,22},{7,5},{8,24},{9,11},... | collective-permute-start | bytes 2359304 | tf_op jit(solution)/shard_map/ppermute | solution.py:703
  308.1 24.1 %collective-permute-start.47 = (bf16[192,1536]{1,0:T(8,128)(2,1)}, bf16[192,1536]{1,0:T(8,128)(2,1)}, u32[]{:S(2)}, u32[]{:S(2)}) collective-permute-start(bf16[192,1536]{1,0:T(8,128)(2,1)} %get-tuple-element.257), channel_id=1, source_target_pairs={{0,1},{1,0},{2,3},{3,2},{4,5},{5,4},{6,7},{7,6},{8,9},{9,8},{10,11... | collective-permute-start | bytes 1769480 | tf_op jit(solution)/shard_map/ppermute | solution.py:669
  331.6 26.3 %collective-permute-start.49 = (bf16[192,1536]{1,0:T(8,128)(2,1)}, bf16[192,1536]{1,0:T(8,128)(2,1)}, u32[]{:S(2)}, u32[]{:S(2)}) collective-permute-start(bf16[192,1536]{1,0:T(8,128)(2,1)} %get-tuple-element.259), channel_id=1, source_target_pairs={{0,1},{1,0},{2,3},{3,2},{4,5},{5,4},{6,7},{7,6},{8,9},{9,8},{10,11... | collective-permute-start | bytes 1769480 | tf_op jit(solution)/shard_map/ppermute | solution.py:669
  332.1 27.5 %collective-permute-start.46 = (bf16[192,1536]{1,0:T(8,128)(2,1)}, bf16[192,1536]{1,0:T(8,128)(2,1)}, u32[]{:S(2)}, u32[]{:S(2)}) collective-permute-start(bf16[192,1536]{1,0:T(8,128)(2,1)} %get-tuple-element.255), channel_id=1, source_target_pairs={{0,1},{1,0},{2,3},{3,2},{4,5},{5,4},{6,7},{7,6},{8,9},{9,8},{10,11... | collective-permute-start | bytes 1769480 | tf_op jit(solution)/shard_map/ppermute | solution.py:669
  334.2 25.5 %collective-permute-start.48 = (bf16[192,1536]{1,0:T(8,128)(2,1)}, bf16[192,1536]{1,0:T(8,128)(2,1)S(1)}, u32[]{:S(2)}, u32[]{:S(2)}) collective-permute-start(bf16[192,1536]{1,0:T(8,128)(2,1)} %add_convert_fusion.5), channel_id=1, source_target_pairs={{0,16},{1,3},{2,18},{3,1},{4,20},{5,7},{6,22},{7,5},{8,24},{9,11},... | collective-permute-start | bytes 1769480 | tf_op jit(solution)/shard_map/ppermute | solution.py:703
  377.4 28.7 %collective-permute-start.60 = (bf16[192,1536]{1,0:T(8,128)(2,1)}, bf16[192,1536]{1,0:T(8,128)(2,1)S(1)}, u32[]{:S(2)}, u32[]{:S(2)}) collective-permute-start(bf16[192,1536]{1,0:T(8,128)(2,1)} %get-tuple-element.284), channel_id=1, source_target_pairs={{0,1},{1,0},{2,3},{3,2},{4,5},{5,4},{6,7},{7,6},{8,9},{9,8},{10,11... | collective-permute-start | bytes 1769480 | tf_op jit(solution)/shard_map/ppermute | solution.py:669
  399.7 30.0 %collective-permute-start.37 = (bf16[256,1536]{1,0:T(8,128)(2,1)}, bf16[256,1536]{1,0:T(8,128)(2,1)}, u32[]{:S(2)}, u32[]{:S(2)}) collective-permute-start(bf16[256,1536]{1,0:T(8,128)(2,1)} %get-tuple-element.234), channel_id=1, source_target_pairs={{0,16},{1,17},{2,18},{3,19},{4,20},{5,21},{6,22},{7,23},{8,24},{9,... | collective-permute-start | bytes 2359304 | tf_op jit(solution)/shard_map/ppermute | solution.py:669
  400.2 29.6 %collective-permute-start.36 = (bf16[256,1536]{1,0:T(8,128)(2,1)}, bf16[256,1536]{1,0:T(8,128)(2,1)}, u32[]{:S(2)}, u32[]{:S(2)}) collective-permute-start(bf16[256,1536]{1,0:T(8,128)(2,1)} %get-tuple-element.233), channel_id=1, source_target_pairs={{0,2},{1,3},{2,0},{3,1},{4,6},{5,7},{6,4},{7,5},{8,10},{9,11},{10,... | collective-permute-start | bytes 2359304 | tf_op jit(solution)/shard_map/ppermute | solution.py:669
  406.9 48.0 %collective-permute-start.45 = (bf16[384,1536]{1,0:T(8,128)(2,1)}, bf16[384,1536]{1,0:T(8,128)(2,1)S(1)}, u32[]{:S(2)}, u32[]{:S(2)}) collective-permute-start(bf16[384,1536]{1,0:T(8,128)(2,1)} %get-tuple-element.248), channel_id=1, source_target_pairs={{0,16},{1,17},{2,18},{3,19},{4,20},{5,21},{6,22},{7,23},{8,24},{9,... | collective-permute-start | bytes 3538952 | tf_op jit(solution)/shard_map/ppermute | solution.py:669
  412.9 54.3 %collective-permute-start.50 = (bf16[1024,1536]{1,0:T(8,128)(2,1)}, bf16[1024,1536]{1,0:T(8,128)(2,1)}, u32[]{:S(2)}, u32[]{:S(2)}) collective-permute-start(bf16[1024,1536]{1,0:T(8,128)(2,1)} %get-tuple-element.274), channel_id=1, source_target_pairs={{0,1},{1,0},{2,3},{3,2},{4,5},{5,4},{6,7},{7,6},{8,9},{9,8},{10,11... | collective-permute-start | bytes 9437192 | tf_op jit(solution)/shard_map/ppermute | solution.py:669
  438.1 19.8 %collective-permute-start.66 = (bf16[48,1536]{1,0:T(8,128)(2,1)S(1)}, bf16[48,1536]{1,0:T(8,128)(2,1)}, u32[]{:S(2)}, u32[]{:S(2)}) collective-permute-start(bf16[48,1536]{1,0:T(8,128)(2,1)S(1)} %add_convert_fusion.6), channel_id=1, source_target_pairs={{0,16},{1,17},{2,18},{3,19},{4,20},{5,21},{6,22},{7,23},{8,24},{9,... | collective-permute-start | bytes 442376 | tf_op jit(solution)/shard_map/ppermute | solution.py:669
  486.2 20.7 %collective-permute-start.53 = (bf16[256,1536]{1,0:T(8,128)(2,1)}, bf16[256,1536]{1,0:T(8,128)(2,1)S(1)}, u32[]{:S(2)}, u32[]{:S(2)}) collective-permute-start(bf16[256,1536]{1,0:T(8,128)(2,1)} %get-tuple-element.344), channel_id=1, source_target_pairs={{0,16},{1,17},{2,18},{3,19},{4,20},{5,21},{6,22},{7,23},{8,24},{9,... | collective-permute-start | bytes 2359304 | tf_op jit(solution)/shard_map/ppermute | solution.py:669
  (98 other events, 838.9 us)
Sparse Core Ops, SparseCore 0:
  15.1 50.3 all-gather.2
  84.5 89.4 all-gather.4
  292.7 84.5 reduce-scatter.2
  458.0 38.3 reduce-scatter.4

commit v3 on v2

--- a/solution.py
+++ b/solution.py
@@ -169,16 +169,54 @@
     )(place.reshape(1), *values)
 
 
+def out_project_kernel(half, place_ref, grp_ref, near_ref, far_ref, x_ref, gain_ref, mid_ref, sec_ref, held):
+    size = near_ref.shape[0] // 4
+    for b in range(8):
+        other = place_ref[0] ^ order(b)
+        w = (near_ref, far_ref)[b // 4][b % 4 * size : (b % 4 + 1) * size, :]
+        part = dot(w, grp_ref[...], 1, 0)
+        for z in range(size // half):
+            start = pl.multiple_of((z * 8 + (other & 3) * 2 + (other >> 2)) * half, half)
+            held[pl.ds(start, half), :] = part[z * half : (z + 1) * half, :]
+    middle = x_ref[...] + held[...].T
+    mid_ref[...] = middle
+    sec_ref[...] = rms_norm(middle, gain_ref[...]).astype(BF)
+
+
+def out_project(grouped, near, far, x, gain, place, lines, half):
+    n = grouped.shape[1]
+    if half % 16:
+        w_out = join([near, far], place, lines, half)
+        middle = x + dot(grouped, w_out, 0, 1)
+        return middle, rms_norm(middle, gain).astype(BF)
+    whole = lambda shape: pl.BlockSpec(shape, lambda t: (0, 0))
+    return pl.pallas_call(
+        functools.partial(out_project_kernel, half),
+        cost_estimate=cost(6),
+        grid=(1,),
+        in_specs=[
+            pl.BlockSpec(memory_space=pltpu.SMEM),
+            whole((D, n)), whole(near.shape), whole(far.shape), whole((n, D)), whole((1, D)),
+        ],
+        out_specs=[whole((n, D)), whole((n, D))],
+        out_shape=[jax.ShapeDtypeStruct((n, D), F32), jax.ShapeDtypeStruct((n, D), BF)],
+        scratch_shapes=[pltpu.VMEM((D, n), F32)],
+        compiler_params=pltpu.CompilerParams(vmem_limit_bytes=60 * 2**20),
+    )(place.reshape(1), grouped, near, far, x, gain.reshape(1, D))
+
+
 def out_grad_kernel(place_ref, branch_ref, grouped_ref, *refs):
-    outs, held = refs[:-1], refs[-1]
-    lines = outs[0].shape[0] // (held.shape[0] // 8)
+    *outs, far_ref, held = refs
     wide, half = held.shape[0], held.shape[0] // 8
+    size = outs[0].shape[0]
+    lines = size // half
     for z in range(lines):
         held[...] = dot(branch_ref[:, z * wide : (z + 1) * wide], grouped_ref[...], 0, 1)
-        for b, ref in enumerate(outs):
+        for b in range(8):
             other = place_ref[0] ^ order(b)
             start = pl.multiple_of((other & 3) * 2 * half + (other >> 2) * half, half)
-            ref[z * half : (z + 1) * half, :] = held[pl.ds(start, half), :].astype(ref.dtype)
+            ref, first = (outs[b], 0) if b < 4 else (far_ref, (b - 4) * size)
+            ref[first + z * half : first + (z + 1) * half, :] = held[pl.ds(start, half), :].astype(BF)
 
 
 def out_weight_grad(branch, grouped, place, lines, half):
@@ -189,9 +227,8 @@
         for b in range(8):
             other = place ^ order(b)
             block = lax.dynamic_slice(full, (0, other & 3, other >> 2, 0, 0), (lines, 1, 1, half, D))
-            blocks.append(block.reshape(lines * half, D).astype(F32 if b < 4 else BF))
-        return blocks
-    vmem = pl.BlockSpec(memory_space=pltpu.VMEM)
+            blocks.append(block.reshape(lines * half, D).astype(BF))
+        return blocks[:4] + [jnp.concatenate(blocks[4:], axis=0)]
     return pl.pallas_call(
         out_grad_kernel,
         cost_estimate=cost(0),
@@ -201,9 +238,9 @@
             pl.BlockSpec((n, D), lambda t: (0, 0)),
             pl.BlockSpec((D, n), lambda t: (0, 0)),
         ],
-        out_specs=[pl.BlockSpec((lines * half, D), lambda t: (0, 0))] * 8,
+        out_specs=[pl.BlockSpec((c * lines * half, D), lambda t: (0, 0)) for c in (1, 1, 1, 1, 4)],
         out_shape=[
-            jax.ShapeDtypeStruct((lines * half, D), F32 if b < 4 else BF) for b in range(8)
+            jax.ShapeDtypeStruct((c * lines * half, D), BF) for c in (1, 1, 1, 1, 4)
         ],
         scratch_shapes=[pltpu.VMEM((8 * half, D), F32)],
         compiler_params=pltpu.CompilerParams(vmem_limit_bytes=60 * 2**20),
@@ -247,12 +284,24 @@
     return hidden, d_gate, (d_hidden * act).astype(BF)
 
 
-def ffn_kernel(s_ref, o_ref, w_ref, hid_ref, dgu_ref, ds_ref, yo_ref):
+def ffn_kernel(counts, *refs):
+    runs = len(counts)
+    w_ref, hid_ref, dgu_ref, *sums = refs[2 * runs : -2]
+    t, ends = pl.program_id(0), [sum(counts[: r + 1]) for r in range(runs)]
+
+    for r in range(runs if runs > 1 else 0):
+
+        @pl.when((t >= ends[r] - counts[r]) & (t < ends[r]))
+        def _():
+            refs[-2][...] = refs[r][...]
+            refs[-1][...] = refs[runs + r][...]
+
     lines, wide = w_ref.shape[0], w_ref.shape[1] // 3
     w_gu = w_ref[:, : 2 * wide, :].reshape(-1, D)
     w_down = w_ref[:, 2 * wide :, :].reshape(-1, D)
-    gu = dot(s_ref[...], w_gu, 1, 1)
-    dh = dot(o_ref[...], w_down, 1, 1)
+    s, o = (refs[-2][...], refs[-1][...]) if runs > 1 else (refs[0][...], refs[1][...])
+    gu = dot(s, w_gu, 1, 1)
+    dh = dot(o, w_down, 1, 1)
     for z in range(lines):
         lo, mid, hi = 2 * z * wide, (2 * z + 1) * wide, (2 * z + 2) * wide
         cut_h = slice(z * wide, (z + 1) * wide)
@@ -260,14 +309,24 @@
         hid_ref[:, cut_h] = hidden
         dgu_ref[:, lo:mid] = d_gate
         dgu_ref[:, mid:hi] = d_up
-    ds_ref[...] = dot(dgu_ref[...], w_gu, 1, 0).astype(ds_ref.dtype)
-    yo_ref[...] = dot(hid_ref[...], w_down, 1, 0).astype(yo_ref.dtype)
-
-
-def ffn(second, d_ffn, w_ffn, n, dtype, start, count):
-    rows, lines, wide = count * n, w_ffn.shape[0], w_ffn.shape[1] // 3
+    ds = dot(dgu_ref[...], w_gu, 1, 0).astype(BF)
+    yo = dot(hid_ref[...], w_down, 1, 0).astype(BF)
+    for r in range(runs):
+
+        @pl.when((t >= ends[r] - counts[r]) & (t < ends[r]))
+        def _():
+            sums[2 * r][...] = ds
+            sums[2 * r + 1][...] = yo
+
+
+def ffn(sources, w_ffn, n, time):
+    counts = [count for _, _, _, _, count in sources]
+    rows, lines, wide = sum(counts) * n, w_ffn.shape[0], w_ffn.shape[1] // 3
     if wide % 128:
-        second, d_ffn = (v[start * n : start * n + rows] for v in (second, d_ffn))
+        second, d_ffn = (
+            jnp.concatenate([src[i][src[2 + i] * n : (src[2 + i] + src[4]) * n] for src in sources], axis=0)
+            for i in range(2)
+        )
         w_gu = w_ffn[:, : 2 * wide].reshape(-1, D)
         w_down = w_ffn[:, 2 * wide :].reshape(-1, D)
         gu = dot(second, w_gu, 1, 1).reshape(rows, lines, 2, wide)
@@ -275,147 +334,166 @@
         hidden, d_gate, d_up = gated(gu[:, :, 0], gu[:, :, 1], dh)
         hidden = hidden.reshape(rows, lines * wide)
         d_gu = jnp.stack([d_gate, d_up], axis=2).reshape(rows, 2 * lines * wide)
-        return hidden, d_gu, dot(d_gu, w_gu, 1, 0).astype(dtype), dot(hidden, w_down, 1, 0).astype(dtype)
-    out = lambda width: pl.BlockSpec((n, width), lambda b: (b, 0))
-    block = pl.BlockSpec((n, D), lambda b: (b + start, 0))
+        ds, yo = dot(d_gu, w_gu, 1, 0).astype(BF), dot(hidden, w_down, 1, 0).astype(BF)
+        at, sums = 0, []
+        for count in counts:
+            sums += [v[at : at + count * n] for v in (ds, yo)]
+            at += count * n
+        return [hidden, d_gu] + sums
+
+    def spec(part, first):
+        start, count = sum(counts[:part]), counts[part]
+        return pl.BlockSpec((n, D), lambda t: (jnp.clip(t - start, 0, count - 1) + first, 0))
+
+    out = lambda width: pl.BlockSpec((n, width), lambda t: (t, 0))
     return pl.pallas_call(
-        ffn_kernel,
-        cost_estimate=cost(3.8 * count),
-        grid=(count,),
-        in_specs=[block, block, pl.BlockSpec(w_ffn.shape, lambda b: (0, 0, 0))],
-        out_specs=[out(lines * wide), out(2 * lines * wide), out(D), out(D)],
+        functools.partial(ffn_kernel, counts),
+        cost_estimate=cost(time),
+        grid=(rows // n,),
+        in_specs=[spec(p, src[2 + i]) for i in range(2) for p, src in enumerate(sources)]
+        + [pl.BlockSpec(memory_space=pltpu.VMEM)],
+        out_specs=[out(lines * wide), out(2 * lines * wide)]
+        + [spec(p, 0) for p in range(len(sources)) for _ in range(2)],
         out_shape=[
             jax.ShapeDtypeStruct((rows, lines * wide), BF),
             jax.ShapeDtypeStruct((rows, 2 * lines * wide), BF),
-            jax.ShapeDtypeStruct((rows, D), dtype),
-            jax.ShapeDtypeStruct((rows, D), dtype),
-        ],
-        compiler_params=pltpu.CompilerParams(vmem_limit_bytes=60 * 2**20),
-    )(second, d_ffn, w_ffn)
-
-
-def ffn_grad_kernel(counts, *refs):
-    runs = len(counts)
+        ]
+        + [jax.ShapeDtypeStruct((src[4] * n, D), BF) for src in sources for _ in range(2)],
+        scratch_shapes=[pltpu.VMEM((n, D), BF)] * 2,
+        compiler_params=pltpu.CompilerParams(vmem_limit_bytes=58 * 2**20),
+    )(*(src[i] for i in range(2) for src in sources), w_ffn)
+
+
+def ffn_grad_kernel(runs, *refs):
     hid, dgu, sec, dff = (refs[i * runs : (i + 1) * runs] for i in range(4))
     out_ref, gu_ref, down_ref = refs[4 * runs :]
-    t = pl.program_id(0)
-    start = 0
-    for r in range(runs):
-
-        @pl.when((t >= start) & (t < start + counts[r]))
-        def _():
-            gu = dot(dgu[r][...], sec[r][...], 0, 0)
-            down = dot(hid[r][...], dff[r][...], 0, 0)
-            if r == 0:
-                gu_ref[...] = jnp.where(t == 0, gu, gu_ref[...] + gu)
-                down_ref[...] = jnp.where(t == 0, down, down_ref[...] + down)
-            else:
-                gu_ref[...] += gu
-                down_ref[...] += down
-
-        start += counts[r]
-
-    @pl.when(t == start - 1)
+
+    @pl.when(pl.program_id(0) == 0)
     def _():
-        lines, wide = out_ref.shape[0], out_ref.shape[1] // 3
-        for z in range(lines):
-            out_ref[z, : 2 * wide, :] = gu_ref[2 * z * wide : 2 * (z + 1) * wide, :].astype(BF)
-            out_ref[z, 2 * wide :, :] = down_ref[z * wide : (z + 1) * wide, :].astype(BF)
-
-
-def ffn_grad(hidden, d_gu, second, d_ffn, lines, wide, n):
-    counts = [h.shape[0] // n for h in hidden]
+        start = 0
+        for h, d in zip(hid, dgu):
+            rows = h.shape[0]
+            gu_ref[:, start : start + rows] = d[...].T
+            down_ref[:, start : start + rows] = h[...].T
+            start += rows
+
+    lines, wide = out_ref.shape[0], out_ref.shape[1] // 3
+    gu, down, start = 0.0, 0.0, 0
+    for a, b in zip(sec, dff):
+        rows = slice(start, start + a.shape[0])
+        gu = gu + dot(gu_ref[:, rows], a[...], 1, 0)
+        down = down + dot(down_ref[:, rows], b[...], 1, 0)
+        start += a.shape[0]
+    for z in range(lines):
+        out_ref[z, : 2 * wide, :] = gu[2 * z * wide : 2 * (z + 1) * wide, :].astype(BF)
+        out_ref[z, 2 * wide :, :] = down[z * wide : (z + 1) * wide, :].astype(BF)
+
+
+def ffn_grad(hidden, d_gu, second, d_ffn, lines, wide):
     if wide % 128:
-        rows = lambda group: [v[f * n : (f + c) * n] for (v, f), c in zip(group, counts)]
-        gu = sum(dot(a, b, 0, 0) for a, b in zip(d_gu, rows(second))).reshape(lines, 2 * wide, D)
-        down = sum(dot(a, b, 0, 0) for a, b in zip(hidden, rows(d_ffn))).reshape(lines, wide, D)
+        rows = lambda group: [v[f * c : (f + 1) * c] for v, c, f in group]
+        gu = sum(dot(a, b, 0, 0) for a, b in zip(rows(d_gu), rows(second))).reshape(lines, 2 * wide, D)
+        down = sum(dot(a, b, 0, 0) for a, b in zip(rows(hidden), rows(d_ffn))).reshape(lines, wide, D)
         return jnp.concatenate([gu, down], axis=1).astype(BF)
-    hidden, d_gu = ([(v, 0) for v in group] for group in (hidden, d_gu))
-    specs, starts = [], [sum(counts[:r]) for r in range(len(counts))]
-    for group in (hidden, d_gu, second, d_ffn):
-        for (value, first), start, count in zip(group, starts, counts):
-            specs.append(
-                pl.BlockSpec(
-                    (n, value.shape[1]),
-                    lambda t, s=start, c=count, f=first: (jnp.clip(t - s, 0, c - 1) + f, 0),
-                )
-            )
-    out = (lines, 3 * wide, D)
+    step = 256
+    whole = [
+        pl.BlockSpec((c, v.shape[1]), lambda t, f=f: (f, 0)) for v, c, f in (*hidden, *d_gu)
+    ]
+    slab = [pl.BlockSpec((c, step), lambda t, f=f: (f, t)) for _, c, f in (*second, *d_ffn)]
+    out, tall = (lines, 3 * wide), sum(c for _, c, _ in hidden)
     return pl.pallas_call(
-        functools.partial(ffn_grad_kernel, counts),
-        cost_estimate=cost(18),
-        grid=(sum(counts),),
-        in_specs=specs,
-        out_specs=pl.BlockSpec(out, lambda t: (0, 0, 0)),
-        out_shape=jax.ShapeDtypeStruct(out, BF),
-        scratch_shapes=[pltpu.VMEM((2 * lines * wide, D), F32), pltpu.VMEM((lines * wide, D), F32)],
+        functools.partial(ffn_grad_kernel, len(hidden)),
+        cost_estimate=cost(14),
+        grid=(D // step,),
+        in_specs=whole + slab,
+        out_specs=pl.BlockSpec(out + (step,), lambda t: (0, 0, t)),
+        out_shape=jax.ShapeDtypeStruct(out + (D,), BF),
+        scratch_shapes=[
+            pltpu.VMEM((2 * lines * wide, tall), BF),
+            pltpu.VMEM((lines * wide, tall), BF),
+        ],
         compiler_params=pltpu.CompilerParams(vmem_limit_bytes=60 * 2**20),
-    )(*(v for group in (hidden, d_gu, second, d_ffn) for v, _ in group))
+    )(*(v for group in (hidden, d_gu, second, d_ffn) for v, _, _ in group))
+
+
+def qkv_grad_kernel(count, *refs):
+    parts, (near_ref, far_ref, out_ref, held) = refs[:count], refs[count:]
+    n = parts[0].shape[1]
+
+    @pl.when(pl.program_id(0) == 0)
+    def _():
+        for b, part in enumerate(parts):
+            held[:, b * n : (b + 1) * n] = part[...]
+
+    rows = near_ref.shape[0]
+    out_ref[...] = (
+        dot(held[:, :rows], near_ref[...], 1, 0) + dot(held[:, rows:], far_ref[...], 1, 0)
+    ).astype(BF)
+
+
+def qkv_grad(parts, near, far, cols):
+    rows, n = parts[0].shape
+    if cols % 16:
+        half = len(parts) // 2
+        grads = (jnp.concatenate(p, axis=1) for p in (parts[:half], parts[half:]))
+        return sum(dot(g, v, 1, 0) for g, v in zip(grads, (near, far))).astype(BF)
+    step = 256
+    slab = pl.BlockSpec((near.shape[0], step), lambda t: (0, t))
+    return pl.pallas_call(
+        functools.partial(qkv_grad_kernel, len(parts)),
+        cost_estimate=cost(6),
+        grid=(D // step,),
+        in_specs=[pl.BlockSpec((rows, n), lambda t: (0, 0))] * len(parts) + [slab, slab],
+        out_specs=pl.BlockSpec((rows, step), lambda t: (0, t)),
+        out_shape=jax.ShapeDtypeStruct((rows, D), BF),
+        scratch_shapes=[pltpu.VMEM((rows, len(parts) * n), BF)],
+        compiler_params=pltpu.CompilerParams(vmem_limit_bytes=60 * 2**20),
+    )(*parts, near, far)
 
 
 def back_project_kernel(count, *refs):
-    parts, (x_ref, normed_ref, w_ref) = refs[:count], refs[count : count + 3]
-    before, (dn_ref, out_ref, gain_ref, g_ref) = refs[count + 3 : -4], refs[-4:]
-    rows = g_ref.shape[0]
+    parts, (x_ref, w_ref, dn_ref, gain_ref) = refs[:count], refs[count:]
+    rows = parts[0].shape[0]
     w = w_ref[:, : rows // w_ref.shape[0], :].reshape(rows, D)
     t = pl.program_id(0)
 
     @pl.when(t == 0)
     def _():
-        if before:
-            g_ref[...] = before[0][...]
-            gain_ref[...] = before[1][...]
-        else:
-            g_ref[...] = jnp.zeros_like(g_ref)
-            gain_ref[...] = jnp.zeros_like(gain_ref)
+        gain_ref[...] = jnp.zeros_like(gain_ref)
 
     for b in range(count):
 
         @pl.when(t == b)
         def _():
-            grad = parts[b][...]
-            g_ref[...] += dot(grad, normed_ref[...], 1, 0)
-            dn = dot(grad, w, 0, 0)
-            dn_ref[...] = dn.astype(dn_ref.dtype)
+            dn = dot(parts[b][...], w, 0, 0)
+            dn_ref[...] = dn.astype(BF)
             x = x_ref[...].astype(F32)
             hat = x * lax.rsqrt(jnp.mean(x * x, axis=1, keepdims=True) + 1e-05)
             gain_ref[...] += jnp.sum(dn * hat, axis=0, keepdims=True)
 
-    @pl.when(t == count - 1)
-    def _():
-        out_ref[...] = g_ref[...].astype(out_ref.dtype)
-
-
-def back_project(parts, x, normed, w_attn, cols, n, dtype, before=()):
+
+def back_project(parts, x, first, w_attn, cols, n, time):
     lines, count = w_attn.shape[0], len(parts)
     rows = lines * cols
     if cols % 16:
-        grad = jnp.concatenate(parts, axis=1)
-        dn = dot(grad, w_attn[:, :cols].reshape(rows, D), 0, 0)
-        values = x.astype(F32)
+        dn = dot(jnp.concatenate(parts, axis=1), w_attn[:, :cols].reshape(rows, D), 0, 0)
+        values = x[first * n : (first + count) * n].astype(F32)
         hat = values * lax.rsqrt(jnp.mean(values * values, axis=1, keepdims=True) + 1e-05)
-        sums = (dot(grad, normed, 1, 0), jnp.sum(dn * hat, axis=0, keepdims=True))
-        if before:
-            sums = (sums[0] + before[0], sums[1] + before[1])
-        return (dn.astype(dtype),) + sums
-    block = pl.BlockSpec((n, D), lambda b: (b, 0))
+        return dn.astype(BF), jnp.sum(dn * hat, axis=0, keepdims=True)
     whole = lambda shape: pl.BlockSpec(shape, lambda b: (0,) * len(shape))
     return pl.pallas_call(
         functools.partial(back_project_kernel, count),
-        cost_estimate=cost(2.5 * count),
+        cost_estimate=cost(time),
         grid=(count,),
         in_specs=[whole((rows, n))] * count
-        + [block, block, whole(w_attn.shape)]
-        + [whole(v.shape) for v in before],
-        out_specs=[block, whole((rows, D)), whole((1, D))],
+        + [pl.BlockSpec((n, D), lambda b: (b + first, 0)), whole(w_attn.shape)],
+        out_specs=[pl.BlockSpec((n, D), lambda b: (b, 0)), whole((1, D))],
         out_shape=[
-            jax.ShapeDtypeStruct((count * n, D), dtype),
-            jax.ShapeDtypeStruct((rows, D), BF if before else F32),
+            jax.ShapeDtypeStruct((count * n, D), BF),
             jax.ShapeDtypeStruct((1, D), F32),
         ],
-        scratch_shapes=[pltpu.VMEM((rows, D), F32)],
         compiler_params=pltpu.CompilerParams(vmem_limit_bytes=60 * 2**20),
-    )(*parts, x, normed, w_attn, *before)
+    )(*parts, x, w_attn)
 
 
 def doc_masks(drow_ref, dcol_ref, allow_ref, same_ref):
@@ -437,22 +515,22 @@
     @pl.when(g == 0)
     def _():
         doc_masks(drow_ref, dcol_ref, allow_ref, same_ref)
-        pad_ref[0:8, :] = jnp.zeros((8, n), F32)
+        pad_ref[:, 0:8, :] = jnp.zeros((2, 8, n), F32)
 
     for e in range(2):
         q = q_ref[e * HD : (e + 1) * HD, :]
         k = k_ref[e * HD : (e + 1) * HD, :]
         logits = dot(q, k, 0, 0) * (HD ** (-0.5))
-        pad_ref[8 : 8 + n, :] = jnp.where(allow_ref[...] > 0, logits, 0.0)
+        pad_ref[e, 8 : 8 + n, :] = jnp.where(allow_ref[...] > 0, logits, 0.0)
         for a in range(CQ):
-            part = jnp.where(same_ref[...] > 0, pad_ref[8 - a : 8 - a + n, :], 0.0)
+            part = jnp.where(same_ref[...] > 0, pad_ref[e, 8 - a : 8 - a + n, :], 0.0)
             hi, lo = split(part)
-            xh_ref[:, a * n : (a + 1) * n] = hi
-            xl_ref[:, a * n : (a + 1) * n] = lo
+            xh_ref[e, :, a * n : (a + 1) * n] = hi
+            xl_ref[e, :, a * n : (a + 1) * n] = lo
         conv = (
-            dot(xh_ref[...], th_ref[e], 1, 0)
-            + dot(xh_ref[...], tl_ref[e], 1, 0)
-            + dot(xl_ref[...], th_ref[e], 1, 0)
+            dot(xh_ref[e], th_ref[e], 1, 0)
+            + dot(xh_ref[e], tl_ref[e], 1, 0)
+            + dot(xl_ref[e], th_ref[e], 1, 0)
         )
         scores = jnp.where(allow_ref[...] > 0, conv, NEG)
         weights = jnp.exp(scores - jnp.max(scores, axis=1, keepdims=True))
@@ -492,8 +570,8 @@
         ],
         input_output_aliases={9: 2} if before else {},
         scratch_shapes=[
-            pltpu.VMEM((n, n), F32), pltpu.VMEM((n, n), F32), pltpu.VMEM((n + 8, n), F32),
-            pltpu.VMEM((n, CQ * n), BF), pltpu.VMEM((n, CQ * n), BF),
+            pltpu.VMEM((n, n), F32), pltpu.VMEM((n, n), F32), pltpu.VMEM((2, n + 8, n), F32),
+            pltpu.VMEM((2, n, CQ * n), BF), pltpu.VMEM((2, n, CQ * n), BF),
         ],
         compiler_params=pltpu.CompilerParams(vmem_limit_bytes=60 * 2**20),
     )(
@@ -503,9 +581,11 @@
 
 
 def attend_back_kernel(
-    mix_ref, q_ref, k_ref, v_ref, tt_ref, drow_ref, dcol_ref, gain_ref, prob_ref, att_ref, dgrp_ref, *refs
+    first, mix_ref, q_ref, k_ref, v_ref, tt_ref, drow_ref, dcol_ref, gain_ref,
+    prob_a_ref, prob_b_ref, att_a_ref, att_b_ref, dgrp_ref,
+    d_ref, dgain_ref, dtap_ref, dmix_ref,
+    allow_ref, same_ref, pad_ref, y_ref, dm_ref, prob_ref, att_ref,
 ):
-    d_ref, dgain_ref, dtap_ref, dmix_ref, allow_ref, same_ref, pad_ref, y_ref, dm_ref = refs[-9:]
     g = pl.program_id(0)
     n = q_ref.shape[1]
     scale = HD ** (-0.5)
@@ -513,7 +593,17 @@
     @pl.when(g == 0)
     def _():
         doc_masks(drow_ref, dcol_ref, allow_ref, same_ref)
-        pad_ref[n : n + 8, :] = jnp.zeros((8, n), F32)
+        pad_ref[:, n : n + 8, :] = jnp.zeros((2, 8, n), F32)
+
+    @pl.when(g < first)
+    def _():
+        prob_ref[...] = prob_a_ref[...]
+        att_ref[...] = att_a_ref[...]
+
+    @pl.when(g >= first)
+    def _():
+        prob_ref[...] = prob_b_ref[...]
+        att_ref[...] = att_b_ref[...]
 
     for c in range(2):
         rows = slice(c * HD, (c + 1) * HD)
@@ -549,17 +639,17 @@
         masked_t = dot(k, q, 0, 0) * scale
         prob = prob_ref[e]
         dprob = mix_ref[g, e] * dm_ref[0] + mix_ref[g, 2 + e] * dm_ref[1]
-        pad_ref[0:n, :] = prob * (dprob - jnp.sum(prob * dprob, axis=1, keepdims=True))
+        pad_ref[e, 0:n, :] = prob * (dprob - jnp.sum(prob * dprob, axis=1, keepdims=True))
         for a in range(CQ):
-            y_ref[:, a * n : (a + 1) * n] = jnp.where(same_ref[...] > 0, pad_ref[a : a + n, :], 0.0).astype(BF)
-        dlog = jnp.where(allowed, dot(y_ref[...], tt_ref[e], 1, 0), 0.0).astype(BF)
+            y_ref[e, :, a * n : (a + 1) * n] = jnp.where(same_ref[...] > 0, pad_ref[e, a : a + n, :], 0.0).astype(BF)
+        dlog = jnp.where(allowed, dot(y_ref[e], tt_ref[e], 1, 0), 0.0).astype(BF)
         d_ref[0, rows, :] = (dot(k, dlog, 1, 1) * scale).astype(BF)
         d_ref[1, rows, :] = (dot(q, dlog, 1, 0) * scale).astype(BF)
         krow = lax.broadcasted_iota(jnp.int32, (n, n), 0)
         qcol = lax.broadcasted_iota(jnp.int32, (n, n), 1)
         masked_t = jnp.where((same_ref[...] > 0) & (krow <= qcol), masked_t, 0.0).astype(BF)
         for a in range(CQ):
-            full = dot(masked_t, y_ref[:, a * n : (a + 1) * n], 1, 0)
+            full = dot(masked_t, y_ref[e, :, a * n : (a + 1) * n], 1, 0)
             fold = jnp.zeros((128, 128), F32)
             blocks = n // 128
             for r in range(blocks):
@@ -575,52 +665,59 @@
             dtap_ref[e, 8 * a : 8 * a + 8, :] = lined
 
 
-def attend_back(packed_t, docs, tt, mix, gain, prob, att, dgrp, start, count, before=()):
+def attend_back(packed_t, docs, tt, mix, gain, probs, atts, dgrp):
     n = packed_t.shape[1]
+    first = probs[0].shape[0] // 2
     blk = lambda off: pl.BlockSpec((PW, n), lambda g: (g + off, 0))
     whole = lambda s: pl.BlockSpec(s, lambda g: (0, 0))
-    thin = lambda off: pl.BlockSpec((PW, 1), lambda g: (g + off, 0))
-    rows = count * PW
-    d_packed, dgain, dtap, dmix = pl.pallas_call(
-        attend_back_kernel,
-        cost_estimate=cost(2.7 * count),
-        grid=(count,),
+    thin = pl.BlockSpec((PW, 1), lambda g: (g, 0))
+    low = lambda g: jnp.minimum(g, first - 1)
+    high = lambda g: jnp.maximum(g - first, 0)
+    return pl.pallas_call(
+        functools.partial(attend_back_kernel, first),
+        cost_estimate=cost(2.7 * PAIRS),
+        grid=(PAIRS,),
         in_specs=[
             pl.BlockSpec(memory_space=pltpu.SMEM),
-            blk(start), blk(PAIRS + start), blk(2 * PAIRS + start),
-            pl.BlockSpec((2, CQ * n, n), lambda g: (g + start, 0, 0)),
-            whole((1, n)), whole((n, 1)), thin(start),
-            pl.BlockSpec((2, n, n), lambda g: (g, 0, 0)),
-            blk(0), blk(start),
-        ]
-        + [pl.BlockSpec(memory_space=pl.ANY)] * len(before),
+            blk(0), blk(PAIRS), blk(2 * PAIRS),
+            pl.BlockSpec((2, CQ * n, n), lambda g: (g, 0, 0)),
+            whole((1, n)), whole((n, 1)), thin,
+            pl.BlockSpec((2, n, n), lambda g: (low(g), 0, 0)),
+            pl.BlockSpec((2, n, n), lambda g: (high(g), 0, 0)),
+            pl.BlockSpec((PW, n), lambda g: (low(g), 0)),
+            pl.BlockSpec((PW, n), lambda g: (high(g), 0)),
+            blk(0),
+        ],
         out_specs=[
-            pl.BlockSpec((3, PW, n), lambda g: (0, g + start, 0)), thin(0),
+            pl.BlockSpec((3, PW, n), lambda g: (0, g, 0)), thin,
             pl.BlockSpec((2, 8 * CQ, 128), lambda g: (g, 0, 0)),
             pl.BlockSpec((1, 8, n), lambda g: (g, 0, 0)),
         ],
         out_shape=[
             jax.ShapeDtypeStruct((3, D, n), BF),
-            jax.ShapeDtypeStruct((rows, 1), F32),
-            jax.ShapeDtypeStruct((2 * count, 8 * CQ, 128), F32),
-            jax.ShapeDtypeStruct((count, 8, n), F32),
+            jax.ShapeDtypeStruct((D, 1), F32),
+            jax.ShapeDtypeStruct((H, 8 * CQ, 128), F32),
+            jax.ShapeDtypeStruct((PAIRS, 8, n), F32),
         ],
         scratch_shapes=[
-            pltpu.VMEM((n, n), F32), pltpu.VMEM((n, n), F32), pltpu.VMEM((n + 8, n), F32),
-            pltpu.VMEM((n, CQ * n), BF), pltpu.VMEM((2, n, n), F32),
-        ],
-        input_output_aliases={11: 0} if before else {},
+            pltpu.VMEM((n, n), F32), pltpu.VMEM((n, n), F32), pltpu.VMEM((2, n + 8, n), F32),
+            pltpu.VMEM((2, n, CQ * n), BF), pltpu.VMEM((2, n, n), F32),
+            pltpu.VMEM((2, n, n), F32), pltpu.VMEM((PW, n), F32),
+        ],
         compiler_params=pltpu.CompilerParams(vmem_limit_bytes=60 * 2**20),
     )(
-        mix[start : start + count].reshape(count, 4), packed_t, packed_t, packed_t, tt,
-        docs.reshape(1, n), docs.reshape(n, 1), gain, prob, att, dgrp, *before,
-    )
+        mix.reshape(PAIRS, 4), packed_t, packed_t, packed_t, tt,
+        docs.reshape(1, n), docs.reshape(n, 1), gain, *probs, *atts, dgrp,
+    )
+
+
+def fold_sums(dgain, dtap, dmix):
     lane = jnp.arange(128)[None, None, :] - jnp.arange(8)[None, :, None]
     tap = jnp.arange(CK)[:, None, None] - CK // 2
     pick = (jnp.remainder(lane - tap, 128) == 0).astype(F32)
-    dtap = jnp.sum(dtap.reshape(2 * count, CQ, 1, 8, 128) * pick, axis=(3, 4))
+    dtap = jnp.sum(dtap.reshape(H, CQ, 1, 8, 128) * pick, axis=(3, 4))
     dmix = jnp.sum(dmix[:, :4, :], axis=2)
-    return d_packed, dgain, dtap.reshape(2 * count, CQ * CK), dmix.reshape(count, 2, 2)
+    return jnp.concatenate([dgain[:, 0], dtap.reshape(-1), dmix.reshape(-1)])
 
 
 def rms_norm(values, gain):
@@ -699,11 +796,20 @@
         return lax.dynamic_update_slice(near, corner, (3 * value.shape[0], 0))
 
     def scatter_corner(self, near, far):
-        own, to_x, to_y, last = (a + b.astype(F32) for a, b in zip(near, far))
+        own, to_x, to_y, last = (a.astype(F32) + b.astype(F32) for a, b in zip(near, far))
         corner = lax.ppermute(last.astype(BF), self.axes, self.corner).astype(F32)
         to_x = (to_x + jnp.where(self.odd, 0.0, corner)).astype(BF)
         to_y = (to_y + jnp.where(self.odd, corner, 0.0)).astype(BF)
         return own, to_x, to_y
+
+    def send_corner(self, near, far):
+        return lax.ppermute((near.astype(F32) + far.astype(F32)).astype(BF), self.axes, self.corner)
+
+    def with_corner(self, near, far, corner):
+        corner = corner.astype(F32)
+        to_x, to_y = (a.astype(F32) + b.astype(F32) for a, b in zip(near, far))
+        to_x = (to_x + jnp.where(self.odd, 0.0, corner)).astype(BF)
+        return to_x, (to_y + jnp.where(self.odd, corner, 0.0)).astype(BF)
 
     def scatter_last(self, own, to_x, to_y):
         return own + self.hop(to_x, 0, 2).astype(F32) + self.hop(to_y, 1, 0).astype(F32)
@@ -718,10 +824,10 @@
         part = lambda d: lax.dynamic_slice_in_dim(value, (line ^ d) * rows, rows, axis=0)
         return sum([self.hop(part(d), 0, 4 * d).astype(F32) for d in range(1, 4)], part(0).astype(F32))
 
-    def sum_small(self, value):
-        value = value + self.hop(value, 1, 0)
-        for _, perm in self.doubling:
-            value = value + lax.ppermute(value, self.axes, perm)
+    def sum_small(self, value, bits):
+        for bit, perm in self.doubling:
+            if bit in bits:
+                value = value + lax.ppermute(value, self.axes, perm)
         return value
 
     def both_halves(self, half, axis=0, other=None):
@@ -732,9 +838,9 @@
             [jnp.where(first, half, other), jnp.where(first, other, half)], axis=axis
         ).astype(F32)
 
-    def own_half(self, shard):
+    def own_half(self, shard, rep=None):
         rows = shard.shape[0] // 2
-        return lax.dynamic_slice_in_dim(shard, self.rep * rows, rows, axis=0)
+        return lax.dynamic_slice_in_dim(shard, (self.rep if rep is None else rep) * rows, rows, axis=0)
 
 
 def on_device(
@@ -764,108 +870,144 @@
     rows_of = lambda v: [v[b * n : (b + 1) * n] for b in range(v.shape[0] // n)]
 
     attn_half = jnp.concatenate([net.own_half(qkv_weight.T), net.own_half(out_weight.T)], axis=0)
-    attn_half, tokens = fence(attn_half, tokens)
     w_attn = net.gather_line(attn_half).reshape(lines, -1, D)
     x_side = net.sides(tokens)
-    ffn_half = jnp.concatenate(
-        [net.own_half(gate_weight.T), net.own_half(up_weight.T), net.own_half(down_weight)], axis=0
-    )
+    d_low = out_grad.astype(BF)
+    d_side = net.sides(d_low)
     taps = band_taps(conv_kernel, n)
-    gains = net.gather_small(jnp.stack([norm_gain, group_gain, ffn_gain])[None])
-    *x_side, ffn_half, gains, d_low, taps_hi, taps_lo, taps_back = fence(
-        *x_side, ffn_half, gains, out_grad.astype(BF), *taps
-    )
-    w_ffn = net.gather_line(ffn_half).reshape(lines, -1, D)
-    gains = gains.transpose(1, 0, 2).reshape(3, D).astype(F32)
-    corner = net.far_corner(*x_side)
-    d_side = net.sides(d_low)
-    w_attn = fence(w_attn, time=100)[0]
-    corner, *d_side, w_attn = fence(corner, *d_side, w_attn)
-    x_near = net.near_blocks(tokens, *x_side, corner)
+    gains, *sides = fence(
+        jnp.stack([norm_gain, group_gain, ffn_gain])[None], *x_side, *d_side, *taps
+    )
+    x_side, d_side, (taps_hi, taps_lo, taps_back) = sides[:2], sides[2:4], sides[4:]
+    rep = jnp.broadcast_to(net.rep, (8, 128))
+    x_near, rep = fence(net.near_blocks(tokens, *x_side, net.far_corner(*x_side)), rep)
     x_far = net.hop(x_near, 0, 1)
     d_near = net.near_blocks(d_low, *d_side, net.far_corner(*d_side))
+    gains = net.gather_small(gains)
+    w_attn = fence(w_attn, time=100)[0]
+    x_far = fence(x_far, time=40)[0]
+    d_near = fence(d_near, time=60)[0]
+    ffn_half = jnp.concatenate(
+        [net.own_half(v, rep[0, 0]) for v in (gate_weight.T, up_weight.T, down_weight)], axis=0
+    )
+    w_attn, d_near, x_far, gains, ffn_half = fence(w_attn, d_near, x_far, gains, ffn_half)
+    gains = gains.transpose(1, 0, 2).reshape(3, D).astype(F32)
+    w_ffn = net.gather_line(ffn_half).reshape(lines, -1, D)
+    w_cls = w_attn[:, cols:].reshape(-1, D)
     inputs = tokens.astype(F32)
 
     norm_near, parts = project(x_near, gains[0], w_attn, cols, n)
+    norm_near, x_far, *parts = fence(norm_near, x_far, *parts)
     norm_far, more = project(x_far, gains[0], w_attn, cols, n)
     pieces = [net.hop_block(p, b) for b, p in enumerate((*parts, *more))]
-    *pieces, w_cls, d_near = fence(*pieces, w_attn[:, cols:].reshape(-1, D), d_near)
     d_far = net.hop(d_near, 0, 1)
+    pieces = fence(*pieces, time=45)
+    *pieces, w_cls, d_far = fence(*pieces, w_cls, d_far)
     w_side = (*net.sides(w_cls), net.hop(w_cls, 1, 2))
     packed_t = join(pieces, net.place, lines, cols)
     group_col = gains[1].reshape(D, 1)
-    heads = PAIRS // 2
+    heads = 5
     front = functools.partial(attend, packed_t, doc_ids, taps_hi, taps_lo, head_mix, group_col)
     *w_side, prob_a, att_a, grouped = fence(*w_side, *front(0, heads))
-    w_near = (w_cls, *w_side)
-    w_far = [net.hop(w, 0, 1) for w in w_near]
-    *w_far, prob_b, att_b, grouped = fence(*w_far, *front(heads, PAIRS - heads, (grouped,)))
-    w_out = join([*w_near, *w_far], net.place, lines, half_out)
-
-    middle = inputs + dot(grouped, w_out, 0, 1)
-    second = rms_norm(middle, gains[2]).astype(BF)
+    w_near = jnp.concatenate([w_cls, *w_side], axis=0)
+    w_far, prob_b, att_b, grouped = fence(
+        net.hop(w_near, 0, 1), *front(heads, PAIRS - heads, (grouped,))
+    )
+    middle, second = out_project(grouped, w_near, w_far, inputs, gains[2], net.place, lines, half_out)
+    w_near, w_far, second = fence(w_near, w_far, second)
+    w_out = join([w_near, w_far], net.place, lines, half_out)
     s_side = net.sides(second)
-    s_near = net.near_blocks(second, *s_side, net.far_corner(*s_side))
-    s_far = net.hop(s_near, 0, 1)
-
+    s_corner = net.far_corner(*s_side)
+    s_a = jnp.concatenate([second, s_side[0]], axis=0)
+    far_a = net.hop(s_a, 0, 1)
     w_ffn = fence(w_ffn, time=100)[0]
-    run_a = ffn(s_near, d_near, w_ffn, n, F32, 0, 2)
-    *run_a, s_far = fence(*run_a, s_far)
-    run_f = ffn(s_far, d_far, w_ffn, n, BF, 0, 4)
-    run_b = ffn(s_near, d_near, w_ffn, n, F32, 2, 2)
-    ds_far, yo_far = net.hop(run_f[2], 0, 1), net.hop(run_f[3], 0, 1)
-    own, to_x, to_y = net.scatter_corner(rows_of(run_a[2]) + rows_of(run_b[2]), rows_of(ds_far))
-    acts = [r[i] for i in range(2) for r in (run_a, run_f, run_b)]
-    to_x, to_y, *acts = fence(to_x, to_y, *acts)
+    run_a = ffn([(s_a, d_near, 0, 0, 2)], w_ffn, n, 7)
+    s_corner, far_a, w_out, *run_a = fence(s_corner, far_a, w_out, *run_a)
+    s_b = jnp.concatenate([s_side[1], s_corner], axis=0)
+    far_b = net.hop(s_b, 0, 1)
+    run_f = ffn([(far_a, d_far, 0, 0, 2), (far_b, d_far, 0, 2, 2)], w_ffn, n, 14)
+    ds_f, ds_g = net.hop(run_f[2], 0, 1), net.hop(run_f[4], 0, 1)
+    run_b = ffn([(s_b, d_near, 0, 2, 2)], w_ffn, n, 7)
+    ds_f, ds_g, *run_b = fence(ds_f, ds_g, *run_b)
+    corner = net.send_corner(run_b[2][n:], ds_g[n:])
+    to_x, to_y = net.with_corner((run_a[2][n:], run_b[2][:n]), (ds_f[n:], ds_g[:n]), corner)
+    own = run_a[2][:n].astype(F32) + ds_f[:n].astype(F32)
+    to_x, to_y, *acts = fence(to_x, to_y, *[r[i] for i in range(2) for r in (run_a, run_f, run_b)])
+    yo_f, yo_g = net.hop(run_f[3], 0, 1), net.hop(run_f[5], 0, 1)
     d_second = net.scatter_last(own, to_x, to_y)
+    blocks = lambda a, f, b: [(a, 2 * n, 0), (f, 2 * n, 0), (f, 2 * n, 1), (b, 2 * n, 0)]
     g_ffn = ffn_grad(
-        acts[:3], acts[3:], [(s_near, 0), (s_far, 0), (s_near, 2)], [(d_near, 0), (d_far, 0), (d_near, 2)],
-        lines, wide, n,
-    )
-    d_second, yo_far, g_ffn = fence(d_second, yo_far, g_ffn)
-    g_ffn = fence(net.scatter_line(g_ffn.reshape(-1, D)), time=60)[0]
+        blocks(*acts[:3]),
+        blocks(*acts[3:]),
+        [(s_a, 2 * n, 0), (far_a, 2 * n, 0), (far_b, 2 * n, 0), (s_b, 2 * n, 0)],
+        [(d_near, 2 * n, 0), (d_far, 2 * n, 0), (d_far, 2 * n, 1), (d_near, 2 * n, 1)],
+        lines, wide,
+    )
+    d_second, yo_f, yo_g, g_ffn = fence(d_second, yo_f, yo_g, g_ffn)
+    g_ffn = fence(net.scatter_line(g_ffn.reshape(-1, D)), time=80)[0]
 
     d_norm, g_ffn_gain = rms_back(middle, gains[2], d_second)
     d_middle = out_grad + d_norm
     branch = d_middle.astype(BF)
     d_grouped = dot(w_out, branch, 0, 1)
-    back = functools.partial(attend_back, packed_t, doc_ids, taps_back, head_mix, group_col)
-    own, to_x, to_y = net.scatter_corner(rows_of(run_a[3]) + rows_of(run_b[3]), rows_of(yo_far))
-    first = back(prob_a, att_a, d_grouped, 0, heads)
-    to_x, to_y, *first = fence(to_x, to_y, *first)
-    layer_out = (middle + net.scatter_last(own, to_x, to_y)).astype(BF)
-    d_packed, *last = back(prob_b, att_b, d_grouped, heads, PAIRS - heads, first[:1])
-    g_group, g_taps, g_mix = (jnp.concatenate([a, b], axis=0) for a, b in zip(first[1:], last))
+    corner = net.send_corner(run_b[3][n:], yo_g[n:])
+    to_x, to_y = net.with_corner((run_a[3][n:], run_b[3][:n]), (yo_f[n:], yo_g[:n]), corner)
+    own = run_a[3][:n].astype(F32) + yo_f[:n].astype(F32)
+    to_x, to_y, d_grouped = fence(to_x, to_y, d_grouped)
+    along_x, along_y = net.hop(to_x, 0, 2), net.hop(to_y, 1, 0)
+    d_packed, g_group, g_taps, g_mix = attend_back(
+        packed_t, doc_ids, taps_back, head_mix, group_col, (prob_a, prob_b), (att_a, att_b), d_grouped
+    )
+    along_x, along_y, d_packed = fence(along_x, along_y, d_packed)
+    layer_out = (middle + (own + along_x.astype(F32) + along_y.astype(F32))).astype(BF)
     pieces = cut(d_packed.reshape(3 * D, n), net.place, lines, cols)
+    *pieces, branch = fence(*pieces, branch)
     pieces = [net.hop_block(p, b) for b, p in enumerate(pieces)]
     g_blocks = out_weight_grad(branch, grouped, net.place, lines, half_out)
-    g_far = [net.hop(g, 0, 1) for g in g_blocks[4:]]
-    *pieces, g_ffn = fence(*pieces, g_ffn)
+    pieces = fence(*pieces, time=52)
+    *pieces, g_far, sums = fence(
+        *pieces, net.hop(g_blocks[4], 0, 1), fold_sums(g_group, g_taps, g_mix)
+    )
+    size = lines * half_out
+    g_far = [g_far[b * size : (b + 1) * size] for b in range(4)]
     own, to_x, to_y = net.scatter_corner(g_blocks[:4], g_far)
+    g_qkv, g_ffn, *pieces = fence(qkv_grad(pieces, norm_near, norm_far, cols), g_ffn, *pieces)
+    g_qkv = fence(net.scatter_line(g_qkv), time=20)[0]
     g_other = net.hop(g_ffn, 1, 0)
-    far = back_project(pieces[4:], x_far, norm_far, w_attn, cols, n, BF)
-    to_x, to_y, *far = fence(to_x, to_y, *far)
-    g_out = net.scatter_last(own, to_x, to_y)
+    near_c = back_project(pieces[3:4], x_near, 3, w_attn, cols, n, 1)
+    far = back_project(pieces[4:], x_far, 0, w_attn, cols, n, 8)
+    to_x, to_y, *rest = fence(to_x, to_y, *near_c, *far)
+    near_c, far = rest[:2], rest[2:]
     dn_far = net.hop(far[0], 0, 1)
-    near = back_project(pieces[:4], x_near, norm_near, w_attn, cols, n, F32, far[1:])
-    g_other, *near = fence(g_other, *near)
-    g_qkv = fence(net.scatter_line(near[1]), time=30)[0]
-    g_qkv = net.both_halves(g_qkv).T
-    g_out = net.both_halves(net.scatter_line_small(g_out).astype(BF)).T
+    along_x, along_y = net.hop(to_x, 0, 2), net.hop(to_y, 1, 0)
+    corner = (near_c[0].astype(F32) + dn_far[3 * n :].astype(F32)).astype(BF)
+    corner, *pieces = fence(corner, *pieces[:3])
+    corner = net.hop(corner, 0, 2)
+    *near, g_other, corner = fence(
+        *back_project(pieces, x_near, 0, w_attn, cols, n, 1), g_other, corner
+    )
+    small = jnp.concatenate([near_c[1][0] + near[1][0] + far[1][0], g_ffn_gain, sums])
+    small = net.sum_small(small, [bit for bit, _ in net.doubling if bit > 2])
+    to_x, to_y = (near[0][b * n : (b + 1) * n].astype(F32) + dn_far[b * n : (b + 1) * n].astype(F32) for b in (1, 2))
+    to_x, to_y = to_x.astype(BF), (to_y + corner.astype(F32)).astype(BF)
+    to_x, to_y, small, g_other, along_x, along_y = fence(to_x, to_y, small, g_other, along_x, along_y)
+    sent = fence(net.hop(to_x, 0, 2), net.hop(to_y, 1, 0), time=30)
+    g_out = net.scatter_line_small(own + along_x.astype(F32) + along_y.astype(F32)).astype(BF)
+    *sent, small, g_out, g_qkv = fence(*sent, small, g_out, g_qkv)
+    small = net.sum_small(small, [1, 2])
+    small = small + net.hop(small, 1, 0)
+    d_normed = near[0][:n].astype(F32) + dn_far[:n].astype(F32) + sent[0].astype(F32) + sent[1].astype(F32)
+    g_out = net.both_halves(g_out).T
     shape = (3, wide, D)
     g_ffn = net.both_halves(g_ffn.reshape(shape), 1, g_other.reshape(shape))
     g_gate, g_up, g_down = g_ffn[0].T, g_ffn[1].T, g_ffn[2]
-    own, to_x, to_y = net.scatter_corner(rows_of(near[0]), rows_of(dn_far))
-    d_normed = net.scatter_last(own, to_x, to_y)
+    g_qkv = net.both_halves(g_qkv).T
     d_in = rms_back(inputs, gains[0], d_normed)[0]
     input_grad = d_middle + d_in
 
-    small = net.sum_small(
-        jnp.concatenate([near[2][0], g_group[:, 0], g_ffn_gain, g_taps.reshape(-1), g_mix.reshape(-1)])
-    )
     part = D // shards
     gain_grads = [
-        lax.dynamic_slice_in_dim(small, b * D + net.fsdp * part, part) for b in range(3)
+        lax.dynamic_slice_in_dim(small, b * D + net.fsdp * part, part) for b in (0, 2, 1)
     ]
     g_taps = small[3 * D : 3 * D + H * CQ * CK].reshape(H, CQ * CK)
     g_mix = small[3 * D + H * CQ * CK :].reshape(PAIRS, 2, 2)

time: 527 us -> 495 us (0.939)
  waiting for transfers between devices: 140 us -> 103 us
  local copies, waits for them, and re-layouts: 41.4 us -> 52.7 us
  Pallas kernels: 178 us -> 188 us
  starting transfers between devices: 66.8 us -> 57.4 us
  other arithmetic: 72.5 us -> 65.5 us
    pallas_call x6 -> x7, Pallas kernels: 78.8 us -> 94.5 us  [the longest x3 38.2 us: ffn(): pl.pallas_call(functools.partial(ffn_kernel, counts), cost_estimate=cost(...]
    convert_element_type x6 -> x11, other arithmetic: 10.5 us -> 23.9 us  [the longest x2 6.27 us: with_corner(): return (to_x, (to_y + jnp.where(self.odd, corner, 0.0)).astype(BF))]
    ppermute x3, waiting for transfers between devices: 15.1 us -> 1.9 us  [far_corner(): lax.ppermute(jnp.where(self.odd, along_y, along_x), self.axes, self.corner)]
    ppermute x0 -> x2, waiting for transfers between devices: none -> 13.1 us  [send_corner(): lax.ppermute((near.astype(F32) + far.astype(F32)).astype(BF), self.axes,...]
    all_gather x2, waiting for transfers between devices: 12.3 us -> 1.43 us  [gather_line(): lax.all_gather(value, 'fsdp', axis=0, tiled=True, axis_index_groups=self....]
    unnamed x124 -> x149, local copies, waits for them, and re-layouts: 16.4 us -> 27.1 us
    ppermute x4 -> x1, waiting for transfers between devices: 10.7 us -> 0.12 us  [scatter_corner(): corner = lax.ppermute(last.astype(BF), self.axes, self.corner).astype(F32)]
    convert_element_type x3 -> x1, other arithmetic: 11.2 us -> 2.89 us  [scatter_corner(): to_y = (to_y + jnp.where(self.odd, corner, 0.0)).astype(BF)]
  transfers between devices with their start and end apart: 71 -> 68, of which waited for: 30 -> 26; matrix products, arithmetic and copies ran while one was open for 20% -> 21% of each run, Pallas kernels for 31% -> 32%
where the time goes in v3:
time: 495 us; the launch traced here: 488 us
  Pallas kernels  188 us (38%)
  waiting for transfers between devices  103 us (21%)
  other arithmetic  65.5 us (13%)
  starting transfers between devices  57.4 us (12%)
  local copies, waits for them, and re-layouts  52.7 us (11%)
  between operations  15.9 us (3%)
  matrix products  5.25 us (1%)
    ppermute x50, waiting for transfers between devices, hop(): return lax.ppermute(value, self.axes, self.hops[dy, di])  77.7 us
    ppermute x50, starting transfers between devices, hop(): return lax.ppermute(value, self.axes, self.hops[dy, di])  41.7 us
    pallas_call x3, Pallas kernels, ffn(): pl.pallas_call(functools.partial(ffn_kernel, counts), cost_estimate=cost(...  38.2 us
    unnamed x149, local copies, waits for them, and re-layouts  27.1 us
    pallas_call x2, Pallas kernels, attend(): pl.pallas_call(attend_kernel, cost_estimate=cost(2.7 * count), grid=(coun...  26.8 us
    pallas_call x1, Pallas kernels, attend_back(): pl.pallas_call(functools.partial(attend_back_kernel, first), cost_estimat...  23.1 us
    pallas_call x3, Pallas kernels, back_project(): pl.pallas_call(functools.partial(back_project_kernel, count), cost_estima...  18.3 us
    pallas_call x1, Pallas kernels, ffn_grad(): pl.pallas_call(functools.partial(ffn_grad_kernel, len(hidden)), cost_esti...  17.6 us
  transfers between devices with their start and end apart: 68, of which 26 were waited for; matrix products, arithmetic and copies ran while one was open for 21% of the time, Pallas kernels for 32%

profile of v3, /device:TPU:0, one launch (start us, length us, event | category | flops | bytes accessed | tf_op | source)
XLA Modules:
  0.0 487.7 jit_solution(2539138405731393059)
XLA Ops:
  19.2 16.1 %shard_map.220 = (bf16[16,1536,256]{2,1,0:T(8,128)(2,1)}, bf16[16,1536,256]{2,1,0:T(8,128)(2,1)}, bf16[16,1536,256]{2,1,0:T(8,128)(2,1)}) custom-call(f32[16,8,256]{2,1,0:T(8,128)} %pad.7.fwd_ref, f32[16,8,256]{2,1,0:T(8,128)} %pad.8.bwd_ref), custom_call_target="tpu_custom_call" | custom-call | flops 8000000000 | tf_op jit(solution)/shard_map/pallas_call | solution.py:63
  35.3 9.5 %collective-permute-done.2.refs_3_ = bf16[256,1536]{1,0:T(8,128)(2,1)S(1)} collective-permute-done((bf16[256,1536]{1,0:T(8,128)(2,1)}, bf16[256,1536]{1,0:T(8,128)(2,1)S(1)}, u32[]{:S(2)}, u32[]{:S(2)}) %collective-permute-start.2) | collective-permute-done | bytes 786464 | tf_op jit(solution)/shard_map/ppermute | solution.py:766
  54.1 4.6 maximum_maximum_fusion.1
  77.6 7.4 %shard_map.227 = (bf16[1024,1536]{1,0:T(8,128)(2,1)}, bf16[576,256]{1,0:T(8,128)(2,1)}, bf16[576,256]{1,0:T(8,128)(2,1)}, bf16[576,256]{1,0:T(8,128)(2,1)}, bf16[576,256]{1,0:T(8,128)(2,1)}) custom-call(bf16[1024,1536]{1,0:T(8,128)(2,1)} %get-tuple-element.222.x_ref.refs_1_.refs_3_, f32[1,1536]{1,0:T(1,128)} %slice.168.gain_ref, ...), custom_call_target="tpu_custom_call" | custom-call | flops 2400000000 | tf_op jit(solution)/shard_map/pallas_call | solution.py:109
  88.5 7.6 %shard_map.229 = (bf16[1024,1536]{1,0:T(8,128)(2,1)}, bf16[576,256]{1,0:T(8,128)(2,1)}, bf16[576,256]{1,0:T(8,128)(2,1)}, bf16[576,256]{1,0:T(8,128)(2,1)}, bf16[576,256]{1,0:T(8,128)(2,1)}) custom-call(bf16[1024,1536]{1,0:T(8,128)(2,1)} %get-tuple-element.239.x_ref.refs_4_, f32[1,1536]{1,0:T(1,128)} %slice.168.gain_ref, ...), custom_call_target="tpu_custom_call" | custom-call | flops 2400000000 | tf_op jit(solution)/shard_map/pallas_call | solution.py:109
  108.4 7.0 %collective-permute-done.16.refs_6_ = bf16[576,256]{1,0:T(8,128)(2,1)S(1)} collective-permute-done((bf16[576,256]{1,0:T(8,128)(2,1)}, bf16[576,256]{1,0:T(8,128)(2,1)S(1)}, u32[]{:S(2)}, u32[]{:S(2)}) %collective-permute-start.16) | collective-permute-done | bytes 294944 | tf_op jit(solution)/shard_map/ppermute | solution.py:766
  124.2 15.9 %shard_map.233 = (f32[10,256,256]{2,1,0:T(8,128)}, f32[960,256]{1,0:T(8,128)}, bf16[1536,256]{1,0:T(8,128)(2,1)}) custom-call(f32[5,4]{1,0:T(8,128)} %copy.203.mix_ref, bf16[4608,256]{1,0:T(8,128)(2,1)} %bitcast.49, bf16[4608,256]{1,0:T(8,128)(2,1)} %bitcast.50, bf16[4608,256]{1,0:T(8,128)(2,1)} %bitcast.51, ...), custom_call_target="tpu_custom_call" | custom-call | flops 6750000128 | tf_op jit(solution)/shard_map/pallas_call | solution.py:554
  140.1 5.9 %collective-permute-done.20.refs_1_ = bf16[192,1536]{1,0:T(8,128)(2,1)S(1)} collective-permute-done((bf16[192,1536]{1,0:T(8,128)(2,1)}, bf16[192,1536]{1,0:T(8,128)(2,1)S(1)}, u32[]{:S(2)}, u32[]{:S(2)}) %collective-permute-start.20) | collective-permute-done | bytes 589856 | tf_op jit(solution)/shard_map/ppermute | solution.py:766
  153.5 10.9 %shard_map.235 = (f32[6,256,256]{2,1,0:T(8,128)}, f32[576,256]{1,0:T(8,128)}, bf16[1536,256]{1,0:T(8,128)(2,1)}) custom-call(f32[3,4]{1,0:T(4,128)} %copy.206.mix_ref, bf16[4608,256]{1,0:T(8,128)(2,1)} %bitcast.52, bf16[4608,256]{1,0:T(8,128)(2,1)} %bitcast.53, bf16[4608,256]{1,0:T(8,128)(2,1)} %bitcast.54, ...), custom_call_target="tpu_custom_call", output_to_operand_aliasing={{2}: (9, {})} | custom-call | flops 4049999872 | tf_op jit(solution)/shard_map/pallas_call | solution.py:554
  165.9 6.5 %shard_map.237 = (f32[256,1536]{1,0:T(8,128)}, bf16[256,1536]{1,0:T(8,128)(2,1)}) custom-call(s32[1]{0:T(128)} %bitcast.place_ref, bf16[1536,256]{1,0:T(8,128)(2,1)} %get-tuple-element.274.grp_ref.grouped_ref, bf16[768,1536]{1,0:T(8,128)(2,1)} %constant_dynamic-update-slice_fusion.near_ref.refs_0_, bf16[768,1536]{1,0:T(8,128)(2,1)} %get-tuple-element.275.far_ref.refs_1_, ...), custom_call_target="tpu_custom_call" | custom-call | flops 3000000000 | tf_op jit(solution)/shard_map/pallas_call | solution.py:193
  173.9 4.9 %shard_map.239 = bf16[4,4,2,48,1536]{4,3,2,1,0:T(8,128)(2,1)} custom-call(s32[1]{0:T(128)} %bitcast.place_ref, bf16[768,1536]{1,0:T(8,128)(2,1)} %get-tuple-element.279.refs_0_, bf16[768,1536]{1,0:T(8,128)(2,1)} %get-tuple-element.280.refs_1_), custom_call_target="tpu_custom_call" | custom-call | flops 1000000000 | tf_op jit(solution)/shard_map/pallas_call | solution.py:161
  179.8 12.8 %collective-permute-done.23 = bf16[256,1536]{1,0:T(8,128)(2,1)S(1)} collective-permute-done((bf16[256,1536]{1,0:T(8,128)(2,1)}, bf16[256,1536]{1,0:T(8,128)(2,1)S(1)}, u32[]{:S(2)}, u32[]{:S(2)}) %collective-permute-start.23) | collective-permute-done | bytes 786464 | tf_op jit(solution)/shard_map/ppermute | solution.py:766
  197.1 10.1 %shard_map.241 = (bf16[512,512]{1,0:T(8,128)(2,1)}, bf16[512,1024]{1,0:T(8,128)(2,1)}, bf16[512,1536]{1,0:T(8,128)(2,1)}, bf16[512,1536]{1,0:T(8,128)(2,1)}) custom-call(bf16[512,1536]{1,0:T(8,128)(2,1)} %get-tuple-element.482.refs_0_.refs_8_, bf16[1024,1536]{1,0:T(8,128)(2,1)} %get-tuple-element.252.refs_1_.refs_12_.refs_15_, ...), custom_call_target="tpu_custom_call" | custom-call | flops 3500000000 | tf_op jit(solution)/shard_map/pallas_call | solution.py:349
  210.7 3.6 collective-permute-done.27.refs_1_.refs_10_
  215.5 17.9 %shard_map.243 = (bf16[1024,512]{1,0:T(8,128)(2,1)}, bf16[1024,1024]{1,0:T(8,128)(2,1)}, bf16[512,1536]{1,0:T(8,128)(2,1)}, bf16[512,1536]{1,0:T(8,128)(2,1)}, b...) custom-call(bf16[512,1536]{1,0:T(8,128)(2,1)} %get-tuple-element.288.refs_0_.refs_9_, bf16[512,1536]{1,0:T(8,128)(2,1)} %copy-done.42, ...), custom_call_target="tpu_custom_call" | custom-call | flops 7000000000 | tf_op jit(solution)/shard_map/pallas_call | solution.py:349
  233.9 10.2 %shard_map.244 = (bf16[512,512]{1,0:T(8,128)(2,1)}, bf16[512,1024]{1,0:T(8,128)(2,1)}, bf16[512,1536]{1,0:T(8,128)(2,1)}, bf16[512,1536]{1,0:T(8,128)(2,1)}) custom-call(bf16[512,1536]{1,0:T(8,128)(2,1)} %constant_dynamic-update-slice_fusion.6.refs_0_.refs_11_, bf16[1024,1536]{1,0:T(8,128)(2,1)} %get-tuple-element.252.refs_1_.refs_12_.refs_15_, ...), custom_call_target="tpu_custom_call" | custom-call | flops 3500000000 | tf_op jit(solution)/shard_map/pallas_call | solution.py:349
  249.0 10.0 %collective-permute-done.30 = bf16[256,1536]{1,0:T(8,128)(2,1)S(1)} collective-permute-done((bf16[256,1536]{1,0:T(8,128)(2,1)S(1)}, bf16[256,1536]{1,0:T(8,128)(2,1)S(1)}, u32[]{:S(2)}, u32[]{:S(2)}) %collective-permute-start.30) | collective-permute-done | bytes 786464 | tf_op jit(solution)/shard_map/ppermute | solution.py:806
  265.4 17.6 %shard_map.247.refs_3_ = bf16[4,384,1536]{2,1,0:T(8,128)(2,1)} custom-call(bf16[512,512]{1,0:T(8,128)(2,1)} %get-tuple-element.310.refs_0_, bf16[1024,512]{1,0:T(8,128)(2,1)} %get-tuple-element.311.refs_1_.refs_2_, bf16[1024,512]{1,0:T(8,128)(2,1)} %get-tuple-element.311.refs_1_.refs_2_, bf16[512,512]{1,0:T(8,128)(2,1)} %get-tuple-element.312.refs_3_, ...), custom_call_target="tpu_custom_call" | custom-call | flops 7000000000 | tf_op jit(solution)/shard_map/pallas_call | solution.py:404
  294.1 5.3 %fusion.20.refs_2_ = f32[1536,256]{1,0:T(8,128)} fusion(bf16[1536,1536]{1,0:T(8,128)(2,1)} %get-tuple-element.319, bf16[256,1536]{1,0:T(8,128)(2,1)S(1)} %get-tuple-element.463.refs_8_), kind=kOutput, calls=%fused_computation.115 | convolution fusion | flops 1207959552 | bytes 7077888 | tf_op jit(solution)/shard_map/dot_general | solution.py:26
  306.9 23.1 %shard_map.250 = (bf16[3,1536,256]{2,1,0:T(8,128)(2,1)}, f32[1536,1]{1,0:T(8,128)}, f32[16,48,128]{2,1,0:T(8,128)}, f32[8,8,256]{2,1,0:T(8,128)}) custom-call(f32[8,4]{1,0:T(8,128)} %copy.209.mix_ref, bf16[4608,256]{1,0:T(8,128)(2,1)} %bitcast.55, bf16[4608,256]{1,0:T(8,128)(2,1)} %bitcast.56, bf16[4608,256]{1,0:T(8,128)(2,1)} %bitcast.57, ...), custom_call_target="tpu_custom_call" | custom-call | flops 10800000000 | tf_op jit(solution)/shard_map/pallas_call | solution.py:676
  339.2 5.5 %collective-permute-done.38.refs_1_ = bf16[576,256]{1,0:T(8,128)(2,1)S(1)} collective-permute-done((bf16[576,256]{1,0:T(8,128)(2,1)}, bf16[576,256]{1,0:T(8,128)(2,1)S(1)}, u32[]{:S(2)}, u32[]{:S(2)}) %collective-permute-start.38) | collective-permute-done | bytes 294944 | tf_op jit(solution)/shard_map/ppermute | solution.py:766
  352.3 5.6 %shard_map.254 = (bf16[192,1536]{1,0:T(8,128)(2,1)}, bf16[192,1536]{1,0:T(8,128)(2,1)}, bf16[192,1536]{1,0:T(8,128)(2,1)}, bf16[192,1536]{1,0:T(8,128)(2,1)}, bf16[768,1536]{1,0:T(8,128)(2,1)}) custom-call(s32[1]{0:T(128)} %bitcast.place_ref, bf16[256,1536]{1,0:T(8,128)(2,1)} %get-tuple-element.341.branch_ref, ...), custom_call_target="tpu_custom_call" | custom-call | tf_op jit(solution)/shard_map/pallas_call | solution.py:232
  358.0 4.5 collective-permute-done.43.refs_6_
  367.4 9.0 %shard_map.257.refs_0_ = bf16[576,1536]{1,0:T(8,128)(2,1)} custom-call(bf16[576,256]{1,0:T(8,128)(2,1)} %get-tuple-element.366.refs_0_.refs_2_, bf16[576,256]{1,0:T(8,128)(2,1)} %get-tuple-element.367.refs_1_.refs_3_, bf16[576,256]{1,0:T(8,128)(2,1)} %get-tuple-element.368.refs_2_.refs_4_, bf16[576,256]{1,0:T(8,128)(2,1)} %get-tuple-element.369.refs_3_.refs_5_, ...), custom_call_target="tpu_custom_call" | custom-call | flops 3000000000 | tf_op jit(solution)/shard_map/pallas_call | solution.py:442
  379.5 3.7 shard_map.260
  383.2 7.9 %shard_map.261 = (bf16[1024,1536]{1,0:T(8,128)(2,1)}, f32[1,1536]{1,0:T(1,128)}) custom-call(bf16[576,256]{1,0:T(8,128)(2,1)} %get-tuple-element.380.refs_0_, bf16[576,256]{1,0:T(8,128)(2,1)} %get-tuple-element.381.refs_1_, bf16[576,256]{1,0:T(8,128)(2,1)} %get-tuple-element.382.refs_2_, bf16[576,256]{1,0:T(8,128)(2,1)} %get-tuple-element.383.refs_3_, ...), custom_call_target="tpu_custom_call" | custom-call | flops 4000000000 | tf_op jit(solution)/shard_map/pallas_call | solution.py:484
  393.5 3.6 collective-permute-done.47
  405.7 6.7 %shard_map.264 = (bf16[768,1536]{1,0:T(8,128)(2,1)}, f32[1,1536]{1,0:T(1,128)}) custom-call(bf16[576,256]{1,0:T(8,128)(2,1)} %get-tuple-element.391.refs_0_, bf16[576,256]{1,0:T(8,128)(2,1)} %get-tuple-element.392.refs_1_, bf16[576,256]{1,0:T(8,128)(2,1)} %get-tuple-element.393.refs_2_, bf16[1024,1536]{1,0:T(8,128)(2,1)} %get-tuple-element.222.x_ref.refs_1_.refs_3_, ...), custom_call_target="tpu_custom_call" | custom-call | flops 500000000 | tf_op jit(solution)/shard_map/pallas_call | solution.py:484
  412.4 9.2 %collective-permute-done.48.refs_2_ = bf16[384,1536]{1,0:T(8,128)(2,1)} collective-permute-done((bf16[384,1536]{1,0:T(8,128)(2,1)}, bf16[384,1536]{1,0:T(8,128)(2,1)}, u32[]{:S(2)}, u32[]{:S(2)}) %collective-permute-start.48) | collective-permute-done | bytes 1179680 | tf_op jit(solution)/shard_map/ppermute | solution.py:766
  424.0 3.7 reduce-scatter.5.cloned.1.call-done.refs_0_
  462.6 3.5 multiply_add_fusion
  466.1 8.9 %collective-permute-done.61 = f32[5696]{0:T(1024)S(1)} collective-permute-done((f32[5696]{0:T(1024)S(1)}, f32[5696]{0:T(1024)S(1)}, u32[]{:S(2)}, u32[]{:S(2)}) %collective-permute-start.61) | collective-permute-done | bytes 22816 | tf_op jit(solution)/shard_map/ppermute | solution.py:766
  (411 shorter events, 193.3 us)
Async XLA Ops:
  7.2 68.3 %all-gather.3.cloned.1.call-start = ((), (), s32[]{:S(2)}) async-start(), calls=%async_computation.2 | async-start | bytes 2949120 | tf_op jit(solution)/shard_map/all_gather | solution.py:772
  7.2 28.0 %collective-permute-start = (bf16[256,1536]{1,0:T(8,128)(2,1)}, bf16[256,1536]{1,0:T(8,128)(2,1)S(1)}, u32[]{:S(2)}, u32[]{:S(2)}) collective-permute-start(bf16[256,1536]{1,0:T(8,128)(2,1)} %param.13), channel_id=1, source_target_pairs={{0,2},{1,3},{2,0},{3,1},{4,6},{5,7},{6,4},{7,5},{8,10},{9,11},{10,... | collective-permute-start | bytes 2359304 | tf_op jit(solution)/shard_map/ppermute | solution.py:766
  10.2 25.1 %collective-permute-start.1 = (bf16[256,1536]{1,0:T(8,128)(2,1)}, bf16[256,1536]{1,0:T(8,128)(2,1)S(1)}, u32[]{:S(2)}, u32[]{:S(2)}) collective-permute-start(bf16[256,1536]{1,0:T(8,128)(2,1)} %param.13), channel_id=1, source_target_pairs={{0,16},{1,17},{2,18},{3,19},{4,20},{5,21},{6,22},{7,23},{8,24},{9,... | collective-permute-start | bytes 2359304 | tf_op jit(solution)/shard_map/ppermute | solution.py:766
  14.1 30.7 %collective-permute-start.2 = (bf16[256,1536]{1,0:T(8,128)(2,1)}, bf16[256,1536]{1,0:T(8,128)(2,1)S(1)}, u32[]{:S(2)}, u32[]{:S(2)}) collective-permute-start(bf16[256,1536]{1,0:T(8,128)(2,1)} %convert_element_type.220), channel_id=1, source_target_pairs={{0,2},{1,3},{2,0},{3,1},{4,6},{5,7},{6,4},{7,5},{8,10},{9,11},{10,... | collective-permute-start | bytes 2359304 | tf_op jit(solution)/shard_map/ppermute | solution.py:766
  14.7 31.7 %collective-permute-start.3 = (bf16[256,1536]{1,0:T(8,128)(2,1)}, bf16[256,1536]{1,0:T(8,128)(2,1)}, u32[]{:S(2)}, u32[]{:S(2)}) collective-permute-start(bf16[256,1536]{1,0:T(8,128)(2,1)} %convert_element_type.220), channel_id=1, source_target_pairs={{0,16},{1,17},{2,18},{3,19},{4,20},{5,21},{6,22},{7,23},{8,24},{9,... | collective-permute-start | bytes 2359304 | tf_op jit(solution)/shard_map/ppermute | solution.py:766
  16.6 180.5 %all-gather.5.cloned.1.call-start = ((), (), s32[]{:S(2)}) async-start(), calls=%async_computation.3 | async-start | bytes 5898240 | tf_op jit(solution)/shard_map/all_gather | solution.py:772
  76.3 40.1 %collective-permute-start.18 = (bf16[1024,1536]{1,0:T(8,128)(2,1)}, bf16[1024,1536]{1,0:T(8,128)(2,1)}, u32[]{:S(2)}, u32[]{:S(2)}) collective-permute-start(bf16[1024,1536]{1,0:T(8,128)(2,1)} %get-tuple-element.252.refs_1_.refs_12_.refs_15_), channel_id=1, source_target_pairs={{0,1},{1,0},{2,3},{3,2},{4,5},{5,4},{6,7},{7,6},{8,9},{9,8},{10,11... | collective-permute-start | bytes 9437192 | tf_op jit(solution)/shard_map/ppermute | solution.py:766
  107.8 271.6 %reduce-scatter.3.cloned.1.call-start = ((), (), s32[]{:S(2)}) async-start(), calls=%async_computation.4 | async-start | bytes 5898240 | tf_op jit(solution)/shard_map/reduce_scatter | solution.py:775
  116.3 23.7 %collective-permute-start.19 = (bf16[192,1536]{1,0:T(8,128)(2,1)}, bf16[192,1536]{1,0:T(8,128)(2,1)S(1)}, u32[]{:S(2)}, u32[]{:S(2)}) collective-permute-start(bf16[192,1536]{1,0:T(8,128)(2,1)} %get-tuple-element.253), channel_id=1, source_target_pairs={{0,2},{1,3},{2,0},{3,1},{4,6},{5,7},{6,4},{7,5},{8,10},{9,11},{10,... | collective-permute-start | bytes 1769480 | tf_op jit(solution)/shard_map/ppermute | solution.py:766
  117.4 28.6 %collective-permute-start.20 = (bf16[192,1536]{1,0:T(8,128)(2,1)}, bf16[192,1536]{1,0:T(8,128)(2,1)S(1)}, u32[]{:S(2)}, u32[]{:S(2)}) collective-permute-start(bf16[192,1536]{1,0:T(8,128)(2,1)} %get-tuple-element.253), channel_id=1, source_target_pairs={{0,16},{1,17},{2,18},{3,19},{4,20},{5,21},{6,22},{7,23},{8,24},{9,... | collective-permute-start | bytes 1769480 | tf_op jit(solution)/shard_map/ppermute | solution.py:766
  118.9 27.1 %collective-permute-start.21 = (bf16[192,1536]{1,0:T(8,128)(2,1)}, bf16[192,1536]{1,0:T(8,128)(2,1)S(1)}, u32[]{:S(2)}, u32[]{:S(2)}) collective-permute-start(bf16[192,1536]{1,0:T(8,128)(2,1)} %get-tuple-element.253), channel_id=1, source_target_pairs={{0,18},{1,19},{2,16},{3,17},{4,22},{5,23},{6,20},{7,21},{8,26},{9,... | collective-permute-start | bytes 1769480 | tf_op jit(solution)/shard_map/ppermute | solution.py:766
  172.4 20.2 %collective-permute-start.23 = (bf16[256,1536]{1,0:T(8,128)(2,1)}, bf16[256,1536]{1,0:T(8,128)(2,1)S(1)}, u32[]{:S(2)}, u32[]{:S(2)}) collective-permute-start(bf16[256,1536]{1,0:T(8,128)(2,1)} %get-tuple-element.278), channel_id=1, source_target_pairs={{0,16},{1,17},{2,18},{3,19},{4,20},{5,21},{6,22},{7,23},{8,24},{9,... | collective-permute-start | bytes 2359304 | tf_op jit(solution)/shard_map/ppermute | solution.py:766
  172.9 19.9 %collective-permute-start.24 = (bf16[256,1536]{1,0:T(8,128)(2,1)}, bf16[256,1536]{1,0:T(8,128)(2,1)S(1)}, u32[]{:S(2)}, u32[]{:S(2)}) collective-permute-start(bf16[256,1536]{1,0:T(8,128)(2,1)} %get-tuple-element.278), channel_id=1, source_target_pairs={{0,2},{1,3},{2,0},{3,1},{4,6},{5,7},{6,4},{7,5},{8,10},{9,11},{10,... | collective-permute-start | bytes 2359304 | tf_op jit(solution)/shard_map/ppermute | solution.py:766
  248.5 37.4 %collective-permute-start.33 = (bf16[512,1536]{1,0:T(8,128)(2,1)}, bf16[512,1536]{1,0:T(8,128)(2,1)}, u32[]{:S(2)}, u32[]{:S(2)}) collective-permute-start(bf16[512,1536]{1,0:T(8,128)(2,1)} %get-tuple-element.308), channel_id=1, source_target_pairs={{0,1},{1,0},{2,3},{3,2},{4,5},{5,4},{6,7},{7,6},{8,9},{9,8},{10,11... | collective-permute-start | bytes 4718600 | tf_op jit(solution)/shard_map/ppermute | solution.py:766
  248.5 37.4 %collective-permute-start.34 = (bf16[512,1536]{1,0:T(8,128)(2,1)}, bf16[512,1536]{1,0:T(8,128)(2,1)S(1)}, u32[]{:S(2)}, u32[]{:S(2)}) collective-permute-start(bf16[512,1536]{1,0:T(8,128)(2,1)} %get-tuple-element.309), channel_id=1, source_target_pairs={{0,1},{1,0},{2,3},{3,2},{4,5},{5,4},{6,7},{7,6},{8,9},{9,8},{10,11... | collective-permute-start | bytes 4718600 | tf_op jit(solution)/shard_map/ppermute | solution.py:766
  262.4 20.6 %collective-permute-start.32 = (bf16[256,1536]{1,0:T(8,128)(2,1)}, bf16[256,1536]{1,0:T(8,128)(2,1)S(1)}, u32[]{:S(2)}, u32[]{:S(2)}) collective-permute-start(bf16[256,1536]{1,0:T(8,128)(2,1)} %get-tuple-element.307), channel_id=1, source_target_pairs={{0,16},{1,17},{2,18},{3,19},{4,20},{5,21},{6,22},{7,23},{8,24},{9,... | collective-permute-start | bytes 2359304 | tf_op jit(solution)/shard_map/ppermute | solution.py:766
  263.9 19.1 %collective-permute-start.31 = (bf16[256,1536]{1,0:T(8,128)(2,1)}, bf16[256,1536]{1,0:T(8,128)(2,1)S(1)}, u32[]{:S(2)}, u32[]{:S(2)}) collective-permute-start(bf16[256,1536]{1,0:T(8,128)(2,1)} %get-tuple-element.306), channel_id=1, source_target_pairs={{0,2},{1,3},{2,0},{3,1},{4,6},{5,7},{6,4},{7,5},{8,10},{9,11},{10,... | collective-permute-start | bytes 2359304 | tf_op jit(solution)/shard_map/ppermute | solution.py:766
  287.1 140.6 %reduce-scatter.5.cloned.1.call-start = ((), (), s32[]{:S(2)}) async-start(), calls=%async_computation.5 | async-start | bytes 2211840 | tf_op jit(solution)/shard_map/reduce_scatter | solution.py:775
  305.4 24.6 %collective-permute-start.36 = (bf16[256,1536]{1,0:T(8,128)(2,1)}, bf16[256,1536]{1,0:T(8,128)(2,1)S(1)}, u32[]{:S(2)}, u32[]{:S(2)}) collective-permute-start(bf16[256,1536]{1,0:T(8,128)(2,1)} %get-tuple-element.321), channel_id=1, source_target_pairs={{0,2},{1,3},{2,0},{3,1},{4,6},{5,7},{6,4},{7,5},{8,10},{9,11},{10,... | collective-permute-start | bytes 2359304 | tf_op jit(solution)/shard_map/ppermute | solution.py:766
  306.3 23.7 %collective-permute-start.37 = (bf16[256,1536]{1,0:T(8,128)(2,1)}, bf16[256,1536]{1,0:T(8,128)(2,1)S(1)}, u32[]{:S(2)}, u32[]{:S(2)}) collective-permute-start(bf16[256,1536]{1,0:T(8,128)(2,1)} %get-tuple-element.322), channel_id=1, source_target_pairs={{0,16},{1,17},{2,18},{3,19},{4,20},{5,21},{6,22},{7,23},{8,24},{9,... | collective-permute-start | bytes 2359304 | tf_op jit(solution)/shard_map/ppermute | solution.py:766
  337.1 20.8 %collective-permute-start.40 = (bf16[576,256]{1,0:T(8,128)(2,1)}, bf16[576,256]{1,0:T(8,128)(2,1)S(1)}, u32[]{:S(2)}, u32[]{:S(2)}) collective-permute-start(bf16[576,256]{1,0:T(8,128)(2,1)} %get-tuple-element.346), channel_id=1, source_target_pairs={{0,18},{1,19},{2,16},{3,17},{4,22},{5,23},{6,20},{7,21},{8,26},{9,... | collective-permute-start | bytes 884744 | tf_op jit(solution)/shard_map/ppermute | solution.py:766
  338.1 20.0 %collective-permute-start.41 = (bf16[576,256]{1,0:T(8,128)(2,1)}, bf16[576,256]{1,0:T(8,128)(2,1)S(1)}, u32[]{:S(2)}, u32[]{:S(2)}) collective-permute-start(bf16[576,256]{1,0:T(8,128)(2,1)} %get-tuple-element.347), channel_id=1, source_target_pairs={{0,1},{1,0},{2,3},{3,2},{4,5},{5,4},{6,7},{7,6},{8,9},{9,8},{10,11... | collective-permute-start | bytes 884744 | tf_op jit(solution)/shard_map/ppermute | solution.py:766
  338.1 20.0 %collective-permute-start.42 = (bf16[576,256]{1,0:T(8,128)(2,1)}, bf16[576,256]{1,0:T(8,128)(2,1)S(1)}, u32[]{:S(2)}, u32[]{:S(2)}) collective-permute-start(bf16[576,256]{1,0:T(8,128)(2,1)} %get-tuple-element.348), channel_id=1, source_target_pairs={{0,3},{1,2},{2,1},{3,0},{4,7},{5,6},{6,5},{7,4},{8,11},{9,10},{10,... | collective-permute-start | bytes 884744 | tf_op jit(solution)/shard_map/ppermute | solution.py:766
  344.7 17.8 %collective-permute-start.43 = (bf16[576,256]{1,0:T(8,128)(2,1)}, bf16[576,256]{1,0:T(8,128)(2,1)S(1)}, u32[]{:S(2)}, u32[]{:S(2)}) collective-permute-start(bf16[576,256]{1,0:T(8,128)(2,1)} %get-tuple-element.349), channel_id=1, source_target_pairs={{0,17},{1,16},{2,19},{3,18},{4,21},{5,20},{6,23},{7,22},{8,25},{9,... | collective-permute-start | bytes 884744 | tf_op jit(solution)/shard_map/ppermute | solution.py:766
  392.4 29.2 %collective-permute-start.48 = (bf16[384,1536]{1,0:T(8,128)(2,1)}, bf16[384,1536]{1,0:T(8,128)(2,1)}, u32[]{:S(2)}, u32[]{:S(2)}) collective-permute-start(bf16[384,1536]{1,0:T(8,128)(2,1)} %get-tuple-element.396), channel_id=1, source_target_pairs={{0,16},{1,17},{2,18},{3,19},{4,20},{5,21},{6,22},{7,23},{8,24},{9,... | collective-permute-start | bytes 3538952 | tf_op jit(solution)/shard_map/ppermute | solution.py:766
  399.3 22.3 %collective-permute-start.49 = (bf16[256,1536]{1,0:T(8,128)(2,1)}, bf16[256,1536]{1,0:T(8,128)(2,1)S(1)}, u32[]{:S(2)}, u32[]{:S(2)}) collective-permute-start(bf16[256,1536]{1,0:T(8,128)(2,1)} %get-tuple-element.397), channel_id=1, source_target_pairs={{0,2},{1,3},{2,0},{3,1},{4,6},{5,7},{6,4},{7,5},{8,10},{9,11},{10,... | collective-permute-start | bytes 2359304 | tf_op jit(solution)/shard_map/ppermute | solution.py:766
  403.7 29.5 %collective-permute-start.52 = (bf16[192,1536]{1,0:T(8,128)(2,1)}, bf16[192,1536]{1,0:T(8,128)(2,1)}, u32[]{:S(2)}, u32[]{:S(2)}) collective-permute-start(bf16[192,1536]{1,0:T(8,128)(2,1)} %get-tuple-element.405), channel_id=1, source_target_pairs={{0,2},{1,3},{2,0},{3,1},{4,6},{5,7},{6,4},{7,5},{8,10},{9,11},{10,... | collective-permute-start | bytes 1769480 | tf_op jit(solution)/shard_map/ppermute | solution.py:766
  404.7 28.5 %collective-permute-start.53 = (bf16[192,1536]{1,0:T(8,128)(2,1)}, bf16[192,1536]{1,0:T(8,128)(2,1)}, u32[]{:S(2)}, u32[]{:S(2)}) collective-permute-start(bf16[192,1536]{1,0:T(8,128)(2,1)} %get-tuple-element.406), channel_id=1, source_target_pairs={{0,16},{1,17},{2,18},{3,19},{4,20},{5,21},{6,22},{7,23},{8,24},{9,... | collective-permute-start | bytes 1769480 | tf_op jit(solution)/shard_map/ppermute | solution.py:766
  433.2 22.6 %collective-permute-start.54 = (bf16[256,1536]{1,0:T(8,128)(2,1)}, bf16[256,1536]{1,0:T(8,128)(2,1)}, u32[]{:S(2)}, u32[]{:S(2)}) collective-permute-start(bf16[256,1536]{1,0:T(8,128)(2,1)} %get-tuple-element.407), channel_id=1, source_target_pairs={{0,2},{1,3},{2,0},{3,1},{4,6},{5,7},{6,4},{7,5},{8,10},{9,11},{10,... | collective-permute-start | bytes 2359304 | tf_op jit(solution)/shard_map/ppermute | solution.py:766
  434.7 21.1 %collective-permute-start.55 = (bf16[256,1536]{1,0:T(8,128)(2,1)}, bf16[256,1536]{1,0:T(8,128)(2,1)}, u32[]{:S(2)}, u32[]{:S(2)}) collective-permute-start(bf16[256,1536]{1,0:T(8,128)(2,1)} %get-tuple-element.408), channel_id=1, source_target_pairs={{0,16},{1,17},{2,18},{3,19},{4,20},{5,21},{6,22},{7,23},{8,24},{9,... | collective-permute-start | bytes 2359304 | tf_op jit(solution)/shard_map/ppermute | solution.py:766
  458.7 19.3 %collective-permute-start.62 = (bf16[144,1536]{1,0:T(8,128)(2,1)}, bf16[144,1536]{1,0:T(8,128)(2,1)}, u32[]{:S(2)}, u32[]{:S(2)}) collective-permute-start(bf16[144,1536]{1,0:T(8,128)(2,1)} %get-tuple-element.419), channel_id=1, source_target_pairs={{0,16},{1,17},{2,18},{3,19},{4,20},{5,21},{6,22},{7,23},{8,24},{9,... | collective-permute-start | bytes 1327112 | tf_op jit(solution)/shard_map/ppermute | solution.py:766
  459.3 17.8 %collective-permute-start.63 = (bf16[48,1536]{1,0:T(8,128)(2,1)S(1)}, bf16[48,1536]{1,0:T(8,128)(2,1)S(1)}, u32[]{:S(2)}, u32[]{:S(2)}) collective-permute-start(bf16[48,1536]{1,0:T(8,128)(2,1)S(1)} %copy-done.43), channel_id=1, source_target_pairs={{0,16},{1,17},{2,18},{3,19},{4,20},{5,21},{6,22},{7,23},{8,24},{9,... | collective-permute-start | bytes 442376 | tf_op jit(solution)/shard_map/ppermute | solution.py:766
  (106 other events, 717.2 us)
Sparse Core Ops, SparseCore 0:
  16.7 52.4 all-gather.2
  107.9 89.1 all-gather.4
  287.2 82.3 reduce-scatter.2
  391.3 36.3 reduce-scatter.4

commit v4 on v3

--- a/solution.py
+++ b/solution.py
@@ -108,7 +108,7 @@
         return normed, [part[:, b * n : (b + 1) * n] for b in range(count)]
     out = pl.pallas_call(
         project_kernel,
-        cost_estimate=cost(1.2 * count),
+        cost_estimate=cost(0),
         grid=(count,),
         in_specs=[
             pl.BlockSpec((n, D), lambda b: (b, 0)),
@@ -169,12 +169,26 @@
     )(place.reshape(1), *values)
 
 
-def out_project_kernel(half, place_ref, grp_ref, near_ref, far_ref, x_ref, gain_ref, mid_ref, sec_ref, held):
-    size = near_ref.shape[0] // 4
+def out_blocks_kernel(grp_ref, w_ref, out_ref):
+    out_ref[...] = dot(w_ref[...], grp_ref[...], 1, 0)
+
+
+def out_blocks(grouped, w):
+    n = grouped.shape[1]
+    return pl.pallas_call(
+        out_blocks_kernel,
+        cost_estimate=cost(0),
+        out_shape=jax.ShapeDtypeStruct((w.shape[0], n), F32),
+        compiler_params=pltpu.CompilerParams(vmem_limit_bytes=60 * 2**20),
+    )(grouped, w)
+
+
+def out_project_kernel(half, place_ref, grp_ref, far_ref, near_ref, x_ref, gain_ref, mid_ref, sec_ref, held):
+    size = far_ref.shape[0] // 4
     for b in range(8):
         other = place_ref[0] ^ order(b)
-        w = (near_ref, far_ref)[b // 4][b % 4 * size : (b % 4 + 1) * size, :]
-        part = dot(w, grp_ref[...], 1, 0)
+        rows = slice(b % 4 * size, (b % 4 + 1) * size)
+        part = near_ref[rows, :] if b < 4 else dot(far_ref[rows, :], grp_ref[...], 1, 0)
         for z in range(size // half):
             start = pl.multiple_of((z * 8 + (other & 3) * 2 + (other >> 2)) * half, half)
             held[pl.ds(start, half), :] = part[z * half : (z + 1) * half, :]
@@ -183,7 +197,7 @@
     sec_ref[...] = rms_norm(middle, gain_ref[...]).astype(BF)
 
 
-def out_project(grouped, near, far, x, gain, place, lines, half):
+def out_project(grouped, near, far, out_near, x, gain, place, lines, half):
     n = grouped.shape[1]
     if half % 16:
         w_out = join([near, far], place, lines, half)
@@ -192,17 +206,48 @@
     whole = lambda shape: pl.BlockSpec(shape, lambda t: (0, 0))
     return pl.pallas_call(
         functools.partial(out_project_kernel, half),
-        cost_estimate=cost(6),
+        cost_estimate=cost(0),
         grid=(1,),
         in_specs=[
             pl.BlockSpec(memory_space=pltpu.SMEM),
-            whole((D, n)), whole(near.shape), whole(far.shape), whole((n, D)), whole((1, D)),
+            whole((D, n)), whole(far.shape), whole(out_near.shape), whole((n, D)), whole((1, D)),
         ],
         out_specs=[whole((n, D)), whole((n, D))],
         out_shape=[jax.ShapeDtypeStruct((n, D), F32), jax.ShapeDtypeStruct((n, D), BF)],
         scratch_shapes=[pltpu.VMEM((D, n), F32)],
         compiler_params=pltpu.CompilerParams(vmem_limit_bytes=60 * 2**20),
-    )(place.reshape(1), grouped, near, far, x, gain.reshape(1, D))
+    )(place.reshape(1), grouped, far, out_near, x, gain.reshape(1, D))
+
+
+def back_middle_kernel(
+    a_ref, f_ref, sx_ref, sy_ref, mid_ref, dy_ref, gain_ref, w_ref, dm_ref, branch_ref, dgrp_ref, dgain_ref
+):
+    d_second = sum(r[...].astype(F32) for r in (a_ref, f_ref, sx_ref, sy_ref))
+    d_norm, dgain = rms_back(mid_ref[...], gain_ref[...], d_second)
+    d_middle = dy_ref[...] + d_norm
+    dm_ref[...] = d_middle
+    branch = d_middle.astype(BF)
+    branch_ref[...] = branch
+    dgain_ref[...] = dgain[None]
+    dgrp_ref[...] = dot(branch, w_ref[...], 1, 0).T
+
+
+def back_middle(own, far, along_x, along_y, middle, out_grad, gain, w_out):
+    n = middle.shape[0]
+    block = pl.BlockSpec((n, D), lambda t: (0, 0))
+    whole = lambda shape: pl.BlockSpec(shape, lambda t: (0, 0))
+    return pl.pallas_call(
+        back_middle_kernel,
+        cost_estimate=cost(6),
+        grid=(1,),
+        in_specs=[block] * 6 + [whole((1, D)), whole((D, D))],
+        out_specs=[block, block, whole((D, n)), whole((1, D))],
+        out_shape=[
+            jax.ShapeDtypeStruct((n, D), F32), jax.ShapeDtypeStruct((n, D), BF),
+            jax.ShapeDtypeStruct((D, n), F32), jax.ShapeDtypeStruct((1, D), F32),
+        ],
+        compiler_params=pltpu.CompilerParams(vmem_limit_bytes=60 * 2**20),
+    )(own, far, along_x, along_y, middle, out_grad, gain.reshape(1, D), w_out)
 
 
 def out_grad_kernel(place_ref, branch_ref, grouped_ref, *refs):
@@ -451,49 +496,41 @@
     )(*parts, near, far)
 
 
-def back_project_kernel(count, *refs):
-    parts, (x_ref, w_ref, dn_ref, gain_ref) = refs[:count], refs[count:]
-    rows = parts[0].shape[0]
-    w = w_ref[:, : rows // w_ref.shape[0], :].reshape(rows, D)
-    t = pl.program_id(0)
-
-    @pl.when(t == 0)
-    def _():
-        gain_ref[...] = jnp.zeros_like(gain_ref)
-
-    for b in range(count):
-
-        @pl.when(t == b)
-        def _():
-            dn = dot(parts[b][...], w, 0, 0)
-            dn_ref[...] = dn.astype(BF)
-            x = x_ref[...].astype(F32)
-            hat = x * lax.rsqrt(jnp.mean(x * x, axis=1, keepdims=True) + 1e-05)
-            gain_ref[...] += jnp.sum(dn * hat, axis=0, keepdims=True)
-
-
-def back_project(parts, x, first, w_attn, cols, n, time):
-    lines, count = w_attn.shape[0], len(parts)
-    rows = lines * cols
-    if cols % 16:
-        dn = dot(jnp.concatenate(parts, axis=1), w_attn[:, :cols].reshape(rows, D), 0, 0)
-        values = x[first * n : (first + count) * n].astype(F32)
-        hat = values * lax.rsqrt(jnp.mean(values * values, axis=1, keepdims=True) + 1e-05)
-        return dn.astype(BF), jnp.sum(dn * hat, axis=0, keepdims=True)
-    whole = lambda shape: pl.BlockSpec(shape, lambda b: (0,) * len(shape))
-    return pl.pallas_call(
-        functools.partial(back_project_kernel, count),
-        cost_estimate=cost(time),
-        grid=(count,),
-        in_specs=[whole((rows, n))] * count
-        + [pl.BlockSpec((n, D), lambda b: (b + first, 0)), whole(w_attn.shape)],
-        out_specs=[pl.BlockSpec((n, D), lambda b: (b, 0)), whole((1, D))],
-        out_shape=[
-            jax.ShapeDtypeStruct((count * n, D), BF),
-            jax.ShapeDtypeStruct((1, D), F32),
-        ],
-        compiler_params=pltpu.CompilerParams(vmem_limit_bytes=60 * 2**20),
-    )(*parts, x, w_attn)
+def normed_back_kernel(*refs):
+    count = len(refs) // 2
+    refs[-1][...] = sum(dot(p[...], w[...], 0, 0) for p, w in zip(refs[:count], refs[count:-1]))
+
+
+def normed_back(parts, weights):
+    vmem = pl.BlockSpec(memory_space=pltpu.VMEM)
+    return pl.pallas_call(
+        normed_back_kernel,
+        cost_estimate=cost(1),
+        in_specs=[vmem] * (2 * len(parts)),
+        out_specs=vmem,
+        out_shape=jax.ShapeDtypeStruct((parts[0].shape[1], D), F32),
+        compiler_params=pltpu.CompilerParams(vmem_limit_bytes=60 * 2**20),
+    )(*parts, *weights)
+
+
+def input_back_kernel(*refs):
+    p_ref, p2_ref, w_ref, w2_ref, before_ref, x_ref, dm_ref, gain_ref, out_ref, dgain_ref = refs
+    d_normed = before_ref[...] + dot(p_ref[...], w_ref[...], 0, 0) + dot(p2_ref[...], w2_ref[...], 0, 0)
+    d_in, dgain = rms_back(x_ref[...].astype(F32), gain_ref[...], d_normed)
+    out_ref[...] = dm_ref[...] + d_in
+    dgain_ref[...] = dgain[None]
+
+
+def input_back(parts, weights, before, x, d_middle, gain):
+    vmem = pl.BlockSpec(memory_space=pltpu.VMEM)
+    return pl.pallas_call(
+        input_back_kernel,
+        cost_estimate=cost(5),
+        in_specs=[vmem] * 8,
+        out_specs=[vmem] * 2,
+        out_shape=[jax.ShapeDtypeStruct(x.shape, F32), jax.ShapeDtypeStruct((1, D), F32)],
+        compiler_params=pltpu.CompilerParams(vmem_limit_bytes=60 * 2**20),
+    )(*parts, *weights, before, x, d_middle, gain.reshape(1, D))
 
 
 def doc_masks(drow_ref, dcol_ref, allow_ref, same_ref):
@@ -553,7 +590,7 @@
     whole = lambda s: pl.BlockSpec(s, lambda g: (0, 0))
     return pl.pallas_call(
         attend_kernel,
-        cost_estimate=cost(2.7 * count),
+        cost_estimate=cost(0),
         grid=(count,),
         in_specs=[
             pl.BlockSpec(memory_space=pltpu.SMEM),
@@ -581,10 +618,9 @@
 
 
 def attend_back_kernel(
-    first, mix_ref, q_ref, k_ref, v_ref, tt_ref, drow_ref, dcol_ref, gain_ref,
-    prob_a_ref, prob_b_ref, att_a_ref, att_b_ref, dgrp_ref,
+    mix_ref, q_ref, k_ref, v_ref, tt_ref, drow_ref, dcol_ref, gain_ref, prob_ref, att_ref, dgrp_ref,
     d_ref, dgain_ref, dtap_ref, dmix_ref,
-    allow_ref, same_ref, pad_ref, y_ref, dm_ref, prob_ref, att_ref,
+    allow_ref, same_ref, pad_ref, y_ref, dm_ref,
 ):
     g = pl.program_id(0)
     n = q_ref.shape[1]
@@ -594,16 +630,6 @@
     def _():
         doc_masks(drow_ref, dcol_ref, allow_ref, same_ref)
         pad_ref[:, n : n + 8, :] = jnp.zeros((2, 8, n), F32)
-
-    @pl.when(g < first)
-    def _():
-        prob_ref[...] = prob_a_ref[...]
-        att_ref[...] = att_a_ref[...]
-
-    @pl.when(g >= first)
-    def _():
-        prob_ref[...] = prob_b_ref[...]
-        att_ref[...] = att_b_ref[...]
 
     for c in range(2):
         rows = slice(c * HD, (c + 1) * HD)
@@ -665,28 +691,22 @@
             dtap_ref[e, 8 * a : 8 * a + 8, :] = lined
 
 
-def attend_back(packed_t, docs, tt, mix, gain, probs, atts, dgrp):
+def attend_back(packed_t, docs, tt, mix, gain, prob, att, dgrp):
     n = packed_t.shape[1]
-    first = probs[0].shape[0] // 2
     blk = lambda off: pl.BlockSpec((PW, n), lambda g: (g + off, 0))
     whole = lambda s: pl.BlockSpec(s, lambda g: (0, 0))
     thin = pl.BlockSpec((PW, 1), lambda g: (g, 0))
-    low = lambda g: jnp.minimum(g, first - 1)
-    high = lambda g: jnp.maximum(g - first, 0)
-    return pl.pallas_call(
-        functools.partial(attend_back_kernel, first),
-        cost_estimate=cost(2.7 * PAIRS),
+    return pl.pallas_call(
+        attend_back_kernel,
+        cost_estimate=cost(24),
         grid=(PAIRS,),
         in_specs=[
             pl.BlockSpec(memory_space=pltpu.SMEM),
             blk(0), blk(PAIRS), blk(2 * PAIRS),
             pl.BlockSpec((2, CQ * n, n), lambda g: (g, 0, 0)),
             whole((1, n)), whole((n, 1)), thin,
-            pl.BlockSpec((2, n, n), lambda g: (low(g), 0, 0)),
-            pl.BlockSpec((2, n, n), lambda g: (high(g), 0, 0)),
-            pl.BlockSpec((PW, n), lambda g: (low(g), 0)),
-            pl.BlockSpec((PW, n), lambda g: (high(g), 0)),
-            blk(0),
+            pl.BlockSpec((2, n, n), lambda g: (g, 0, 0)),
+            blk(0), blk(0),
         ],
         out_specs=[
             pl.BlockSpec((3, PW, n), lambda g: (0, g, 0)), thin,
@@ -702,12 +722,11 @@
         scratch_shapes=[
             pltpu.VMEM((n, n), F32), pltpu.VMEM((n, n), F32), pltpu.VMEM((2, n + 8, n), F32),
             pltpu.VMEM((2, n, CQ * n), BF), pltpu.VMEM((2, n, n), F32),
-            pltpu.VMEM((2, n, n), F32), pltpu.VMEM((PW, n), F32),
         ],
         compiler_params=pltpu.CompilerParams(vmem_limit_bytes=60 * 2**20),
     )(
         mix.reshape(PAIRS, 4), packed_t, packed_t, packed_t, tt,
-        docs.reshape(1, n), docs.reshape(n, 1), gain, *probs, *atts, dgrp,
+        docs.reshape(1, n), docs.reshape(n, 1), gain, prob, att, dgrp,
     )
 
 
@@ -871,6 +890,10 @@
 
     attn_half = jnp.concatenate([net.own_half(qkv_weight.T), net.own_half(out_weight.T)], axis=0)
     w_attn = net.gather_line(attn_half).reshape(lines, -1, D)
+    ffn_half = jnp.concatenate(
+        [net.own_half(v) for v in (gate_weight.T, up_weight.T, down_weight)], axis=0
+    )
+    w_ffn = net.gather_line(ffn_half).reshape(lines, -1, D)
     x_side = net.sides(tokens)
     d_low = out_grad.astype(BF)
     d_side = net.sides(d_low)
@@ -879,62 +902,64 @@
         jnp.stack([norm_gain, group_gain, ffn_gain])[None], *x_side, *d_side, *taps
     )
     x_side, d_side, (taps_hi, taps_lo, taps_back) = sides[:2], sides[2:4], sides[4:]
-    rep = jnp.broadcast_to(net.rep, (8, 128))
-    x_near, rep = fence(net.near_blocks(tokens, *x_side, net.far_corner(*x_side)), rep)
+    x_near = net.near_blocks(tokens, *x_side, net.far_corner(*x_side))
     x_far = net.hop(x_near, 0, 1)
     d_near = net.near_blocks(d_low, *d_side, net.far_corner(*d_side))
     gains = net.gather_small(gains)
     w_attn = fence(w_attn, time=100)[0]
     x_far = fence(x_far, time=40)[0]
     d_near = fence(d_near, time=60)[0]
-    ffn_half = jnp.concatenate(
-        [net.own_half(v, rep[0, 0]) for v in (gate_weight.T, up_weight.T, down_weight)], axis=0
-    )
-    w_attn, d_near, x_far, gains, ffn_half = fence(w_attn, d_near, x_far, gains, ffn_half)
+    w_attn, d_near, x_far, gains = fence(w_attn, d_near, x_far, gains)
     gains = gains.transpose(1, 0, 2).reshape(3, D).astype(F32)
-    w_ffn = net.gather_line(ffn_half).reshape(lines, -1, D)
     w_cls = w_attn[:, cols:].reshape(-1, D)
     inputs = tokens.astype(F32)
 
     norm_near, parts = project(x_near, gains[0], w_attn, cols, n)
-    norm_near, x_far, *parts = fence(norm_near, x_far, *parts)
+    norm_near, x_far, d_far, *parts = fence(norm_near, x_far, net.hop(d_near, 0, 1), *parts)
     norm_far, more = project(x_far, gains[0], w_attn, cols, n)
     pieces = [net.hop_block(p, b) for b, p in enumerate((*parts, *more))]
-    d_far = net.hop(d_near, 0, 1)
     pieces = fence(*pieces, time=45)
-    *pieces, w_cls, d_far = fence(*pieces, w_cls, d_far)
+    w_qkv = w_attn[:, :cols].reshape(-1, D)
+    *pieces, w_cls, d_far, w_qkv = fence(*pieces, w_cls, d_far, w_qkv)
     w_side = (*net.sides(w_cls), net.hop(w_cls, 1, 2))
     packed_t = join(pieces, net.place, lines, cols)
     group_col = gains[1].reshape(D, 1)
-    heads = 5
-    front = functools.partial(attend, packed_t, doc_ids, taps_hi, taps_lo, head_mix, group_col)
-    *w_side, prob_a, att_a, grouped = fence(*w_side, *front(0, heads))
+    *w_side, probs, attended, grouped = fence(
+        *w_side,
+        *attend(packed_t, doc_ids, taps_hi, taps_lo, head_mix, group_col, 0, PAIRS),
+    )
     w_near = jnp.concatenate([w_cls, *w_side], axis=0)
-    w_far, prob_b, att_b, grouped = fence(
-        net.hop(w_near, 0, 1), *front(heads, PAIRS - heads, (grouped,))
-    )
-    middle, second = out_project(grouped, w_near, w_far, inputs, gains[2], net.place, lines, half_out)
+    out_near, w_far = fence(out_blocks(grouped, w_near), net.hop(w_near, 0, 1))
+    middle, second = out_project(
+        grouped, w_near, w_far, out_near, inputs, gains[2], net.place, lines, half_out
+    )
     w_near, w_far, second = fence(w_near, w_far, second)
     w_out = join([w_near, w_far], net.place, lines, half_out)
-    s_side = net.sides(second)
+    *s_side, w_out = fence(*net.sides(second), w_out)
     s_corner = net.far_corner(*s_side)
     s_a = jnp.concatenate([second, s_side[0]], axis=0)
     far_a = net.hop(s_a, 0, 1)
-    w_ffn = fence(w_ffn, time=100)[0]
+    w_ffn = fence(w_ffn, time=40)[0]
     run_a = ffn([(s_a, d_near, 0, 0, 2)], w_ffn, n, 7)
-    s_corner, far_a, w_out, *run_a = fence(s_corner, far_a, w_out, *run_a)
+    s_corner, far_a, w_qkv, *run_a = fence(s_corner, far_a, w_qkv, *run_a)
+    w_side = net.sides(w_qkv)
     s_b = jnp.concatenate([s_side[1], s_corner], axis=0)
     far_b = net.hop(s_b, 0, 1)
-    run_f = ffn([(far_a, d_far, 0, 0, 2), (far_b, d_far, 0, 2, 2)], w_ffn, n, 14)
-    ds_f, ds_g = net.hop(run_f[2], 0, 1), net.hop(run_f[4], 0, 1)
     run_b = ffn([(s_b, d_near, 0, 2, 2)], w_ffn, n, 7)
-    ds_f, ds_g, *run_b = fence(ds_f, ds_g, *run_b)
+    far_a, far_b, *run_b = fence(far_a, far_b, *run_b)
+    run_f = ffn([(far_a, d_far, 0, 0, 2), (far_b, d_far, 0, 2, 2)], w_ffn, n, 2)
+    ds_g, *w_side = fence(net.hop(run_f[4], 0, 1), *w_side)
+    size_q = lines * cols // 2
     corner = net.send_corner(run_b[2][n:], ds_g[n:])
+    ds_f, yo_f, yo_g = (net.hop(run_f[i], 0, 1) for i in (2, 3, 5))
     to_x, to_y = net.with_corner((run_a[2][n:], run_b[2][:n]), (ds_f[n:], ds_g[:n]), corner)
-    own = run_a[2][:n].astype(F32) + ds_f[:n].astype(F32)
-    to_x, to_y, *acts = fence(to_x, to_y, *[r[i] for i in range(2) for r in (run_a, run_f, run_b)])
-    yo_f, yo_g = net.hop(run_f[3], 0, 1), net.hop(run_f[5], 0, 1)
-    d_second = net.scatter_last(own, to_x, to_y)
+    last = (run_b[3][n:].astype(F32) + yo_g[n:].astype(F32)).astype(BF)
+    to_x, to_y, last, *rest = fence(
+        to_x, to_y, last, w_qkv, *w_side, w_side[1][:size_q], w_side[0][size_q:], *[r[i] for i in range(2) for r in (run_a, run_f, run_b)]
+    )
+    w_near, w_corner, acts = rest[:3], rest[3:5], rest[5:]
+    w_far = [net.hop(w, 0, 1) for w in w_near]
+    along_x, along_y = net.hop(to_x, 0, 2), net.hop(to_y, 1, 0)
     blocks = lambda a, f, b: [(a, 2 * n, 0), (f, 2 * n, 0), (f, 2 * n, 1), (b, 2 * n, 0)]
     g_ffn = ffn_grad(
         blocks(*acts[:3]),
@@ -943,67 +968,56 @@
         [(d_near, 2 * n, 0), (d_far, 2 * n, 0), (d_far, 2 * n, 1), (d_near, 2 * n, 1)],
         lines, wide,
     )
-    d_second, yo_f, yo_g, g_ffn = fence(d_second, yo_f, yo_g, g_ffn)
+    along_x, along_y, last, g_ffn, *w_far = fence(along_x, along_y, last, g_ffn, *w_far)
     g_ffn = fence(net.scatter_line(g_ffn.reshape(-1, D)), time=80)[0]
-
-    d_norm, g_ffn_gain = rms_back(middle, gains[2], d_second)
-    d_middle = out_grad + d_norm
-    branch = d_middle.astype(BF)
-    d_grouped = dot(w_out, branch, 0, 1)
-    corner = net.send_corner(run_b[3][n:], yo_g[n:])
+    corner = lax.ppermute(last, net.axes, net.corner)
+    d_middle, branch, d_grouped, g_ffn_gain = back_middle(
+        run_a[2], ds_f, along_x, along_y, middle, out_grad, gains[2], w_out
+    )
     to_x, to_y = net.with_corner((run_a[3][n:], run_b[3][:n]), (yo_f[n:], yo_g[:n]), corner)
     own = run_a[3][:n].astype(F32) + yo_f[:n].astype(F32)
-    to_x, to_y, d_grouped = fence(to_x, to_y, d_grouped)
+    to_x, to_y, d_grouped, *w_corner = fence(to_x, to_y, d_grouped, *w_corner)
+    w_corner = (net.hop(w_corner[0], 0, 2), net.hop(w_corner[1], 1, 0))
     along_x, along_y = net.hop(to_x, 0, 2), net.hop(to_y, 1, 0)
     d_packed, g_group, g_taps, g_mix = attend_back(
-        packed_t, doc_ids, taps_back, head_mix, group_col, (prob_a, prob_b), (att_a, att_b), d_grouped
-    )
-    along_x, along_y, d_packed = fence(along_x, along_y, d_packed)
+        packed_t, doc_ids, taps_back, head_mix, group_col, probs, attended, d_grouped
+    )
+    along_x, along_y, d_packed, *w_corner = fence(along_x, along_y, d_packed, *w_corner)
+    w_near.append(jnp.concatenate(w_corner, axis=0))
+    w_far.append(net.hop(w_near[3], 0, 1))
     layer_out = (middle + (own + along_x.astype(F32) + along_y.astype(F32))).astype(BF)
     pieces = cut(d_packed.reshape(3 * D, n), net.place, lines, cols)
-    *pieces, branch = fence(*pieces, branch)
-    pieces = [net.hop_block(p, b) for b, p in enumerate(pieces)]
+    *cuts, branch = fence(*pieces, branch)
+    pieces = [net.hop_block(p, b) for b, p in enumerate(cuts)]
     g_blocks = out_weight_grad(branch, grouped, net.place, lines, half_out)
     pieces = fence(*pieces, time=52)
-    *pieces, g_far, sums = fence(
-        *pieces, net.hop(g_blocks[4], 0, 1), fold_sums(g_group, g_taps, g_mix)
-    )
+    g_far, sums, w_near[3], w_far[3], *pieces = fence(
+        net.hop(g_blocks[4], 0, 1), fold_sums(g_group, g_taps, g_mix), w_near[3], w_far[3], *pieces, *cuts
+    )
+    pieces, cuts = pieces[:8], pieces[8:]
     size = lines * half_out
     g_far = [g_far[b * size : (b + 1) * size] for b in range(4)]
-    own, to_x, to_y = net.scatter_corner(g_blocks[:4], g_far)
-    g_qkv, g_ffn, *pieces = fence(qkv_grad(pieces, norm_near, norm_far, cols), g_ffn, *pieces)
+    out_own, to_x, to_y = net.scatter_corner(g_blocks[:4], g_far)
+    g_qkv, g_ffn, to_x, to_y, *cuts = fence(
+        qkv_grad(pieces, norm_near, norm_far, cols), g_ffn, to_x, to_y, *cuts
+    )
     g_qkv = fence(net.scatter_line(g_qkv), time=20)[0]
     g_other = net.hop(g_ffn, 1, 0)
-    near_c = back_project(pieces[3:4], x_near, 3, w_attn, cols, n, 1)
-    far = back_project(pieces[4:], x_far, 0, w_attn, cols, n, 8)
-    to_x, to_y, *rest = fence(to_x, to_y, *near_c, *far)
-    near_c, far = rest[:2], rest[2:]
-    dn_far = net.hop(far[0], 0, 1)
     along_x, along_y = net.hop(to_x, 0, 2), net.hop(to_y, 1, 0)
-    corner = (near_c[0].astype(F32) + dn_far[3 * n :].astype(F32)).astype(BF)
-    corner, *pieces = fence(corner, *pieces[:3])
-    corner = net.hop(corner, 0, 2)
-    *near, g_other, corner = fence(
-        *back_project(pieces, x_near, 0, w_attn, cols, n, 1), g_other, corner
-    )
-    small = jnp.concatenate([near_c[1][0] + near[1][0] + far[1][0], g_ffn_gain, sums])
-    small = net.sum_small(small, [bit for bit, _ in net.doubling if bit > 2])
-    to_x, to_y = (near[0][b * n : (b + 1) * n].astype(F32) + dn_far[b * n : (b + 1) * n].astype(F32) for b in (1, 2))
-    to_x, to_y = to_x.astype(BF), (to_y + corner.astype(F32)).astype(BF)
-    to_x, to_y, small, g_other, along_x, along_y = fence(to_x, to_y, small, g_other, along_x, along_y)
-    sent = fence(net.hop(to_x, 0, 2), net.hop(to_y, 1, 0), time=30)
-    g_out = net.scatter_line_small(own + along_x.astype(F32) + along_y.astype(F32)).astype(BF)
-    *sent, small, g_out, g_qkv = fence(*sent, small, g_out, g_qkv)
-    small = net.sum_small(small, [1, 2])
+    d_normed = normed_back([*cuts[:3], *cuts[4:7]], [*w_near[:3], *w_far[:3]])
+    input_grad, g_norm = input_back([cuts[3], cuts[7]], [w_near[3], w_far[3]], d_normed, tokens, d_middle, gains[0])
+    small = jnp.concatenate([g_norm[0], g_ffn_gain[0], sums])
+    small = net.sum_small(small, [bit for bit, _ in net.doubling])
+    along_x, along_y, g_other = fence(along_x, along_y, g_other, time=20)
+    along_x, along_y, g_other, small, g_qkv = fence(along_x, along_y, g_other, small, g_qkv)
+    q_other = net.hop(g_qkv, 1, 0)
     small = small + net.hop(small, 1, 0)
-    d_normed = near[0][:n].astype(F32) + dn_far[:n].astype(F32) + sent[0].astype(F32) + sent[1].astype(F32)
+    g_out = net.scatter_line_small(out_own + along_x.astype(F32) + along_y.astype(F32)).astype(BF)
     g_out = net.both_halves(g_out).T
     shape = (3, wide, D)
     g_ffn = net.both_halves(g_ffn.reshape(shape), 1, g_other.reshape(shape))
     g_gate, g_up, g_down = g_ffn[0].T, g_ffn[1].T, g_ffn[2]
-    g_qkv = net.both_halves(g_qkv).T
-    d_in = rms_back(inputs, gains[0], d_normed)[0]
-    input_grad = d_middle + d_in
+    g_qkv = net.both_halves(g_qkv, 0, q_other).T
 
     part = D // shards
     gain_grads = [

time: 495 us -> 483 us (0.976)
  other arithmetic: 65.5 us -> 52.7 us
  Pallas kernels: 188 us -> 194 us
  matrix products: 5.25 us -> 0 us
    ppermute x4, waiting for transfers between devices: 1.72 us -> 8.98 us  [sum_small(): value = value + lax.ppermute(value, self.axes, perm)]
    add x3 -> x0, other arithmetic: 7.1 us -> none  [the longest x1 3.5 us: on_device(): input_grad = d_middle + d_in]
    ppermute x2 -> x1, waiting for transfers between devices: 13.1 us -> 6.13 us  [send_corner(): lax.ppermute((near.astype(F32) + far.astype(F32)).astype(BF), self.axes,...]
    convert_element_type x4 -> x2, other arithmetic: 8.82 us -> 2.44 us  [the longest x1 2.36 us: on_device(): last = (run_b[3][n:].astype(F32) + yo_g[n:].astype(F32)).astype(BF)]
    pallas_call x8, Pallas kernels: 83.1 us -> 89.5 us  [the longest x1 23.6 us: attend(): pl.pallas_call(attend_kernel, cost_estimate=cost(0), grid=(count,), in_sp...]
    dot_general x1 -> x0, matrix products: 5.25 us -> none  [dot(): lax.dot_general(a, b, (((ca,), (cb,)), ((), ())), preferred_element_type=...]
    ppermute x50 -> x54, starting transfers between devices: 41.7 us -> 46.1 us  [hop(): return lax.ppermute(value, self.axes, self.hops[dy, di])]
    ppermute x50 -> x54, waiting for transfers between devices: 77.7 us -> 80.4 us  [hop(): return lax.ppermute(value, self.axes, self.hops[dy, di])]
  transfers between devices with their start and end apart: 68 -> 72, of which waited for: 26 -> 31; matrix products, arithmetic and copies ran while one was open for 21% -> 17% of each run, Pallas kernels for 32% -> 41%
where the time goes in v4:
time: 483 us; the launch traced here: 475 us
  Pallas kernels  194 us (40%)
  waiting for transfers between devices  103 us (21%)
  starting transfers between devices  62.1 us (13%)
  other arithmetic  52.7 us (11%)
  local copies, waits for them, and re-layouts  48.9 us (10%)
  between operations  15 us (3%)
    ppermute x54, waiting for transfers between devices, hop(): return lax.ppermute(value, self.axes, self.hops[dy, di])  80.4 us
    ppermute x54, starting transfers between devices, hop(): return lax.ppermute(value, self.axes, self.hops[dy, di])  46.1 us
    pallas_call x3, Pallas kernels, ffn(): pl.pallas_call(functools.partial(ffn_kernel, counts), cost_estimate=cost(...  38.4 us
    unnamed x129, local copies, waits for them, and re-layouts  25.4 us
    pallas_call x1, Pallas kernels, attend(): pl.pallas_call(attend_kernel, cost_estimate=cost(0), grid=(count,), in_sp...  23.6 us
    pallas_call x1, Pallas kernels, attend_back(): pl.pallas_call(attend_back_kernel, cost_estimate=cost(24), grid=(PAIRS,),...  22.3 us
    pallas_call x1, Pallas kernels, ffn_grad(): pl.pallas_call(functools.partial(ffn_grad_kernel, len(hidden)), cost_esti...  17.7 us
    pallas_call x1, Pallas kernels, band_taps(): pl.pallas_call(taps_kernel, cost_estimate=cost(16), grid=(H,), in_specs=[...  16 us
  transfers between devices with their start and end apart: 72, of which 31 were waited for; matrix products, arithmetic and copies ran while one was open for 17% of the time, Pallas kernels for 41%

profile of v4, /device:TPU:0, one launch (start us, length us, event | category | flops | bytes accessed | tf_op | source)
XLA Modules:
  0.0 475.3 jit_solution(9113276041862511815)
XLA Ops:
  19.2 16.0 %shard_map.220 = (bf16[16,1536,256]{2,1,0:T(8,128)(2,1)}, bf16[16,1536,256]{2,1,0:T(8,128)(2,1)}, bf16[16,1536,256]{2,1,0:T(8,128)(2,1)}) custom-call(f32[16,8,256]{2,1,0:T(8,128)} %pad.7.fwd_ref, f32[16,8,256]{2,1,0:T(8,128)} %pad.8.bwd_ref), custom_call_target="tpu_custom_call" | custom-call | flops 8000000000 | tf_op jit(solution)/shard_map/pallas_call | solution.py:63
  35.3 9.6 %collective-permute-done.2.refs_3_ = bf16[256,1536]{1,0:T(8,128)(2,1)S(1)} collective-permute-done((bf16[256,1536]{1,0:T(8,128)(2,1)}, bf16[256,1536]{1,0:T(8,128)(2,1)S(1)}, u32[]{:S(2)}, u32[]{:S(2)}) %collective-permute-start.2) | collective-permute-done | bytes 786464 | tf_op jit(solution)/shard_map/ppermute | solution.py:785
  58.9 8.4 %maximum_maximum_fusion.1 = (bf16[1024,1536]{1,0:T(8,128)(2,1)}, bf16[1024,1536]{1,0:T(8,128)(2,1)}) fusion(bf16[256,1536]{1,0:T(8,128)(2,1)} %get-tuple-element.229, bf16[256,1536]{1,0:T(8,128)(2,1)S(1)} %copy-done.19, bf16[256,1536]{1,0:T(8,128)(2,1)} %convert_element_type.163, bf16[1024]{0:T(1024)(128)(2,1)S(1)} %pad.38.clone, ...), kind=kLoop, calls=%fused_computation.2 | loop fusion | flops 23592960 | bytes 11012096 | tf_op jit(solution)/shard_map/concatenate | solution.py:814
  78.1 7.4 %shard_map.226 = (bf16[1024,1536]{1,0:T(8,128)(2,1)}, bf16[576,256]{1,0:T(8,128)(2,1)}, bf16[576,256]{1,0:T(8,128)(2,1)}, bf16[576,256]{1,0:T(8,128)(2,1)}, bf16[576,256]{1,0:T(8,128)(2,1)}) custom-call(bf16[1024,1536]{1,0:T(8,128)(2,1)} %constant_dynamic-update-slice_fusion.11.x_ref, f32[1,1536]{1,0:T(1,128)} %slice.138.gain_ref.refs_7_, ...), custom_call_target="tpu_custom_call" | custom-call | tf_op jit(solution)/shard_map/pallas_call | solution.py:109
  91.8 7.4 %shard_map.228 = (bf16[1024,1536]{1,0:T(8,128)(2,1)}, bf16[576,256]{1,0:T(8,128)(2,1)}, bf16[576,256]{1,0:T(8,128)(2,1)}, bf16[576,256]{1,0:T(8,128)(2,1)}, bf16[576,256]{1,0:T(8,128)(2,1)}) custom-call(bf16[1024,1536]{1,0:T(8,128)(2,1)} %get-tuple-element.244.x_ref, f32[1,1536]{1,0:T(1,128)} %slice.138.gain_ref.refs_7_, ...), custom_call_target="tpu_custom_call" | custom-call | tf_op jit(solution)/shard_map/pallas_call | solution.py:109
  109.1 6.1 %collective-permute-done.17.refs_6_ = bf16[576,256]{1,0:T(8,128)(2,1)} collective-permute-done((bf16[576,256]{1,0:T(8,128)(2,1)}, bf16[576,256]{1,0:T(8,128)(2,1)}, u32[]{:S(2)}, u32[]{:S(2)}) %collective-permute-start.17) | collective-permute-done | bytes 294944 | tf_op jit(solution)/shard_map/ppermute | solution.py:785
  122.8 3.4 shard_map.231
  126.2 23.6 %shard_map.232 = (f32[16,256,256]{2,1,0:T(8,128)}, f32[1536,256]{1,0:T(8,128)}, bf16[1536,256]{1,0:T(8,128)(2,1)}) custom-call(f32[8,4]{1,0:T(8,128)} %copy.205.mix_ref, bf16[4608,256]{1,0:T(8,128)(2,1)} %bitcast.45, bf16[4608,256]{1,0:T(8,128)(2,1)} %bitcast.46, bf16[4608,256]{1,0:T(8,128)(2,1)} %bitcast.47, ...), custom_call_target="tpu_custom_call" | custom-call | tf_op jit(solution)/shard_map/pallas_call | solution.py:591
  157.7 3.6 shard_map.234.refs_0_
  162.8 5.3 %shard_map.236 = (f32[256,1536]{1,0:T(8,128)}, bf16[256,1536]{1,0:T(8,128)(2,1)}) custom-call(s32[1]{0:T(128)} %bitcast.place_ref, bf16[1536,256]{1,0:T(8,128)(2,1)} %get-tuple-element.272.grp_ref.grouped_ref, bf16[768,1536]{1,0:T(8,128)(2,1)} %get-tuple-element.276.far_ref.refs_1_, f32[768,256]{1,0:T(8,128)} %get-tuple-element.277.near_ref, ...), custom_call_target="tpu_custom_call" | custom-call | tf_op jit(solution)/shard_map/pallas_call | solution.py:207
  170.4 4.9 %shard_map.238 = bf16[4,4,2,48,1536]{4,3,2,1,0:T(8,128)(2,1)} custom-call(s32[1]{0:T(128)} %bitcast.place_ref, bf16[768,1536]{1,0:T(8,128)(2,1)} %get-tuple-element.281.refs_0_, bf16[768,1536]{1,0:T(8,128)(2,1)} %get-tuple-element.282.refs_1_), custom_call_target="tpu_custom_call" | custom-call | flops 1000000000 | tf_op jit(solution)/shard_map/pallas_call | solution.py:161
  176.5 11.8 %collective-permute-done.23.refs_0_ = bf16[256,1536]{1,0:T(8,128)(2,1)S(1)} collective-permute-done((bf16[256,1536]{1,0:T(8,128)(2,1)}, bf16[256,1536]{1,0:T(8,128)(2,1)S(1)}, u32[]{:S(2)}, u32[]{:S(2)}) %collective-permute-start.23) | collective-permute-done | bytes 786464 | tf_op jit(solution)/shard_map/ppermute | solution.py:785
  195.1 10.2 %shard_map.241 = (bf16[512,512]{1,0:T(8,128)(2,1)}, bf16[512,1024]{1,0:T(8,128)(2,1)}, bf16[512,1536]{1,0:T(8,128)(2,1)}, bf16[512,1536]{1,0:T(8,128)(2,1)}) custom-call(bf16[512,1536]{1,0:T(8,128)(2,1)} %copy-done.26, bf16[1024,1536]{1,0:T(8,128)(2,1)} %get-tuple-element.235.refs_1_.refs_12_.refs_15_, bf16[4,384,1536]{2,1,0:T(8,128)(2,1)} %shard_map.240.refs_2_.refs_4_), custom_call_target="tpu_custom_call" | custom-call | flops 3500000000 | tf_op jit(solution)/shard_map/pallas_call | solution.py:394
  211.5 10.3 %shard_map.243 = (bf16[512,512]{1,0:T(8,128)(2,1)}, bf16[512,1024]{1,0:T(8,128)(2,1)}, bf16[512,1536]{1,0:T(8,128)(2,1)}, bf16[512,1536]{1,0:T(8,128)(2,1)}) custom-call(bf16[512,1536]{1,0:T(8,128)(2,1)} %constant_dynamic-update-slice_fusion.6.refs_0_.refs_11_, bf16[1024,1536]{1,0:T(8,128)(2,1)} %get-tuple-element.235.refs_1_.refs_12_.refs_15_, ...), custom_call_target="tpu_custom_call" | custom-call | flops 3500000000 | tf_op jit(solution)/shard_map/pallas_call | solution.py:394
  221.8 18.0 %shard_map.245 = (bf16[1024,512]{1,0:T(8,128)(2,1)}, bf16[1024,1024]{1,0:T(8,128)(2,1)}, bf16[512,1536]{1,0:T(8,128)(2,1)}, bf16[512,1536]{1,0:T(8,128)(2,1)}, b...) custom-call(bf16[512,1536]{1,0:T(8,128)(2,1)} %get-tuple-element.297.refs_0_.refs_9_, ...), custom_call_target="tpu_custom_call" | custom-call | flops 1000000000 | tf_op jit(solution)/shard_map/pallas_call | solution.py:394
  240.4 9.4 %collective-permute-done.31.refs_1_ = bf16[576,1536]{1,0:T(8,128)(2,1)S(1)} collective-permute-done((bf16[576,1536]{1,0:T(8,128)(2,1)}, bf16[576,1536]{1,0:T(8,128)(2,1)S(1)}, u32[]{:S(2)}, u32[]{:S(2)}) %collective-permute-start.31) | collective-permute-done | bytes 1769504 | tf_op jit(solution)/shard_map/ppermute | solution.py:785
  259.8 6.1 %collective-permute-done.33 = bf16[256,1536]{1,0:T(8,128)(2,1)S(1)} collective-permute-done((bf16[256,1536]{1,0:T(8,128)(2,1)S(1)}, bf16[256,1536]{1,0:T(8,128)(2,1)S(1)}, u32[]{:S(2)}, u32[]{:S(2)}) %collective-permute-start.33) | collective-permute-done | bytes 786464 | tf_op jit(solution)/shard_map/ppermute | solution.py:825
  266.0 3.2 fusion.3
  272.0 17.7 %shard_map.248.refs_3_ = bf16[4,384,1536]{2,1,0:T(8,128)(2,1)} custom-call(bf16[512,512]{1,0:T(8,128)(2,1)} %get-tuple-element.320.refs_0_, bf16[1024,512]{1,0:T(8,128)(2,1)} %get-tuple-element.321.refs_1_.refs_2_, bf16[1024,512]{1,0:T(8,128)(2,1)} %get-tuple-element.321.refs_1_.refs_2_, bf16[512,512]{1,0:T(8,128)(2,1)} %get-tuple-element.322.refs_3_, ...), custom_call_target="tpu_custom_call" | custom-call | flops 7000000000 | tf_op jit(solution)/shard_map/pallas_call | solution.py:449
  295.0 8.8 %shard_map.250 = (f32[256,1536]{1,0:T(8,128)}, bf16[256,1536]{1,0:T(8,128)(2,1)}, f32[1536,256]{1,0:T(8,128)}, f32[1,1536]{1,0:T(1,128)}) custom-call(bf16[512,1536]{1,0:T(8,128)(2,1)} %get-tuple-element.301.a_ref, bf16[512,1536]{1,0:T(8,128)(2,1)} %collective-permute-done.29.f_ref, bf16[256,1536]{1,0:T(8,128)(2,1)} %get-tuple-element.330.sx_ref, ...), custom_call_target="tpu_custom_call" | custom-call | flops 3000000000 | tf_op jit(solution)/shard_map/pallas_call | solution.py:239
  305.5 3.5 fusion.7
  313.0 22.3 %shard_map.252 = (bf16[3,1536,256]{2,1,0:T(8,128)(2,1)}, f32[1536,1]{1,0:T(8,128)}, f32[16,48,128]{2,1,0:T(8,128)}, f32[8,8,256]{2,1,0:T(8,128)}) custom-call(f32[8,4]{1,0:T(8,128)} %copy.205.mix_ref, bf16[4608,256]{1,0:T(8,128)(2,1)} %bitcast.48, bf16[4608,256]{1,0:T(8,128)(2,1)} %bitcast.49, bf16[4608,256]{1,0:T(8,128)(2,1)} %bitcast.50, ...), custom_call_target="tpu_custom_call" | custom-call | flops 12000000000 | tf_op jit(solution)/shard_map/pallas_call | solution.py:699
  335.3 11.0 %collective-permute-done.43.refs_3_ = bf16[288,1536]{1,0:T(8,128)(2,1)S(1)} collective-permute-done((bf16[288,1536]{1,0:T(8,128)(2,1)}, bf16[288,1536]{1,0:T(8,128)(2,1)S(1)}, u32[]{:S(2)}, u32[]{:S(2)}) %collective-permute-start.43) | collective-permute-done | bytes 884768 | tf_op jit(solution)/shard_map/ppermute | solution.py:785
  347.4 3.4 shard_map.254
  363.8 5.6 %shard_map.256 = (bf16[192,1536]{1,0:T(8,128)(2,1)}, bf16[192,1536]{1,0:T(8,128)(2,1)}, bf16[192,1536]{1,0:T(8,128)(2,1)}, bf16[192,1536]{1,0:T(8,128)(2,1)}, bf16[768,1536]{1,0:T(8,128)(2,1)}) custom-call(s32[1]{0:T(128)} %bitcast.place_ref, bf16[256,1536]{1,0:T(8,128)(2,1)} %get-tuple-element.357.branch_ref, ...), custom_call_target="tpu_custom_call" | custom-call | tf_op jit(solution)/shard_map/pallas_call | solution.py:277
  373.6 4.4 collective-permute-done.52.refs_6_
  384.3 9.3 %shard_map.259.refs_0_ = bf16[576,1536]{1,0:T(8,128)(2,1)} custom-call(bf16[576,256]{1,0:T(8,128)(2,1)} %get-tuple-element.380.refs_0_, bf16[576,256]{1,0:T(8,128)(2,1)} %get-tuple-element.381.refs_1_, bf16[576,256]{1,0:T(8,128)(2,1)} %get-tuple-element.382.refs_2_, bf16[576,256]{1,0:T(8,128)(2,1)} %get-tuple-element.383.refs_3_, ...), custom_call_target="tpu_custom_call" | custom-call | flops 3000000000 | tf_op jit(solution)/shard_map/pallas_call | solution.py:487
  398.5 9.9 %shard_map.262.refs_4_ = f32[256,1536]{1,0:T(8,128)} custom-call(bf16[576,256]{1,0:T(8,128)(2,1)} %get-tuple-element.407.refs_0_, bf16[576,256]{1,0:T(8,128)(2,1)} %get-tuple-element.408.refs_1_, bf16[576,256]{1,0:T(8,128)(2,1)} %get-tuple-element.409.refs_2_, bf16[576,256]{1,0:T(8,128)(2,1)} %get-tuple-element.410.refs_3_, ...), custom_call_target="tpu_custom_call" | custom-call | flops 500000000 | tf_op jit(solution)/shard_map/pallas_call | solution.py:506
  408.4 6.4 %shard_map.263 = (f32[256,1536]{1,0:T(8,128)}, f32[1,1536]{1,0:T(1,128)}) custom-call(bf16[576,256]{1,0:T(8,128)(2,1)} %get-tuple-element.403.refs_0_, bf16[576,256]{1,0:T(8,128)(2,1)} %get-tuple-element.404.refs_1_, bf16[576,1536]{1,0:T(8,128)(2,1)} %get-tuple-element.405.refs_2_, bf16[576,1536]{1,0:T(8,128)(2,1)} %get-tuple-element.406.refs_3_, ...), custom_call_target="tpu_custom_call" | custom-call | flops 2500000000 | tf_op jit(solution)/shard_map/pallas_call | solution.py:526
  426.4 3.0 add_convert_fusion
  432.8 3.6 collective-permute-done.55.refs_0_
  451.0 6.5 %collective-permute-done.65 = bf16[48,1536]{1,0:T(8,128)(2,1)S(1)} collective-permute-done((bf16[48,1536]{1,0:T(8,128)(2,1)S(1)}, bf16[48,1536]{1,0:T(8,128)(2,1)S(1)}, u32[]{:S(2)}, u32[]{:S(2)}) %collective-permute-start.65) | collective-permute-done | bytes 147488 | tf_op jit(solution)/shard_map/ppermute | solution.py:785
  (380 shorter events, 180.1 us)
Async XLA Ops:
  7.2 65.1 %all-gather.3.cloned.1.call-start = ((), (), s32[]{:S(2)}) async-start(), calls=%async_computation.2 | async-start | bytes 2949120 | tf_op jit(solution)/shard_map/all_gather | solution.py:791
  7.2 28.0 %collective-permute-start = (bf16[256,1536]{1,0:T(8,128)(2,1)}, bf16[256,1536]{1,0:T(8,128)(2,1)S(1)}, u32[]{:S(2)}, u32[]{:S(2)}) collective-permute-start(bf16[256,1536]{1,0:T(8,128)(2,1)} %refs_5_.1), channel_id=1, source_target_pairs={{0,2},{1,3},{2,0},{3,1},{4,6},{5,7},{6,4},{7,5},{8,10},{9,11},{10,... | collective-permute-start | bytes 2359304 | tf_op jit(solution)/shard_map/ppermute | solution.py:785
  10.2 25.0 %collective-permute-start.1 = (bf16[256,1536]{1,0:T(8,128)(2,1)}, bf16[256,1536]{1,0:T(8,128)(2,1)S(1)}, u32[]{:S(2)}, u32[]{:S(2)}) collective-permute-start(bf16[256,1536]{1,0:T(8,128)(2,1)} %refs_5_.1), channel_id=1, source_target_pairs={{0,16},{1,17},{2,18},{3,19},{4,20},{5,21},{6,22},{7,23},{8,24},{9,... | collective-permute-start | bytes 2359304 | tf_op jit(solution)/shard_map/ppermute | solution.py:785
  14.1 30.7 %collective-permute-start.2 = (bf16[256,1536]{1,0:T(8,128)(2,1)}, bf16[256,1536]{1,0:T(8,128)(2,1)S(1)}, u32[]{:S(2)}, u32[]{:S(2)}) collective-permute-start(bf16[256,1536]{1,0:T(8,128)(2,1)} %convert_element_type.163), channel_id=1, source_target_pairs={{0,2},{1,3},{2,0},{3,1},{4,6},{5,7},{6,4},{7,5},{8,10},{9,11},{10,... | collective-permute-start | bytes 2359304 | tf_op jit(solution)/shard_map/ppermute | solution.py:785
  14.7 31.7 %collective-permute-start.3 = (bf16[256,1536]{1,0:T(8,128)(2,1)}, bf16[256,1536]{1,0:T(8,128)(2,1)}, u32[]{:S(2)}, u32[]{:S(2)}) collective-permute-start(bf16[256,1536]{1,0:T(8,128)(2,1)} %convert_element_type.163), channel_id=1, source_target_pairs={{0,16},{1,17},{2,18},{3,19},{4,20},{5,21},{6,22},{7,23},{8,24},{9,... | collective-permute-start | bytes 2359304 | tf_op jit(solution)/shard_map/ppermute | solution.py:785
  16.6 178.5 %all-gather.5.cloned.1.call-start = ((), (), s32[]{:S(2)}) async-start(), calls=%async_computation.3 | async-start | bytes 5898240 | tf_op jit(solution)/shard_map/all_gather | solution.py:791
  50.8 17.1 %collective-permute-start.4 = (bf16[256,1536]{1,0:T(8,128)(2,1)S(1)}, bf16[256,1536]{1,0:T(8,128)(2,1)S(1)}, u32[]{:S(2)}, u32[]{:S(2)}) collective-permute-start(bf16[256,1536]{1,0:T(8,128)(2,1)S(1)} %broadcast_select_fusion.4), channel_id=1, source_target_pairs={{0,16},{1,3},{2,18},{3,1},{4,20},{5,7},{6,22},{7,5},{8,24},{9,11},... | collective-permute-start | bytes 2359304 | tf_op jit(solution)/shard_map/ppermute | solution.py:811
  54.2 17.1 %collective-permute-start.5 = (bf16[256,1536]{1,0:T(8,128)(2,1)S(1)}, bf16[256,1536]{1,0:T(8,128)(2,1)S(1)}, u32[]{:S(2)}, u32[]{:S(2)}) collective-permute-start(bf16[256,1536]{1,0:T(8,128)(2,1)S(1)} %broadcast_select_fusion.3), channel_id=1, source_target_pairs={{0,16},{1,3},{2,18},{3,1},{4,20},{5,7},{6,22},{7,5},{8,24},{9,11},... | collective-permute-start | bytes 2359304 | tf_op jit(solution)/shard_map/ppermute | solution.py:811
  104.3 292.1 %reduce-scatter.3.cloned.1.call-start = ((), (), s32[]{:S(2)}) async-start(), calls=%async_computation.4 | async-start | bytes 5898240 | tf_op jit(solution)/shard_map/reduce_scatter | solution.py:794
  116.2 34.4 %collective-permute-start.19 = (bf16[192,1536]{1,0:T(8,128)(2,1)}, bf16[192,1536]{1,0:T(8,128)(2,1)S(1)}, u32[]{:S(2)}, u32[]{:S(2)}) collective-permute-start(bf16[192,1536]{1,0:T(8,128)(2,1)} %get-tuple-element.258), channel_id=1, source_target_pairs={{0,2},{1,3},{2,0},{3,1},{4,6},{5,7},{6,4},{7,5},{8,10},{9,11},{10,... | collective-permute-start | bytes 1769480 | tf_op jit(solution)/shard_map/ppermute | solution.py:785
  117.2 33.5 %collective-permute-start.20 = (bf16[192,1536]{1,0:T(8,128)(2,1)}, bf16[192,1536]{1,0:T(8,128)(2,1)S(1)}, u32[]{:S(2)}, u32[]{:S(2)}) collective-permute-start(bf16[192,1536]{1,0:T(8,128)(2,1)} %get-tuple-element.258), channel_id=1, source_target_pairs={{0,16},{1,17},{2,18},{3,19},{4,20},{5,21},{6,22},{7,23},{8,24},{9,... | collective-permute-start | bytes 1769480 | tf_op jit(solution)/shard_map/ppermute | solution.py:785
  118.6 32.1 %collective-permute-start.21 = (bf16[192,1536]{1,0:T(8,128)(2,1)}, bf16[192,1536]{1,0:T(8,128)(2,1)S(1)}, u32[]{:S(2)}, u32[]{:S(2)}) collective-permute-start(bf16[192,1536]{1,0:T(8,128)(2,1)} %get-tuple-element.258), channel_id=1, source_target_pairs={{0,18},{1,19},{2,16},{3,17},{4,22},{5,23},{6,20},{7,21},{8,26},{9,... | collective-permute-start | bytes 1769480 | tf_op jit(solution)/shard_map/ppermute | solution.py:785
  168.1 20.2 %collective-permute-start.23 = (bf16[256,1536]{1,0:T(8,128)(2,1)}, bf16[256,1536]{1,0:T(8,128)(2,1)S(1)}, u32[]{:S(2)}, u32[]{:S(2)}) collective-permute-start(bf16[256,1536]{1,0:T(8,128)(2,1)} %get-tuple-element.280), channel_id=1, source_target_pairs={{0,2},{1,3},{2,0},{3,1},{4,6},{5,7},{6,4},{7,5},{8,10},{9,11},{10,... | collective-permute-start | bytes 2359304 | tf_op jit(solution)/shard_map/ppermute | solution.py:785
  169.0 19.9 %collective-permute-start.24 = (bf16[256,1536]{1,0:T(8,128)(2,1)}, bf16[256,1536]{1,0:T(8,128)(2,1)S(1)}, u32[]{:S(2)}, u32[]{:S(2)}) collective-permute-start(bf16[256,1536]{1,0:T(8,128)(2,1)} %get-tuple-element.280), channel_id=1, source_target_pairs={{0,16},{1,17},{2,18},{3,19},{4,20},{5,21},{6,22},{7,23},{8,24},{9,... | collective-permute-start | bytes 2359304 | tf_op jit(solution)/shard_map/ppermute | solution.py:785
  208.6 41.2 %collective-permute-start.31 = (bf16[576,1536]{1,0:T(8,128)(2,1)}, bf16[576,1536]{1,0:T(8,128)(2,1)S(1)}, u32[]{:S(2)}, u32[]{:S(2)}) collective-permute-start(bf16[576,1536]{1,0:T(8,128)(2,1)} %get-tuple-element.305.refs_3_), channel_id=1, source_target_pairs={{0,2},{1,3},{2,0},{3,1},{4,6},{5,7},{6,4},{7,5},{8,10},{9,11},{10,... | collective-permute-start | bytes 5308424 | tf_op jit(solution)/shard_map/ppermute | solution.py:785
  210.1 41.0 %collective-permute-start.32 = (bf16[576,1536]{1,0:T(8,128)(2,1)}, bf16[576,1536]{1,0:T(8,128)(2,1)S(1)}, u32[]{:S(2)}, u32[]{:S(2)}) collective-permute-start(bf16[576,1536]{1,0:T(8,128)(2,1)} %get-tuple-element.305.refs_3_), channel_id=1, source_target_pairs={{0,16},{1,17},{2,18},{3,19},{4,20},{5,21},{6,22},{7,23},{8,24},{9,... | collective-permute-start | bytes 5308424 | tf_op jit(solution)/shard_map/ppermute | solution.py:785
  239.8 17.7 %collective-permute-start.34 = (bf16[512,1536]{1,0:T(8,128)(2,1)}, bf16[512,1536]{1,0:T(8,128)(2,1)}, u32[]{:S(2)}, u32[]{:S(2)}) collective-permute-start(bf16[512,1536]{1,0:T(8,128)(2,1)} %get-tuple-element.308), channel_id=1, source_target_pairs={{0,1},{1,0},{2,3},{3,2},{4,5},{5,4},{6,7},{7,6},{8,9},{9,8},{10,11... | collective-permute-start | bytes 4718600 | tf_op jit(solution)/shard_map/ppermute | solution.py:785
  240.3 19.6 %collective-permute-start.29 = (bf16[512,1536]{1,0:T(8,128)(2,1)}, bf16[512,1536]{1,0:T(8,128)(2,1)}, u32[]{:S(2)}, u32[]{:S(2)}) collective-permute-start(bf16[512,1536]{1,0:T(8,128)(2,1)} %get-tuple-element.302), channel_id=1, source_target_pairs={{0,1},{1,0},{2,3},{3,2},{4,5},{5,4},{6,7},{7,6},{8,9},{9,8},{10,11... | collective-permute-start | bytes 4718600 | tf_op jit(solution)/shard_map/ppermute | solution.py:785
  269.2 21.3 %collective-permute-start.37 = (bf16[576,1536]{1,0:T(8,128)(2,1)}, bf16[576,1536]{1,0:T(8,128)(2,1)S(1)}, u32[]{:S(2)}, u32[]{:S(2)}) collective-permute-start(bf16[576,1536]{1,0:T(8,128)(2,1)} %get-tuple-element.326.refs_6_), channel_id=1, source_target_pairs={{0,1},{1,0},{2,3},{3,2},{4,5},{5,4},{6,7},{7,6},{8,9},{9,8},{10,11... | collective-permute-start | bytes 5308424 | tf_op jit(solution)/shard_map/ppermute | solution.py:785
  269.2 21.3 %collective-permute-start.38 = (bf16[576,1536]{1,0:T(8,128)(2,1)}, bf16[576,1536]{1,0:T(8,128)(2,1)S(1)}, u32[]{:S(2)}, u32[]{:S(2)}) collective-permute-start(bf16[576,1536]{1,0:T(8,128)(2,1)} %get-tuple-element.327.refs_7_), channel_id=1, source_target_pairs={{0,1},{1,0},{2,3},{3,2},{4,5},{5,4},{6,7},{7,6},{8,9},{9,8},{10,11... | collective-permute-start | bytes 5308424 | tf_op jit(solution)/shard_map/ppermute | solution.py:785
  269.7 20.8 %collective-permute-start.39 = (bf16[576,1536]{1,0:T(8,128)(2,1)}, bf16[576,1536]{1,0:T(8,128)(2,1)}, u32[]{:S(2)}, u32[]{:S(2)}) collective-permute-start(bf16[576,1536]{1,0:T(8,128)(2,1)} %get-tuple-element.328.refs_8_), channel_id=1, source_target_pairs={{0,1},{1,0},{2,3},{3,2},{4,5},{5,4},{6,7},{7,6},{8,9},{9,8},{10,11... | collective-permute-start | bytes 5308424 | tf_op jit(solution)/shard_map/ppermute | solution.py:785
  269.7 20.3 %collective-permute-start.35 = (bf16[256,1536]{1,0:T(8,128)(2,1)}, bf16[256,1536]{1,0:T(8,128)(2,1)}, u32[]{:S(2)}, u32[]{:S(2)}) collective-permute-start(bf16[256,1536]{1,0:T(8,128)(2,1)} %get-tuple-element.317), channel_id=1, source_target_pairs={{0,2},{1,3},{2,0},{3,1},{4,6},{5,7},{6,4},{7,5},{8,10},{9,11},{10,... | collective-permute-start | bytes 2359304 | tf_op jit(solution)/shard_map/ppermute | solution.py:785
  270.5 20.0 %collective-permute-start.36 = (bf16[256,1536]{1,0:T(8,128)(2,1)}, bf16[256,1536]{1,0:T(8,128)(2,1)}, u32[]{:S(2)}, u32[]{:S(2)}) collective-permute-start(bf16[256,1536]{1,0:T(8,128)(2,1)} %get-tuple-element.318), channel_id=1, source_target_pairs={{0,16},{1,17},{2,18},{3,19},{4,20},{5,21},{6,22},{7,23},{8,24},{9,... | collective-permute-start | bytes 2359304 | tf_op jit(solution)/shard_map/ppermute | solution.py:785
  292.4 146.1 %reduce-scatter.5.cloned.1.call-start = ((), (), s32[]{:S(2)}) async-start(), calls=%async_computation.5 | async-start | bytes 2211840 | tf_op jit(solution)/shard_map/reduce_scatter | solution.py:794
  309.0 26.3 %collective-permute-start.41 = (bf16[256,1536]{1,0:T(8,128)(2,1)}, bf16[256,1536]{1,0:T(8,128)(2,1)}, u32[]{:S(2)}, u32[]{:S(2)}) collective-permute-start(bf16[256,1536]{1,0:T(8,128)(2,1)} %get-tuple-element.336), channel_id=1, source_target_pairs={{0,2},{1,3},{2,0},{3,1},{4,6},{5,7},{6,4},{7,5},{8,10},{9,11},{10,... | collective-permute-start | bytes 2359304 | tf_op jit(solution)/shard_map/ppermute | solution.py:785
  310.2 25.1 %collective-permute-start.42 = (bf16[256,1536]{1,0:T(8,128)(2,1)}, bf16[256,1536]{1,0:T(8,128)(2,1)}, u32[]{:S(2)}, u32[]{:S(2)}) collective-permute-start(bf16[256,1536]{1,0:T(8,128)(2,1)} %get-tuple-element.337), channel_id=1, source_target_pairs={{0,16},{1,17},{2,18},{3,19},{4,20},{5,21},{6,22},{7,23},{8,24},{9,... | collective-permute-start | bytes 2359304 | tf_op jit(solution)/shard_map/ppermute | solution.py:785
  311.7 34.7 %collective-permute-start.43 = (bf16[288,1536]{1,0:T(8,128)(2,1)}, bf16[288,1536]{1,0:T(8,128)(2,1)S(1)}, u32[]{:S(2)}, u32[]{:S(2)}) collective-permute-start(bf16[288,1536]{1,0:T(8,128)(2,1)} %get-tuple-element.343), channel_id=1, source_target_pairs={{0,2},{1,3},{2,0},{3,1},{4,6},{5,7},{6,4},{7,5},{8,10},{9,11},{10,... | collective-permute-start | bytes 2654216 | tf_op jit(solution)/shard_map/ppermute | solution.py:785
  312.5 34.9 %collective-permute-start.44 = (bf16[288,1536]{1,0:T(8,128)(2,1)}, bf16[288,1536]{1,0:T(8,128)(2,1)}, u32[]{:S(2)}, u32[]{:S(2)}) collective-permute-start(bf16[288,1536]{1,0:T(8,128)(2,1)} %get-tuple-element.344), channel_id=1, source_target_pairs={{0,16},{1,17},{2,18},{3,19},{4,20},{5,21},{6,22},{7,23},{8,24},{9,... | collective-permute-start | bytes 2654216 | tf_op jit(solution)/shard_map/ppermute | solution.py:785
  360.7 17.2 %collective-permute-start.52 = (bf16[576,256]{1,0:T(8,128)(2,1)}, bf16[576,256]{1,0:T(8,128)(2,1)}, u32[]{:S(2)}, u32[]{:S(2)}) collective-permute-start(bf16[576,256]{1,0:T(8,128)(2,1)} %get-tuple-element.370.refs_18_), channel_id=1, source_target_pairs={{0,17},{1,16},{2,19},{3,18},{4,21},{5,20},{6,23},{7,22},{8,25},{9,... | collective-permute-start | bytes 884744 | tf_op jit(solution)/shard_map/ppermute | solution.py:785
  397.1 41.3 %collective-permute-start.57 = (bf16[384,1536]{1,0:T(8,128)(2,1)}, bf16[384,1536]{1,0:T(8,128)(2,1)}, u32[]{:S(2)}, u32[]{:S(2)}) collective-permute-start(bf16[384,1536]{1,0:T(8,128)(2,1)} %get-tuple-element.420), channel_id=1, source_target_pairs={{0,16},{1,17},{2,18},{3,19},{4,20},{5,21},{6,22},{7,23},{8,24},{9,... | collective-permute-start | bytes 3538952 | tf_op jit(solution)/shard_map/ppermute | solution.py:785
  438.5 24.2 %collective-permute-start.62 = (f32[5696]{0:T(1024)}, f32[5696]{0:T(1024)S(1)}, u32[]{:S(2)}, u32[]{:S(2)}) collective-permute-start(f32[5696]{0:T(1024)} %get-tuple-element.428), channel_id=1, source_target_pairs={{0,16},{1,17},{2,18},{3,19},{4,20},{5,21},{6,22},{7,23},{8,24},{9,... | collective-permute-start | bytes 68360 | tf_op jit(solution)/shard_map/ppermute | solution.py:785
  439.1 26.6 %collective-permute-start.63 = (bf16[144,1536]{1,0:T(8,128)(2,1)}, bf16[144,1536]{1,0:T(8,128)(2,1)}, u32[]{:S(2)}, u32[]{:S(2)}) collective-permute-start(bf16[144,1536]{1,0:T(8,128)(2,1)} %get-tuple-element.429), channel_id=1, source_target_pairs={{0,16},{1,17},{2,18},{3,19},{4,20},{5,21},{6,22},{7,23},{8,24},{9,... | collective-permute-start | bytes 1327112 | tf_op jit(solution)/shard_map/ppermute | solution.py:785
  (99 other events, 685.8 us)
Sparse Core Ops, SparseCore 0:
  16.7 52.4 all-gather.2
  104.5 90.6 all-gather.4
  292.5 84.2 reduce-scatter.2
  396.6 38.1 reduce-scatter.4

commit v5 on v4

--- a/solution.py
+++ b/solution.py
@@ -974,26 +974,24 @@
     d_middle, branch, d_grouped, g_ffn_gain = back_middle(
         run_a[2], ds_f, along_x, along_y, middle, out_grad, gains[2], w_out
     )
-    to_x, to_y = net.with_corner((run_a[3][n:], run_b[3][:n]), (yo_f[n:], yo_g[:n]), corner)
-    own = run_a[3][:n].astype(F32) + yo_f[:n].astype(F32)
-    to_x, to_y, d_grouped, *w_corner = fence(to_x, to_y, d_grouped, *w_corner)
+    d_grouped, *w_corner = fence(d_grouped, *w_corner)
     w_corner = (net.hop(w_corner[0], 0, 2), net.hop(w_corner[1], 1, 0))
-    along_x, along_y = net.hop(to_x, 0, 2), net.hop(to_y, 1, 0)
     d_packed, g_group, g_taps, g_mix = attend_back(
         packed_t, doc_ids, taps_back, head_mix, group_col, probs, attended, d_grouped
     )
-    along_x, along_y, d_packed, *w_corner = fence(along_x, along_y, d_packed, *w_corner)
+    d_packed, corner, *w_corner = fence(d_packed, corner, *w_corner)
+    y_x, y_y = net.with_corner((run_a[3][n:], run_b[3][:n]), (yo_f[n:], yo_g[:n]), corner)
     w_near.append(jnp.concatenate(w_corner, axis=0))
     w_far.append(net.hop(w_near[3], 0, 1))
-    layer_out = (middle + (own + along_x.astype(F32) + along_y.astype(F32))).astype(BF)
     pieces = cut(d_packed.reshape(3 * D, n), net.place, lines, cols)
     *cuts, branch = fence(*pieces, branch)
     pieces = [net.hop_block(p, b) for b, p in enumerate(cuts)]
     g_blocks = out_weight_grad(branch, grouped, net.place, lines, half_out)
     pieces = fence(*pieces, time=52)
-    g_far, sums, w_near[3], w_far[3], *pieces = fence(
-        net.hop(g_blocks[4], 0, 1), fold_sums(g_group, g_taps, g_mix), w_near[3], w_far[3], *pieces, *cuts
-    )
+    g_far, sums, w_near[3], w_far[3], y_x, y_y, *pieces = fence(
+        net.hop(g_blocks[4], 0, 1), fold_sums(g_group, g_taps, g_mix), w_near[3], w_far[3], y_x, y_y, *pieces, *cuts
+    )
+    y_x, y_y = net.hop(y_x, 0, 2), net.hop(y_y, 1, 0)
     pieces, cuts = pieces[:8], pieces[8:]
     size = lines * half_out
     g_far = [g_far[b * size : (b + 1) * size] for b in range(4)]
@@ -1008,11 +1006,13 @@
     input_grad, g_norm = input_back([cuts[3], cuts[7]], [w_near[3], w_far[3]], d_normed, tokens, d_middle, gains[0])
     small = jnp.concatenate([g_norm[0], g_ffn_gain[0], sums])
     small = net.sum_small(small, [bit for bit, _ in net.doubling])
-    along_x, along_y, g_other = fence(along_x, along_y, g_other, time=20)
-    along_x, along_y, g_other, small, g_qkv = fence(along_x, along_y, g_other, small, g_qkv)
+    g_other, y_x, y_y = fence(g_other, y_x, y_y, time=20)
+    g_out = net.scatter_line_small(out_own + along_x.astype(F32) + along_y.astype(F32)).astype(BF)
+    own = run_a[3][:n].astype(F32) + yo_f[:n].astype(F32)
+    layer_out = (middle + (own + y_x.astype(F32) + y_y.astype(F32))).astype(BF)
+    g_out, g_other, small, g_qkv = fence(g_out, g_other, small, g_qkv)
     q_other = net.hop(g_qkv, 1, 0)
     small = small + net.hop(small, 1, 0)
-    g_out = net.scatter_line_small(out_own + along_x.astype(F32) + along_y.astype(F32)).astype(BF)
     g_out = net.both_halves(g_out).T
     shape = (3, wide, D)
     g_ffn = net.both_halves(g_ffn.reshape(shape), 1, g_other.reshape(shape))

time: 483 us -> 479 us (level)
    ppermute x54, waiting for transfers between devices: 80.4 us -> 70.7 us  [hop(): return lax.ppermute(value, self.axes, self.hops[dy, di])]
    ppermute x4, waiting for transfers between devices: 8.98 us -> 17 us  [sum_small(): value = value + lax.ppermute(value, self.axes, perm)]
    unnamed x129 -> x147, local copies, waits for them, and re-layouts: 25.4 us -> 28.2 us
  transfers between devices with their start and end apart: 72 -> 72, of which waited for: 31 -> 30; matrix products, arithmetic and copies ran while one was open for 17% -> 17% of each run, Pallas kernels for 41% -> 41%
where the time goes in v5:
time: 479 us; the launch traced here: 472 us
  Pallas kernels  193 us (40%)
  waiting for transfers between devices  100 us (21%)
  starting transfers between devices  58.5 us (12%)
  other arithmetic  53.9 us (11%)
  local copies, waits for them, and re-layouts  50.5 us (11%)
  between operations  15 us (3%)
    ppermute x54, waiting for transfers between devices, hop(): return lax.ppermute(value, self.axes, self.hops[dy, di])  70.7 us
    ppermute x54, starting transfers between devices, hop(): return lax.ppermute(value, self.axes, self.hops[dy, di])  41.4 us
    pallas_call x3, Pallas kernels, ffn(): pl.pallas_call(functools.partial(ffn_kernel, counts), cost_estimate=cost(...  38.2 us
    unnamed x147, local copies, waits for them, and re-layouts  28.2 us
    pallas_call x1, Pallas kernels, attend(): pl.pallas_call(attend_kernel, cost_estimate=cost(0), grid=(count,), in_sp...  23.6 us
    pallas_call x1, Pallas kernels, attend_back(): pl.pallas_call(attend_back_kernel, cost_estimate=cost(24), grid=(PAIRS,),...  22.2 us
    pallas_call x1, Pallas kernels, ffn_grad(): pl.pallas_call(functools.partial(ffn_grad_kernel, len(hidden)), cost_esti...  17.6 us
    ppermute x4, waiting for transfers between devices, sum_small(): value = value + lax.ppermute(value, self.axes, perm)  17 us
  transfers between devices with their start and end apart: 72, of which 30 were waited for; matrix products, arithmetic and copies ran while one was open for 17% of the time, Pallas kernels for 41%

profile of v5, /device:TPU:0, one launch (start us, length us, event | category | flops | bytes accessed | tf_op | source)
XLA Modules:
  0.0 471.5 jit_solution(11333637753010246573)
XLA Ops:
  19.2 16.0 %shard_map.220 = (bf16[16,1536,256]{2,1,0:T(8,128)(2,1)}, bf16[16,1536,256]{2,1,0:T(8,128)(2,1)}, bf16[16,1536,256]{2,1,0:T(8,128)(2,1)}) custom-call(f32[16,8,256]{2,1,0:T(8,128)} %pad.7.fwd_ref, f32[16,8,256]{2,1,0:T(8,128)} %pad.8.bwd_ref), custom_call_target="tpu_custom_call" | custom-call | flops 8000000000 | tf_op jit(solution)/shard_map/pallas_call | solution.py:63
  35.3 9.6 %collective-permute-done.2.refs_3_ = bf16[256,1536]{1,0:T(8,128)(2,1)S(1)} collective-permute-done((bf16[256,1536]{1,0:T(8,128)(2,1)}, bf16[256,1536]{1,0:T(8,128)(2,1)S(1)}, u32[]{:S(2)}, u32[]{:S(2)}) %collective-permute-start.2) | collective-permute-done | bytes 786464 | tf_op jit(solution)/shard_map/ppermute | solution.py:785
  58.9 8.5 %maximum_maximum_fusion.1 = (bf16[1024,1536]{1,0:T(8,128)(2,1)}, bf16[1024,1536]{1,0:T(8,128)(2,1)}) fusion(bf16[256,1536]{1,0:T(8,128)(2,1)} %get-tuple-element.227, bf16[256,1536]{1,0:T(8,128)(2,1)S(1)} %copy-done.19, bf16[256,1536]{1,0:T(8,128)(2,1)} %convert_element_type.163, bf16[1024]{0:T(1024)(128)(2,1)S(1)} %pad.38.clone, ...), kind=kLoop, calls=%fused_computation.2 | loop fusion | flops 23592960 | bytes 11012096 | tf_op jit(solution)/shard_map/concatenate | solution.py:814
  78.1 7.4 %shard_map.226 = (bf16[1024,1536]{1,0:T(8,128)(2,1)}, bf16[576,256]{1,0:T(8,128)(2,1)}, bf16[576,256]{1,0:T(8,128)(2,1)}, bf16[576,256]{1,0:T(8,128)(2,1)}, bf16[576,256]{1,0:T(8,128)(2,1)}) custom-call(bf16[1024,1536]{1,0:T(8,128)(2,1)} %constant_dynamic-update-slice_fusion.11.x_ref, f32[1,1536]{1,0:T(1,128)} %slice.138.gain_ref.refs_7_, ...), custom_call_target="tpu_custom_call" | custom-call | tf_op jit(solution)/shard_map/pallas_call | solution.py:109
  91.9 7.5 %shard_map.228 = (bf16[1024,1536]{1,0:T(8,128)(2,1)}, bf16[576,256]{1,0:T(8,128)(2,1)}, bf16[576,256]{1,0:T(8,128)(2,1)}, bf16[576,256]{1,0:T(8,128)(2,1)}, bf16[576,256]{1,0:T(8,128)(2,1)}) custom-call(bf16[1024,1536]{1,0:T(8,128)(2,1)} %get-tuple-element.242.x_ref, f32[1,1536]{1,0:T(1,128)} %slice.138.gain_ref.refs_7_, ...), custom_call_target="tpu_custom_call" | custom-call | tf_op jit(solution)/shard_map/pallas_call | solution.py:109
  109.2 6.2 %collective-permute-done.17.refs_6_ = bf16[576,256]{1,0:T(8,128)(2,1)} collective-permute-done((bf16[576,256]{1,0:T(8,128)(2,1)}, bf16[576,256]{1,0:T(8,128)(2,1)}, u32[]{:S(2)}, u32[]{:S(2)}) %collective-permute-start.17) | collective-permute-done | bytes 294944 | tf_op jit(solution)/shard_map/ppermute | solution.py:785
  122.8 3.4 shard_map.231
  126.2 23.6 %shard_map.232 = (f32[16,256,256]{2,1,0:T(8,128)}, f32[1536,256]{1,0:T(8,128)}, bf16[1536,256]{1,0:T(8,128)(2,1)}) custom-call(f32[8,4]{1,0:T(8,128)} %copy.203.mix_ref, bf16[4608,256]{1,0:T(8,128)(2,1)} %bitcast.45, bf16[4608,256]{1,0:T(8,128)(2,1)} %bitcast.46, bf16[4608,256]{1,0:T(8,128)(2,1)} %bitcast.47, ...), custom_call_target="tpu_custom_call" | custom-call | tf_op jit(solution)/shard_map/pallas_call | solution.py:591
  157.7 3.6 shard_map.234.refs_0_
  162.8 5.3 %shard_map.236 = (f32[256,1536]{1,0:T(8,128)}, bf16[256,1536]{1,0:T(8,128)(2,1)}) custom-call(s32[1]{0:T(128)} %bitcast.place_ref, bf16[1536,256]{1,0:T(8,128)(2,1)} %get-tuple-element.270.grp_ref.grouped_ref, bf16[768,1536]{1,0:T(8,128)(2,1)} %get-tuple-element.274.far_ref.refs_1_, f32[768,256]{1,0:T(8,128)} %get-tuple-element.275.near_ref, ...), custom_call_target="tpu_custom_call" | custom-call | tf_op jit(solution)/shard_map/pallas_call | solution.py:207
  170.5 4.9 %shard_map.238 = bf16[4,4,2,48,1536]{4,3,2,1,0:T(8,128)(2,1)} custom-call(s32[1]{0:T(128)} %bitcast.place_ref, bf16[768,1536]{1,0:T(8,128)(2,1)} %get-tuple-element.279.refs_0_, bf16[768,1536]{1,0:T(8,128)(2,1)} %get-tuple-element.280.refs_1_), custom_call_target="tpu_custom_call" | custom-call | flops 1000000000 | tf_op jit(solution)/shard_map/pallas_call | solution.py:161
  176.5 11.7 %collective-permute-done.23.refs_0_ = bf16[256,1536]{1,0:T(8,128)(2,1)S(1)} collective-permute-done((bf16[256,1536]{1,0:T(8,128)(2,1)}, bf16[256,1536]{1,0:T(8,128)(2,1)S(1)}, u32[]{:S(2)}, u32[]{:S(2)}) %collective-permute-start.23) | collective-permute-done | bytes 786464 | tf_op jit(solution)/shard_map/ppermute | solution.py:785
  195.2 10.2 %shard_map.241 = (bf16[512,512]{1,0:T(8,128)(2,1)}, bf16[512,1024]{1,0:T(8,128)(2,1)}, bf16[512,1536]{1,0:T(8,128)(2,1)}, bf16[512,1536]{1,0:T(8,128)(2,1)}) custom-call(bf16[512,1536]{1,0:T(8,128)(2,1)} %copy-done.29, bf16[1024,1536]{1,0:T(8,128)(2,1)} %get-tuple-element.233.refs_1_.refs_12_.refs_15_, bf16[4,384,1536]{2,1,0:T(8,128)(2,1)} %shard_map.240.refs_2_.refs_4_), custom_call_target="tpu_custom_call" | custom-call | flops 3500000000 | tf_op jit(solution)/shard_map/pallas_call | solution.py:394
  211.6 10.1 %shard_map.243 = (bf16[512,512]{1,0:T(8,128)(2,1)}, bf16[512,1024]{1,0:T(8,128)(2,1)}, bf16[512,1536]{1,0:T(8,128)(2,1)}, bf16[512,1536]{1,0:T(8,128)(2,1)}) custom-call(bf16[512,1536]{1,0:T(8,128)(2,1)} %constant_dynamic-update-slice_fusion.6.refs_0_.refs_11_, bf16[1024,1536]{1,0:T(8,128)(2,1)} %get-tuple-element.233.refs_1_.refs_12_.refs_15_, ...), custom_call_target="tpu_custom_call" | custom-call | flops 3500000000 | tf_op jit(solution)/shard_map/pallas_call | solution.py:394
  221.8 17.9 %shard_map.245 = (bf16[1024,512]{1,0:T(8,128)(2,1)}, bf16[1024,1024]{1,0:T(8,128)(2,1)}, bf16[512,1536]{1,0:T(8,128)(2,1)}, bf16[512,1536]{1,0:T(8,128)(2,1)}, b...) custom-call(bf16[512,1536]{1,0:T(8,128)(2,1)} %get-tuple-element.295.refs_0_.refs_9_, ...), custom_call_target="tpu_custom_call" | custom-call | flops 1000000000 | tf_op jit(solution)/shard_map/pallas_call | solution.py:394
  240.2 9.6 %collective-permute-done.31.refs_1_ = bf16[576,1536]{1,0:T(8,128)(2,1)S(1)} collective-permute-done((bf16[576,1536]{1,0:T(8,128)(2,1)}, bf16[576,1536]{1,0:T(8,128)(2,1)S(1)}, u32[]{:S(2)}, u32[]{:S(2)}) %collective-permute-start.31) | collective-permute-done | bytes 1769504 | tf_op jit(solution)/shard_map/ppermute | solution.py:785
  259.9 6.2 %collective-permute-done.33 = bf16[256,1536]{1,0:T(8,128)(2,1)S(1)} collective-permute-done((bf16[256,1536]{1,0:T(8,128)(2,1)S(1)}, bf16[256,1536]{1,0:T(8,128)(2,1)S(1)}, u32[]{:S(2)}, u32[]{:S(2)}) %collective-permute-start.33) | collective-permute-done | bytes 786464 | tf_op jit(solution)/shard_map/ppermute | solution.py:825
  266.1 3.1 fusion.3
  272.1 17.6 %shard_map.248.refs_3_ = bf16[4,384,1536]{2,1,0:T(8,128)(2,1)} custom-call(bf16[512,512]{1,0:T(8,128)(2,1)} %get-tuple-element.321.refs_0_, bf16[1024,512]{1,0:T(8,128)(2,1)} %get-tuple-element.322.refs_1_.refs_2_, bf16[1024,512]{1,0:T(8,128)(2,1)} %get-tuple-element.322.refs_1_.refs_2_, bf16[512,512]{1,0:T(8,128)(2,1)} %get-tuple-element.323.refs_3_, ...), custom_call_target="tpu_custom_call" | custom-call | flops 7000000000 | tf_op jit(solution)/shard_map/pallas_call | solution.py:449
  295.0 8.7 %shard_map.250 = (f32[256,1536]{1,0:T(8,128)}, bf16[256,1536]{1,0:T(8,128)(2,1)}, f32[1536,256]{1,0:T(8,128)}, f32[1,1536]{1,0:T(1,128)}) custom-call(bf16[512,1536]{1,0:T(8,128)(2,1)} %get-tuple-element.302.a_ref, bf16[512,1536]{1,0:T(8,128)(2,1)} %collective-permute-done.29.f_ref, bf16[256,1536]{1,0:T(8,128)(2,1)} %get-tuple-element.330.sx_ref, ...), custom_call_target="tpu_custom_call" | custom-call | flops 3000000000 | tf_op jit(solution)/shard_map/pallas_call | solution.py:239
  304.9 22.2 %shard_map.252 = (bf16[3,1536,256]{2,1,0:T(8,128)(2,1)}, f32[1536,1]{1,0:T(8,128)}, f32[16,48,128]{2,1,0:T(8,128)}, f32[8,8,256]{2,1,0:T(8,128)}) custom-call(f32[8,4]{1,0:T(8,128)} %copy.203.mix_ref, bf16[4608,256]{1,0:T(8,128)(2,1)} %bitcast.48, bf16[4608,256]{1,0:T(8,128)(2,1)} %bitcast.49, bf16[4608,256]{1,0:T(8,128)(2,1)} %bitcast.50, ...), custom_call_target="tpu_custom_call" | custom-call | flops 12000000000 | tf_op jit(solution)/shard_map/pallas_call | solution.py:699
  334.6 3.3 shard_map.254
  342.7 3.5 fusion.7
  352.0 5.6 %shard_map.256 = (bf16[192,1536]{1,0:T(8,128)(2,1)}, bf16[192,1536]{1,0:T(8,128)(2,1)}, bf16[192,1536]{1,0:T(8,128)(2,1)}, bf16[192,1536]{1,0:T(8,128)(2,1)}, bf16[768,1536]{1,0:T(8,128)(2,1)}) custom-call(s32[1]{0:T(128)} %bitcast.place_ref, bf16[256,1536]{1,0:T(8,128)(2,1)} %get-tuple-element.351.branch_ref, ...), custom_call_target="tpu_custom_call" | custom-call | tf_op jit(solution)/shard_map/pallas_call | solution.py:277
  361.7 4.2 collective-permute-done.50.refs_6_
  371.8 9.4 %shard_map.259.refs_0_ = bf16[576,1536]{1,0:T(8,128)(2,1)} custom-call(bf16[576,256]{1,0:T(8,128)(2,1)} %get-tuple-element.375.refs_0_, bf16[576,256]{1,0:T(8,128)(2,1)} %get-tuple-element.376.refs_1_, bf16[576,256]{1,0:T(8,128)(2,1)} %get-tuple-element.377.refs_2_, bf16[576,256]{1,0:T(8,128)(2,1)} %get-tuple-element.378.refs_3_, ...), custom_call_target="tpu_custom_call" | custom-call | flops 3000000000 | tf_op jit(solution)/shard_map/pallas_call | solution.py:487
  390.2 9.9 %shard_map.263.refs_4_ = f32[256,1536]{1,0:T(8,128)} custom-call(bf16[576,256]{1,0:T(8,128)(2,1)} %get-tuple-element.407.refs_0_, bf16[576,256]{1,0:T(8,128)(2,1)} %get-tuple-element.408.refs_1_, bf16[576,256]{1,0:T(8,128)(2,1)} %get-tuple-element.409.refs_2_, bf16[576,256]{1,0:T(8,128)(2,1)} %get-tuple-element.410.refs_3_, ...), custom_call_target="tpu_custom_call" | custom-call | flops 500000000 | tf_op jit(solution)/shard_map/pallas_call | solution.py:506
  400.1 6.4 %shard_map.264 = (f32[256,1536]{1,0:T(8,128)}, f32[1,1536]{1,0:T(1,128)}) custom-call(bf16[576,256]{1,0:T(8,128)(2,1)} %get-tuple-element.403.refs_0_, bf16[576,256]{1,0:T(8,128)(2,1)} %get-tuple-element.404.refs_1_, bf16[576,1536]{1,0:T(8,128)(2,1)} %get-tuple-element.405.refs_2_, bf16[576,1536]{1,0:T(8,128)(2,1)} %get-tuple-element.406.refs_3_, ...), custom_call_target="tpu_custom_call" | custom-call | flops 2500000000 | tf_op jit(solution)/shard_map/pallas_call | solution.py:526
  411.1 6.8 %collective-permute-done.62 = f32[5696]{0:T(1024)S(1)} collective-permute-done((f32[5696]{0:T(1024)S(1)}, f32[5696]{0:T(1024)S(1)}, u32[]{:S(2)}, u32[]{:S(2)}) %collective-permute-start.62) | collective-permute-done | bytes 22816 | tf_op jit(solution)/shard_map/ppermute | solution.py:849
  423.6 7.3 %collective-permute-done.64 = f32[5696]{0:T(1024)S(1)} collective-permute-done((f32[5696]{0:T(1024)S(1)}, f32[5696]{0:T(1024)S(1)}, u32[]{:S(2)}, u32[]{:S(2)}) %collective-permute-start.64) | collective-permute-done | bytes 22816 | tf_op jit(solution)/shard_map/ppermute | solution.py:849
  433.2 6.2 %collective-permute-done.59 = bf16[48,1536]{1,0:T(8,128)(2,1)S(1)} collective-permute-done((bf16[48,1536]{1,0:T(8,128)(2,1)S(1)}, bf16[48,1536]{1,0:T(8,128)(2,1)S(1)}, u32[]{:S(2)}, u32[]{:S(2)}) %collective-permute-start.59) | collective-permute-done | bytes 147488 | tf_op jit(solution)/shard_map/ppermute | solution.py:785
  457.0 4.1 collective-permute-done.67
  (398 shorter events, 176.5 us)
Async XLA Ops:
  7.2 65.1 %all-gather.3.cloned.1.call-start = ((), (), s32[]{:S(2)}) async-start(), calls=%async_computation.2 | async-start | bytes 2949120 | tf_op jit(solution)/shard_map/all_gather | solution.py:791
  7.2 28.0 %collective-permute-start = (bf16[256,1536]{1,0:T(8,128)(2,1)}, bf16[256,1536]{1,0:T(8,128)(2,1)S(1)}, u32[]{:S(2)}, u32[]{:S(2)}) collective-permute-start(bf16[256,1536]{1,0:T(8,128)(2,1)} %refs_5_.1), channel_id=1, source_target_pairs={{0,2},{1,3},{2,0},{3,1},{4,6},{5,7},{6,4},{7,5},{8,10},{9,11},{10,... | collective-permute-start | bytes 2359304 | tf_op jit(solution)/shard_map/ppermute | solution.py:785
  10.2 25.0 %collective-permute-start.1 = (bf16[256,1536]{1,0:T(8,128)(2,1)}, bf16[256,1536]{1,0:T(8,128)(2,1)S(1)}, u32[]{:S(2)}, u32[]{:S(2)}) collective-permute-start(bf16[256,1536]{1,0:T(8,128)(2,1)} %refs_5_.1), channel_id=1, source_target_pairs={{0,16},{1,17},{2,18},{3,19},{4,20},{5,21},{6,22},{7,23},{8,24},{9,... | collective-permute-start | bytes 2359304 | tf_op jit(solution)/shard_map/ppermute | solution.py:785
  14.1 30.7 %collective-permute-start.2 = (bf16[256,1536]{1,0:T(8,128)(2,1)}, bf16[256,1536]{1,0:T(8,128)(2,1)S(1)}, u32[]{:S(2)}, u32[]{:S(2)}) collective-permute-start(bf16[256,1536]{1,0:T(8,128)(2,1)} %convert_element_type.163), channel_id=1, source_target_pairs={{0,2},{1,3},{2,0},{3,1},{4,6},{5,7},{6,4},{7,5},{8,10},{9,11},{10,... | collective-permute-start | bytes 2359304 | tf_op jit(solution)/shard_map/ppermute | solution.py:785
  14.7 31.7 %collective-permute-start.3 = (bf16[256,1536]{1,0:T(8,128)(2,1)}, bf16[256,1536]{1,0:T(8,128)(2,1)}, u32[]{:S(2)}, u32[]{:S(2)}) collective-permute-start(bf16[256,1536]{1,0:T(8,128)(2,1)} %convert_element_type.163), channel_id=1, source_target_pairs={{0,16},{1,17},{2,18},{3,19},{4,20},{5,21},{6,22},{7,23},{8,24},{9,... | collective-permute-start | bytes 2359304 | tf_op jit(solution)/shard_map/ppermute | solution.py:785
  16.6 178.6 %all-gather.5.cloned.1.call-start = ((), (), s32[]{:S(2)}) async-start(), calls=%async_computation.3 | async-start | bytes 5898240 | tf_op jit(solution)/shard_map/all_gather | solution.py:791
  104.5 280.2 %reduce-scatter.3.cloned.1.call-start = ((), (), s32[]{:S(2)}) async-start(), calls=%async_computation.4 | async-start | bytes 5898240 | tf_op jit(solution)/shard_map/reduce_scatter | solution.py:794
  116.3 34.4 %collective-permute-start.19 = (bf16[192,1536]{1,0:T(8,128)(2,1)}, bf16[192,1536]{1,0:T(8,128)(2,1)S(1)}, u32[]{:S(2)}, u32[]{:S(2)}) collective-permute-start(bf16[192,1536]{1,0:T(8,128)(2,1)} %get-tuple-element.256), channel_id=1, source_target_pairs={{0,2},{1,3},{2,0},{3,1},{4,6},{5,7},{6,4},{7,5},{8,10},{9,11},{10,... | collective-permute-start | bytes 1769480 | tf_op jit(solution)/shard_map/ppermute | solution.py:785
  117.2 33.4 %collective-permute-start.20 = (bf16[192,1536]{1,0:T(8,128)(2,1)}, bf16[192,1536]{1,0:T(8,128)(2,1)S(1)}, u32[]{:S(2)}, u32[]{:S(2)}) collective-permute-start(bf16[192,1536]{1,0:T(8,128)(2,1)} %get-tuple-element.256), channel_id=1, source_target_pairs={{0,16},{1,17},{2,18},{3,19},{4,20},{5,21},{6,22},{7,23},{8,24},{9,... | collective-permute-start | bytes 1769480 | tf_op jit(solution)/shard_map/ppermute | solution.py:785
  118.7 32.0 %collective-permute-start.21 = (bf16[192,1536]{1,0:T(8,128)(2,1)}, bf16[192,1536]{1,0:T(8,128)(2,1)S(1)}, u32[]{:S(2)}, u32[]{:S(2)}) collective-permute-start(bf16[192,1536]{1,0:T(8,128)(2,1)} %get-tuple-element.256), channel_id=1, source_target_pairs={{0,18},{1,19},{2,16},{3,17},{4,22},{5,23},{6,20},{7,21},{8,26},{9,... | collective-permute-start | bytes 1769480 | tf_op jit(solution)/shard_map/ppermute | solution.py:785
  168.1 20.2 %collective-permute-start.23 = (bf16[256,1536]{1,0:T(8,128)(2,1)}, bf16[256,1536]{1,0:T(8,128)(2,1)S(1)}, u32[]{:S(2)}, u32[]{:S(2)}) collective-permute-start(bf16[256,1536]{1,0:T(8,128)(2,1)} %get-tuple-element.278), channel_id=1, source_target_pairs={{0,2},{1,3},{2,0},{3,1},{4,6},{5,7},{6,4},{7,5},{8,10},{9,11},{10,... | collective-permute-start | bytes 2359304 | tf_op jit(solution)/shard_map/ppermute | solution.py:785
  169.0 19.9 %collective-permute-start.24 = (bf16[256,1536]{1,0:T(8,128)(2,1)}, bf16[256,1536]{1,0:T(8,128)(2,1)S(1)}, u32[]{:S(2)}, u32[]{:S(2)}) collective-permute-start(bf16[256,1536]{1,0:T(8,128)(2,1)} %get-tuple-element.278), channel_id=1, source_target_pairs={{0,16},{1,17},{2,18},{3,19},{4,20},{5,21},{6,22},{7,23},{8,24},{9,... | collective-permute-start | bytes 2359304 | tf_op jit(solution)/shard_map/ppermute | solution.py:785
  208.6 41.2 %collective-permute-start.31 = (bf16[576,1536]{1,0:T(8,128)(2,1)}, bf16[576,1536]{1,0:T(8,128)(2,1)S(1)}, u32[]{:S(2)}, u32[]{:S(2)}) collective-permute-start(bf16[576,1536]{1,0:T(8,128)(2,1)} %get-tuple-element.306.refs_3_), channel_id=1, source_target_pairs={{0,2},{1,3},{2,0},{3,1},{4,6},{5,7},{6,4},{7,5},{8,10},{9,11},{10,... | collective-permute-start | bytes 5308424 | tf_op jit(solution)/shard_map/ppermute | solution.py:785
  210.1 41.0 %collective-permute-start.32 = (bf16[576,1536]{1,0:T(8,128)(2,1)}, bf16[576,1536]{1,0:T(8,128)(2,1)S(1)}, u32[]{:S(2)}, u32[]{:S(2)}) collective-permute-start(bf16[576,1536]{1,0:T(8,128)(2,1)} %get-tuple-element.306.refs_3_), channel_id=1, source_target_pairs={{0,16},{1,17},{2,18},{3,19},{4,20},{5,21},{6,22},{7,23},{8,24},{9,... | collective-permute-start | bytes 5308424 | tf_op jit(solution)/shard_map/ppermute | solution.py:785
  269.2 21.3 %collective-permute-start.37 = (bf16[576,1536]{1,0:T(8,128)(2,1)}, bf16[576,1536]{1,0:T(8,128)(2,1)S(1)}, u32[]{:S(2)}, u32[]{:S(2)}) collective-permute-start(bf16[576,1536]{1,0:T(8,128)(2,1)} %get-tuple-element.327.refs_6_), channel_id=1, source_target_pairs={{0,1},{1,0},{2,3},{3,2},{4,5},{5,4},{6,7},{7,6},{8,9},{9,8},{10,11... | collective-permute-start | bytes 5308424 | tf_op jit(solution)/shard_map/ppermute | solution.py:785
  269.2 21.3 %collective-permute-start.38 = (bf16[576,1536]{1,0:T(8,128)(2,1)}, bf16[576,1536]{1,0:T(8,128)(2,1)S(1)}, u32[]{:S(2)}, u32[]{:S(2)}) collective-permute-start(bf16[576,1536]{1,0:T(8,128)(2,1)} %get-tuple-element.328.refs_7_), channel_id=1, source_target_pairs={{0,1},{1,0},{2,3},{3,2},{4,5},{5,4},{6,7},{7,6},{8,9},{9,8},{10,11... | collective-permute-start | bytes 5308424 | tf_op jit(solution)/shard_map/ppermute | solution.py:785
  269.7 20.9 %collective-permute-start.39 = (bf16[576,1536]{1,0:T(8,128)(2,1)}, bf16[576,1536]{1,0:T(8,128)(2,1)}, u32[]{:S(2)}, u32[]{:S(2)}) collective-permute-start(bf16[576,1536]{1,0:T(8,128)(2,1)} %get-tuple-element.329.refs_8_), channel_id=1, source_target_pairs={{0,1},{1,0},{2,3},{3,2},{4,5},{5,4},{6,7},{7,6},{8,9},{9,8},{10,11... | collective-permute-start | bytes 5308424 | tf_op jit(solution)/shard_map/ppermute | solution.py:785
  269.7 20.3 %collective-permute-start.35 = (bf16[256,1536]{1,0:T(8,128)(2,1)}, bf16[256,1536]{1,0:T(8,128)(2,1)}, u32[]{:S(2)}, u32[]{:S(2)}) collective-permute-start(bf16[256,1536]{1,0:T(8,128)(2,1)} %get-tuple-element.318), channel_id=1, source_target_pairs={{0,2},{1,3},{2,0},{3,1},{4,6},{5,7},{6,4},{7,5},{8,10},{9,11},{10,... | collective-permute-start | bytes 2359304 | tf_op jit(solution)/shard_map/ppermute | solution.py:785
  270.6 20.0 %collective-permute-start.36 = (bf16[256,1536]{1,0:T(8,128)(2,1)}, bf16[256,1536]{1,0:T(8,128)(2,1)}, u32[]{:S(2)}, u32[]{:S(2)}) collective-permute-start(bf16[256,1536]{1,0:T(8,128)(2,1)} %get-tuple-element.319), channel_id=1, source_target_pairs={{0,16},{1,17},{2,18},{3,19},{4,20},{5,21},{6,22},{7,23},{8,24},{9,... | collective-permute-start | bytes 2359304 | tf_op jit(solution)/shard_map/ppermute | solution.py:785
  292.4 153.2 %reduce-scatter.5.cloned.1.call-start = ((), (), s32[]{:S(2)}) async-start(), calls=%async_computation.5 | async-start | bytes 2211840 | tf_op jit(solution)/shard_map/reduce_scatter | solution.py:794
  292.6 49.0 %collective-permute-start.28 = (bf16[512,1536]{1,0:T(8,128)(2,1)}, bf16[512,1536]{1,0:T(8,128)(2,1)}, u32[]{:S(2)}, u32[]{:S(2)}) collective-permute-start(bf16[512,1536]{1,0:T(8,128)(2,1)} %get-tuple-element.298), channel_id=1, source_target_pairs={{0,1},{1,0},{2,3},{3,2},{4,5},{5,4},{6,7},{7,6},{8,9},{9,8},{10,11... | collective-permute-start | bytes 4718600 | tf_op jit(solution)/shard_map/ppermute | solution.py:785
  293.5 39.6 %collective-permute-start.40 = (bf16[256,1536]{1,0:T(8,128)(2,1)S(1)}, bf16[256,1536]{1,0:T(8,128)(2,1)S(1)}, u32[]{:S(2)}, u32[]{:S(2)}) collective-permute-start(bf16[256,1536]{1,0:T(8,128)(2,1)S(1)} %copy-done.20), channel_id=1, source_target_pairs={{0,16},{1,3},{2,18},{3,1},{4,20},{5,7},{6,22},{7,5},{8,24},{9,11},... | collective-permute-start | bytes 2359304 | tf_op jit(solution)/shard_map/ppermute | solution.py:973
  303.7 29.4 %collective-permute-start.41 = (bf16[288,1536]{1,0:T(8,128)(2,1)}, bf16[288,1536]{1,0:T(8,128)(2,1)S(1)}, u32[]{:S(2)}, u32[]{:S(2)}) collective-permute-start(bf16[288,1536]{1,0:T(8,128)(2,1)} %get-tuple-element.339), channel_id=1, source_target_pairs={{0,2},{1,3},{2,0},{3,1},{4,6},{5,7},{6,4},{7,5},{8,10},{9,11},{10,... | collective-permute-start | bytes 2654216 | tf_op jit(solution)/shard_map/ppermute | solution.py:785
  304.9 28.3 %collective-permute-start.42 = (bf16[288,1536]{1,0:T(8,128)(2,1)}, bf16[288,1536]{1,0:T(8,128)(2,1)S(1)}, u32[]{:S(2)}, u32[]{:S(2)}) collective-permute-start(bf16[288,1536]{1,0:T(8,128)(2,1)} %get-tuple-element.340), channel_id=1, source_target_pairs={{0,16},{1,17},{2,18},{3,19},{4,20},{5,21},{6,22},{7,23},{8,24},{9,... | collective-permute-start | bytes 2654216 | tf_op jit(solution)/shard_map/ppermute | solution.py:785
  341.6 20.1 %collective-permute-start.48 = (bf16[576,256]{1,0:T(8,128)(2,1)}, bf16[576,256]{1,0:T(8,128)(2,1)}, u32[]{:S(2)}, u32[]{:S(2)}) collective-permute-start(bf16[576,256]{1,0:T(8,128)(2,1)} %get-tuple-element.363.refs_18_), channel_id=1, source_target_pairs={{0,1},{1,0},{2,3},{3,2},{4,5},{5,4},{6,7},{7,6},{8,9},{9,8},{10,11... | collective-permute-start | bytes 884744 | tf_op jit(solution)/shard_map/ppermute | solution.py:785
  341.6 20.1 %collective-permute-start.49 = (bf16[576,256]{1,0:T(8,128)(2,1)}, bf16[576,256]{1,0:T(8,128)(2,1)}, u32[]{:S(2)}, u32[]{:S(2)}) collective-permute-start(bf16[576,256]{1,0:T(8,128)(2,1)} %get-tuple-element.364.refs_19_), channel_id=1, source_target_pairs={{0,3},{1,2},{2,1},{3,0},{4,7},{5,6},{6,5},{7,4},{8,11},{9,10},{10,... | collective-permute-start | bytes 884744 | tf_op jit(solution)/shard_map/ppermute | solution.py:785
  384.6 22.6 %collective-permute-start.57 = (bf16[192,1536]{1,0:T(8,128)(2,1)}, bf16[192,1536]{1,0:T(8,128)(2,1)S(1)}, u32[]{:S(2)}, u32[]{:S(2)}) collective-permute-start(bf16[192,1536]{1,0:T(8,128)(2,1)} %get-tuple-element.420), channel_id=1, source_target_pairs={{0,16},{1,17},{2,18},{3,19},{4,20},{5,21},{6,22},{7,23},{8,24},{9,... | collective-permute-start | bytes 1769480 | tf_op jit(solution)/shard_map/ppermute | solution.py:785
  386.0 21.3 %collective-permute-start.56 = (bf16[192,1536]{1,0:T(8,128)(2,1)}, bf16[192,1536]{1,0:T(8,128)(2,1)}, u32[]{:S(2)}, u32[]{:S(2)}) collective-permute-start(bf16[192,1536]{1,0:T(8,128)(2,1)} %get-tuple-element.419), channel_id=1, source_target_pairs={{0,2},{1,3},{2,0},{3,1},{4,6},{5,7},{6,4},{7,5},{8,10},{9,11},{10,... | collective-permute-start | bytes 1769480 | tf_op jit(solution)/shard_map/ppermute | solution.py:785
  386.9 53.5 %collective-permute-start.54 = (bf16[256,1536]{1,0:T(8,128)(2,1)}, bf16[256,1536]{1,0:T(8,128)(2,1)}, u32[]{:S(2)}, u32[]{:S(2)}) collective-permute-start(bf16[256,1536]{1,0:T(8,128)(2,1)} %get-tuple-element.399), channel_id=1, source_target_pairs={{0,2},{1,3},{2,0},{3,1},{4,6},{5,7},{6,4},{7,5},{8,10},{9,11},{10,... | collective-permute-start | bytes 2359304 | tf_op jit(solution)/shard_map/ppermute | solution.py:785
  388.1 52.2 %collective-permute-start.55 = (bf16[256,1536]{1,0:T(8,128)(2,1)}, bf16[256,1536]{1,0:T(8,128)(2,1)}, u32[]{:S(2)}, u32[]{:S(2)}) collective-permute-start(bf16[256,1536]{1,0:T(8,128)(2,1)} %get-tuple-element.400), channel_id=1, source_target_pairs={{0,16},{1,17},{2,18},{3,19},{4,20},{5,21},{6,22},{7,23},{8,24},{9,... | collective-permute-start | bytes 2359304 | tf_op jit(solution)/shard_map/ppermute | solution.py:785
  388.8 53.7 %collective-permute-start.53 = (bf16[384,1536]{1,0:T(8,128)(2,1)}, bf16[384,1536]{1,0:T(8,128)(2,1)}, u32[]{:S(2)}, u32[]{:S(2)}) collective-permute-start(bf16[384,1536]{1,0:T(8,128)(2,1)} %get-tuple-element.398), channel_id=1, source_target_pairs={{0,16},{1,17},{2,18},{3,19},{4,20},{5,21},{6,22},{7,23},{8,24},{9,... | collective-permute-start | bytes 3538952 | tf_op jit(solution)/shard_map/ppermute | solution.py:785
  409.8 21.1 %collective-permute-start.60 = (bf16[48,1536]{1,0:T(8,128)(2,1)S(1)}, bf16[48,1536]{1,0:T(8,128)(2,1)S(1)}, u32[]{:S(2)}, u32[]{:S(2)}) collective-permute-start(bf16[48,1536]{1,0:T(8,128)(2,1)S(1)} %get-tuple-element.486), channel_id=1, source_target_pairs={{0,12},{1,13},{2,14},{3,15},{4,8},{5,9},{6,10},{7,11},{8,4},{9,5},... | collective-permute-start | bytes 442376 | tf_op jit(solution)/shard_map/ppermute | solution.py:785
  (108 other events, 729.5 us)
Sparse Core Ops, SparseCore 0:
  16.7 52.4 all-gather.2
  104.6 90.5 all-gather.4
  292.5 84.1 reduce-scatter.2
  390.3 40.1 reduce-scatter.4

commit v6 on v5

--- a/solution.py
+++ b/solution.py
@@ -909,7 +909,7 @@
     w_attn = fence(w_attn, time=100)[0]
     x_far = fence(x_far, time=40)[0]
     d_near = fence(d_near, time=60)[0]
-    w_attn, d_near, x_far, gains = fence(w_attn, d_near, x_far, gains)
+    w_attn, d_near, gains = fence(w_attn, d_near, gains)
     gains = gains.transpose(1, 0, 2).reshape(3, D).astype(F32)
     w_cls = w_attn[:, cols:].reshape(-1, D)
     inputs = tokens.astype(F32)

time: 479 us -> 477 us (level)
    unnamed x147 -> x145, local copies, waits for them, and re-layouts: 28.2 us -> 26.7 us
  transfers between devices with their start and end apart: 72 -> 72, of which waited for: 30 -> 28; matrix products, arithmetic and copies ran while one was open for 17% -> 17% of each run, Pallas kernels for 41% -> 41%
where the time goes in v6:
time: 477 us; the launch traced here: 469 us
  Pallas kernels  193 us (40%)
  waiting for transfers between devices  98.2 us (21%)
  starting transfers between devices  59.4 us (12%)
  other arithmetic  54 us (11%)
  local copies, waits for them, and re-layouts  49 us (10%)
  between operations  15 us (3%)
    ppermute x54, waiting for transfers between devices, hop(): return lax.ppermute(value, self.axes, self.hops[dy, di])  68.5 us
    ppermute x54, starting transfers between devices, hop(): return lax.ppermute(value, self.axes, self.hops[dy, di])  43.8 us
    pallas_call x3, Pallas kernels, ffn(): pl.pallas_call(functools.partial(ffn_kernel, counts), cost_estimate=cost(...  38.2 us
    unnamed x145, local copies, waits for them, and re-layouts  26.7 us
    pallas_call x1, Pallas kernels, attend(): pl.pallas_call(attend_kernel, cost_estimate=cost(0), grid=(count,), in_sp...  23.6 us
    pallas_call x1, Pallas kernels, attend_back(): pl.pallas_call(attend_back_kernel, cost_estimate=cost(24), grid=(PAIRS,),...  22.2 us
    pallas_call x1, Pallas kernels, ffn_grad(): pl.pallas_call(functools.partial(ffn_grad_kernel, len(hidden)), cost_esti...  17.6 us
    pallas_call x1, Pallas kernels, band_taps(): pl.pallas_call(taps_kernel, cost_estimate=cost(16), grid=(H,), in_specs=[...  16 us
  transfers between devices with their start and end apart: 72, of which 28 were waited for; matrix products, arithmetic and copies ran while one was open for 17% of the time, Pallas kernels for 41%

profile of v6, /device:TPU:0, one launch (start us, length us, event | category | flops | bytes accessed | tf_op | source)
XLA Modules:
  0.0 468.8 jit_solution(18196315345326048977)
XLA Ops:
  19.2 16.0 %shard_map.220 = (bf16[16,1536,256]{2,1,0:T(8,128)(2,1)}, bf16[16,1536,256]{2,1,0:T(8,128)(2,1)}, bf16[16,1536,256]{2,1,0:T(8,128)(2,1)}) custom-call(f32[16,8,256]{2,1,0:T(8,128)} %pad.7.fwd_ref, f32[16,8,256]{2,1,0:T(8,128)} %pad.8.bwd_ref), custom_call_target="tpu_custom_call" | custom-call | flops 8000000000 | tf_op jit(solution)/shard_map/pallas_call | solution.py:63
  35.3 9.5 %collective-permute-done.2.refs_3_ = bf16[256,1536]{1,0:T(8,128)(2,1)S(1)} collective-permute-done((bf16[256,1536]{1,0:T(8,128)(2,1)}, bf16[256,1536]{1,0:T(8,128)(2,1)S(1)}, u32[]{:S(2)}, u32[]{:S(2)}) %collective-permute-start.2) | collective-permute-done | bytes 786464 | tf_op jit(solution)/shard_map/ppermute | solution.py:785
  58.9 8.5 %maximum_maximum_fusion.1 = (bf16[1024,1536]{1,0:T(8,128)(2,1)}, bf16[1024,1536]{1,0:T(8,128)(2,1)}) fusion(bf16[256,1536]{1,0:T(8,128)(2,1)} %get-tuple-element.226, bf16[256,1536]{1,0:T(8,128)(2,1)S(1)} %copy-done.18, bf16[256,1536]{1,0:T(8,128)(2,1)} %convert_element_type.163, bf16[1024]{0:T(1024)(128)(2,1)S(1)} %pad.38.clone, ...), kind=kLoop, calls=%fused_computation.2 | loop fusion | flops 23592960 | bytes 11012096 | tf_op jit(solution)/shard_map/concatenate | solution.py:814
  73.8 7.4 %shard_map.225 = (bf16[1024,1536]{1,0:T(8,128)(2,1)}, bf16[576,256]{1,0:T(8,128)(2,1)}, bf16[576,256]{1,0:T(8,128)(2,1)}, bf16[576,256]{1,0:T(8,128)(2,1)}, bf16[576,256]{1,0:T(8,128)(2,1)}) custom-call(bf16[1024,1536]{1,0:T(8,128)(2,1)} %constant_dynamic-update-slice_fusion.11.x_ref, f32[1,1536]{1,0:T(1,128)} %slice.138.gain_ref.refs_7_, ...), custom_call_target="tpu_custom_call" | custom-call | tf_op jit(solution)/shard_map/pallas_call | solution.py:109
  87.5 7.6 %shard_map.228 = (bf16[1024,1536]{1,0:T(8,128)(2,1)}, bf16[576,256]{1,0:T(8,128)(2,1)}, bf16[576,256]{1,0:T(8,128)(2,1)}, bf16[576,256]{1,0:T(8,128)(2,1)}, bf16[576,256]{1,0:T(8,128)(2,1)}) custom-call(bf16[1024,1536]{1,0:T(8,128)(2,1)} %get-tuple-element.240.x_ref, f32[1,1536]{1,0:T(1,128)} %slice.138.gain_ref.refs_7_, ...), custom_call_target="tpu_custom_call" | custom-call | tf_op jit(solution)/shard_map/pallas_call | solution.py:109
  104.8 6.5 %collective-permute-done.17.refs_6_ = bf16[576,256]{1,0:T(8,128)(2,1)} collective-permute-done((bf16[576,256]{1,0:T(8,128)(2,1)}, bf16[576,256]{1,0:T(8,128)(2,1)}, u32[]{:S(2)}, u32[]{:S(2)}) %collective-permute-start.17) | collective-permute-done | bytes 294944 | tf_op jit(solution)/shard_map/ppermute | solution.py:785
  118.7 3.4 shard_map.231
  122.2 23.6 %shard_map.232 = (f32[16,256,256]{2,1,0:T(8,128)}, f32[1536,256]{1,0:T(8,128)}, bf16[1536,256]{1,0:T(8,128)(2,1)}) custom-call(f32[8,4]{1,0:T(8,128)} %copy.202.mix_ref, bf16[4608,256]{1,0:T(8,128)(2,1)} %bitcast.45, bf16[4608,256]{1,0:T(8,128)(2,1)} %bitcast.46, bf16[4608,256]{1,0:T(8,128)(2,1)} %bitcast.47, ...), custom_call_target="tpu_custom_call" | custom-call | tf_op jit(solution)/shard_map/pallas_call | solution.py:591
  153.7 3.6 shard_map.234.refs_0_
  158.8 5.3 %shard_map.236 = (f32[256,1536]{1,0:T(8,128)}, bf16[256,1536]{1,0:T(8,128)(2,1)}) custom-call(s32[1]{0:T(128)} %bitcast.place_ref, bf16[1536,256]{1,0:T(8,128)(2,1)} %get-tuple-element.268.grp_ref.grouped_ref, bf16[768,1536]{1,0:T(8,128)(2,1)} %get-tuple-element.272.far_ref.refs_1_, f32[768,256]{1,0:T(8,128)} %get-tuple-element.273.near_ref, ...), custom_call_target="tpu_custom_call" | custom-call | tf_op jit(solution)/shard_map/pallas_call | solution.py:207
  166.5 4.9 %shard_map.238 = bf16[4,4,2,48,1536]{4,3,2,1,0:T(8,128)(2,1)} custom-call(s32[1]{0:T(128)} %bitcast.place_ref, bf16[768,1536]{1,0:T(8,128)(2,1)} %get-tuple-element.277.refs_0_, bf16[768,1536]{1,0:T(8,128)(2,1)} %get-tuple-element.278.refs_1_), custom_call_target="tpu_custom_call" | custom-call | flops 1000000000 | tf_op jit(solution)/shard_map/pallas_call | solution.py:161
  172.5 11.7 %collective-permute-done.23.refs_0_ = bf16[256,1536]{1,0:T(8,128)(2,1)S(1)} collective-permute-done((bf16[256,1536]{1,0:T(8,128)(2,1)}, bf16[256,1536]{1,0:T(8,128)(2,1)S(1)}, u32[]{:S(2)}, u32[]{:S(2)}) %collective-permute-start.23) | collective-permute-done | bytes 786464 | tf_op jit(solution)/shard_map/ppermute | solution.py:785
  192.2 10.2 %shard_map.241 = (bf16[512,512]{1,0:T(8,128)(2,1)}, bf16[512,1024]{1,0:T(8,128)(2,1)}, bf16[512,1536]{1,0:T(8,128)(2,1)}, bf16[512,1536]{1,0:T(8,128)(2,1)}) custom-call(bf16[512,1536]{1,0:T(8,128)(2,1)} %copy-done.28, bf16[1024,1536]{1,0:T(8,128)(2,1)} %get-tuple-element.231.refs_1_.refs_12_.refs_15_, bf16[4,384,1536]{2,1,0:T(8,128)(2,1)} %shard_map.240.refs_2_.refs_4_), custom_call_target="tpu_custom_call" | custom-call | flops 3500000000 | tf_op jit(solution)/shard_map/pallas_call | solution.py:394
  208.7 10.1 %shard_map.243 = (bf16[512,512]{1,0:T(8,128)(2,1)}, bf16[512,1024]{1,0:T(8,128)(2,1)}, bf16[512,1536]{1,0:T(8,128)(2,1)}, bf16[512,1536]{1,0:T(8,128)(2,1)}) custom-call(bf16[512,1536]{1,0:T(8,128)(2,1)} %constant_dynamic-update-slice_fusion.6.refs_0_.refs_11_, bf16[1024,1536]{1,0:T(8,128)(2,1)} %get-tuple-element.231.refs_1_.refs_12_.refs_15_, ...), custom_call_target="tpu_custom_call" | custom-call | flops 3500000000 | tf_op jit(solution)/shard_map/pallas_call | solution.py:394
  218.8 17.9 %shard_map.245 = (bf16[1024,512]{1,0:T(8,128)(2,1)}, bf16[1024,1024]{1,0:T(8,128)(2,1)}, bf16[512,1536]{1,0:T(8,128)(2,1)}, bf16[512,1536]{1,0:T(8,128)(2,1)}, b...) custom-call(bf16[512,1536]{1,0:T(8,128)(2,1)} %get-tuple-element.293.refs_0_.refs_9_, ...), custom_call_target="tpu_custom_call" | custom-call | flops 1000000000 | tf_op jit(solution)/shard_map/pallas_call | solution.py:394
  237.3 9.6 %collective-permute-done.31.refs_1_ = bf16[576,1536]{1,0:T(8,128)(2,1)S(1)} collective-permute-done((bf16[576,1536]{1,0:T(8,128)(2,1)}, bf16[576,1536]{1,0:T(8,128)(2,1)S(1)}, u32[]{:S(2)}, u32[]{:S(2)}) %collective-permute-start.31) | collective-permute-done | bytes 1769504 | tf_op jit(solution)/shard_map/ppermute | solution.py:785
  256.9 6.2 %collective-permute-done.33 = bf16[256,1536]{1,0:T(8,128)(2,1)S(1)} collective-permute-done((bf16[256,1536]{1,0:T(8,128)(2,1)S(1)}, bf16[256,1536]{1,0:T(8,128)(2,1)S(1)}, u32[]{:S(2)}, u32[]{:S(2)}) %collective-permute-start.33) | collective-permute-done | bytes 786464 | tf_op jit(solution)/shard_map/ppermute | solution.py:825
  269.1 17.6 %shard_map.248.refs_3_ = bf16[4,384,1536]{2,1,0:T(8,128)(2,1)} custom-call(bf16[512,512]{1,0:T(8,128)(2,1)} %get-tuple-element.319.refs_0_, bf16[1024,512]{1,0:T(8,128)(2,1)} %get-tuple-element.320.refs_1_.refs_2_, bf16[1024,512]{1,0:T(8,128)(2,1)} %get-tuple-element.320.refs_1_.refs_2_, bf16[512,512]{1,0:T(8,128)(2,1)} %get-tuple-element.321.refs_3_, ...), custom_call_target="tpu_custom_call" | custom-call | flops 7000000000 | tf_op jit(solution)/shard_map/pallas_call | solution.py:449
  292.0 8.7 %shard_map.250 = (f32[256,1536]{1,0:T(8,128)}, bf16[256,1536]{1,0:T(8,128)(2,1)}, f32[1536,256]{1,0:T(8,128)}, f32[1,1536]{1,0:T(1,128)}) custom-call(bf16[512,1536]{1,0:T(8,128)(2,1)} %get-tuple-element.300.a_ref, bf16[512,1536]{1,0:T(8,128)(2,1)} %collective-permute-done.29.f_ref, bf16[256,1536]{1,0:T(8,128)(2,1)} %get-tuple-element.328.sx_ref, ...), custom_call_target="tpu_custom_call" | custom-call | flops 3000000000 | tf_op jit(solution)/shard_map/pallas_call | solution.py:239
  301.9 22.2 %shard_map.252 = (bf16[3,1536,256]{2,1,0:T(8,128)(2,1)}, f32[1536,1]{1,0:T(8,128)}, f32[16,48,128]{2,1,0:T(8,128)}, f32[8,8,256]{2,1,0:T(8,128)}) custom-call(f32[8,4]{1,0:T(8,128)} %copy.202.mix_ref, bf16[4608,256]{1,0:T(8,128)(2,1)} %bitcast.48, bf16[4608,256]{1,0:T(8,128)(2,1)} %bitcast.49, bf16[4608,256]{1,0:T(8,128)(2,1)} %bitcast.50, ...), custom_call_target="tpu_custom_call" | custom-call | flops 12000000000 | tf_op jit(solution)/shard_map/pallas_call | solution.py:699
  331.6 3.3 shard_map.254
  339.7 3.5 fusion.7
  349.0 5.6 %shard_map.256 = (bf16[192,1536]{1,0:T(8,128)(2,1)}, bf16[192,1536]{1,0:T(8,128)(2,1)}, bf16[192,1536]{1,0:T(8,128)(2,1)}, bf16[192,1536]{1,0:T(8,128)(2,1)}, bf16[768,1536]{1,0:T(8,128)(2,1)}) custom-call(s32[1]{0:T(128)} %bitcast.place_ref, bf16[256,1536]{1,0:T(8,128)(2,1)} %get-tuple-element.349.branch_ref, ...), custom_call_target="tpu_custom_call" | custom-call | tf_op jit(solution)/shard_map/pallas_call | solution.py:277
  358.8 4.2 collective-permute-done.50.refs_6_
  368.9 9.4 %shard_map.259.refs_0_ = bf16[576,1536]{1,0:T(8,128)(2,1)} custom-call(bf16[576,256]{1,0:T(8,128)(2,1)} %get-tuple-element.373.refs_0_, bf16[576,256]{1,0:T(8,128)(2,1)} %get-tuple-element.374.refs_1_, bf16[576,256]{1,0:T(8,128)(2,1)} %get-tuple-element.375.refs_2_, bf16[576,256]{1,0:T(8,128)(2,1)} %get-tuple-element.376.refs_3_, ...), custom_call_target="tpu_custom_call" | custom-call | flops 3000000000 | tf_op jit(solution)/shard_map/pallas_call | solution.py:487
  387.2 9.9 %shard_map.263.refs_4_ = f32[256,1536]{1,0:T(8,128)} custom-call(bf16[576,256]{1,0:T(8,128)(2,1)} %get-tuple-element.405.refs_0_, bf16[576,256]{1,0:T(8,128)(2,1)} %get-tuple-element.406.refs_1_, bf16[576,256]{1,0:T(8,128)(2,1)} %get-tuple-element.407.refs_2_, bf16[576,256]{1,0:T(8,128)(2,1)} %get-tuple-element.408.refs_3_, ...), custom_call_target="tpu_custom_call" | custom-call | flops 500000000 | tf_op jit(solution)/shard_map/pallas_call | solution.py:506
  397.1 6.4 %shard_map.264 = (f32[256,1536]{1,0:T(8,128)}, f32[1,1536]{1,0:T(1,128)}) custom-call(bf16[576,256]{1,0:T(8,128)(2,1)} %get-tuple-element.401.refs_0_, bf16[576,256]{1,0:T(8,128)(2,1)} %get-tuple-element.402.refs_1_, bf16[576,1536]{1,0:T(8,128)(2,1)} %get-tuple-element.403.refs_2_, bf16[576,1536]{1,0:T(8,128)(2,1)} %get-tuple-element.404.refs_3_, ...), custom_call_target="tpu_custom_call" | custom-call | flops 2500000000 | tf_op jit(solution)/shard_map/pallas_call | solution.py:526
  408.6 6.3 %collective-permute-done.62 = f32[5696]{0:T(1024)S(1)} collective-permute-done((f32[5696]{0:T(1024)S(1)}, f32[5696]{0:T(1024)S(1)}, u32[]{:S(2)}, u32[]{:S(2)}) %collective-permute-start.62) | collective-permute-done | bytes 22816 | tf_op jit(solution)/shard_map/ppermute | solution.py:849
  414.9 4.6 collective-permute-done.63
  420.6 5.1 %collective-permute-done.64 = f32[5696]{0:T(1024)S(1)} collective-permute-done((f32[5696]{0:T(1024)S(1)}, f32[5696]{0:T(1024)S(1)}, u32[]{:S(2)}, u32[]{:S(2)}) %collective-permute-start.64) | collective-permute-done | bytes 22816 | tf_op jit(solution)/shard_map/ppermute | solution.py:849
  430.0 6.3 %collective-permute-done.59 = bf16[48,1536]{1,0:T(8,128)(2,1)S(1)} collective-permute-done((bf16[48,1536]{1,0:T(8,128)(2,1)S(1)}, bf16[48,1536]{1,0:T(8,128)(2,1)S(1)}, u32[]{:S(2)}, u32[]{:S(2)}) %collective-permute-start.59) | collective-permute-done | bytes 147488 | tf_op jit(solution)/shard_map/ppermute | solution.py:785
  453.9 4.4 collective-permute-done.67
  (396 shorter events, 174.3 us)
Async XLA Ops:
  7.2 65.1 %all-gather.3.cloned.1.call-start = ((), (), s32[]{:S(2)}) async-start(), calls=%async_computation.2 | async-start | bytes 2949120 | tf_op jit(solution)/shard_map/all_gather | solution.py:791
  7.2 28.0 %collective-permute-start = (bf16[256,1536]{1,0:T(8,128)(2,1)}, bf16[256,1536]{1,0:T(8,128)(2,1)S(1)}, u32[]{:S(2)}, u32[]{:S(2)}) collective-permute-start(bf16[256,1536]{1,0:T(8,128)(2,1)} %refs_5_.1), channel_id=1, source_target_pairs={{0,2},{1,3},{2,0},{3,1},{4,6},{5,7},{6,4},{7,5},{8,10},{9,11},{10,... | collective-permute-start | bytes 2359304 | tf_op jit(solution)/shard_map/ppermute | solution.py:785
  10.2 25.0 %collective-permute-start.1 = (bf16[256,1536]{1,0:T(8,128)(2,1)}, bf16[256,1536]{1,0:T(8,128)(2,1)S(1)}, u32[]{:S(2)}, u32[]{:S(2)}) collective-permute-start(bf16[256,1536]{1,0:T(8,128)(2,1)} %refs_5_.1), channel_id=1, source_target_pairs={{0,16},{1,17},{2,18},{3,19},{4,20},{5,21},{6,22},{7,23},{8,24},{9,... | collective-permute-start | bytes 2359304 | tf_op jit(solution)/shard_map/ppermute | solution.py:785
  14.1 30.7 %collective-permute-start.2 = (bf16[256,1536]{1,0:T(8,128)(2,1)}, bf16[256,1536]{1,0:T(8,128)(2,1)S(1)}, u32[]{:S(2)}, u32[]{:S(2)}) collective-permute-start(bf16[256,1536]{1,0:T(8,128)(2,1)} %convert_element_type.163), channel_id=1, source_target_pairs={{0,2},{1,3},{2,0},{3,1},{4,6},{5,7},{6,4},{7,5},{8,10},{9,11},{10,... | collective-permute-start | bytes 2359304 | tf_op jit(solution)/shard_map/ppermute | solution.py:785
  14.7 31.7 %collective-permute-start.3 = (bf16[256,1536]{1,0:T(8,128)(2,1)}, bf16[256,1536]{1,0:T(8,128)(2,1)}, u32[]{:S(2)}, u32[]{:S(2)}) collective-permute-start(bf16[256,1536]{1,0:T(8,128)(2,1)} %convert_element_type.163), channel_id=1, source_target_pairs={{0,16},{1,17},{2,18},{3,19},{4,20},{5,21},{6,22},{7,23},{8,24},{9,... | collective-permute-start | bytes 2359304 | tf_op jit(solution)/shard_map/ppermute | solution.py:785
  16.6 175.6 %all-gather.5.cloned.1.call-start = ((), (), s32[]{:S(2)}) async-start(), calls=%async_computation.3 | async-start | bytes 5898240 | tf_op jit(solution)/shard_map/all_gather | solution.py:791
  100.6 281.1 %reduce-scatter.3.cloned.1.call-start = ((), (), s32[]{:S(2)}) async-start(), calls=%async_computation.4 | async-start | bytes 5898240 | tf_op jit(solution)/shard_map/reduce_scatter | solution.py:794
  112.2 34.4 %collective-permute-start.19 = (bf16[192,1536]{1,0:T(8,128)(2,1)}, bf16[192,1536]{1,0:T(8,128)(2,1)S(1)}, u32[]{:S(2)}, u32[]{:S(2)}) collective-permute-start(bf16[192,1536]{1,0:T(8,128)(2,1)} %get-tuple-element.254), channel_id=1, source_target_pairs={{0,2},{1,3},{2,0},{3,1},{4,6},{5,7},{6,4},{7,5},{8,10},{9,11},{10,... | collective-permute-start | bytes 1769480 | tf_op jit(solution)/shard_map/ppermute | solution.py:785
  113.2 33.4 %collective-permute-start.20 = (bf16[192,1536]{1,0:T(8,128)(2,1)}, bf16[192,1536]{1,0:T(8,128)(2,1)S(1)}, u32[]{:S(2)}, u32[]{:S(2)}) collective-permute-start(bf16[192,1536]{1,0:T(8,128)(2,1)} %get-tuple-element.254), channel_id=1, source_target_pairs={{0,16},{1,17},{2,18},{3,19},{4,20},{5,21},{6,22},{7,23},{8,24},{9,... | collective-permute-start | bytes 1769480 | tf_op jit(solution)/shard_map/ppermute | solution.py:785
  114.7 32.0 %collective-permute-start.21 = (bf16[192,1536]{1,0:T(8,128)(2,1)}, bf16[192,1536]{1,0:T(8,128)(2,1)S(1)}, u32[]{:S(2)}, u32[]{:S(2)}) collective-permute-start(bf16[192,1536]{1,0:T(8,128)(2,1)} %get-tuple-element.254), channel_id=1, source_target_pairs={{0,18},{1,19},{2,16},{3,17},{4,22},{5,23},{6,20},{7,21},{8,26},{9,... | collective-permute-start | bytes 1769480 | tf_op jit(solution)/shard_map/ppermute | solution.py:785
  164.0 20.2 %collective-permute-start.23 = (bf16[256,1536]{1,0:T(8,128)(2,1)}, bf16[256,1536]{1,0:T(8,128)(2,1)S(1)}, u32[]{:S(2)}, u32[]{:S(2)}) collective-permute-start(bf16[256,1536]{1,0:T(8,128)(2,1)} %get-tuple-element.276), channel_id=1, source_target_pairs={{0,2},{1,3},{2,0},{3,1},{4,6},{5,7},{6,4},{7,5},{8,10},{9,11},{10,... | collective-permute-start | bytes 2359304 | tf_op jit(solution)/shard_map/ppermute | solution.py:785
  165.0 19.9 %collective-permute-start.24 = (bf16[256,1536]{1,0:T(8,128)(2,1)}, bf16[256,1536]{1,0:T(8,128)(2,1)S(1)}, u32[]{:S(2)}, u32[]{:S(2)}) collective-permute-start(bf16[256,1536]{1,0:T(8,128)(2,1)} %get-tuple-element.276), channel_id=1, source_target_pairs={{0,16},{1,17},{2,18},{3,19},{4,20},{5,21},{6,22},{7,23},{8,24},{9,... | collective-permute-start | bytes 2359304 | tf_op jit(solution)/shard_map/ppermute | solution.py:785
  205.7 41.2 %collective-permute-start.31 = (bf16[576,1536]{1,0:T(8,128)(2,1)}, bf16[576,1536]{1,0:T(8,128)(2,1)S(1)}, u32[]{:S(2)}, u32[]{:S(2)}) collective-permute-start(bf16[576,1536]{1,0:T(8,128)(2,1)} %get-tuple-element.304.refs_3_), channel_id=1, source_target_pairs={{0,2},{1,3},{2,0},{3,1},{4,6},{5,7},{6,4},{7,5},{8,10},{9,11},{10,... | collective-permute-start | bytes 5308424 | tf_op jit(solution)/shard_map/ppermute | solution.py:785
  207.2 41.0 %collective-permute-start.32 = (bf16[576,1536]{1,0:T(8,128)(2,1)}, bf16[576,1536]{1,0:T(8,128)(2,1)S(1)}, u32[]{:S(2)}, u32[]{:S(2)}) collective-permute-start(bf16[576,1536]{1,0:T(8,128)(2,1)} %get-tuple-element.304.refs_3_), channel_id=1, source_target_pairs={{0,16},{1,17},{2,18},{3,19},{4,20},{5,21},{6,22},{7,23},{8,24},{9,... | collective-permute-start | bytes 5308424 | tf_op jit(solution)/shard_map/ppermute | solution.py:785
  237.2 19.7 %collective-permute-start.29 = (bf16[512,1536]{1,0:T(8,128)(2,1)}, bf16[512,1536]{1,0:T(8,128)(2,1)}, u32[]{:S(2)}, u32[]{:S(2)}) collective-permute-start(bf16[512,1536]{1,0:T(8,128)(2,1)} %get-tuple-element.301), channel_id=1, source_target_pairs={{0,1},{1,0},{2,3},{3,2},{4,5},{5,4},{6,7},{7,6},{8,9},{9,8},{10,11... | collective-permute-start | bytes 4718600 | tf_op jit(solution)/shard_map/ppermute | solution.py:785
  266.3 21.3 %collective-permute-start.37 = (bf16[576,1536]{1,0:T(8,128)(2,1)}, bf16[576,1536]{1,0:T(8,128)(2,1)S(1)}, u32[]{:S(2)}, u32[]{:S(2)}) collective-permute-start(bf16[576,1536]{1,0:T(8,128)(2,1)} %get-tuple-element.325.refs_6_), channel_id=1, source_target_pairs={{0,1},{1,0},{2,3},{3,2},{4,5},{5,4},{6,7},{7,6},{8,9},{9,8},{10,11... | collective-permute-start | bytes 5308424 | tf_op jit(solution)/shard_map/ppermute | solution.py:785
  266.3 21.3 %collective-permute-start.38 = (bf16[576,1536]{1,0:T(8,128)(2,1)}, bf16[576,1536]{1,0:T(8,128)(2,1)S(1)}, u32[]{:S(2)}, u32[]{:S(2)}) collective-permute-start(bf16[576,1536]{1,0:T(8,128)(2,1)} %get-tuple-element.326.refs_7_), channel_id=1, source_target_pairs={{0,1},{1,0},{2,3},{3,2},{4,5},{5,4},{6,7},{7,6},{8,9},{9,8},{10,11... | collective-permute-start | bytes 5308424 | tf_op jit(solution)/shard_map/ppermute | solution.py:785
  266.8 20.9 %collective-permute-start.39 = (bf16[576,1536]{1,0:T(8,128)(2,1)}, bf16[576,1536]{1,0:T(8,128)(2,1)}, u32[]{:S(2)}, u32[]{:S(2)}) collective-permute-start(bf16[576,1536]{1,0:T(8,128)(2,1)} %get-tuple-element.327.refs_8_), channel_id=1, source_target_pairs={{0,1},{1,0},{2,3},{3,2},{4,5},{5,4},{6,7},{7,6},{8,9},{9,8},{10,11... | collective-permute-start | bytes 5308424 | tf_op jit(solution)/shard_map/ppermute | solution.py:785
  266.8 20.3 %collective-permute-start.35 = (bf16[256,1536]{1,0:T(8,128)(2,1)}, bf16[256,1536]{1,0:T(8,128)(2,1)}, u32[]{:S(2)}, u32[]{:S(2)}) collective-permute-start(bf16[256,1536]{1,0:T(8,128)(2,1)} %get-tuple-element.316), channel_id=1, source_target_pairs={{0,2},{1,3},{2,0},{3,1},{4,6},{5,7},{6,4},{7,5},{8,10},{9,11},{10,... | collective-permute-start | bytes 2359304 | tf_op jit(solution)/shard_map/ppermute | solution.py:785
  267.6 20.0 %collective-permute-start.36 = (bf16[256,1536]{1,0:T(8,128)(2,1)}, bf16[256,1536]{1,0:T(8,128)(2,1)}, u32[]{:S(2)}, u32[]{:S(2)}) collective-permute-start(bf16[256,1536]{1,0:T(8,128)(2,1)} %get-tuple-element.317), channel_id=1, source_target_pairs={{0,16},{1,17},{2,18},{3,19},{4,20},{5,21},{6,22},{7,23},{8,24},{9,... | collective-permute-start | bytes 2359304 | tf_op jit(solution)/shard_map/ppermute | solution.py:785
  289.4 153.1 %reduce-scatter.5.cloned.1.call-start = ((), (), s32[]{:S(2)}) async-start(), calls=%async_computation.5 | async-start | bytes 2211840 | tf_op jit(solution)/shard_map/reduce_scatter | solution.py:794
  289.6 49.0 %collective-permute-start.28 = (bf16[512,1536]{1,0:T(8,128)(2,1)}, bf16[512,1536]{1,0:T(8,128)(2,1)}, u32[]{:S(2)}, u32[]{:S(2)}) collective-permute-start(bf16[512,1536]{1,0:T(8,128)(2,1)} %get-tuple-element.296), channel_id=1, source_target_pairs={{0,1},{1,0},{2,3},{3,2},{4,5},{5,4},{6,7},{7,6},{8,9},{9,8},{10,11... | collective-permute-start | bytes 4718600 | tf_op jit(solution)/shard_map/ppermute | solution.py:785
  290.5 39.6 %collective-permute-start.40 = (bf16[256,1536]{1,0:T(8,128)(2,1)S(1)}, bf16[256,1536]{1,0:T(8,128)(2,1)S(1)}, u32[]{:S(2)}, u32[]{:S(2)}) collective-permute-start(bf16[256,1536]{1,0:T(8,128)(2,1)S(1)} %copy-done.19), channel_id=1, source_target_pairs={{0,16},{1,3},{2,18},{3,1},{4,20},{5,7},{6,22},{7,5},{8,24},{9,11},... | collective-permute-start | bytes 2359304 | tf_op jit(solution)/shard_map/ppermute | solution.py:973
  300.7 29.4 %collective-permute-start.41 = (bf16[288,1536]{1,0:T(8,128)(2,1)}, bf16[288,1536]{1,0:T(8,128)(2,1)S(1)}, u32[]{:S(2)}, u32[]{:S(2)}) collective-permute-start(bf16[288,1536]{1,0:T(8,128)(2,1)} %get-tuple-element.337), channel_id=1, source_target_pairs={{0,2},{1,3},{2,0},{3,1},{4,6},{5,7},{6,4},{7,5},{8,10},{9,11},{10,... | collective-permute-start | bytes 2654216 | tf_op jit(solution)/shard_map/ppermute | solution.py:785
  301.9 28.2 %collective-permute-start.42 = (bf16[288,1536]{1,0:T(8,128)(2,1)}, bf16[288,1536]{1,0:T(8,128)(2,1)S(1)}, u32[]{:S(2)}, u32[]{:S(2)}) collective-permute-start(bf16[288,1536]{1,0:T(8,128)(2,1)} %get-tuple-element.338), channel_id=1, source_target_pairs={{0,16},{1,17},{2,18},{3,19},{4,20},{5,21},{6,22},{7,23},{8,24},{9,... | collective-permute-start | bytes 2654216 | tf_op jit(solution)/shard_map/ppermute | solution.py:785
  338.6 20.1 %collective-permute-start.48 = (bf16[576,256]{1,0:T(8,128)(2,1)}, bf16[576,256]{1,0:T(8,128)(2,1)}, u32[]{:S(2)}, u32[]{:S(2)}) collective-permute-start(bf16[576,256]{1,0:T(8,128)(2,1)} %get-tuple-element.361.refs_18_), channel_id=1, source_target_pairs={{0,1},{1,0},{2,3},{3,2},{4,5},{5,4},{6,7},{7,6},{8,9},{9,8},{10,11... | collective-permute-start | bytes 884744 | tf_op jit(solution)/shard_map/ppermute | solution.py:785
  338.6 20.2 %collective-permute-start.49 = (bf16[576,256]{1,0:T(8,128)(2,1)}, bf16[576,256]{1,0:T(8,128)(2,1)}, u32[]{:S(2)}, u32[]{:S(2)}) collective-permute-start(bf16[576,256]{1,0:T(8,128)(2,1)} %get-tuple-element.362.refs_19_), channel_id=1, source_target_pairs={{0,3},{1,2},{2,1},{3,0},{4,7},{5,6},{6,5},{7,4},{8,11},{9,10},{10,... | collective-permute-start | bytes 884744 | tf_op jit(solution)/shard_map/ppermute | solution.py:785
  381.7 22.5 %collective-permute-start.57 = (bf16[192,1536]{1,0:T(8,128)(2,1)}, bf16[192,1536]{1,0:T(8,128)(2,1)S(1)}, u32[]{:S(2)}, u32[]{:S(2)}) collective-permute-start(bf16[192,1536]{1,0:T(8,128)(2,1)} %get-tuple-element.418), channel_id=1, source_target_pairs={{0,16},{1,17},{2,18},{3,19},{4,20},{5,21},{6,22},{7,23},{8,24},{9,... | collective-permute-start | bytes 1769480 | tf_op jit(solution)/shard_map/ppermute | solution.py:785
  383.0 21.3 %collective-permute-start.56 = (bf16[192,1536]{1,0:T(8,128)(2,1)}, bf16[192,1536]{1,0:T(8,128)(2,1)}, u32[]{:S(2)}, u32[]{:S(2)}) collective-permute-start(bf16[192,1536]{1,0:T(8,128)(2,1)} %get-tuple-element.417), channel_id=1, source_target_pairs={{0,2},{1,3},{2,0},{3,1},{4,6},{5,7},{6,4},{7,5},{8,10},{9,11},{10,... | collective-permute-start | bytes 1769480 | tf_op jit(solution)/shard_map/ppermute | solution.py:785
  383.9 53.2 %collective-permute-start.54 = (bf16[256,1536]{1,0:T(8,128)(2,1)}, bf16[256,1536]{1,0:T(8,128)(2,1)}, u32[]{:S(2)}, u32[]{:S(2)}) collective-permute-start(bf16[256,1536]{1,0:T(8,128)(2,1)} %get-tuple-element.397), channel_id=1, source_target_pairs={{0,2},{1,3},{2,0},{3,1},{4,6},{5,7},{6,4},{7,5},{8,10},{9,11},{10,... | collective-permute-start | bytes 2359304 | tf_op jit(solution)/shard_map/ppermute | solution.py:785
  385.2 51.9 %collective-permute-start.55 = (bf16[256,1536]{1,0:T(8,128)(2,1)}, bf16[256,1536]{1,0:T(8,128)(2,1)}, u32[]{:S(2)}, u32[]{:S(2)}) collective-permute-start(bf16[256,1536]{1,0:T(8,128)(2,1)} %get-tuple-element.398), channel_id=1, source_target_pairs={{0,16},{1,17},{2,18},{3,19},{4,20},{5,21},{6,22},{7,23},{8,24},{9,... | collective-permute-start | bytes 2359304 | tf_op jit(solution)/shard_map/ppermute | solution.py:785
  385.9 53.7 %collective-permute-start.53 = (bf16[384,1536]{1,0:T(8,128)(2,1)}, bf16[384,1536]{1,0:T(8,128)(2,1)}, u32[]{:S(2)}, u32[]{:S(2)}) collective-permute-start(bf16[384,1536]{1,0:T(8,128)(2,1)} %get-tuple-element.396), channel_id=1, source_target_pairs={{0,16},{1,17},{2,18},{3,19},{4,20},{5,21},{6,22},{7,23},{8,24},{9,... | collective-permute-start | bytes 3538952 | tf_op jit(solution)/shard_map/ppermute | solution.py:785
  (107 other events, 741.1 us)
Sparse Core Ops, SparseCore 0:
  16.7 52.4 all-gather.2
  100.7 91.5 all-gather.4
  289.5 84.1 reduce-scatter.2
  387.3 40.5 reduce-scatter.4
